TPU v7x, 32 devices: a whole 2x2x4 slice. The times are simulated.
32 devices in a mesh: dp: 8 (over z, x), tensor: 4 (over y, core).
Axes of the slice: x: 2, y: 2, z: 4, core: 2. Of those that a mesh axis runs over, the one named last changes fastest.
Arguments:
- token_ids: int32 [16, 1024], P('dp', 'tensor'), may hold values from 0 to 32
- mask_pos: int32 [16, 160], P('dp'), may hold values from 0 to 1023, as said below
- mask_target: int32 [16, 160], P('dp'), may hold values from 0 to 32
- mask_count: int32 [16], P('dp'), may hold values from 1 to 160, as said below
- weight_in: float32 [2, 480, 1440], P(None, 'dp', 'tensor'), may hold values from -0.25 to 0.25
- weight_out: float32 [2, 480, 480], P(None, 'tensor', 'dp'), may hold values from -6 to 6
- weight_up: float32 [2, 480, 1920], P(None, 'dp', 'tensor'), may hold values from -0.25 to 0.25
- weight_down: float32 [2, 1920, 480], P(None, 'tensor', 'dp'), may hold values from -0.125 to 0.125
- norm_params: float32 [10, 480], replicated, may hold values from -2 to 2, as said below
- vocab_table: float32 [33, 480], replicated, may hold values from -0.6 to 0.6
- first_in: float32 [2, 480, 1440], P(None, 'dp', 'tensor'), may hold values from -0.0078125 to 0.0078125
- first_out: float32 [2, 480, 480], P(None, 'tensor', 'dp'), may hold values from -0.0078125 to 0.0078125
- first_up: float32 [2, 480, 1920], P(None, 'dp', 'tensor'), may hold values from -0.0078125 to 0.0078125
- first_down: float32 [2, 1920, 480], P(None, 'tensor', 'dp'), may hold values from -0.0078125 to 0.0078125
- first_norm: float32 [10, 480], replicated, may hold values from -0.25 to 0.25
- first_vocab: float32 [33, 480], replicated, may hold values from -0.25 to 0.25
- second_in: float32 [2, 480, 1440], P(None, 'dp', 'tensor'), may hold values from 1.9929846e-06 to 7.971938e-06
- second_out: float32 [2, 480, 480], P(None, 'tensor', 'dp'), may hold values from 1.9929846e-06 to 7.971938e-06
- second_up: float32 [2, 480, 1920], P(None, 'dp', 'tensor'), may hold values from 1.9929846e-06 to 7.971938e-06
- second_down: float32 [2, 1920, 480], P(None, 'tensor', 'dp'), may hold values from 1.9929846e-06 to 7.971938e-06
- second_norm: float32 [10, 480], replicated, may hold values from 0.00390625 to 0.015625
- second_vocab: float32 [33, 480], replicated, may hold values from 0.00390625 to 0.015625
Outputs:
- loss_total: float32 [], replicated
- mask_total: float32 [], replicated
- master_in: float32 [2, 480, 1440], P(None, 'dp', 'tensor')
- master_out: float32 [2, 480, 480], P(None, 'tensor', 'dp')
- master_up: float32 [2, 480, 1920], P(None, 'dp', 'tensor')
- master_down: float32 [2, 1920, 480], P(None, 'tensor', 'dp')
- master_norm: float32 [10, 480], replicated
- master_vocab: float32 [33, 480], replicated
- mean_in: float32 [2, 480, 1440], P(None, 'dp', 'tensor')
- mean_out: float32 [2, 480, 480], P(None, 'tensor', 'dp')
- mean_up: float32 [2, 480, 1920], P(None, 'dp', 'tensor')
- mean_down: float32 [2, 1920, 480], P(None, 'tensor', 'dp')
- mean_norm: float32 [10, 480], replicated
- mean_vocab: float32 [33, 480], replicated
- square_in: float32 [2, 480, 1440], P(None, 'dp', 'tensor')
- square_out: float32 [2, 480, 480], P(None, 'tensor', 'dp')
- square_up: float32 [2, 480, 1920], P(None, 'dp', 'tensor')
- square_down: float32 [2, 1920, 480], P(None, 'tensor', 'dp')
- square_norm: float32 [10, 480], replicated
- square_vocab: float32 [33, 480], replicated
- copy_in: bfloat16 [2, 480, 1440], P(None, 'dp', 'tensor')
- copy_out: bfloat16 [2, 480, 480], P(None, 'tensor', 'dp')
- copy_up: bfloat16 [2, 480, 1920], P(None, 'dp', 'tensor')
- copy_down: bfloat16 [2, 1920, 480], P(None, 'tensor', 'dp')
- copy_vocab: bfloat16 [33, 480], replicated
Inputs may be any that keep to these rules, and one draw needn't show every extreme that they name: `mask_pos`: positions within one sequence; the 160 slots of a sequence name distinct positions. `mask_count`: slots below a sequence's count are live, the others are ignored; the last sequence has all 160 live. `norm_params`: even rows near one, odd rows of both signs.
All inputs are finite; a program needn't handle non-finite values.
Results may differ from a plain program's by a relative error of at most 0.0016.
The roundings to bfloat16 on the way count: a program that leaves them out, or rounds other values in their place, can miss the bound.
Values may be sent and summed in bfloat16 or wider, within the bound.
No kernel may reach another device: no remote copies, remote signals or barrier semaphores. Data moves between devices by JAX's collectives and lax.ppermute only.
A program may use at most 320 MiB of HBM per device.

v0:
```python
import jax
import jax.numpy as jnp
from jax import lax
from jax.sharding import PartitionSpec as P

HEAD = 24
STEP = 5


norm_eps = 1e-05
step_rates = (0.02, 0.3, 0.02, 0.02, 0.3, 0.05)
beta_first = 0.5
beta_second = 0.5
adam_eps = 1e-08
weight_decay = 0.01
highest = lax.Precision.HIGHEST
brain = jnp.bfloat16
protein_chain = jnp.float32


def normalize_features(resid, gain, shift):
    centre = resid - jnp.mean(resid, -1, keepdims=True)
    spread = jnp.mean(centre * centre, -1, keepdims=True)
    return centre * lax.rsqrt(spread + norm_eps) * gain + shift


def rotary_tables(length, size):
    half_size = size // 2
    freqs = 10000.0 ** (-jnp.arange(half_size, dtype=jnp.float32) * 2.0 / size)
    angles = jnp.arange(length, dtype=jnp.float32)[:, None] * freqs[None, :]
    return (jnp.cos(angles)[:, None, :], jnp.sin(angles)[:, None, :])


def rotate(values, cosine, sine):
    half_size = values.shape[-1] // 2
    first, second = (values[..., :half_size], values[..., half_size:])
    return jnp.concatenate([first * cosine - second * sine, second * cosine + first * sine], -1)


def unrotate(grads, cosine, sine):
    half_size = grads.shape[-1] // 2
    first, second = (grads[..., :half_size], grads[..., half_size:])
    return jnp.concatenate([first * cosine + second * sine, second * cosine - first * sine], -1)


def attend_block(query, keys, values, scale):
    scores = (
        jnp.einsum("sqhe,skhe->shqk", query, keys, preferred_element_type=protein_chain) * scale
    )
    row_peak = jnp.max(scores, -1, keepdims=True)
    weights = jnp.exp(scores - row_peak)
    row_total = jnp.sum(weights, -1, keepdims=True)
    softmax_rows = (weights / row_total).astype(brain)
    blended_tokens = jnp.einsum(
        "shqk,skhe->sqhe", softmax_rows, values, preferred_element_type=protein_chain
    )
    return (blended_tokens, (row_peak + jnp.log(row_total))[..., 0])


def attend_back(query, keys, values, gradient_mixed_rows, logsum, scale):
    scores = (
        jnp.einsum("sqhe,skhe->shqk", query, keys, preferred_element_type=protein_chain) * scale
    )
    softmax_rows = jnp.exp(scores - logsum[..., None])
    grad_rows = jnp.einsum(
        "sqhe,skhe->shqk", gradient_mixed_rows, values, preferred_element_type=protein_chain
    )
    inner = jnp.sum(softmax_rows * grad_rows, -1, keepdims=True)
    grad_scores = (softmax_rows * (grad_rows - inner)).astype(brain)
    grad_query = (
        jnp.einsum("shqk,skhe->sqhe", grad_scores, keys, preferred_element_type=protein_chain)
        * scale
    )
    grad_keys = (
        jnp.einsum("shqk,sqhe->skhe", grad_scores, query, preferred_element_type=protein_chain)
        * scale
    )
    grad_values = jnp.einsum(
        "shqk,sqhe->skhe",
        softmax_rows.astype(brain),
        gradient_mixed_rows,
        preferred_element_type=protein_chain,
    )
    return (grad_query, grad_keys, grad_values)


def forward_layer(resid, weights, gains, cosine, sine, scale, block):
    input_matrix, projection_result, up_matrix, down_matrix = weights
    normed = normalize_features(resid, gains[0], gains[1]).astype(brain)
    whole_sequence = lax.all_gather(normed, "tensor", axis=1, tiled=True)
    seq_count, length = (whole_sequence.shape[0], whole_sequence.shape[1])
    packed_rows = jnp.einsum(
        "awf,fr->awr", whole_sequence, input_matrix, preferred_element_type=protein_chain
    )
    packed_rows = packed_rows.reshape(seq_count, length, -1, 3, HEAD)
    query = rotate(packed_rows[:, :, :, 0], cosine, sine).astype(brain)
    keys = rotate(packed_rows[:, :, :, 1], cosine, sine).astype(brain)
    values = packed_rows[:, :, :, 2].astype(brain)
    outputs = []
    logsums = []
    for start in range(0, length, block):
        mixed_part, logsum_part = attend_block(query[:, start : start + block], keys, values, scale)
        outputs.append(mixed_part)
        logsums.append(logsum_part)
    blended_tokens = jnp.concatenate(outputs, 1).reshape(seq_count, length, -1).astype(brain)
    logsum = jnp.concatenate(logsums, 2)
    attended = lax.psum_scatter(
        jnp.einsum(
            "xok,kr->xor", blended_tokens, projection_result, preferred_element_type=protein_chain
        ),
        "tensor",
        scatter_dimension=1,
        tiled=True,
    )
    resid_mid = resid + attended
    normed_mid = normalize_features(resid_mid, gains[2], gains[3]).astype(brain)
    whole_sequence_middle = lax.all_gather(normed_mid, "tensor", axis=1, tiled=True)
    hidden_state = jnp.einsum(
        "kjo,op->kjp", whole_sequence_middle, up_matrix, preferred_element_type=protein_chain
    )
    active_rows = jax.nn.gelu(hidden_state, approximate=False).astype(brain)
    feed = lax.psum_scatter(
        jnp.einsum("rbq,qy->rby", active_rows, down_matrix, preferred_element_type=protein_chain),
        "tensor",
        scatter_dimension=1,
        tiled=True,
    )
    saved = (
        resid,
        whole_sequence,
        query,
        keys,
        values,
        blended_tokens,
        logsum,
        resid_mid,
        whole_sequence_middle,
        hidden_state,
        active_rows,
    )
    return (resid_mid + feed, saved)


def backward_layer(grad_resid, saved, weights, gains, cosine, sine, scale, block):
    (
        resid,
        whole_sequence,
        query,
        keys,
        values,
        blended_tokens,
        logsum,
        resid_mid,
        whole_sequence_middle,
        hidden_state,
        active_rows,
    ) = saved
    input_matrix, projection_result, up_matrix, down_matrix = weights
    gradient_feedforward = lax.all_gather(grad_resid.astype(brain), "tensor", axis=1, tiled=True)
    gradient_down_weight = jnp.einsum(
        "nyg,nyt->gt", active_rows, gradient_feedforward, preferred_element_type=protein_chain
    )
    gradient_active_rows = jnp.einsum(
        "xou,eu->xoe", gradient_feedforward, down_matrix, preferred_element_type=protein_chain
    )
    _, gelu_back = jax.vjp(lambda inner: jax.nn.gelu(inner, approximate=False), hidden_state)
    gradient_hidden_state = gelu_back(gradient_active_rows)[0].astype(brain)
    gradient_up_weight = jnp.einsum(
        "cqz,cqk->zk",
        whole_sequence_middle,
        gradient_hidden_state,
        preferred_element_type=protein_chain,
    )
    grad_normed_mid = lax.psum_scatter(
        jnp.einsum(
            "erj,aj->era", gradient_hidden_state, up_matrix, preferred_element_type=protein_chain
        ),
        "tensor",
        scatter_dimension=1,
        tiled=True,
    )
    _, norm_back = jax.vjp(normalize_features, resid_mid, gains[2], gains[3])
    grad_mid, gain_two, shift_two = norm_back(grad_normed_mid)
    grad_mid = grad_mid + grad_resid
    gradient_attention = lax.all_gather(grad_mid.astype(brain), "tensor", axis=1, tiled=True)
    seq_count, length = (gradient_attention.shape[0], gradient_attention.shape[1])
    gradient_output_weight = jnp.einsum(
        "beu,bev->uv", blended_tokens, gradient_attention, preferred_element_type=protein_chain
    )
    gradient_mixed_rows = jnp.einsum(
        "zwb,vb->zwv", gradient_attention, projection_result, preferred_element_type=protein_chain
    ).astype(brain)
    gradient_mixed_rows = gradient_mixed_rows.reshape(seq_count, length, -1, HEAD)
    grad_keys = jnp.zeros(keys.shape, protein_chain)
    grad_values = jnp.zeros(values.shape, protein_chain)
    query_parts = []
    for start in range(0, length, block):
        part_query, part_keys, part_values = attend_back(
            query[:, start : start + block],
            keys,
            values,
            gradient_mixed_rows[:, start : start + block],
            logsum[:, :, start : start + block],
            scale,
        )
        query_parts.append(part_query)
        grad_keys = grad_keys + part_keys
        grad_values = grad_values + part_values
    grad_query = unrotate(jnp.concatenate(query_parts, 1), cosine, sine)
    grad_keys = unrotate(grad_keys, cosine, sine)
    gradient_packed_rows = (
        jnp.stack([grad_query, grad_keys, grad_values], 3)
        .reshape(seq_count, length, -1)
        .astype(brain)
    )
    gradient_input_weight = jnp.einsum(
        "pfz,pfh->zh", whole_sequence, gradient_packed_rows, preferred_element_type=protein_chain
    )
    grad_whole = lax.psum_scatter(
        jnp.einsum(
            "hft,wt->hfw", gradient_packed_rows, input_matrix, preferred_element_type=protein_chain
        ),
        "tensor",
        scatter_dimension=1,
        tiled=True,
    )
    _, norm_back = jax.vjp(normalize_features, resid, gains[0], gains[1])
    grad_low, gain_one, shift_one = norm_back(grad_whole)
    grad_gains = jnp.stack([gain_one, shift_one, gain_two, shift_two])
    return (
        grad_low + grad_mid,
        (gradient_input_weight, gradient_output_weight, gradient_up_weight, gradient_down_weight),
        grad_gains,
    )


def adamw(master, first, second, grad, step_rate):
    mean = beta_first * first + (1.0 - beta_first) * grad
    square = beta_second * second + (1.0 - beta_second) * grad * grad
    corrected = mean / (1.0 - beta_first**STEP)
    rescaled_values = square / (1.0 - beta_second**STEP)
    fresh = master - step_rate * (
        corrected / (jnp.sqrt(rescaled_values) + adam_eps) + weight_decay * master
    )
    return (fresh, mean, square)


def shards(
    token_ids,
    mask_pos,
    mask_target,
    mask_count,
    weight_in,
    weight_out,
    weight_up,
    weight_down,
    norm_params,
    vocab_table,
    first_in,
    first_out,
    first_up,
    first_down,
    first_norm,
    first_vocab,
    second_in,
    second_out,
    second_up,
    second_down,
    second_norm,
    second_vocab,
):
    layer_total = weight_in.shape[0]
    local_len = token_ids.shape[1]
    length = local_len * lax.axis_size("tensor")
    vocab = vocab_table.shape[0]
    slot_count = mask_pos.shape[1]
    count_total = lax.psum(jnp.sum(mask_count).astype(protein_chain), "dp")
    gathered = (
        lax.all_gather(weight_in.astype(brain), "dp", axis=1, tiled=True),
        lax.all_gather(weight_out.astype(brain), "dp", axis=2, tiled=True),
        lax.all_gather(weight_up.astype(brain), "dp", axis=1, tiled=True),
        lax.all_gather(weight_down.astype(brain), "dp", axis=2, tiled=True),
    )
    vocab_low = vocab_table.astype(brain)
    cosine, sine = rotary_tables(length, HEAD)
    scale = HEAD ** (-0.5)
    block = min(512, length)
    token_hot = token_ids[:, :, None] == jnp.arange(vocab)[None, None, :]
    resid = jnp.einsum(
        "sqv,vd->sqd", token_hot.astype(brain), vocab_low, preferred_element_type=protein_chain
    )
    kept = []
    for layer_at in range(layer_total):
        layer_weights = tuple((matrix[layer_at] for matrix in gathered))
        resid, saved = forward_layer(
            resid,
            layer_weights,
            norm_params[4 * layer_at : 4 * layer_at + 4],
            cosine,
            sine,
            scale,
            block,
        )
        kept.append(saved)
    final_gain = norm_params[4 * layer_total]
    final_shift = norm_params[4 * layer_total + 1]
    final = normalize_features(resid, final_gain, final_shift).astype(brain)
    offset = lax.axis_index("tensor") * local_len
    live = jnp.arange(slot_count)[None, :] < mask_count[:, None]
    where_hot = ((mask_pos - offset)[:, :, None] == jnp.arange(local_len)[None, None, :]) & live[
        :, :, None
    ]
    picked = jnp.einsum(
        "smq,sqd->smd", where_hot.astype(brain), final, preferred_element_type=protein_chain
    ).astype(brain)
    present = jnp.sum(where_hot.astype(protein_chain), -1)
    logits = jnp.einsum("smd,vd->smv", picked, vocab_low, preferred_element_type=protein_chain)
    row_peak = jnp.max(logits, -1, keepdims=True)
    logsum = row_peak[..., 0] + jnp.log(jnp.sum(jnp.exp(logits - row_peak), -1))
    target_hot = (mask_target[:, :, None] == jnp.arange(vocab)[None, None, :]).astype(protein_chain)
    target_logit = jnp.sum(logits * target_hot, -1)
    loss_local = jnp.sum((logsum - target_logit) * present)
    grad_logits = (
        (jnp.exp(logits - logsum[..., None]) - target_hot) * (present / count_total)[..., None]
    ).astype(brain)
    grad_vocab = jnp.einsum(
        "smv,smd->vd", grad_logits, picked, preferred_element_type=protein_chain
    )
    grad_picked = jnp.einsum(
        "smv,vd->smd", grad_logits, vocab_low, preferred_element_type=protein_chain
    )
    grad_final = jnp.einsum(
        "smq,smd->sqd", where_hot.astype(protein_chain), grad_picked, precision=highest
    )
    _, norm_back = jax.vjp(normalize_features, resid, final_gain, final_shift)
    grad_resid, grad_final_gain, grad_final_shift = norm_back(grad_final)
    layer_grads = [None] * layer_total
    gain_grads = [None] * layer_total
    for layer_at in reversed(range(layer_total)):
        layer_weights = tuple((matrix[layer_at] for matrix in gathered))
        grad_resid, layer_grads[layer_at], gain_grads[layer_at] = backward_layer(
            grad_resid,
            kept[layer_at],
            layer_weights,
            norm_params[4 * layer_at : 4 * layer_at + 4],
            cosine,
            sine,
            scale,
            block,
        )
    stacked = tuple((jnp.stack([entry[which] for entry in layer_grads]) for which in range(4)))
    stacked = (
        lax.psum_scatter(stacked[0], "dp", scatter_dimension=1, tiled=True),
        lax.psum_scatter(stacked[1], "dp", scatter_dimension=2, tiled=True),
        lax.psum_scatter(stacked[2], "dp", scatter_dimension=1, tiled=True),
        lax.psum_scatter(stacked[3], "dp", scatter_dimension=2, tiled=True),
    )
    grad_vocab = grad_vocab + jnp.einsum(
        "sqv,sqd->vd", token_hot.astype(protein_chain), grad_resid, precision=highest
    )
    grad_norms = jnp.concatenate(gain_grads + [jnp.stack([grad_final_gain, grad_final_shift])], 0)
    grad_norms, grad_vocab, loss_total = lax.psum(
        (grad_norms, grad_vocab, loss_local), ("dp", "tensor")
    )
    masters = (weight_in, weight_out, weight_up, weight_down, norm_params, vocab_table)
    firsts = (first_in, first_out, first_up, first_down, first_norm, first_vocab)
    elapsed_time = (second_in, second_out, second_up, second_down, second_norm, second_vocab)
    grads = (stacked[0], stacked[1], stacked[2], stacked[3], grad_norms, grad_vocab)
    results = [
        adamw(masters[which], firsts[which], elapsed_time[which], grads[which], step_rates[which])
        for which in range(6)
    ]
    news = [entry[0] for entry in results]
    means = [entry[1] for entry in results]
    squares = [entry[2] for entry in results]
    copies = [news[which].astype(brain) for which in (0, 1, 2, 3, 5)]
    return (
        loss_total,
        count_total,
        news[0],
        news[1],
        news[2],
        news[3],
        news[4],
        news[5],
        means[0],
        means[1],
        means[2],
        means[3],
        means[4],
        means[5],
        squares[0],
        squares[1],
        squares[2],
        squares[3],
        squares[4],
        squares[5],
        copies[0],
        copies[1],
        copies[2],
        copies[3],
        copies[4],
    )


def solution(mesh):
    placed = (
        P("dp", "tensor"),
        P("dp", None),
        P("dp", None),
        P("dp"),
        P(None, "dp", "tensor"),
        P(None, "tensor", "dp"),
        P(None, "dp", "tensor"),
        P(None, "tensor", "dp"),
        P(),
        P(),
        P(None, "dp", "tensor"),
        P(None, "tensor", "dp"),
        P(None, "dp", "tensor"),
        P(None, "tensor", "dp"),
        P(),
        P(),
        P(None, "dp", "tensor"),
        P(None, "tensor", "dp"),
        P(None, "dp", "tensor"),
        P(None, "tensor", "dp"),
        P(),
        P(),
    )
    return jax.shard_map(
        shards,
        mesh=mesh,
        in_specs=placed,
        out_specs=(
            P(),
            P(),
            P(None, "dp", "tensor"),
            P(None, "tensor", "dp"),
            P(None, "dp", "tensor"),
            P(None, "tensor", "dp"),
            P(),
            P(),
            P(None, "dp", "tensor"),
            P(None, "tensor", "dp"),
            P(None, "dp", "tensor"),
            P(None, "tensor", "dp"),
            P(),
            P(),
            P(None, "dp", "tensor"),
            P(None, "tensor", "dp"),
            P(None, "dp", "tensor"),
            P(None, "tensor", "dp"),
            P(),
            P(),
            P(None, "dp", "tensor"),
            P(None, "tensor", "dp"),
            P(None, "dp", "tensor"),
            P(None, "tensor", "dp"),
            P(),
        ),
        check_vma=False,
    )
```

profile of v0, /device:TPU:0, one launch (start us, length us, event | category | flops | bytes accessed | tf_op | source)
XLA Modules:
  0.0 1302.4 jit_solution(473719704592035950)
XLA Ops:
  11.9 33.7 %all_gather.37 = bf16[2,480,360]{2,0,1:T(2,128)(2,1)S(1)} all-gather(bf16[2,60,360]{2,0,1:T(2,128)(2,1)S(1)} %convert_element_type.182), channel_id=1, replica_groups=mesh['dp'=8,'tensor'=4] {'dp'}, dimensions={1}, use_global_device_ids=true | all-gather | bytes 777600 | tf_op jit(solution)/shard_map/all_gather | solution.py:279
  48.6 30.7 %all_gather.38 = bf16[2,120,480]{1,0,2:T(2,128)(2,1)S(1)} all-gather(bf16[2,120,60]{1,0,2:T(2,128)(2,1)S(1)} %convert_element_type.186), channel_id=1, replica_groups=mesh['dp'=8,'tensor'=4] {'dp'}, dimensions={2}, use_global_device_ids=true | all-gather | bytes 259200 | tf_op jit(solution)/shard_map/all_gather | solution.py:280
  88.6 9.3 multiply_reduce_fusion.7
  101.8 4.6 fusion.1
  106.5 9.2 fusion.58
  115.7 9.5 fusion
  125.2 9.2 fusion.59
  137.2 44.0 %reduce-scatter.9.cloned.1.call-done = f32[2,256,480]{1,2,0:T(8,128)} async-done(((f32[2,1024,480]{1,2,0:T(8,128)}), f32[2,256,480]{1,2,0:T(8,128)}) %reduce-scatter.9.cloned.1.call-update) | async-done | bytes 983056 | tf_op jit(solution)/shard_map/reduce_scatter | solution.py:107
  184.0 32.7 %all_gather.40 = bf16[2,480,480]{2,0,1:T(2,128)(2,1)S(1)} all-gather(bf16[2,60,480]{2,0,1:T(2,128)(2,1)S(1)} %convert_element_type.188), channel_id=1, replica_groups=mesh['dp'=8,'tensor'=4] {'dp'}, dimensions={1}, use_global_device_ids=true | all-gather | bytes 1036800 | tf_op jit(solution)/shard_map/all_gather | solution.py:281
  220.3 32.6 %all_gather.41 = bf16[2,480,480]{1,0,2:T(2,128)(2,1)S(1)} all-gather(bf16[2,480,60]{1,0,2:T(2,128)(2,1)S(1)} %convert_element_type.190), channel_id=1, replica_groups=mesh['dp'=8,'tensor'=4] {'dp'}, dimensions={2}, use_global_device_ids=true | all-gather | bytes 1036800 | tf_op jit(solution)/shard_map/all_gather | solution.py:282
  255.3 4.2 fusion.65
  259.6 9.8 multiply_convert_fusion.5
  274.0 43.5 %reduce-scatter.11.cloned.1.call-done = f32[2,256,480]{1,2,0:T(8,128)} async-done(((f32[2,1024,480]{1,2,0:T(8,128)}), f32[2,256,480]{1,2,0:T(8,128)}) %reduce-scatter.11.cloned.1.call-update) | async-done | bytes 983056 | tf_op jit(solution)/shard_map/reduce_scatter | solution.py:122
  321.5 20.8 %all-gather.13.cloned.1.call-done = bf16[2,1024,480]{1,2,0:T(8,128)(2,1)} async-done(((bf16[2,256,480]{1,2,0:T(8,128)(2,1)}), bf16[2,1024,480]{1,2,0:T(8,128)(2,1)}) %all-gather.13.cloned.1.call-update) | async-done | bytes 1966096 | tf_op jit(solution)/shard_map/all_gather | solution.py:90
  348.7 9.2 multiply_reduce_fusion.5
  362.0 4.6 fusion.3
  366.7 9.2 fusion.56
  375.9 9.5 fusion.2
  385.4 21.1 %fusion.57 = bf16[2,5,24,512]{3,2,1,0:T(8,128)(2,1)S(1)} fusion(f32[2,5,512,1024]{3,2,1,0:T(8,128)} %get-tuple-element.209, f32[2,5,512]{2,1,0:T(8,128)S(1)} %fusion.2, f32[2,5,512]{2,1,0:T(8,128)S(1)} %get-tuple-element.208, f32[2,1024,5,3,24]{1,4,3,2,0:T(8,128)S(1)} %fusion.32), kind=kOutput, calls=%fused_computation.123 | convolution fusion | flops 272752640 | bytes 21774336 | tf_op jit(solution)/shard_map/shqk,skhe->sqhe/dot_general | solution.py:54
  409.3 43.0 %reduce-scatter.13.cloned.1.call-done = f32[2,256,480]{1,2,0:T(8,128)} async-done(((f32[2,1024,480]{1,2,0:T(8,128)}), f32[2,256,480]{1,2,0:T(8,128)}) %reduce-scatter.13.cloned.1.call-update) | async-done | bytes 983056 | tf_op jit(solution)/shard_map/reduce_scatter | solution.py:107
  457.0 20.0 %all-gather.15.cloned.1.call-done = bf16[2,1024,480]{1,2,0:T(8,128)(2,1)} async-done(((bf16[2,256,480]{1,2,0:T(8,128)(2,1)}), bf16[2,1024,480]{1,2,0:T(8,128)(2,1)}) %all-gather.15.cloned.1.call-update) | async-done | bytes 1966096 | tf_op jit(solution)/shard_map/all_gather | solution.py:117
  481.1 9.8 multiply_convert_fusion.4
  496.7 21.9 %psum.29 = f32[]{:T(128)} all-reduce(f32[]{:T(128)S(6)} %convert_element_type.200), channel_id=1, replica_groups=mesh['dp'=8,'tensor'=4] {'dp'}, use_global_device_ids=true, to_apply=%region_29.0 | all-reduce | flops 1 | bytes 8 | tf_op jit(solution)/shard_map/psum | solution.py:277
  519.0 19.4 %reduce-scatter.15.cloned.1.call-done = f32[2,256,480]{1,2,0:T(8,128)} async-done(((f32[2,1024,480]{1,2,0:T(8,128)}), f32[2,256,480]{1,2,0:T(8,128)}) %reduce-scatter.15.cloned.1.call-update) | async-done | bytes 983056 | tf_op jit(solution)/shard_map/reduce_scatter | solution.py:122
  546.4 22.2 %all-gather.17.cloned.1.call-done = bf16[2,1024,480]{1,2,0:T(8,128)(2,1)} async-done(((bf16[2,256,480]{1,2,0:T(8,128)(2,1)}), bf16[2,1024,480]{1,2,0:T(8,128)(2,1)}) %all-gather.17.cloned.1.call-update) | async-done | bytes 1966096 | tf_op jit(solution)/shard_map/all_gather | solution.py:159
  568.6 6.6 add_convert_fusion.1
  579.8 43.0 %reduce-scatter.17.cloned.1.call-done = f32[2,256,480]{1,2,0:T(8,128)} async-done(((f32[2,1024,480]{1,2,0:T(8,128)}), f32[2,256,480]{1,2,0:T(8,128)}) %reduce-scatter.17.cloned.1.call-update) | async-done | bytes 983056 | tf_op jit(solution)/shard_map/reduce_scatter | solution.py:174
  632.0 20.6 %all-gather.19.cloned.1.call-done = bf16[2,1024,480]{1,2,0:T(8,128)(2,1)} async-done(((bf16[2,256,480]{1,2,0:T(8,128)(2,1)}), bf16[2,1024,480]{1,2,0:T(8,128)(2,1)}) %all-gather.19.cloned.1.call-update) | async-done | bytes 1966096 | tf_op jit(solution)/shard_map/all_gather | solution.py:185
  654.6 10.6 fusion.10
  665.2 13.7 %multiply_reduce_fusion.2 = (f32[2,5,512]{2,1,0:T(8,128)S(1)}, f32[2,5,512,1024]{3,2,1,0:T(8,128)}) fusion(f32[2,5,512,1024]{3,2,1,0:T(8,128)} %copy-done.1, f32[2,5,512]{2,1,0:T(8,128)S(1)} %log_add_fusion.1, bf16[2,1024,5,24]{1,3,2,0:T(8,128)(2,1)S(1)} %bitcast.266, f32[2,1024,5,3,24]{1,4,3,2,0:T(8,128)S(1)} %copy-done.41), kind=kOutput, calls=%fused_computation.6 | convolution fusion | flops 272624640 | bytes 42733568 | tf_op jit(solution)/shard_map/sqhe,skhe->shqk/dot_general | solution.py:65
  678.9 13.8 %multiply_reduce_fusion.3 = (f32[2,5,512]{2,1,0:T(8,128)S(1)}, f32[2,5,512,1024]{3,2,1,0:T(8,128)}) fusion(f32[2,5,512,1024]{3,2,1,0:T(8,128)} %get-tuple-element.209, f32[2,5,512]{2,1,0:T(8,128)S(1)} %log_add_fusion.2, bf16[2,1024,5,24]{1,3,2,0:T(8,128)(2,1)S(1)} %bitcast.267, f32[2,1024,5,3,24]{1,4,3,2,0:T(8,128)S(1)} %copy-done.41), kind=kOutput, calls=%fused_computation.9 | convolution fusion | flops 272624640 | bytes 42733568 | tf_op jit(solution)/shard_map/sqhe,skhe->shqk/dot_general | solution.py:65
  692.6 14.3 %multiply_convert_fusion.3 = bf16[2,5,512,1024]{3,2,1,0:T(8,128)(2,1)S(1)} fusion(f32[2,5,512,1024]{3,2,1,0:T(8,128)} %get-tuple-element.217, f32[2,5,512,1024]{3,2,1,0:T(8,128)} %get-tuple-element.209, f32[2,5,512]{2,1,0:T(8,128)S(1)} %get-tuple-element.216, f32[2,5,512]{2,1,0:T(8,128)S(1)} %log_add_fusion.2), kind=kLoop, calls=%fused_computation.8 | loop fusion | flops 26214400 | bytes 52469760 | tf_op jit(solution)/shard_map/convert_element_type | solution.py:69
  713.3 11.0 fusion.49
  724.4 14.0 %multiply_convert_fusion.2 = bf16[2,5,512,1024]{3,2,1,0:T(8,128)(2,1)} fusion(f32[2,5,512,1024]{3,2,1,0:T(8,128)} %get-tuple-element.215, f32[2,5,512,1024]{3,2,1,0:T(8,128)S(1)} %bitcast.256, f32[2,5,512]{2,1,0:T(8,128)S(1)} %get-tuple-element.214, f32[2,5,512]{2,1,0:T(8,128)S(1)} %log_add_fusion.1), kind=kLoop, calls=%fused_computation.5 | loop fusion | flops 26214400 | bytes 52469760 | tf_op jit(solution)/shard_map/convert_element_type | solution.py:69
  738.4 7.0 fusion.54
  752.8 43.0 %reduce-scatter.19.cloned.1.call-done = f32[2,256,480]{1,2,0:T(8,128)} async-done(((f32[2,1024,480]{1,2,0:T(8,128)}), f32[2,256,480]{1,2,0:T(8,128)}) %reduce-scatter.19.cloned.1.call-update) | async-done | bytes 983056 | tf_op jit(solution)/shard_map/reduce_scatter | solution.py:219
  801.7 22.0 %all-gather.21.cloned.1.call-done = bf16[2,1024,480]{1,2,0:T(8,128)(2,1)} async-done(((bf16[2,256,480]{1,2,0:T(8,128)(2,1)}), bf16[2,1024,480]{1,2,0:T(8,128)(2,1)}) %all-gather.21.cloned.1.call-update) | async-done | bytes 1966096 | tf_op jit(solution)/shard_map/all_gather | solution.py:159
  823.7 6.3 add_convert_fusion
  834.8 43.0 %reduce-scatter.21.cloned.1.call-done = f32[2,256,480]{1,2,0:T(8,128)} async-done(((f32[2,1024,480]{1,2,0:T(8,128)}), f32[2,256,480]{1,2,0:T(8,128)}) %reduce-scatter.21.cloned.1.call-update) | async-done | bytes 983056 | tf_op jit(solution)/shard_map/reduce_scatter | solution.py:174
  908.1 9.9 fusion.8
  918.0 13.8 %multiply_reduce_fusion = (f32[2,5,512]{2,1,0:T(8,128)S(1)}, f32[2,5,512,1024]{3,2,1,0:T(8,128)}) fusion(f32[2,5,512,1024]{3,2,1,0:T(8,128)} %copy-done, f32[2,5,512]{2,1,0:T(8,128)S(1)} %log_add_fusion, bf16[2,1024,5,24]{1,3,2,0:T(8,128)(2,1)S(1)} %bitcast.262, f32[2,1024,5,3,24]{1,4,3,2,0:T(8,128)S(1)} %copy-done.39), kind=kOutput, calls=%fused_computation.1 | convolution fusion | flops 272624640 | bytes 42733568 | tf_op jit(solution)/shard_map/sqhe,skhe->shqk/dot_general | solution.py:65
  931.7 13.8 %multiply_reduce_fusion.1 = (f32[2,5,512]{2,1,0:T(8,128)S(1)}, f32[2,5,512,1024]{3,2,1,0:T(8,128)}) fusion(f32[2,5,512,1024]{3,2,1,0:T(8,128)} %get-tuple-element.204, f32[2,5,512]{2,1,0:T(8,128)S(1)} %log_add_fusion.3, bf16[2,1024,5,24]{1,3,2,0:T(8,128)(2,1)S(1)} %bitcast.263, f32[2,1024,5,3,24]{1,4,3,2,0:T(8,128)S(1)} %copy-done.39), kind=kOutput, calls=%fused_computation.4 | convolution fusion | flops 272624640 | bytes 42733568 | tf_op jit(solution)/shard_map/sqhe,skhe->shqk/dot_general | solution.py:65
  945.6 14.6 %multiply_convert_fusion.1 = bf16[2,5,512,1024]{3,2,1,0:T(8,128)(2,1)S(1)} fusion(f32[2,5,512,1024]{3,2,1,0:T(8,128)} %get-tuple-element.221, f32[2,5,512,1024]{3,2,1,0:T(8,128)} %get-tuple-element.204, f32[2,5,512]{2,1,0:T(8,128)S(1)} %get-tuple-element.220, f32[2,5,512]{2,1,0:T(8,128)S(1)} %log_add_fusion.3), kind=kLoop, calls=%fused_computation.3 | loop fusion | flops 26214400 | bytes 52469760 | tf_op jit(solution)/shard_map/convert_element_type | solution.py:69
  968.3 9.1 fusion.43
  977.4 14.5 %multiply_convert_fusion = bf16[2,5,512,1024]{3,2,1,0:T(8,128)(2,1)S(1)} fusion(f32[2,5,512,1024]{3,2,1,0:T(8,128)} %get-tuple-element.219, f32[2,5,512,1024]{3,2,1,0:T(8,128)} %copy-done, f32[2,5,512]{2,1,0:T(8,128)S(1)} %get-tuple-element.218, f32[2,5,512]{2,1,0:T(8,128)S(1)} %log_add_fusion), kind=kLoop, calls=%fused_computation | loop fusion | flops 26214400 | bytes 52469760 | tf_op jit(solution)/shard_map/convert_element_type | solution.py:69
  1007.3 197.5 %all-reduce.9.cloned.1.call-done = (f32[2,480,360]{2,0,1:T(2,128)}, f32[2,120,480]{1,0,2:T(2,128)}, f32[2,480,480]{2,0,1:T(2,128)}, f32[2,480,480]{1,0,2:T(2,128)}) async-done(((f32[2,480,360]{2,0,1:T(2,128)}, f32[2,120,480]{1,0,2:T(2,128)}, f32[2,480,480]{2,0,1:T(2,128)}, f32[2,480,480]{1,0,2:T(2,128)}), (f32[2,480,360]{2,0,1:T(2,128)}, f32[2,120,480]{1,0,2:T(2,128)}, f32[2,480,480]{2,0,1:T(2,128)}, ...) | async-done | bytes 5529616
  1214.6 34.4 %reduce-scatter.23.cloned.1.call-done = f32[2,256,480]{1,2,0:T(8,128)} async-done(((f32[2,1024,480]{1,2,0:T(8,128)}), f32[2,256,480]{1,2,0:T(8,128)}) %reduce-scatter.23.cloned.1.call-update) | async-done | bytes 983056 | tf_op jit(solution)/shard_map/reduce_scatter | solution.py:219
  1253.3 40.8 %all-reduce.10 = (f32[]{:T(128)}, f32[10,480]{1,0:T(8,128)S(1)}, f32[33,480]{1,0:T(8,128)S(1)}) all-reduce(f32[]{:T(128)} %get-tuple-element.136, f32[10,480]{1,0:T(8,128)S(1)} %concatenate.79, f32[33,480]{1,0:T(8,128)S(1)} %fusion.60), channel_id=1, replica_groups=mesh['dp'=8,'tensor'=4] {'dp','tensor'}, use_global_device_ids=true, to_apply=%region_27.0 | all-reduce | flops 20641 | bytes 165128 | tf_op jit(solution)/shard_map/psum | solution.py:362
  (525 shorter events, 183.5 us)
Async XLA Ops:
  7.2 73.5 %all-gather.9.cloned.1.call-start = ((), (), s32[]{:S(2)}) async-start(), calls=%async_computation.8 | async-start | bytes 2457600 | tf_op jit(solution)/shard_map/all_gather | solution.py:90
  8.9 173.8 %copy-start.123 = (f32[1,480]{1,0:T(1,128)}, f32[1,480]{1,0:T(1,128)S(1)}, u32[]{:S(2)}) copy-start(f32[1,480]{1,0:T(1,128)S(1)} %get-tuple-element.192) | copy-start | bytes 5764
  8.9 310.1 %copy-start.130 = (f32[1,480]{1,0:T(1,128)}, f32[1,480]{1,0:T(1,128)S(1)}, u32[]{:S(2)}) copy-start(f32[1,480]{1,0:T(1,128)S(1)} %get-tuple-element.190) | copy-start | bytes 5764
  10.2 171.1 %copy-start.3 = (f32[2,256,480]{1,2,0:T(8,128)}, f32[2,256,480]{1,2,0:T(8,128)S(1)}, u32[]{:S(2)}) copy-start(f32[2,256,480]{1,2,0:T(8,128)S(1)} %get-tuple-element.200) | copy-start | bytes 2949124
  10.3 70.4 %copy-start.143 = (f32[2,256]{1,0:T(2,128)}, f32[2,256]{1,0:T(2,128)S(1)}, u32[]{:S(2)}) copy-start(f32[2,256]{1,0:T(2,128)S(1)} %multiply_reduce_fusion.22) | copy-start | bytes 6148
  11.7 169.5 %reduce-scatter.9.cloned.1.call-start = ((), (), s32[]{:S(2)}) async-start(), calls=%async_computation.9 | async-start | bytes 4915200 | tf_op jit(solution)/shard_map/reduce_scatter | solution.py:107
  79.6 265.4 %copy-start.64 = (f32[1024,12]{0,1:T(8,128)}, f32[1024,12]{0,1:T(8,128)S(1)}, u32[]{:S(2)}) copy-start(f32[1024,12]{0,1:T(8,128)S(1)} %get-tuple-element.197) | copy-start | bytes 147460
  79.7 265.4 %copy-start.66 = (f32[1024,12]{0,1:T(8,128)}, f32[1024,12]{0,1:T(8,128)S(1)}, u32[]{:S(2)}) copy-start(f32[1024,12]{0,1:T(8,128)S(1)} %get-tuple-element.198) | copy-start | bytes 147460
  80.7 53.7 %copy-start.78 = (bf16[1,120,480]{1,0,2:T(2,128)(2,1)}, bf16[1,120,480]{1,0,2:T(2,128)(2,1)S(1)}, u32[]{:S(2)}) copy-start(bf16[1,120,480]{1,0,2:T(2,128)(2,1)S(1)} %get-tuple-element.177) | copy-start | bytes 345604
  137.2 118.2 %all-gather.11.cloned.1.call-start = ((), (), s32[]{:S(2)}) async-start(), calls=%async_computation.10 | async-start | bytes 2457600 | tf_op jit(solution)/shard_map/all_gather | solution.py:117
  182.5 134.9 %copy-start.5 = (f32[2,256,480]{1,2,0:T(8,128)}, f32[2,256,480]{1,2,0:T(8,128)S(1)}, u32[]{:S(2)}) copy-start(f32[2,256,480]{1,2,0:T(8,128)S(1)} %get-tuple-element.149) | copy-start | bytes 2949124
  183.8 133.7 %reduce-scatter.11.cloned.1.call-start = ((), (), s32[]{:S(2)}) async-start(), calls=%async_computation.11 | async-start | bytes 4915200 | tf_op jit(solution)/shard_map/reduce_scatter | solution.py:122
  274.0 68.3 %all-gather.13.cloned.1.call-start = ((), (), s32[]{:S(2)}) async-start(), calls=%async_computation.12 | async-start | bytes 2457600 | tf_op jit(solution)/shard_map/all_gather | solution.py:90
  320.0 132.2 %reduce-scatter.13.cloned.1.call-start = ((), (), s32[]{:S(2)}) async-start(), calls=%async_computation.13 | async-start | bytes 4915200 | tf_op jit(solution)/shard_map/reduce_scatter | solution.py:107
  409.2 67.8 %all-gather.15.cloned.1.call-start = ((), (), s32[]{:S(2)}) async-start(), calls=%async_computation.14 | async-start | bytes 2457600 | tf_op jit(solution)/shard_map/all_gather | solution.py:117
  453.6 169.2 %copy-start.113 = (f32[2,256]{1,0:T(2,128)}, f32[2,256]{1,0:T(2,128)S(1)}, u32[]{:S(2)}) copy-start(f32[2,256]{1,0:T(2,128)S(1)} %broadcast_multiply_fusion.1) | copy-start | bytes 6148
  454.8 83.6 %reduce-scatter.15.cloned.1.call-start = ((), (), s32[]{:S(2)}) async-start(), calls=%async_computation.15 | async-start | bytes 4915200 | tf_op jit(solution)/shard_map/reduce_scatter | solution.py:122
  495.4 73.2 %all-gather.17.cloned.1.call-start = ((), (), s32[]{:S(2)}) async-start(), calls=%async_computation.16 | async-start | bytes 2457600 | tf_op jit(solution)/shard_map/all_gather | solution.py:159
  546.4 76.4 %reduce-scatter.17.cloned.1.call-start = ((), (), s32[]{:S(2)}) async-start(), calls=%async_computation.17 | async-start | bytes 4915200 | tf_op jit(solution)/shard_map/reduce_scatter | solution.py:174
  579.8 72.8 %all-gather.19.cloned.1.call-start = ((), (), s32[]{:S(2)}) async-start(), calls=%async_computation.18 | async-start | bytes 2457600 | tf_op jit(solution)/shard_map/all_gather | solution.py:185
  630.3 165.5 %reduce-scatter.19.cloned.1.call-start = ((), (), s32[]{:S(2)}) async-start(), calls=%async_computation.19 | async-start | bytes 4915200 | tf_op jit(solution)/shard_map/reduce_scatter | solution.py:219
  752.8 71.0 %copy-start.52 = (bf16[1,480,480]{1,0,2:T(2,128)(2,1)S(1)}, bf16[1,480,480]{1,0,2:T(2,128)(2,1)}, u32[]{:S(2)}) copy-start(bf16[1,480,480]{1,0,2:T(2,128)(2,1)} %copy-done.51) | copy-start | bytes 1382404
  752.8 70.9 %all-gather.21.cloned.1.call-start = ((), (), s32[]{:S(2)}) async-start(), calls=%async_computation.20 | async-start | bytes 2457600 | tf_op jit(solution)/shard_map/all_gather | solution.py:159
  801.5 76.3 %reduce-scatter.21.cloned.1.call-start = ((), (), s32[]{:S(2)}) async-start(), calls=%async_computation.21 | async-start | bytes 4915200 | tf_op jit(solution)/shard_map/reduce_scatter | solution.py:174
  834.7 71.4 %all-gather.23.cloned.1.call-start = ((), (), s32[]{:S(2)}) async-start(), calls=%async_computation.22 | async-start | bytes 2457600 | tf_op jit(solution)/shard_map/all_gather | solution.py:185
  883.8 321.0 %all-reduce.9.cloned.1.call-start = ((), (), s32[]{:S(2)}) async-start(), calls=%async_computation.24 | async-start | bytes 11796480
  1002.0 202.7 %copy-start.100 = (f32[2,120,60]{1,0,2:T(2,128)S(1)}, f32[2,120,60]{1,0,2:T(2,128)}, u32[]{:S(2)}) copy-start(f32[2,120,60]{1,0,2:T(2,128)} %param.27) | copy-start | bytes 172804
  1002.1 202.7 %copy-start.116 = (f32[2,120,60]{1,0,2:T(2,128)S(1)}, f32[2,120,60]{1,0,2:T(2,128)}, u32[]{:S(2)}) copy-start(f32[2,120,60]{1,0,2:T(2,128)} %param.33) | copy-start | bytes 172804
  1002.1 202.7 %copy-start.117 = (f32[2,120,60]{1,0,2:T(2,128)S(1)}, f32[2,120,60]{1,0,2:T(2,128)}, u32[]{:S(2)}) copy-start(f32[2,120,60]{1,0,2:T(2,128)} %param.39) | copy-start | bytes 172804
  1002.1 204.4 %copy-start.89 = (f32[2,60,360]{2,0,1:T(2,128)S(1)}, f32[2,60,360]{2,0,1:T(2,128)}, u32[]{:S(2)}) copy-start(f32[2,60,360]{2,0,1:T(2,128)} %param.26) | copy-start | bytes 518404
  1002.1 204.4 %copy-start.101 = (f32[2,60,360]{2,0,1:T(2,128)S(1)}, f32[2,60,360]{2,0,1:T(2,128)}, u32[]{:S(2)}) copy-start(f32[2,60,360]{2,0,1:T(2,128)} %param.32) | copy-start | bytes 518404
  1002.1 246.9 %reduce-scatter.23.cloned.1.call-start = ((), (), s32[]{:S(2)}) async-start(), calls=%async_computation.23 | async-start | bytes 4915200 | tf_op jit(solution)/shard_map/reduce_scatter | solution.py:219
  1005.5 203.5 %copy-start.75 = (f32[2,60,480]{2,0,1:T(2,128)S(1)}, f32[2,60,480]{2,0,1:T(2,128)}, u32[]{:S(2)}) copy-start(f32[2,60,480]{2,0,1:T(2,128)} %param.28) | copy-start | bytes 691204
  1005.5 203.5 %copy-start.96 = (f32[2,60,480]{2,0,1:T(2,128)S(1)}, f32[2,60,480]{2,0,1:T(2,128)}, u32[]{:S(2)}) copy-start(f32[2,60,480]{2,0,1:T(2,128)} %param.34) | copy-start | bytes 691204
  1005.5 203.5 %copy-start.97 = (f32[2,60,480]{2,0,1:T(2,128)S(1)}, f32[2,60,480]{2,0,1:T(2,128)}, u32[]{:S(2)}) copy-start(f32[2,60,480]{2,0,1:T(2,128)} %param.40) | copy-start | bytes 691204
  1005.5 206.2 %copy-start.77 = (f32[2,480,60]{1,0,2:T(2,128)S(1)}, f32[2,480,60]{1,0,2:T(2,128)}, u32[]{:S(2)}) copy-start(f32[2,480,60]{1,0,2:T(2,128)} %param.29) | copy-start | bytes 691204
  1005.5 206.2 %copy-start.98 = (f32[2,480,60]{1,0,2:T(2,128)S(1)}, f32[2,480,60]{1,0,2:T(2,128)}, u32[]{:S(2)}) copy-start(f32[2,480,60]{1,0,2:T(2,128)} %param.35) | copy-start | bytes 691204
  1005.6 243.4 %copy-start.4 = (f32[2,256,480]{1,2,0:T(8,128)S(1)}, f32[2,256,480]{1,2,0:T(8,128)}, u32[]{:S(2)}) copy-start(f32[2,256,480]{1,2,0:T(8,128)} %copy-done.3) | copy-start | bytes 2949124
  1005.6 243.4 %copy-start.112 = (f32[2,256]{1,0:T(2,128)S(1)}, f32[2,256]{1,0:T(2,128)}, u32[]{:S(2)}) copy-start(f32[2,256]{1,0:T(2,128)} %copy-done.111) | copy-start | bytes 6148
  1005.6 243.4 %copy-start.119 = (f32[1,480]{1,0:T(1,128)S(1)}, f32[1,480]{1,0:T(1,128)}, u32[]{:S(2)}) copy-start(f32[1,480]{1,0:T(1,128)} %copy-done.118) | copy-start | bytes 5764
  1007.0 243.5 %copy-start.144 = (f32[2,256]{1,0:T(2,128)S(1)}, f32[2,256]{1,0:T(2,128)}, u32[]{:S(2)}) copy-start(f32[2,256]{1,0:T(2,128)} %copy-done.143) | copy-start | bytes 6148
  1007.0 243.5 %copy-start.127 = (f32[2,256]{1,0:T(2,128)S(1)}, f32[2,256]{1,0:T(2,128)}, u32[]{:S(2)}) copy-start(f32[2,256]{1,0:T(2,128)} %copy-done.126) | copy-start | bytes 6148
  1214.5 79.6 %copy-start.108 = (f32[10,480]{1,0:T(8,128)S(1)}, f32[10,480]{1,0:T(8,128)}, u32[]{:S(2)}) copy-start(f32[10,480]{1,0:T(8,128)} %param.30) | copy-start | bytes 57604
  1214.5 79.6 %copy-start.128 = (f32[10,480]{1,0:T(8,128)S(1)}, f32[10,480]{1,0:T(8,128)}, u32[]{:S(2)}) copy-start(f32[10,480]{1,0:T(8,128)} %param.36) | copy-start | bytes 57604
  1214.5 79.6 %copy-start.129 = (f32[10,480]{1,0:T(8,128)S(1)}, f32[10,480]{1,0:T(8,128)}, u32[]{:S(2)}) copy-start(f32[10,480]{1,0:T(8,128)} %param.42) | copy-start | bytes 57604
  1214.5 80.3 %copy-start.69 = (f32[33,480]{1,0:T(8,128)S(1)}, f32[33,480]{1,0:T(8,128)}, u32[]{:S(2)}) copy-start(f32[33,480]{1,0:T(8,128)} %param.31) | copy-start | bytes 190084
  1214.6 80.3 %copy-start.109 = (f32[33,480]{1,0:T(8,128)S(1)}, f32[33,480]{1,0:T(8,128)}, u32[]{:S(2)}) copy-start(f32[33,480]{1,0:T(8,128)} %param.37) | copy-start | bytes 190084
  1214.6 80.3 %copy-start.110 = (f32[33,480]{1,0:T(8,128)S(1)}, f32[33,480]{1,0:T(8,128)}, u32[]{:S(2)}) copy-start(f32[33,480]{1,0:T(8,128)} %param.43) | copy-start | bytes 190084
  (143 other events, 2458.8 us)
Sparse Core Ops, SparseCore 0:
  11.8 24.7 all-gather.8
  137.3 43.8 reduce-scatter.8
  183.9 22.0 all-gather.10
  274.1 43.3 reduce-scatter.10
  320.1 22.0 all-gather.12
  409.3 42.8 reduce-scatter.12
  454.9 22.0 all-gather.14
  495.5 42.8 reduce-scatter.14
  546.5 22.0 all-gather.16
  579.9 42.9 reduce-scatter.16
  630.5 22.0 all-gather.18
  752.9 42.8 reduce-scatter.18
  801.6 22.0 all-gather.20
  834.8 42.8 reduce-scatter.20
  883.9 22.0 all-gather.22
  1002.1 202.6 all-reduce.8
  1207.2 41.7 reduce-scatter.22
where the time goes:
time: 1310 us; the launch traced here: 1300 us
  waiting for transfers between devices  619 us (47%)
  matrix products  265 us (20%)
  blocking collectives  192 us (15%)
  other arithmetic  160 us (12%)
  local copies, waits for them, and re-layouts  47 us (4%)
  between operations  18 us (1%)
    unnamed x18, waiting for transfers between devices  198 us
    reduce_scatter x2, waiting for transfers between devices, forward_layer(): lax.psum_scatter(jnp.einsum('xok,kr->xor', blended_tokens, projection_res...  86.9 us
    reduce_scatter x2, waiting for transfers between devices, backward_layer(): lax.psum_scatter(jnp.einsum('erj,aj->era', gradient_hidden_state, up_matr...  86 us
    reduce_scatter x2, waiting for transfers between devices, backward_layer(): lax.psum_scatter(jnp.einsum('hft,wt->hfw', gradient_packed_rows, input_ma...  77.4 us
    reduce_scatter x2, waiting for transfers between devices, forward_layer(): lax.psum_scatter(jnp.einsum('rbq,qy->rby', active_rows, down_matrix, pref...  62.9 us
    convert_element_type x4, other arithmetic, attend_back(): grad_scores = (softmax_rows * (grad_rows - inner)).astype(brain)  57.4 us
    dot_general x4, matrix products, attend_back(): jnp.einsum('sqhe,skhe->shqk', gradient_mixed_rows, values, preferred_elem...  55 us
    dot_general x4, matrix products, attend_block(): jnp.einsum('shqk,skhe->sqhe', softmax_rows, values, preferred_element_typ...  48.6 us
  transfers between devices with their start and end apart: 17, of which 15 were waited for; matrix products, arithmetic and copies ran while one was open for 4% of the time, Pallas kernels for 0%

commit v1 on v0

v1 whole, which is shorter than its diff:
```python
import functools
import math

import jax
import jax.numpy as jnp
from jax import lax
from jax.experimental import pallas as pl
from jax.experimental.pallas import tpu as pltpu
from jax.sharding import PartitionSpec as P

HEAD = 24
STEP = 5
LANES = 128
TABLE_ROWS = 40
LOSS_ROW = 10
VMEM_BYTES = 60 * 1024 * 1024

norm_eps = 1e-05
step_rates = (0.02, 0.3, 0.02, 0.02, 0.3, 0.05)
beta_first = 0.5
beta_second = 0.5
adam_eps = 1e-08
weight_decay = 0.01
highest = lax.Precision.HIGHEST
brain = jnp.bfloat16
single = jnp.float32
scale = HEAD ** (-0.5)
scale_two = scale * math.log2(math.e)

params = functools.partial(pltpu.CompilerParams, vmem_limit_bytes=VMEM_BYTES)


def cost(micros):
    return pl.CostEstimate(flops=int(micros * 1.1e9), bytes_accessed=0, transcendentals=0)


class Cube:
    def __init__(self, groups, tensors):
        self.groups = groups
        self.tensors = tensors
        self.devices = groups * tensors
        self.size = self.devices.bit_length() - 1
        self.masks = [1 << at for at in range(self.size)]
        self.folded = groups >= 4
        if self.folded:
            self.masks[-1] |= self.masks[-2]

    def swap(self, x, at):
        mask = self.masks[at]
        pairs = [(device, device ^ mask) for device in range(self.devices)]
        return lax.ppermute(x, ("dp", "tensor"), pairs)

    def outer(self, turn):
        rest = list(range(1, self.size))
        rest = rest[1:2] + rest[:1] + rest[2:]
        turn = turn % len(rest)
        return rest[turn:] + rest[:turn]

    def steps(self, offset):
        bits = [(offset >> at) & 1 for at in range(self.size)]
        if self.folded:
            bits[-2] = bits[-2] ^ bits[-1]
        return bits

    def gather(self, x, order):
        held = x[None]
        for at in order:
            held = jnp.concatenate([held, self.swap(held, at)], 0)
        return held

    def slot(self, offset, order):
        bits = self.steps(offset)
        place = 0
        for rank, at in enumerate(order):
            place = place + (bits[at] << rank)
        return place


def dot(left, right, left_dim=1, right_dim=0):
    return lax.dot_general(
        left, right, (((left_dim,), (right_dim,)), ((), ())), preferred_element_type=single
    )


def split_three(x):
    high = x.astype(brain)
    rest = x - high.astype(single)
    middle = rest.astype(brain)
    return high, middle, (rest - middle.astype(single)).astype(brain)


def dot_exact(hot, x, left_dim=1, right_dim=0):
    high, middle, low = split_three(x)
    tail = dot(hot, middle, left_dim, right_dim) + dot(hot, low, left_dim, right_dim)
    return dot(hot, high, left_dim, right_dim) + tail


def fold_rows(x, op, parts=8):
    size = x.shape[0] // parts
    pieces = [x[at * size : (at + 1) * size] for at in range(parts)]
    while len(pieces) > 1:
        pieces = [op(pieces[at], pieces[at + 1]) for at in range(0, len(pieces), 2)]
    return pieces[0]


def column_max(x):
    return jnp.max(fold_rows(x, jnp.maximum), 0, keepdims=True)


def column_sum(x):
    return jnp.sum(fold_rows(x, jnp.add), 0, keepdims=True)


erf_top = (
    -2.72614225801306e-10,
    2.77068142495902e-08,
    -2.10102402082508e-06,
    -5.69250639462346e-05,
    -7.34990630326855e-04,
    -2.95459980854025e-03,
    -1.60960333262415e-02,
)
erf_bottom = (
    -1.45660718464996e-05,
    -2.13374055278905e-04,
    -1.68282697438203e-03,
    -7.37332916720468e-03,
    -1.42647390514189e-02,
)


def erf(x):
    x = jnp.clip(x, -4.0, 4.0)
    square = x * x
    top = jnp.full_like(x, erf_top[0])
    for term in erf_top[1:]:
        top = top * square + term
    bottom = jnp.full_like(x, erf_bottom[0])
    for term in erf_bottom[1:]:
        bottom = bottom * square + term
    return x * top / bottom


def normal_share(x):
    return 0.5 + 0.5 * erf(x * math.sqrt(0.5))


def gelu(x):
    return x * normal_share(x)


def gelu_slope(x, share):
    return share + x * jnp.exp(-0.5 * x * x) * (1.0 / math.sqrt(2.0 * math.pi))


def rotary_partner(x):
    lane = lax.broadcasted_iota(jnp.int32, x.shape, 1) % HEAD
    return jnp.where(
        lane < HEAD // 2,
        pltpu.roll(x, LANES - HEAD // 2, 1),
        pltpu.roll(x, HEAD // 2, 1),
    )


def rotate(x, cosine, sine):
    return x * cosine + rotary_partner(x) * sine


def unrotate(x, cosine, sine):
    return x * cosine - rotary_partner(x) * sine


class Features:
    def __init__(self, width, groups):
        self.width = width
        self.groups = groups
        self.block = width // groups
        self.padded = -(-self.block // 16) * 16
        self.total = self.padded * groups

    def pad(self, x):
        rows = x.shape[0]
        x = x.reshape(rows, self.groups, self.block)
        x = jnp.pad(x, ((0, 0), (0, 0), (0, self.padded - self.block)))
        return x.reshape(rows, self.total)

    def unpad(self, x):
        rows = x.shape[0]
        x = x.reshape(rows, self.groups, self.padded)[:, :, : self.block]
        return x.reshape(rows, self.width)

    def live(self, shape):
        lane = lax.broadcasted_iota(jnp.int32, shape, 1) % self.padded
        return lane < self.block

    def centred(self, x):
        mean = jnp.sum(x, 1, keepdims=True) * (1.0 / self.width)
        centre = jnp.where(self.live(x.shape), x - mean, 0.0)
        spread = jnp.sum(centre * centre, 1, keepdims=True) * (1.0 / self.width)
        inverse = lax.rsqrt(spread + norm_eps)
        return centre * inverse, inverse

    def norm(self, x, gain, shift):
        unit, _ = self.centred(x)
        return (unit * gain + shift).astype(brain)

    def norm_back(self, unit, inverse, gain, grad):
        scaled = grad * gain
        mean = jnp.sum(scaled, 1, keepdims=True) * (1.0 / self.width)
        along = jnp.sum(scaled * unit, 1, keepdims=True) * (1.0 / self.width)
        back = inverse * (scaled - mean - unit * along)
        return jnp.where(self.live(back.shape), back, 0.0)


class Gathered:
    def __init__(self, ref):
        self.ref = ref

    def block(self, tile, start, stop):
        groups, _, rows, _ = self.ref.shape
        return self.ref[:, tile, :, start:stop].reshape(groups * rows, stop - start)


class Relative:
    def __init__(self, cube, me, refs, cuts, orders):
        self.cube = cube
        self.me = me
        self.refs = refs
        self.cuts = cuts
        self.orders = orders

    def block(self, tile, start, stop):
        pieces = []
        for ref, low, high, order in zip(self.refs, self.cuts[:-1], self.cuts[1:], self.orders):
            first = max(start, low) - low
            last = min(stop, high) - low
            if first >= last:
                continue
            rows = []
            for group in range(self.cube.groups):
                offset = (group * self.cube.tensors + tile) ^ self.me
                rows.append(ref[self.cube.slot(offset, order), :, first:last])
            pieces.append(jnp.concatenate(rows, 0))
        return pieces[0] if len(pieces) == 1 else jnp.concatenate(pieces, 1)


class Scattered:
    def __init__(self, cube, me, keep_ref, send_ref, orders):
        self.cube = cube
        self.me = me
        self.refs = (keep_ref, send_ref)
        self.orders = orders

    def store(self, tile, turn, start, value):
        rows, wide = self.refs[0].shape[2:]
        ref = self.refs[turn & 1]
        width = value.shape[1]
        for group in range(self.cube.groups):
            offset = (group * self.cube.tensors + tile) ^ self.me
            done = 0
            while done < width:
                part, place = divmod(start + done, wide)
                count = min(width - done, wide - place)
                slot = self.cube.slot(offset, self.orders[part][::-1])
                ref[part, slot, :, place : place + count] = value[
                    group * rows : (group + 1) * rows, done : done + count
                ]
                done += count


class Whole:
    def __init__(self, ref):
        self.ref = ref

    def store(self, tile, turn, start, value):
        groups, _, rows, _ = self.ref.shape
        wide = value.shape[1]
        self.ref[:, tile, :, start : start + wide] = value.reshape(groups, rows, wide)


class Layer:
    def __init__(self, weights, base, hidden):
        self.weights = weights
        self.base = base
        self.hidden = hidden

    def out(self, tile):
        return self.weights.block(tile, self.base, self.base + LANES)

    def up(self, tile):
        start = self.base + LANES
        return self.weights.block(tile, start, start + self.hidden)

    def down(self, tile):
        start = self.base + LANES + self.hidden
        return self.weights.block(tile, start, start + self.hidden)


def tile_lanes(tile):
    if isinstance(tile, int):
        return pl.ds(tile * LANES, LANES)
    return pl.ds(pl.multiple_of(tile * LANES, LANES), LANES)


def add_up(parts):
    total = None
    for part in parts:
        total = part if total is None else total + part
    return total


def whole_spec(shape):
    return pl.BlockSpec(shape, lambda at: (0,) * len(shape))


def columns_spec(weights, columns, at_block):
    groups, tiles, rows, _ = weights.shape
    return pl.BlockSpec((groups, tiles, rows, columns), lambda at: (0, 0, 0, at_block))


def scalar_spec():
    return pl.BlockSpec(memory_space=pltpu.SMEM)


def call(kernel, name, ins, in_specs, outs, micros, scratch=()):
    return pl.pallas_call(
        kernel,
        grid=(1,),
        in_specs=in_specs,
        out_specs=[whole_spec(out.shape) for out in outs],
        out_shape=outs,
        scratch_shapes=list(scratch),
        compiler_params=params(),
        cost_estimate=cost(micros),
        name=name,
    )(*ins)


def embed_kernel(
    table_ref, ids_ref, vocab_ref, cos_ref, sin_ref, q_ref, own_ref, other_ref, resid_ref
):
    own = q_ref.shape[0]
    length = ids_ref.shape[1]
    tiles = table_ref.shape[0]
    hot = lax.broadcasted_iota(jnp.int32, (64, length), 0) == ids_ref[...]
    hot = hot.astype(single).T.astype(brain)
    resid_ref[...] = dot(hot[:own], vocab_ref[...])
    hot = hot[:, :TABLE_ROWS]
    cosine = cos_ref[...]
    sine = sin_ref[...]
    for at in range(tiles):
        lanes = slice(at * LANES, (at + 1) * LANES)
        rows = dot_exact(hot, table_ref[at])
        q_ref[:, lanes] = rotate(rows[:own, :LANES], cosine[:own], sine[:own]).astype(brain)
        keys = rotate(rows[:, LANES : 2 * LANES], cosine, sine).astype(brain)
        values = rows[:, 2 * LANES :].astype(brain)
        own_ref[0, :, lanes] = keys[:own]
        own_ref[1, :, lanes] = values[:own]
        other_ref[0, :, lanes] = keys[own:]
        other_ref[1, :, lanes] = values[own:]


def embed(table, ids, vocab, cosine, sine):
    tiles = table.shape[0]
    own = ids.shape[1] // 2
    wide = tiles * LANES
    ins = (table, ids, vocab, cosine, sine)
    outs = [
        jax.ShapeDtypeStruct((own, wide), brain),
        jax.ShapeDtypeStruct((2, own, wide), brain),
        jax.ShapeDtypeStruct((2, own, wide), brain),
        jax.ShapeDtypeStruct((own, vocab.shape[1]), single),
    ]
    return call(embed_kernel, "embed", ins, [whole_spec(x.shape) for x in ins], outs, 6)


def attend_kernel(heads, chunk, q_ref, own_ref, other_ref, out_ref, logsum_ref):
    own = q_ref.shape[0]
    q_turned = q_ref[...].T
    keys = jnp.concatenate([own_ref[0], other_ref[0]], 0)
    v_turned = jnp.concatenate([own_ref[1], other_ref[1]], 0).T
    rows = lax.broadcasted_iota(jnp.int32, (LANES, chunk), 0)
    for start in range(0, own, chunk):
        part = slice(start, start + chunk)
        q_part = q_turned[:, part]
        mixed = jnp.zeros((LANES, chunk), single)
        for head in range(heads):
            mine = (rows >= head * HEAD) & (rows < (head + 1) * HEAD)
            scores = dot(keys, jnp.where(mine, q_part, jnp.zeros_like(q_part)))
            peak = column_max(scores) * scale_two
            weights = jnp.exp2(scores * scale_two - peak)
            total = column_sum(weights)
            probs = (weights * (1.0 / total)).astype(brain)
            mixed = jnp.where(mine, dot(v_turned, probs), mixed)
            logsum_ref[0, head : head + 1, part] = peak + jnp.log2(total)
        out_ref[part, :] = mixed.T.astype(brain)


def attend(q, kv_own, kv_other, heads):
    own, wide = q.shape
    tiles = wide // LANES
    own_spec = pl.BlockSpec((own, LANES), lambda at: (0, at))
    pair_spec = pl.BlockSpec((2, own, LANES), lambda at: (0, 0, at))
    return pl.pallas_call(
        functools.partial(attend_kernel, heads, LANES),
        grid=(tiles,),
        in_specs=[own_spec, pair_spec, pair_spec],
        out_specs=[own_spec, pl.BlockSpec((1, 8, own), lambda at: (at, 0, 0))],
        out_shape=[
            jax.ShapeDtypeStruct((own, wide), brain),
            jax.ShapeDtypeStruct((tiles, 8, own), single),
        ],
        compiler_params=params(),
        cost_estimate=cost(20),
        name="attend",
    )(q, kv_own, kv_other)


def attend_back_kernel(
    heads, chunk, q_ref, kv_own_ref, kv_other_ref, g_ref, logsum_ref, dq_ref, own_ref, other_ref
):
    own = q_ref.shape[0]
    q = q_ref[...]
    grad = g_ref[...]
    q_turned = q.T
    g_turned = grad.T
    keys = jnp.concatenate([kv_own_ref[0], kv_other_ref[0]], 0)
    values = jnp.concatenate([kv_own_ref[1], kv_other_ref[1]], 0)
    k_turned = keys.T
    rows = lax.broadcasted_iota(jnp.int32, (LANES, chunk), 0)
    lanes = lax.broadcasted_iota(jnp.int32, (chunk, LANES), 1)
    none = jnp.zeros((LANES, chunk), brain)
    none_low = jnp.zeros((chunk, LANES), brain)
    for start in range(0, own, chunk):
        part = slice(start, start + chunk)
        dq = jnp.zeros((LANES, chunk), single)
        for head in range(heads):
            mine = (rows >= head * HEAD) & (rows < (head + 1) * HEAD)
            mine_low = (lanes >= head * HEAD) & (lanes < (head + 1) * HEAD)
            scores = dot(keys, jnp.where(mine, q_turned[:, part], none))
            probs = jnp.exp2(scores * scale_two - logsum_ref[0, head : head + 1, part])
            g_probs = dot(values, jnp.where(mine, g_turned[:, part], none))
            inner = column_sum(probs * g_probs)
            g_scores = (probs * (g_probs - inner)).astype(brain)
            dv = dot(probs.astype(brain), jnp.where(mine_low, grad[part, :], none_low))
            dk = dot(g_scores, jnp.where(mine_low, q[part, :], none_low)) * scale
            if start == 0 and head == 0:
                own_ref[0] = dk[:own]
                own_ref[1] = dv[:own]
                other_ref[0] = dk[own:]
                other_ref[1] = dv[own:]
            else:
                own_ref[0] += dk[:own]
                own_ref[1] += dv[:own]
                other_ref[0] += dk[own:]
                other_ref[1] += dv[own:]
            dq = jnp.where(mine, dot(k_turned, g_scores), dq)
        dq_ref[part, :] = (dq * scale).T


def attend_back(q, kv_own, kv_other, grad, logsum, heads):
    own, wide = q.shape
    tiles = wide // LANES
    own_spec = pl.BlockSpec((own, LANES), lambda at: (0, at))
    pair_spec = pl.BlockSpec((2, own, LANES), lambda at: (0, 0, at))
    pair_shape = jax.ShapeDtypeStruct((2, own, wide), single)
    return pl.pallas_call(
        functools.partial(attend_back_kernel, heads, own),
        grid=(tiles,),
        in_specs=[
            own_spec,
            pair_spec,
            pair_spec,
            own_spec,
            pl.BlockSpec((1, 8, own), lambda at: (at, 0, 0)),
        ],
        out_specs=[own_spec, pair_spec, pair_spec],
        out_shape=[jax.ShapeDtypeStruct((own, wide), single), pair_shape, pair_shape],
        compiler_params=params(),
        cost_estimate=cost(33),
        name="attend_back",
    )(q, kv_own, kv_other, grad, logsum)


def attention_out(mixed, resid, layer, tiles):
    parts = [
        dot(mixed[:, at * LANES : (at + 1) * LANES], layer.out(at), 1, 1) for at in range(tiles)
    ]
    return resid + add_up(parts)


def middle_kernel(
    feats, cube, cuts, orders, hidden, me_ref, mixed_ref, resid_ref, *refs
):
    count = len(orders)
    part_refs = refs[:count]
    w_next_ref, norms_ref, cos_ref, sin_ref, mid_ref, next_ref, q_ref, kv_ref = refs[count:]
    layer = Layer(Relative(cube, me_ref[0], part_refs, cuts, orders), 0, hidden)
    tiles = cube.tensors
    mid = attention_out(mixed_ref[...], resid_ref[...], layer, tiles)
    mid_ref[...] = mid
    normed = feats.norm(mid, norms_ref[2:3], norms_ref[3:4])
    parts = []
    for at in range(tiles):
        act = gelu(dot(normed, layer.up(at))).astype(brain)
        parts.append(dot(act, layer.down(at), 1, 1))
    total = mid + add_up(parts)
    next_ref[...] = total
    normed = feats.norm(total, norms_ref[4:5], norms_ref[5:6])
    weights = Gathered(w_next_ref)
    for at in range(tiles):
        lanes = slice(at * LANES, (at + 1) * LANES)
        rows = dot(normed, weights.block(at, 0, 3 * LANES))
        cosine = cos_ref[...]
        sine = sin_ref[...]
        q_ref[:, lanes] = rotate(rows[:, :LANES], cosine, sine).astype(brain)
        kv_ref[0, :, lanes] = rotate(rows[:, LANES : 2 * LANES], cosine, sine).astype(brain)
        kv_ref[1, :, lanes] = rows[:, 2 * LANES :].astype(brain)


def middle(feats, cube, cuts, orders, me, mixed, resid, parts, w_next, norms, cosine, sine):
    own, wide = mixed.shape
    hidden = (cuts[-1] - LANES) // 2
    plain = jax.ShapeDtypeStruct(resid.shape, single)
    outs = [
        plain,
        plain,
        jax.ShapeDtypeStruct((own, wide), brain),
        jax.ShapeDtypeStruct((2, own, wide), brain),
    ]
    in_specs = [
        scalar_spec(),
        whole_spec(mixed.shape),
        whole_spec(resid.shape),
        *[whole_spec(part.shape) for part in parts],
        columns_spec(w_next, 3 * LANES, 0),
        whole_spec(norms.shape),
        whole_spec(cosine.shape),
        whole_spec(sine.shape),
    ]
    ins = (me, mixed, resid, *parts, w_next, norms, cosine, sine)
    kernel = functools.partial(middle_kernel, feats, cube, cuts, orders, hidden)
    return call(kernel, "middle", ins, in_specs, outs, 12)


def feed_back(
    feats, turns, g_resid, mid, normed, mixed_ref, layer, gain, act_ref, slope_ref,
    grads, base, g_mid_ref, g_mixed_ref,
):
    hidden = layer.hidden
    g_low = g_resid.astype(brain)
    g_turned = g_low.T
    normed_turned = normed.T
    parts = []
    for turn, tile in turns:
        g_hidden = (dot(g_low, layer.down(tile)) * slope_ref[turn]).astype(brain)
        grads.store(tile, turn, base + LANES + hidden, dot(g_turned, act_ref[turn]))
        grads.store(tile, turn, base + LANES, dot(normed_turned, g_hidden))
        parts.append(dot(g_hidden, layer.up(tile), 1, 1))
    g_normed = add_up(parts)
    unit, inverse = feats.centred(mid)
    g_gain = jnp.sum(g_normed * unit, 0, keepdims=True)
    g_shift = jnp.sum(g_normed, 0, keepdims=True)
    g_mid = g_resid + feats.norm_back(unit, inverse, gain, g_normed)
    g_mid_ref[...] = g_mid
    g_low = g_mid.astype(brain)
    g_turned = g_low.T
    for turn, tile in turns:
        lanes = tile_lanes(tile)
        g_mixed_ref[:, lanes] = dot(g_low, layer.out(tile)).astype(brain)
        grads.store(tile, turn, base, dot(g_turned, mixed_ref[:, lanes]))
    return g_gain, g_shift


def top_kernel(
    feats, vocab_count, mixed_ref, resid_ref, w_ref, norms_ref, vocab_ref, slot_ref, target_ref,
    count_ref, grads_ref, g_mid_ref, g_mixed_ref, g_norms_ref, g_vocab_ref,
    act_ref, slope_ref,
):
    tiles = w_ref.shape[1]
    layer = Layer(Gathered(w_ref), 3 * LANES, act_ref.shape[2])
    mid = attention_out(mixed_ref[...], resid_ref[...], layer, tiles)
    normed = feats.norm(mid, norms_ref[6:7], norms_ref[7:8])
    parts = []
    for at in range(tiles):
        hidden = dot(normed, layer.up(at))
        share = normal_share(hidden)
        act = (hidden * share).astype(brain)
        act_ref[at] = act
        slope_ref[at] = gelu_slope(hidden, share)
        parts.append(dot(act, layer.down(at), 1, 1))
    total = mid + add_up(parts)
    unit, inverse = feats.centred(total)
    gain = norms_ref[8:9]
    final = (unit * gain + norms_ref[9:10]).astype(brain)
    own = total.shape[0]
    slots = slot_ref.shape[0]
    vocab = vocab_ref[...]
    where_hot = (lax.broadcasted_iota(jnp.int32, (slots, own), 1) == slot_ref[...]).astype(single)
    where_hot = where_hot.astype(brain)
    present = (slot_ref[...] >= 0).astype(single)
    picked = dot(where_hot, final).astype(brain)
    logits = dot(picked, vocab, 1, 1)
    lane = lax.broadcasted_iota(jnp.int32, logits.shape, 1)
    logits = jnp.where(lane < vocab_count, logits, -1e30)
    peak = jnp.max(logits, 1, keepdims=True)
    logsum = peak + jnp.log(jnp.sum(jnp.exp(logits - peak), 1, keepdims=True))
    target_hot = (lane == target_ref[...]).astype(single)
    target_logit = jnp.sum(
        jnp.where(lane < vocab_count, logits * target_hot, 0.0), 1, keepdims=True
    )
    loss = jnp.sum((logsum - target_logit) * present, 0, keepdims=True)
    share = present / count_ref[0:1, 0:1]
    g_logits = ((jnp.exp(logits - logsum) - target_hot) * share).astype(brain)
    g_vocab_ref[...] = dot(g_logits, picked, 0, 0)[:TABLE_ROWS]
    g_picked = dot(g_logits, vocab)
    g_final = dot_exact(where_hot, g_picked, 0, 0)
    g_norms_ref[...] = jnp.zeros_like(g_norms_ref)
    g_norms_ref[8:9] = jnp.sum(g_final * unit, 0, keepdims=True)
    g_norms_ref[9:10] = jnp.sum(g_final, 0, keepdims=True)
    g_norms_ref[LOSS_ROW : LOSS_ROW + 1] = jnp.broadcast_to(loss, (1, g_norms_ref.shape[1]))
    g_resid = feats.norm_back(unit, inverse, gain, g_final)
    g_gain, g_shift = feed_back(
        feats, [(at, at) for at in range(tiles)], g_resid, mid, normed, mixed_ref, layer,
        norms_ref[6:7], act_ref, slope_ref, Whole(grads_ref), 0, g_mid_ref, g_mixed_ref,
    )
    g_norms_ref[6:7] = g_gain
    g_norms_ref[7:8] = g_shift


def top(feats, mixed, resid, weights, columns, norms, vocab, vocab_count, slot, target, count):
    own, wide = mixed.shape
    groups, tiles, rows, _ = weights.shape
    grads = columns - 3 * LANES
    hidden = (grads - LANES) // 2
    outs = [
        jax.ShapeDtypeStruct((groups, tiles, rows, grads), single),
        jax.ShapeDtypeStruct(resid.shape, single),
        jax.ShapeDtypeStruct(mixed.shape, brain),
        jax.ShapeDtypeStruct(norms.shape, single),
        jax.ShapeDtypeStruct((TABLE_ROWS, resid.shape[1]), single),
    ]
    in_specs = [
        whole_spec(mixed.shape),
        whole_spec(resid.shape),
        columns_spec(weights, columns, 0),
        whole_spec(norms.shape),
        whole_spec(vocab.shape),
        whole_spec(slot.shape),
        whole_spec(target.shape),
        whole_spec(count.shape),
    ]
    scratch = [
        pltpu.VMEM((tiles, own, hidden), brain),
        pltpu.VMEM((tiles, own, hidden), single),
    ]
    ins = (mixed, resid, weights, norms, vocab, slot, target, count)
    kernel = functools.partial(top_kernel, feats, vocab_count)
    return call(kernel, "top", ins, in_specs, outs, 21, scratch)


def head_grads(tile, dq_ref, own_ref, other_ref, cosine, sine):
    lanes = tile_lanes(tile)
    g_q = unrotate(dq_ref[:, lanes], cosine, sine)
    g_k = unrotate(own_ref[0, :, lanes] + other_ref[0, :, lanes], cosine, sine)
    g_v = own_ref[1, :, lanes] + other_ref[1, :, lanes]
    return jnp.concatenate([g_q, g_k, g_v], 1).astype(brain)


def lower_kernel(
    feats, cube, cuts, orders, grad_orders, me_ref, dq_ref, own_ref, other_ref, g_mid_in_ref,
    resid_ref, mid_ref, mixed_ref, w_in_ref, *refs
):
    count = len(orders)
    part_refs = refs[:count]
    (
        norms_ref, cos_ref, sin_ref, g_norms_in_ref,
        keep_ref, send_ref, g_mid_ref, g_mixed_ref, g_norms_ref,
        act_ref, slope_ref,
    ) = refs[count:]
    me = me_ref[0]
    tiles = cube.tensors
    turns = [(turn, turn ^ (me & (tiles - 1))) for turn in range(tiles)]
    layer = Layer(Relative(cube, me, part_refs, cuts, orders), 0, act_ref.shape[2])
    weights = Gathered(w_in_ref)
    grads = Scattered(cube, me, keep_ref, send_ref, grad_orders)
    unit, inverse = feats.centred(resid_ref[...])
    gain = norms_ref[4:5]
    normed_turned = (unit * gain + norms_ref[5:6]).astype(brain).T
    cosine = cos_ref[...]
    sine = sin_ref[...]
    parts = []
    for turn, tile in turns:
        g_heads = head_grads(tile, dq_ref, own_ref, other_ref, cosine, sine)
        grads.store(tile, turn, 0, dot(normed_turned, g_heads))
        parts.append(dot(g_heads, weights.block(tile, 0, 3 * LANES), 1, 1))
    g_normed = add_up(parts)
    g_norms_ref[...] = g_norms_in_ref[...]
    g_norms_ref[4:5] = jnp.sum(g_normed * unit, 0, keepdims=True)
    g_norms_ref[5:6] = jnp.sum(g_normed, 0, keepdims=True)
    g_resid = g_mid_in_ref[...] + feats.norm_back(unit, inverse, gain, g_normed)
    mid = mid_ref[...]
    normed = feats.norm(mid, norms_ref[2:3], norms_ref[3:4])
    for turn, tile in turns:
        hidden = dot(normed, layer.up(tile))
        share = normal_share(hidden)
        act_ref[turn] = (hidden * share).astype(brain)
        slope_ref[turn] = gelu_slope(hidden, share)
    g_gain, g_shift = feed_back(
        feats, turns, g_resid, mid, normed, mixed_ref, layer, norms_ref[2:3], act_ref, slope_ref,
        grads, 3 * LANES, g_mid_ref, g_mixed_ref,
    )
    g_norms_ref[2:3] = g_gain
    g_norms_ref[3:4] = g_shift


def lower(
    feats, cube, cuts, orders, grad_orders, me, dq, own_part, other_part, g_mid, resid, mid,
    mixed, w_in, parts, norms, cosine, sine, g_norms,
):
    own, wide = mixed.shape
    tiles = cube.tensors
    rows = w_in.shape[2]
    hidden = (cuts[-1] - LANES) // 2
    columns = cuts[-1] + 3 * LANES
    count = len(grad_orders)
    grads = (count, cube.devices // 2, rows, columns // count)
    outs = [
        jax.ShapeDtypeStruct(grads, single),
        jax.ShapeDtypeStruct(grads, single),
        jax.ShapeDtypeStruct(resid.shape, single),
        jax.ShapeDtypeStruct(mixed.shape, brain),
        jax.ShapeDtypeStruct(norms.shape, single),
    ]
    before = (dq, own_part, other_part, g_mid, resid, mid, mixed)
    after = (norms, cosine, sine, g_norms)
    in_specs = [
        scalar_spec(),
        *[whole_spec(x.shape) for x in before],
        columns_spec(w_in, 3 * LANES, 0),
        *[whole_spec(x.shape) for x in (*parts, *after)],
    ]
    scratch = [
        pltpu.VMEM((tiles, own, hidden), brain),
        pltpu.VMEM((tiles, own, hidden), single),
    ]
    ins = (me, *before, w_in, *parts, *after)
    kernel = functools.partial(lower_kernel, feats, cube, cuts, orders, grad_orders)
    return call(kernel, "lower", ins, in_specs, outs, 22, scratch)


def stacked_lanes(ref, row, value):
    rows = value.shape[0]
    for at in range(value.shape[1] // LANES):
        ref[row : row + rows, :] = value[:, at * LANES : (at + 1) * LANES]
        row += rows
    return row


def side_by_side(x, rows):
    return jnp.concatenate([x[at : at + rows] for at in range(0, x.shape[0], rows)], 1)


def bottom_kernel(
    feats, cube, me_ref, dq_ref, own_ref, other_ref, g_mid_ref, ids_ref, w_ref, norms_ref,
    vocab_ref, g_vocab_in_ref, g_norms_in_ref, cos_ref, sin_ref, keep_ref, send_ref, norms_out_ref,
):
    tiles = cube.tensors
    own = dq_ref.shape[0]
    mine = me_ref[0] & (tiles - 1)
    hot = lax.broadcasted_iota(jnp.int32, (TABLE_ROWS, own), 0) == ids_ref[...]
    hot = hot.astype(single).astype(brain)
    cosine = cos_ref[...]
    sine = sin_ref[...]
    weights = Gathered(w_ref)
    refs = (keep_ref, send_ref)
    rows = [0, 0]
    parts = []
    for turn in range(tiles):
        tile = turn ^ mine
        g_table = dot(hot, head_grads(tile, dq_ref, own_ref, other_ref, cosine, sine))
        rows[turn & 1] = stacked_lanes(refs[turn & 1], rows[turn & 1], g_table)
        weight = weights.block(tile, 0, 3 * LANES)
        high, middle_part, low = split_three(g_table)
        parts.append(dot(high, weight, 1, 1))
        parts.append(dot(middle_part, weight, 1, 1))
        parts.append(dot(low, weight, 1, 1))
    g_normed = add_up(parts)
    unit, inverse = feats.centred(vocab_ref[...].astype(single)[:TABLE_ROWS])
    norms_out_ref[...] = g_norms_in_ref[...]
    norms_out_ref[0:1] = jnp.sum(g_normed * unit, 0, keepdims=True)
    norms_out_ref[1:2] = jnp.sum(g_normed, 0, keepdims=True)
    g_norms = norms_out_ref[...]
    g_rows = feats.norm_back(unit, inverse, norms_ref[0:1], g_normed)
    g_vocab = g_vocab_in_ref[...] + (dot_exact(hot, g_mid_ref[...]) + g_rows)
    for ref, row in zip(refs, rows):
        row = stacked_lanes(ref, row, g_vocab)
        stacked_lanes(ref, row, g_norms)


def bottom(
    feats, cube, me, dq, own_part, other_part, g_mid, ids, w_in, at_block, norms, vocab, g_vocab,
    g_norms, cosine, sine,
):
    tiles = cube.tensors
    table_rows = 3 * TABLE_ROWS * tiles // 2
    vector_rows = (g_vocab.shape[0] + g_norms.shape[0]) * g_vocab.shape[1] // LANES
    out = jax.ShapeDtypeStruct((table_rows + vector_rows, LANES), single)
    before = (dq, own_part, other_part, g_mid, ids)
    after = (norms, vocab, g_vocab, g_norms, cosine, sine)
    in_specs = [
        scalar_spec(),
        *[whole_spec(x.shape) for x in before],
        columns_spec(w_in, 3 * LANES, at_block),
        *[whole_spec(x.shape) for x in after],
    ]
    outs = [out, out, jax.ShapeDtypeStruct(norms.shape, single)]
    ins = (me, *before, w_in, *after)
    kernel = functools.partial(bottom_kernel, feats, cube)
    return call(kernel, "bottom", ins, in_specs, outs, 7)[:2]


def halve_kernel(count, together, keep_ref, *refs):
    got = refs[:1] if together else refs[:count]
    outs = refs[len(got) :]
    size = keep_ref.shape[1]
    half = size // 2
    for part in range(count):
        arrived = got[0].at[part] if together else got[part]
        if size == 1:
            outs[0][part] = keep_ref[part] + arrived[...]
        else:
            outs[0][part] = keep_ref[part, :half] + arrived[:half]
            outs[1 + part][...] = keep_ref[part, half:] + arrived[half:]


def halve(keep, got):
    count, size, rows, wide = keep.shape
    together = not isinstance(got, list)
    got = [got] if together else got
    step = 16
    half = max(size // 2, 1)

    def spec(*lead):
        return pl.BlockSpec((*lead, step, wide), lambda at: (*([0] * len(lead)), at, 0))

    outs = [jax.ShapeDtypeStruct((count, half, rows, wide), single)]
    out_specs = [spec(count, half)]
    if size > 1:
        outs += [jax.ShapeDtypeStruct((half, rows, wide), single)] * count
        out_specs += [spec(half)] * count
    got_specs = [spec(count, size)] if together else [spec(size)] * count
    return pl.pallas_call(
        functools.partial(halve_kernel, count, together),
        grid=(rows // step,),
        in_specs=[spec(count, size), *got_specs],
        out_specs=out_specs,
        out_shape=outs,
        compiler_params=params(),
        cost_estimate=cost(2),
        name="halve",
    )(keep, *got)


def scatter_sums(cube, keep, send, orders):
    got = cube.swap(send, 0)
    for step in range(len(orders[0])):
        keep, *sends = halve(keep, got)
        got = [cube.swap(x, order[step]) for x, order in zip(sends, orders)]
    return halve(keep, got)[0][:, 0]


def normalize_features(resid, gain, shift):
    centre = resid - jnp.mean(resid, -1, keepdims=True)
    spread = jnp.mean(centre * centre, -1, keepdims=True)
    return centre * lax.rsqrt(spread + norm_eps) * gain + shift


def adamw(master, first, second, grad, step_rate):
    mean = beta_first * first + (1.0 - beta_first) * grad
    square = beta_second * second + (1.0 - beta_second) * grad * grad
    corrected = mean / (1.0 - beta_first**STEP)
    rescaled_values = square / (1.0 - beta_second**STEP)
    fresh = master - step_rate * (
        corrected / (jnp.sqrt(rescaled_values) + adam_eps) + weight_decay * master
    )
    return (fresh, mean, square)


def pad_lanes(x, lanes):
    return jnp.pad(x, [(0, 0)] * (x.ndim - 1) + [(0, lanes - x.shape[-1])])


def make_shards(groups, tensors):
    axes = ("dp", "tensor")
    cube = Cube(groups, tensors)

    def shards(
        token_ids,
        mask_pos,
        mask_target,
        mask_count,
        weight_in,
        weight_out,
        weight_up,
        weight_down,
        norm_params,
        vocab_table,
        first_in,
        first_out,
        first_up,
        first_down,
        first_norm,
        first_vocab,
        second_in,
        second_out,
        second_up,
        second_down,
        second_norm,
        second_vocab,
    ):
        layers, block, in_wide = weight_in.shape
        heads = in_wide // (3 * HEAD)
        per_heads = heads * HEAD
        hidden = weight_up.shape[2]
        hidden_padded = -(-hidden // LANES) * LANES
        vocab_count, width = vocab_table.shape
        feats = Features(width, groups)
        local_len = token_ids.shape[1]
        length = local_len * tensors
        own = length // 2
        here = lax.axis_index("tensor")
        group_at = lax.axis_index("dp")
        me = (group_at * tensors + here).astype(jnp.int32).reshape(1)
        sequence = here // 2
        quarters = jnp.stack([here, here ^ 2, here ^ 1, here ^ 3])

        heads_in = weight_in.astype(brain).transpose(1, 0, 2)
        heads_in = heads_in.reshape(block, layers, heads, 3, HEAD).transpose(0, 1, 3, 2, 4)
        heads_in = pad_lanes(heads_in.reshape(block, layers, 3, per_heads), LANES)
        heads_in = heads_in.reshape(block, layers, 3 * LANES)
        feed = jnp.concatenate(
            [
                pad_lanes(weight_out.astype(brain).transpose(2, 0, 1), LANES),
                pad_lanes(weight_up.astype(brain).transpose(1, 0, 2), hidden_padded),
                pad_lanes(weight_down.astype(brain).transpose(2, 0, 1), hidden_padded),
            ],
            2,
        )
        feed_columns = feed.shape[2]
        all_columns = 3 * LANES + feed_columns

        def pad_rows(x):
            return jnp.pad(x, ((0, feats.padded - block), (0, 0)))

        vocab_low = vocab_table.astype(brain)
        vocab_padded = jnp.pad(feats.pad(vocab_low), ((0, 64 - vocab_count), (0, 0)))
        norms = jnp.pad(feats.pad(norm_params), ((0, 16 - norm_params.shape[0]), (0, 0)))

        table_low = normalize_features(
            lax.reduce_precision(vocab_table, 8, 7), norm_params[0], norm_params[1]
        ).astype(brain)
        table_own = lax.dynamic_slice_in_dim(
            table_low.reshape(vocab_count, groups, block), group_at, 1, 1
        )[:, 0]
        table = dot(table_own, heads_in[:, 0])
        extra = jnp.zeros((TABLE_ROWS - vocab_count, 3 * LANES), single)
        extra = extra.at[0, 0].set(jnp.sum(mask_count).astype(single))
        table = jnp.concatenate([table, extra], 0)
        for at in range(2, cube.size):
            table = table + cube.swap(table, at)
        count_total = table[vocab_count, 0]
        ids_row = vocab_count + 1
        table = lax.dynamic_update_slice(
            table, pad_lanes(token_ids.astype(single), 3 * LANES), (ids_row, 0)
        )
        got = cube.swap(table, 1)
        upper = (here & 2) == 2
        pair = jnp.stack([jnp.where(upper, got, table), jnp.where(upper, table, got)])
        got = cube.swap(pair, 0)
        upper = (here & 1) == 1
        table = jnp.stack([jnp.where(upper, got, pair), jnp.where(upper, pair, got)], 1)
        table = table.reshape(tensors, TABLE_ROWS, 3 * LANES)
        ids = jnp.take(table[:, ids_row : ids_row + 2, :local_len], sequence, axis=1)
        ids = jnp.take(ids, quarters, axis=0).reshape(1, length).astype(jnp.int32)

        cuts = (0, LANES + hidden_padded, feed_columns)
        orders = [cube.outer(0) + [0], cube.outer(2) + [0]]
        feed_low = pad_rows(feed[:, 0])
        parts = [
            cube.gather(feed_low[:, low:high], order)
            for low, high, order in zip(cuts[:-1], cuts[1:], orders)
        ]
        rest = pad_rows(jnp.concatenate([heads_in[:, 1], feed[:, 1], heads_in[:, 0]], 1))
        weights = lax.all_gather(rest, axes, axis=0, tiled=False)
        weights = weights.reshape((groups, tensors) + rest.shape)
        low_block = all_columns // (3 * LANES)

        half = HEAD // 2
        freqs = 10000.0 ** (-jnp.arange(half, dtype=single) * 2.0 / HEAD)
        positions = (quarters[:, None] * local_len + jnp.arange(local_len)[None, :]).reshape(length)
        angles = positions.astype(single)[:, None] * freqs[None, :]
        cosine, sine = (jnp.cos(angles), jnp.sin(angles))
        cosine = pad_lanes(jnp.tile(jnp.concatenate([cosine, cosine], 1), (1, heads)), LANES)
        sine = pad_lanes(jnp.tile(jnp.concatenate([-sine, sine], 1), (1, heads)), LANES)
        cos_own, sin_own = (cosine[:own], sine[:own])

        slots = mask_pos.shape[1]
        my_pos = jnp.take(mask_pos, sequence, axis=0)
        my_count = jnp.take(mask_count, sequence, axis=0)
        quarter = my_pos // local_len
        inside = my_pos % local_len
        slot = jnp.where(
            quarter == here, inside, jnp.where(quarter == (here ^ 2), inside + local_len, -1)
        )
        slot = jnp.where(jnp.arange(slots) < my_count, slot, -1).reshape(slots, 1)
        target = jnp.take(mask_target, sequence, axis=0).reshape(slots, 1)
        count = jnp.broadcast_to(count_total, (8, LANES))

        q_low, kv_low, kv_low_other, resid_low = embed(table, ids, vocab_padded, cosine, sine)
        mixed_low, logsum_low = attend(q_low, kv_low, kv_low_other, heads)
        mid_low, resid, q, kv = middle(
            feats, cube, cuts, orders, me, mixed_low, resid_low, parts, weights, norms,
            cos_own, sin_own,
        )
        kv_other = cube.swap(kv, 0)
        mixed, logsum = attend(q, kv, kv_other, heads)
        grads_top, g_mid, g_mixed, g_norms, g_vocab = top(
            feats, mixed, resid, weights, all_columns, norms, vocab_padded, vocab_count, slot,
            target, count,
        )
        grads_top = grads_top.reshape((cube.devices,) + grads_top.shape[2:])
        grads_top = lax.psum_scatter(grads_top, axes, scatter_dimension=0, tiled=True)[0]
        dq, own_part, other_part = attend_back(q, kv, kv_other, g_mixed, logsum, heads)
        got = cube.swap(other_part, 0)
        grad_orders = [cube.outer(turn) for turn in range(4)]
        keep, send, g_mid, g_mixed, g_norms = lower(
            feats, cube, cuts, orders, grad_orders, me, dq, own_part, got, g_mid, resid, mid_low,
            mixed_low, weights, parts, norms, cos_own, sin_own, g_norms,
        )
        grads_low = scatter_sums(cube, keep, send, grad_orders)
        dq, own_part, other_part = attend_back(
            q_low, kv_low, kv_low_other, g_mixed, logsum_low, heads
        )
        got = cube.swap(other_part, 0)
        keep, send = bottom(
            feats, cube, me, dq, own_part, got, g_mid, ids[:, :own], weights, low_block, norms,
            vocab_padded, g_vocab, g_norms, cos_own, sin_own,
        )
        total = keep + cube.swap(send, 0)
        tile_rows = 3 * TABLE_ROWS
        got = cube.swap(total[tile_rows:], 1)
        total = jnp.concatenate(
            [total[:tile_rows] + got[:tile_rows], total[2 * tile_rows :] + got[tile_rows:]], 0
        )
        for at in range(2, cube.size):
            total = total + cube.swap(total, at)
        g_table = side_by_side(total[:tile_rows], TABLE_ROWS)[:vocab_count]
        vocab_rows = TABLE_ROWS * feats.total // LANES
        g_vocab = side_by_side(total[tile_rows : tile_rows + vocab_rows], TABLE_ROWS)
        g_vocab = feats.unpad(g_vocab[:vocab_count])
        g_norms = side_by_side(total[tile_rows + vocab_rows :], norms.shape[0])
        loss_total = g_norms[LOSS_ROW, 0]
        g_norms = feats.unpad(g_norms[: norm_params.shape[0]])
        grads_in_low = lax.dot_general(
            table_own.astype(single),
            g_table,
            (((0,), (0,)), ((), ())),
            precision=highest,
            preferred_element_type=single,
        )

        def unpack_in(grad):
            grad = grad[:block].reshape(block, 3, LANES)[:, :, :per_heads]
            return grad.reshape(block, 3, heads, HEAD).transpose(0, 2, 1, 3).reshape(block, in_wide)

        grads_low = jnp.concatenate(list(grads_low), 1)
        grad_in = jnp.stack([unpack_in(grads_in_low), unpack_in(grads_low[:, : 3 * LANES])], 1)
        both = jnp.stack([grads_low[:block, 3 * LANES :], grads_top[:block]], 1)
        grad_in = grad_in.transpose(1, 0, 2)
        grad_out = both[:, :, :per_heads].transpose(1, 2, 0)
        grad_up = both[:, :, LANES : LANES + hidden].transpose(1, 0, 2)
        start = LANES + hidden_padded
        grad_down = both[:, :, start : start + hidden].transpose(1, 2, 0)

        masters = (weight_in, weight_out, weight_up, weight_down, norm_params, vocab_table)
        firsts = (first_in, first_out, first_up, first_down, first_norm, first_vocab)
        seconds = (second_in, second_out, second_up, second_down, second_norm, second_vocab)
        grads = (grad_in, grad_out, grad_up, grad_down, g_norms, g_vocab)
        results = [
            adamw(masters[which], firsts[which], seconds[which], grads[which], step_rates[which])
            for which in range(6)
        ]
        news = [entry[0] for entry in results]
        means = [entry[1] for entry in results]
        squares = [entry[2] for entry in results]
        copies = [news[which].astype(brain) for which in (0, 1, 2, 3, 5)]
        return (loss_total, count_total, *news, *means, *squares, *copies)

    return shards


def solution(mesh):
    rows_in = P(None, "dp", "tensor")
    rows_out = P(None, "tensor", "dp")
    six = (rows_in, rows_out, rows_in, rows_out, P(), P())
    five = (rows_in, rows_out, rows_in, rows_out, P())
    return jax.shard_map(
        make_shards(mesh.shape["dp"], mesh.shape["tensor"]),
        mesh=mesh,
        in_specs=(P("dp", "tensor"), P("dp", None), P("dp", None), P("dp"), *six, *six, *six),
        out_specs=(P(), P(), *six, *six, *six, *five),
        check_vma=False,
    )
```

time: 1310 us -> 492 us (0.38)
  waiting for transfers between devices: 619 us -> 130 us
  matrix products: 265 us -> 0.51 us
  Pallas kernels: 0 us -> 209 us
  blocking collectives: 192 us -> 0 us
  other arithmetic: 160 us -> 8.36 us
  starting transfers between devices: 1.17 us -> 77.3 us
    reduce_scatter x8 -> x1, waiting for transfers between devices: 313 us -> 0.02 us  [shards(): lax.psum_scatter(grads_top, axes, scatter_dimension=0, tiled=True)[0]]
    dot_general x55 -> x1, matrix products: 265 us -> 0.16 us  [dot(): lax.dot_general(left, right, (((left_dim,), (right_dim,)), ((), ())), pre...]
    pallas_call x0 -> x14, Pallas kernels: none -> 209 us  [the longest x5 71.3 us: call(): pl.pallas_call(kernel, grid=(1,), in_specs=in_specs, out_specs=[whole_spe...]
    unnamed x18 -> x2, waiting for transfers between devices: 198 us -> 0.03 us
    all_gather x4 -> x0, blocking collectives: 130 us -> none  [the longest x1 33.7 us: shards(): lax.all_gather(weight_in.astype(brain), 'dp', axis=1, tiled=True)]
    ppermute x0 -> x40, waiting for transfers between devices: none -> 128 us  [swap(): return lax.ppermute(x, ('dp', 'tensor'), pairs)]
    all_gather x8 -> x1, waiting for transfers between devices: 108 us -> 1.88 us  [shards(): weights = lax.all_gather(rest, axes, axis=0, tiled=False)]
    convert_element_type x20 -> x6, other arithmetic: 87.2 us -> 1.4 us  [the longest x1 0.95 us: shards(): weight_out.astype(brain).transpose(2, 0, 1)]
  transfers between devices with their start and end apart: 17 -> 42, of which waited for: 15 -> 19; matrix products, arithmetic and copies ran while one was open for 4% -> 6% of each run, Pallas kernels for 0% -> 23%
where the time goes in v1:
time: 492 us; the launch traced here: 487 us
  Pallas kernels  209 us (42%)
  waiting for transfers between devices  130 us (26%)
  starting transfers between devices  77.3 us (16%)
  local copies, waits for them, and re-layouts  45.9 us (9%)
  between operations  16.6 us (3%)
  other arithmetic  8.36 us (2%)
    ppermute x40, waiting for transfers between devices, swap(): return lax.ppermute(x, ('dp', 'tensor'), pairs)  128 us
    ppermute x40, starting transfers between devices, swap(): return lax.ppermute(x, ('dp', 'tensor'), pairs)  77.2 us
    pallas_call x5, Pallas kernels, call(): pl.pallas_call(kernel, grid=(1,), in_specs=in_specs, out_specs=[whole_spe...  71.3 us
    pallas_call x2, Pallas kernels, attend_back(): pl.pallas_call(functools.partial(attend_back_kernel, heads, own), grid=(t...  65.6 us
    pallas_call x2, Pallas kernels, attend(): pl.pallas_call(functools.partial(attend_kernel, heads, LANES), grid=(tile...  48.8 us
    unnamed x128, local copies, waits for them, and re-layouts  27.4 us
    pallas_call x5, Pallas kernels, halve(): pl.pallas_call(functools.partial(halve_kernel, count, together), grid=(ro...  23 us
  transfers between devices with their start and end apart: 42, of which 19 were waited for; matrix products, arithmetic and copies ran while one was open for 6% of the time, Pallas kernels for 23%

profile of v1, /device:TPU:0, one launch (start us, length us, event | category | flops | bytes accessed | tf_op | source)
XLA Modules:
  0.0 487.5 jit_solution(16984865903930495898)
XLA Ops:
  13.1 3.0 collective-permute-start
  16.1 1.6 collective-permute-start.10
  25.8 4.1 collective-permute-start.11
  30.5 1.6 collective-permute-start.6
  32.1 2.2 collective-permute-start.2
  35.0 3.3 collective-permute-done.2
  39.7 1.5 collective-permute-start.12
  43.3 3.0 collective-permute-start.7
  48.4 1.5 collective-permute-start.13
  49.9 13.7 %collective-permute-done.7 = bf16[4,64,640]{2,1,0:T(8,128)(2,1)S(1)} collective-permute-done((bf16[4,64,640]{2,1,0:T(8,128)(2,1)S(1)}, bf16[4,64,640]{2,1,0:T(8,128)(2,1)S(1)}, u32[]{:S(2)}, u32[]{:S(2)}) %collective-permute-start.7) | collective-permute-done | bytes 327712 | tf_op jit(solution)/shard_map/ppermute | solution.py:51
  63.7 3.2 collective-permute-start.8
  66.9 6.2 %embed.1 = (bf16[512,512]{1,0:T(8,128)(2,1)}, bf16[2,512,512]{2,1,0:T(8,128)(2,1)}, bf16[2,512,512]{2,1,0:T(8,128)(2,1)}, f32[512,512]{1,0:T(8,128)}) custom-call(f32[4,40,384]{2,1,0:T(8,128)} %bitcast.157, s32[1,1024]{1,0:T(1,128)} %bitcast.164, bf16[64,512]{1,0:T(8,128)(2,1)} %pad.59.vocab_ref, f32[1024,128]{1,0:T(8,128)} %pad.60.cos_ref, ...), custom_call_target="tpu_custom_call" | custom-call | flops 6600000000 | tf_op jit(solution)/shard_map/embed/pallas_call | solution.py:326
  75.9 14.1 %collective-permute-done.8 = bf16[8,64,640]{2,1,0:T(8,128)(2,1)S(1)} collective-permute-done((bf16[8,64,640]{2,1,0:T(8,128)(2,1)S(1)}, bf16[8,64,640]{2,1,0:T(8,128)(2,1)S(1)}, u32[]{:S(2)}, u32[]{:S(2)}) %collective-permute-start.8) | collective-permute-done | bytes 655392 | tf_op jit(solution)/shard_map/ppermute | solution.py:51
  91.3 20.3 %attend.2 = (bf16[512,512]{1,0:T(8,128)(2,1)}, f32[4,8,512]{2,1,0:T(8,128)}) custom-call(bf16[512,512]{1,0:T(8,128)(2,1)} %get-tuple-element.88.q_ref, bf16[2,512,512]{2,1,0:T(8,128)(2,1)} %get-tuple-element.89.own_ref.kv_own_ref, bf16[2,512,512]{2,1,0:T(8,128)(2,1)} %get-tuple-element.90.other_ref.kv_other_ref), custom_call_target="tpu_custom_call" | custom-call | flops 22000001024 | tf_op jit(solution)/shard_map/attend/pallas_call | solution.py:404
  113.9 1.9 all-gather.3.cloned.1.call-done
  115.7 12.2 %middle.1 = (f32[512,512]{1,0:T(8,128)}, f32[512,512]{1,0:T(8,128)}, bf16[512,512]{1,0:T(8,128)(2,1)}, bf16[2,512,512]{2,1,0:T(8,128)(2,1)}) custom-call(s32[1]{0:T(128)} %bitcast.me_ref, bf16[512,512]{1,0:T(8,128)(2,1)} %get-tuple-element.91.mixed_ref, f32[512,512]{1,0:T(8,128)} %get-tuple-element.92.resid_ref, ...), custom_call_target="tpu_custom_call" | custom-call | flops 13200000000 | tf_op jit(solution)/shard_map/middle/pallas_call | solution.py:326
  132.0 28.5 %attend.3 = (bf16[512,512]{1,0:T(8,128)(2,1)}, f32[4,8,512]{2,1,0:T(8,128)}) custom-call(bf16[512,512]{1,0:T(8,128)(2,1)} %get-tuple-element.93.q_ref, bf16[2,512,512]{2,1,0:T(8,128)(2,1)} %get-tuple-element.94.own_ref.kv_own_ref, bf16[2,512,512]{2,1,0:T(8,128)(2,1)} %copy-done.32), custom_call_target="tpu_custom_call" | custom-call | flops 22000001024 | tf_op jit(solution)/shard_map/attend/pallas_call | solution.py:404
  161.8 21.8 %top.1 = (f32[8,4,64,1152]{3,2,1,0:T(8,128)}, f32[512,512]{1,0:T(8,128)}, bf16[512,512]{1,0:T(8,128)(2,1)}, f32[16,512]{1,0:T(8,128)}, f32[40,512]{1,0:T(8,128)}) custom-call(bf16[512,512]{1,0:T(8,128)(2,1)} %get-tuple-element.95.mixed_ref, f32[512,512]{1,0:T(8,128)} %get-tuple-element.96.resid_ref, bf16[8,4,64,1920]{3,2,1,0:T(8,128)(2,1)} %bitcast.171, ...), custom_call_target="tpu_custom_call" | custom-call | flops 23100000256 | tf_op jit(solution)/shard_map/top/pallas_call | solution.py:326
  183.6 32.9 %attend_back.2 = (f32[512,512]{1,0:T(8,128)}, f32[2,512,512]{2,1,0:T(8,128)}, f32[2,512,512]{2,1,0:T(8,128)}) custom-call(bf16[512,512]{1,0:T(8,128)(2,1)} %get-tuple-element.93.q_ref, bf16[2,512,512]{2,1,0:T(8,128)(2,1)} %get-tuple-element.94.own_ref.kv_own_ref, bf16[2,512,512]{2,1,0:T(8,128)(2,1)} %copy-done.32, bf16[512,512]{1,0:T(8,128)(2,1)} %get-tuple-element.97.g_ref, ...), custom_call_target="tpu_custom_call" | custom-call | flops 36300001280 | tf_op jit(solution)/shard_map/attend_back/pallas_call | solution.py:467
  216.9 4.1 collective-permute-done.16.other_ref
  222.3 23.4 %lower.1 = (f32[4,16,64,384]{3,2,1,0:T(8,128)}, f32[4,16,64,384]{3,2,1,0:T(8,128)}, f32[512,512]{1,0:T(8,128)}, bf16[512,512]{1,0:T(8,128)(2,1)}, f32[16,512]{1,0:T(8,128)}) custom-call(s32[1]{0:T(128)} %bitcast.me_ref, f32[512,512]{1,0:T(8,128)} %get-tuple-element.99.dq_ref, f32[2,512,512]{2,1,0:T(8,128)} %get-tuple-element.100.own_ref, ...), custom_call_target="tpu_custom_call" | custom-call | flops 24199999488 | tf_op jit(solution)/shard_map/lower/pallas_call | solution.py:326
  246.0 32.6 %attend_back.3 = (f32[512,512]{1,0:T(8,128)}, f32[2,512,512]{2,1,0:T(8,128)}, f32[2,512,512]{2,1,0:T(8,128)}) custom-call(bf16[512,512]{1,0:T(8,128)(2,1)} %get-tuple-element.88.q_ref, bf16[2,512,512]{2,1,0:T(8,128)(2,1)} %get-tuple-element.89.own_ref.kv_own_ref, bf16[2,512,512]{2,1,0:T(8,128)(2,1)} %get-tuple-element.90.other_ref.kv_other_ref, ...), custom_call_target="tpu_custom_call" | custom-call | flops 36300001280 | tf_op jit(solution)/shard_map/attend_back/pallas_call | solution.py:467
  279.4 3.8 collective-permute-done.17.other_ref
  284.6 7.7 %bottom.1 = (f32[464,128]{1,0:T(8,128)}, f32[464,128]{1,0:T(8,128)}, f32[16,512]{1,0:T(8,128)}) custom-call(s32[1]{0:T(128)} %bitcast.me_ref, f32[512,512]{1,0:T(8,128)} %get-tuple-element.107.dq_ref, f32[2,512,512]{2,1,0:T(8,128)} %get-tuple-element.108.own_ref, f32[2,512,512]{2,1,0:T(8,128)} %copy-done.31, f32[512,512]{1,0:T(8,128)} %get-tuple-element.110.g_mid_ref, ...), custom_call_target="tpu_custom_call" | custom-call | flops 7699999744 | tf_op jit(solution)/shard_map/bottom/pallas_call | solution.py:326
  295.0 1.8 collective-permute-start.19
  296.8 6.3 %collective-permute-done.19 = f32[344,128]{1,0:T(8,128)S(1)} collective-permute-done((f32[344,128]{1,0:T(8,128)S(1)}, f32[344,128]{1,0:T(8,128)S(1)}, u32[]{:S(2)}, u32[]{:S(2)}) %collective-permute-start.19) | collective-permute-done | bytes 176160 | tf_op jit(solution)/shard_map/ppermute | solution.py:51
  304.5 8.9 %collective-permute-done.20 = f32[344,128]{1,0:T(8,128)S(1)} collective-permute-done((f32[344,128]{1,0:T(8,128)S(1)}, f32[344,128]{1,0:T(8,128)S(1)}, u32[]{:S(2)}, u32[]{:S(2)}) %collective-permute-start.20) | collective-permute-done | bytes 176160 | tf_op jit(solution)/shard_map/ppermute | solution.py:51
  313.4 23.9 %collective-permute-start.21 = (f32[344,128]{1,0:T(8,128)S(1)}, f32[344,128]{1,0:T(8,128)S(1)}, u32[]{:S(2)}, u32[]{:S(2)}) collective-permute-start(f32[344,128]{1,0:T(8,128)S(1)} %fusion.34), channel_id=1, source_target_pairs={{0,8},{1,9},{2,10},{3,11},{4,12},{5,13},{6,14},{7,15},{8,0},{9,1},... | collective-permute-start | bytes 528392 | tf_op jit(solution)/shard_map/ppermute | solution.py:51
  337.3 7.5 %halve.5 = (f32[4,8,64,384]{3,2,1,0:T(8,128)}, f32[8,64,384]{2,1,0:T(8,128)}, f32[8,64,384]{2,1,0:T(8,128)}, f32[8,64,384]{2,1,0:T(8,128)}, f32[8,64,384]{2,1,0:T(8,128)}) custom-call(f32[4,16,64,384]{3,2,1,0:T(8,128)} %get-tuple-element.115.keep_ref, f32[4,16,64,384]{3,2,1,0:T(8,128)} %collective-permute-done.23.refs_0_), custom_call_target="tpu_custom_call" | custom-call | flops 2200000000 | tf_op jit(solution)/shard_map/halve/pallas_call | solution.py:853
  347.5 2.1 collective-permute-start.27
  349.6 1.8 collective-permute-start.22
  352.1 46.1 %collective-permute-done.22 = f32[344,128]{1,0:T(8,128)S(1)} collective-permute-done((f32[344,128]{1,0:T(8,128)S(1)}, f32[344,128]{1,0:T(8,128)S(1)}, u32[]{:S(2)}, u32[]{:S(2)}) %collective-permute-start.22) | collective-permute-done | bytes 176160 | tf_op jit(solution)/shard_map/ppermute | solution.py:51
  399.4 5.1 %halve.6 = (f32[4,4,64,384]{3,2,1,0:T(8,128)}, f32[4,64,384]{2,1,0:T(8,128)}, f32[4,64,384]{2,1,0:T(8,128)}, f32[4,64,384]{2,1,0:T(8,128)}, f32[4,64,384]{2,1,0:T(8,128)}) custom-call(f32[4,8,64,384]{3,2,1,0:T(8,128)} %get-tuple-element.117.keep_ref, f32[8,64,384]{2,1,0:T(8,128)} %copy-done.33, f32[8,64,384]{2,1,0:T(8,128)} %copy-done.34, ...), custom_call_target="tpu_custom_call" | custom-call | flops 2200000000 | tf_op jit(solution)/shard_map/halve/pallas_call | solution.py:853
  405.2 5.5 %collective-permute-start.29 = (f32[4,64,384]{2,1,0:T(8,128)}, f32[4,64,384]{2,1,0:T(8,128)S(1)}, u32[]{:S(2)}, u32[]{:S(2)}) collective-permute-start(f32[4,64,384]{2,1,0:T(8,128)} %get-tuple-element.124), channel_id=1, source_target_pairs={{0,8},{1,9},{2,10},{3,11},{4,12},{5,13},{6,14},{7,15},{8,0},{9,1},... | collective-permute-start | bytes 1179656 | tf_op jit(solution)/shard_map/ppermute | solution.py:51
  410.8 1.8 collective-permute-start.30
  414.8 8.7 %collective-permute-done.29.refs_1_ = f32[4,64,384]{2,1,0:T(8,128)S(1)} collective-permute-done((f32[4,64,384]{2,1,0:T(8,128)}, f32[4,64,384]{2,1,0:T(8,128)S(1)}, u32[]{:S(2)}, u32[]{:S(2)}) %collective-permute-start.29) | collective-permute-done | bytes 393248 | tf_op jit(solution)/shard_map/ppermute | solution.py:51
  423.5 8.4 %collective-permute-done.30.refs_2_ = f32[4,64,384]{2,1,0:T(8,128)S(1)} collective-permute-done((f32[4,64,384]{2,1,0:T(8,128)}, f32[4,64,384]{2,1,0:T(8,128)S(1)}, u32[]{:S(2)}, u32[]{:S(2)}) %collective-permute-start.30) | collective-permute-done | bytes 393248 | tf_op jit(solution)/shard_map/ppermute | solution.py:51
  432.8 3.9 halve.7
  436.7 2.0 collective-permute-start.33
  440.1 1.5 collective-permute-start.35
  441.9 2.7 collective-permute-done.32.refs_0_
  444.6 2.3 collective-permute-done.33.refs_1_
  447.7 3.4 halve.8
  451.1 1.8 collective-permute-start.36
  452.8 1.5 collective-permute-start.37
  454.3 1.5 collective-permute-start.38
  459.1 1.5 collective-permute-done.39.refs_3_
  461.3 3.1 halve.9
  (298 shorter events, 69.8 us)
Async XLA Ops:
  7.2 108.5 %all-gather.3.cloned.1.call-start = ((), (), s32[]{:S(2)}) async-start(), calls=%async_computation.2 | async-start | bytes 8110080 | tf_op jit(solution)/shard_map/all_gather | solution.py:995
  10.9 458.4 %reduce-scatter.2.cloned.1.call-start = ((), (), s32[]{:S(2)}) async-start(), calls=%async_computation.1 | async-start | bytes 9732096 | tf_op jit(solution)/shard_map/reduce_scatter | solution.py:1033
  13.1 12.5 %collective-permute-start = (f32[40,384]{1,0:T(8,128)S(1)}, f32[40,384]{1,0:T(8,128)S(1)}, u32[]{:S(2)}, u32[]{:S(2)}) collective-permute-start(f32[40,384]{1,0:T(8,128)S(1)} %select_maximum_fusion), channel_id=1, source_target_pairs={{0,4},{1,5},{2,6},{3,7},{4,0},{5,1},{6,2},{7,3},{8,12},{9,13},{10,... | collective-permute-start | bytes 184328 | tf_op jit(solution)/shard_map/ppermute | solution.py:51
  16.1 9.6 %collective-permute-start.10 = (bf16[1,64,512]{2,1,0:T(8,128)(2,1)S(1)}, bf16[1,64,512]{2,1,0:T(8,128)(2,1)S(1)}, u32[]{:S(2)}, u32[]{:S(2)}) collective-permute-start(bf16[1,64,512]{2,1,0:T(8,128)(2,1)S(1)} %fusion.21), channel_id=1, source_target_pairs={{0,8},{1,9},{2,10},{3,11},{4,12},{5,13},{6,14},{7,15},{8,0},{9,1},... | collective-permute-start | bytes 196616 | tf_op jit(solution)/shard_map/ppermute | solution.py:51
  17.7 12.8 %collective-permute-start.5 = (bf16[1,64,640]{2,1,0:T(8,128)(2,1)S(1)}, bf16[1,64,640]{2,1,0:T(8,128)(2,1)S(1)}, u32[]{:S(2)}, u32[]{:S(2)}) collective-permute-start(bf16[1,64,640]{2,1,0:T(8,128)(2,1)S(1)} %fusion.19), channel_id=1, source_target_pairs={{0,4},{1,5},{2,6},{3,7},{4,0},{5,1},{6,2},{7,3},{8,12},{9,13},{10,... | collective-permute-start | bytes 245768 | tf_op jit(solution)/shard_map/ppermute | solution.py:51
  25.6 6.5 %collective-permute-start.1 = (f32[40,384]{1,0:T(8,128)S(1)}, f32[40,384]{1,0:T(8,128)S(1)}, u32[]{:S(2)}, u32[]{:S(2)}) collective-permute-start(f32[40,384]{1,0:T(8,128)S(1)} %fusion.51), channel_id=1, source_target_pairs={{0,8},{1,9},{2,10},{3,11},{4,12},{5,13},{6,14},{7,15},{8,0},{9,1},... | collective-permute-start | bytes 184328 | tf_op jit(solution)/shard_map/ppermute | solution.py:51
  25.8 13.9 %collective-permute-start.11 = (bf16[2,64,512]{2,1,0:T(8,128)(2,1)S(1)}, bf16[2,64,512]{2,1,0:T(8,128)(2,1)S(1)}, u32[]{:S(2)}, u32[]{:S(2)}) collective-permute-start(bf16[2,64,512]{2,1,0:T(8,128)(2,1)S(1)} %pad_maximum_fusion.10), channel_id=1, source_target_pairs={{0,24},{1,25},{2,26},{3,27},{4,28},{5,29},{6,30},{7,31},{8,16},{9,... | collective-permute-start | bytes 393224 | tf_op jit(solution)/shard_map/ppermute | solution.py:51
  30.5 12.7 %collective-permute-start.6 = (bf16[2,64,640]{2,1,0:T(8,128)(2,1)S(1)}, bf16[2,64,640]{2,1,0:T(8,128)(2,1)S(1)}, u32[]{:S(2)}, u32[]{:S(2)}) collective-permute-start(bf16[2,64,640]{2,1,0:T(8,128)(2,1)S(1)} %pad_maximum_fusion.9), channel_id=1, source_target_pairs={{0,2},{1,3},{2,0},{3,1},{4,6},{5,7},{6,4},{7,5},{8,10},{9,11},{10,... | collective-permute-start | bytes 491528 | tf_op jit(solution)/shard_map/ppermute | solution.py:51
  32.1 6.2 %collective-permute-start.2 = (f32[40,384]{1,0:T(8,128)S(1)}, f32[40,384]{1,0:T(8,128)S(1)}, u32[]{:S(2)}, u32[]{:S(2)}) collective-permute-start(f32[40,384]{1,0:T(8,128)S(1)} %add.239), channel_id=1, source_target_pairs={{0,24},{1,25},{2,26},{3,27},{4,28},{5,29},{6,30},{7,31},{8,16},{9,... | collective-permute-start | bytes 184328 | tf_op jit(solution)/shard_map/ppermute | solution.py:51
  38.9 4.2 collective-permute-start.3
  39.7 8.6 %collective-permute-start.12 = (bf16[4,64,512]{2,1,0:T(8,128)(2,1)S(1)}, bf16[4,64,512]{2,1,0:T(8,128)(2,1)S(1)}, u32[]{:S(2)}, u32[]{:S(2)}) collective-permute-start(bf16[4,64,512]{2,1,0:T(8,128)(2,1)S(1)} %pad_maximum_fusion.6), channel_id=1, source_target_pairs={{0,4},{1,5},{2,6},{3,7},{4,0},{5,1},{6,2},{7,3},{8,12},{9,13},{10,... | collective-permute-start | bytes 786440 | tf_op jit(solution)/shard_map/ppermute | solution.py:51
  43.1 3.9 collective-permute-start.4
  43.3 20.3 %collective-permute-start.7 = (bf16[4,64,640]{2,1,0:T(8,128)(2,1)S(1)}, bf16[4,64,640]{2,1,0:T(8,128)(2,1)S(1)}, u32[]{:S(2)}, u32[]{:S(2)}) collective-permute-start(bf16[4,64,640]{2,1,0:T(8,128)(2,1)S(1)} %pad_maximum_fusion.2), channel_id=1, source_target_pairs={{0,8},{1,9},{2,10},{3,11},{4,12},{5,13},{6,14},{7,15},{8,0},{9,1},... | collective-permute-start | bytes 983048 | tf_op jit(solution)/shard_map/ppermute | solution.py:51
  47.1 19.8 %copy-start.8 = (f32[2,2,40,384]{3,2,1,0:T(8,128)}, f32[2,2,40,384]{3,2,1,0:T(8,128)S(1)}, u32[]{:S(2)}) copy-start(f32[2,2,40,384]{3,2,1,0:T(8,128)S(1)} %copy.136) | copy-start | bytes 737284
  48.4 26.4 %collective-permute-start.13 = (bf16[8,64,512]{2,1,0:T(8,128)(2,1)S(1)}, bf16[8,64,512]{2,1,0:T(8,128)(2,1)S(1)}, u32[]{:S(2)}, u32[]{:S(2)}) collective-permute-start(bf16[8,64,512]{2,1,0:T(8,128)(2,1)S(1)} %pad_maximum_fusion.1), channel_id=1, source_target_pairs={{0,2},{1,3},{2,0},{3,1},{4,6},{5,7},{6,4},{7,5},{8,10},{9,11},{10,... | collective-permute-start | bytes 1572872 | tf_op jit(solution)/shard_map/ppermute | solution.py:51
  63.7 26.3 %collective-permute-start.8 = (bf16[8,64,640]{2,1,0:T(8,128)(2,1)S(1)}, bf16[8,64,640]{2,1,0:T(8,128)(2,1)S(1)}, u32[]{:S(2)}, u32[]{:S(2)}) collective-permute-start(bf16[8,64,640]{2,1,0:T(8,128)(2,1)S(1)} %pad_maximum_fusion), channel_id=1, source_target_pairs={{0,24},{1,25},{2,26},{3,27},{4,28},{5,29},{6,30},{7,31},{8,16},{9,... | collective-permute-start | bytes 1966088 | tf_op jit(solution)/shard_map/ppermute | solution.py:51
  75.9 35.7 %collective-permute-start.14 = (bf16[16,64,512]{2,1,0:T(8,128)(2,1)}, bf16[16,64,512]{2,1,0:T(8,128)(2,1)S(1)}, u32[]{:S(2)}, u32[]{:S(2)}) collective-permute-start(bf16[16,64,512]{2,1,0:T(8,128)(2,1)} %get-tuple-element.273), channel_id=1, source_target_pairs={{0,1},{1,0},{2,3},{3,2},{4,5},{5,4},{6,7},{7,6},{8,9},{9,8},{10,11... | collective-permute-start | bytes 3145736 | tf_op jit(solution)/shard_map/ppermute | solution.py:51
  91.2 21.4 %collective-permute-start.9 = (bf16[16,64,640]{2,1,0:T(8,128)(2,1)}, bf16[16,64,640]{2,1,0:T(8,128)(2,1)S(1)}, u32[]{:S(2)}, u32[]{:S(2)}) collective-permute-start(bf16[16,64,640]{2,1,0:T(8,128)(2,1)} %get-tuple-element.271), channel_id=1, source_target_pairs={{0,1},{1,0},{2,3},{3,2},{4,5},{5,4},{6,7},{7,6},{8,9},{9,8},{10,11... | collective-permute-start | bytes 3932168 | tf_op jit(solution)/shard_map/ppermute | solution.py:51
  115.7 14.5 %copy-start.29 = (s32[2,160]{1,0:T(2,128)S(1)}, s32[2,160]{1,0:T(2,128)}, u32[]{:S(2)}) copy-start(s32[2,160]{1,0:T(2,128)} %param.27) | copy-start | bytes 3844
  128.0 3.1 collective-permute-start.15
  216.5 4.4 collective-permute-start.16
  245.7 91.6 %collective-permute-start.23 = (f32[4,16,64,384]{3,2,1,0:T(8,128)}, f32[4,16,64,384]{3,2,1,0:T(8,128)}, u32[]{:S(2)}, u32[]{:S(2)}) collective-permute-start(f32[4,16,64,384]{3,2,1,0:T(8,128)} %get-tuple-element.116), channel_id=1, source_target_pairs={{0,1},{1,0},{2,3},{3,2},{4,5},{5,4},{6,7},{7,6},{8,9},{9,8},{10,11... | collective-permute-start | bytes 18874376 | tf_op jit(solution)/shard_map/ppermute | solution.py:51
  246.0 32.9 %copy-start.26 = (s32[1,1,4,256]{3,1,2,0:T(1,128)S(1)}, s32[1,1,4,256]{3,1,2,0:T(1,128)}, u32[]{:S(2)}) copy-start(s32[1,1,4,256]{3,1,2,0:T(1,128)} %copy.190) | copy-start | bytes 12292
  278.6 4.6 collective-permute-start.17
  292.3 1.7 collective-permute-start.18
  295.0 8.1 %collective-permute-start.19 = (f32[344,128]{1,0:T(8,128)S(1)}, f32[344,128]{1,0:T(8,128)S(1)}, u32[]{:S(2)}, u32[]{:S(2)}) collective-permute-start(f32[344,128]{1,0:T(8,128)S(1)} %slice.243), channel_id=1, source_target_pairs={{0,2},{1,3},{2,0},{3,1},{4,6},{5,7},{6,4},{7,5},{8,10},{9,11},{10,... | collective-permute-start | bytes 528392 | tf_op jit(solution)/shard_map/ppermute | solution.py:51
  303.2 10.2 %collective-permute-start.20 = (f32[344,128]{1,0:T(8,128)S(1)}, f32[344,128]{1,0:T(8,128)S(1)}, u32[]{:S(2)}, u32[]{:S(2)}) collective-permute-start(f32[344,128]{1,0:T(8,128)S(1)} %pad_maximum_fusion.8), channel_id=1, source_target_pairs={{0,4},{1,5},{2,6},{3,7},{4,0},{5,1},{6,2},{7,3},{8,12},{9,13},{10,... | collective-permute-start | bytes 528392 | tf_op jit(solution)/shard_map/ppermute | solution.py:51
  313.4 36.2 %collective-permute-start.21 = (f32[344,128]{1,0:T(8,128)S(1)}, f32[344,128]{1,0:T(8,128)S(1)}, u32[]{:S(2)}, u32[]{:S(2)}) collective-permute-start(f32[344,128]{1,0:T(8,128)S(1)} %fusion.34), channel_id=1, source_target_pairs={{0,8},{1,9},{2,10},{3,11},{4,12},{5,13},{6,14},{7,15},{8,0},{9,1},... | collective-permute-start | bytes 528392 | tf_op jit(solution)/shard_map/ppermute | solution.py:51
  337.3 14.4 %copy-start.14 = (f32[2,60,360]{2,0,1:T(2,128)S(1)}, f32[2,60,360]{2,0,1:T(2,128)}, u32[]{:S(2)}) copy-start(f32[2,60,360]{2,0,1:T(2,128)} %param.36) | copy-start | bytes 518404
  337.3 14.6 %copy-start.15 = (f32[2,60,360]{2,0,1:T(2,128)S(1)}, f32[2,60,360]{2,0,1:T(2,128)}, u32[]{:S(2)}) copy-start(f32[2,60,360]{2,0,1:T(2,128)} %param.42) | copy-start | bytes 518404
  344.8 53.4 %collective-permute-start.24 = (f32[8,64,384]{2,1,0:T(8,128)}, f32[8,64,384]{2,1,0:T(8,128)S(1)}, u32[]{:S(2)}, u32[]{:S(2)}) collective-permute-start(f32[8,64,384]{2,1,0:T(8,128)} %get-tuple-element.118), channel_id=1, source_target_pairs={{0,4},{1,5},{2,6},{3,7},{4,0},{5,1},{6,2},{7,3},{8,12},{9,13},{10,... | collective-permute-start | bytes 2359304 | tf_op jit(solution)/shard_map/ppermute | solution.py:51
  345.8 52.4 %collective-permute-start.25 = (f32[8,64,384]{2,1,0:T(8,128)}, f32[8,64,384]{2,1,0:T(8,128)S(1)}, u32[]{:S(2)}, u32[]{:S(2)}) collective-permute-start(f32[8,64,384]{2,1,0:T(8,128)} %get-tuple-element.119), channel_id=1, source_target_pairs={{0,2},{1,3},{2,0},{3,1},{4,6},{5,7},{6,4},{7,5},{8,10},{9,11},{10,... | collective-permute-start | bytes 2359304 | tf_op jit(solution)/shard_map/ppermute | solution.py:51
  347.3 51.0 %collective-permute-start.26 = (f32[8,64,384]{2,1,0:T(8,128)}, f32[8,64,384]{2,1,0:T(8,128)}, u32[]{:S(2)}, u32[]{:S(2)}) collective-permute-start(f32[8,64,384]{2,1,0:T(8,128)} %get-tuple-element.120), channel_id=1, source_target_pairs={{0,8},{1,9},{2,10},{3,11},{4,12},{5,13},{6,14},{7,15},{8,0},{9,1},... | collective-permute-start | bytes 2359304 | tf_op jit(solution)/shard_map/ppermute | solution.py:51
  347.5 50.8 %collective-permute-start.27 = (f32[8,64,384]{2,1,0:T(8,128)}, f32[8,64,384]{2,1,0:T(8,128)}, u32[]{:S(2)}, u32[]{:S(2)}) collective-permute-start(f32[8,64,384]{2,1,0:T(8,128)} %get-tuple-element.121), channel_id=1, source_target_pairs={{0,24},{1,25},{2,26},{3,27},{4,28},{5,29},{6,30},{7,31},{8,16},{9,... | collective-permute-start | bytes 2359304 | tf_op jit(solution)/shard_map/ppermute | solution.py:51
  349.6 48.5 %collective-permute-start.22 = (f32[344,128]{1,0:T(8,128)S(1)}, f32[344,128]{1,0:T(8,128)S(1)}, u32[]{:S(2)}, u32[]{:S(2)}) collective-permute-start(f32[344,128]{1,0:T(8,128)S(1)} %add.253), channel_id=1, source_target_pairs={{0,24},{1,25},{2,26},{3,27},{4,28},{5,29},{6,30},{7,31},{8,16},{9,... | collective-permute-start | bytes 528392 | tf_op jit(solution)/shard_map/ppermute | solution.py:51
  404.6 10.2 %collective-permute-start.28 = (f32[4,64,384]{2,1,0:T(8,128)}, f32[4,64,384]{2,1,0:T(8,128)S(1)}, u32[]{:S(2)}, u32[]{:S(2)}) collective-permute-start(f32[4,64,384]{2,1,0:T(8,128)} %get-tuple-element.123), channel_id=1, source_target_pairs={{0,2},{1,3},{2,0},{3,1},{4,6},{5,7},{6,4},{7,5},{8,10},{9,11},{10,... | collective-permute-start | bytes 1179656 | tf_op jit(solution)/shard_map/ppermute | solution.py:51
  405.2 18.3 %collective-permute-start.29 = (f32[4,64,384]{2,1,0:T(8,128)}, f32[4,64,384]{2,1,0:T(8,128)S(1)}, u32[]{:S(2)}, u32[]{:S(2)}) collective-permute-start(f32[4,64,384]{2,1,0:T(8,128)} %get-tuple-element.124), channel_id=1, source_target_pairs={{0,8},{1,9},{2,10},{3,11},{4,12},{5,13},{6,14},{7,15},{8,0},{9,1},... | collective-permute-start | bytes 1179656 | tf_op jit(solution)/shard_map/ppermute | solution.py:51
  410.8 21.1 %collective-permute-start.30 = (f32[4,64,384]{2,1,0:T(8,128)}, f32[4,64,384]{2,1,0:T(8,128)S(1)}, u32[]{:S(2)}, u32[]{:S(2)}) collective-permute-start(f32[4,64,384]{2,1,0:T(8,128)} %get-tuple-element.125), channel_id=1, source_target_pairs={{0,24},{1,25},{2,26},{3,27},{4,28},{5,29},{6,30},{7,31},{8,16},{9,... | collective-permute-start | bytes 1179656 | tf_op jit(solution)/shard_map/ppermute | solution.py:51
  412.5 19.4 %collective-permute-start.31 = (f32[4,64,384]{2,1,0:T(8,128)}, f32[4,64,384]{2,1,0:T(8,128)S(1)}, u32[]{:S(2)}, u32[]{:S(2)}) collective-permute-start(f32[4,64,384]{2,1,0:T(8,128)} %get-tuple-element.126), channel_id=1, source_target_pairs={{0,4},{1,5},{2,6},{3,7},{4,0},{5,1},{6,2},{7,3},{8,12},{9,13},{10,... | collective-permute-start | bytes 1179656 | tf_op jit(solution)/shard_map/ppermute | solution.py:51
  414.8 17.1 %copy-start.35 = (f32[4,64,384]{2,1,0:T(8,128)}, f32[4,64,384]{2,1,0:T(8,128)S(1)}, u32[]{:S(2)}) copy-start(f32[4,64,384]{2,1,0:T(8,128)S(1)} %collective-permute-done.28.refs_0_) | copy-start | bytes 1179652
  436.7 8.0 %collective-permute-start.32 = (f32[2,64,384]{2,1,0:T(8,128)}, f32[2,64,384]{2,1,0:T(8,128)S(1)}, u32[]{:S(2)}, u32[]{:S(2)}) collective-permute-start(f32[2,64,384]{2,1,0:T(8,128)} %get-tuple-element.128), channel_id=1, source_target_pairs={{0,8},{1,9},{2,10},{3,11},{4,12},{5,13},{6,14},{7,15},{8,0},{9,1},... | collective-permute-start | bytes 589832 | tf_op jit(solution)/shard_map/ppermute | solution.py:51
  436.7 10.2 %collective-permute-start.33 = (f32[2,64,384]{2,1,0:T(8,128)}, f32[2,64,384]{2,1,0:T(8,128)S(1)}, u32[]{:S(2)}, u32[]{:S(2)}) collective-permute-start(f32[2,64,384]{2,1,0:T(8,128)} %get-tuple-element.129), channel_id=1, source_target_pairs={{0,24},{1,25},{2,26},{3,27},{4,28},{5,29},{6,30},{7,31},{8,16},{9,... | collective-permute-start | bytes 589832 | tf_op jit(solution)/shard_map/ppermute | solution.py:51
  438.7 8.2 %collective-permute-start.34 = (f32[2,64,384]{2,1,0:T(8,128)}, f32[2,64,384]{2,1,0:T(8,128)S(1)}, u32[]{:S(2)}, u32[]{:S(2)}) collective-permute-start(f32[2,64,384]{2,1,0:T(8,128)} %get-tuple-element.130), channel_id=1, source_target_pairs={{0,4},{1,5},{2,6},{3,7},{4,0},{5,1},{6,2},{7,3},{8,12},{9,13},{10,... | collective-permute-start | bytes 589832 | tf_op jit(solution)/shard_map/ppermute | solution.py:51
  440.1 6.9 %collective-permute-start.35 = (f32[2,64,384]{2,1,0:T(8,128)}, f32[2,64,384]{2,1,0:T(8,128)S(1)}, u32[]{:S(2)}, u32[]{:S(2)}) collective-permute-start(f32[2,64,384]{2,1,0:T(8,128)} %get-tuple-element.131), channel_id=1, source_target_pairs={{0,2},{1,3},{2,0},{3,1},{4,6},{5,7},{6,4},{7,5},{8,10},{9,11},{10,... | collective-permute-start | bytes 589832 | tf_op jit(solution)/shard_map/ppermute | solution.py:51
  451.1 7.3 %collective-permute-start.36 = (f32[1,64,384]{2,1,0:T(8,128)}, f32[1,64,384]{2,1,0:T(8,128)S(1)}, u32[]{:S(2)}, u32[]{:S(2)}) collective-permute-start(f32[1,64,384]{2,1,0:T(8,128)} %get-tuple-element.133), channel_id=1, source_target_pairs={{0,24},{1,25},{2,26},{3,27},{4,28},{5,29},{6,30},{7,31},{8,16},{9,... | collective-permute-start | bytes 294920 | tf_op jit(solution)/shard_map/ppermute | solution.py:51
  452.8 5.5 %collective-permute-start.37 = (f32[1,64,384]{2,1,0:T(8,128)}, f32[1,64,384]{2,1,0:T(8,128)S(1)}, u32[]{:S(2)}, u32[]{:S(2)}) collective-permute-start(f32[1,64,384]{2,1,0:T(8,128)} %get-tuple-element.134), channel_id=1, source_target_pairs={{0,4},{1,5},{2,6},{3,7},{4,0},{5,1},{6,2},{7,3},{8,12},{9,13},{10,... | collective-permute-start | bytes 294920 | tf_op jit(solution)/shard_map/ppermute | solution.py:51
  454.3 4.8 collective-permute-start.38
  455.8 4.8 collective-permute-start.39
  (42 other events, 206.4 us)
Sparse Core Ops, SparseCore 0:
  11.5 104.1 all-gather.2
  217.0 203.3 reduce-scatter.1

commit v2 on v1

--- a/solution.py
+++ b/solution.py
@@ -30,10 +30,6 @@
 params = functools.partial(pltpu.CompilerParams, vmem_limit_bytes=VMEM_BYTES)
 
 
-def cost(micros):
-    return pl.CostEstimate(flops=int(micros * 1.1e9), bytes_accessed=0, transcendentals=0)
-
-
 class Cube:
     def __init__(self, groups, tensors):
         self.groups = groups
@@ -53,20 +49,15 @@
     def outer(self, turn):
         rest = list(range(1, self.size))
         rest = rest[1:2] + rest[:1] + rest[2:]
-        turn = turn % len(rest)
-        return rest[turn:] + rest[:turn]
+        turning = rest[:-1]
+        turn = turn % len(turning)
+        return turning[turn:] + turning[:turn] + rest[-1:]
 
     def steps(self, offset):
         bits = [(offset >> at) & 1 for at in range(self.size)]
         if self.folded:
             bits[-2] = bits[-2] ^ bits[-1]
         return bits
-
-    def gather(self, x, order):
-        held = x[None]
-        for at in order:
-            held = jnp.concatenate([held, self.swap(held, at)], 0)
-        return held
 
     def slot(self, offset, order):
         bits = self.steps(offset)
@@ -221,29 +212,6 @@
         return self.ref[:, tile, :, start:stop].reshape(groups * rows, stop - start)
 
 
-class Relative:
-    def __init__(self, cube, me, refs, cuts, orders):
-        self.cube = cube
-        self.me = me
-        self.refs = refs
-        self.cuts = cuts
-        self.orders = orders
-
-    def block(self, tile, start, stop):
-        pieces = []
-        for ref, low, high, order in zip(self.refs, self.cuts[:-1], self.cuts[1:], self.orders):
-            first = max(start, low) - low
-            last = min(stop, high) - low
-            if first >= last:
-                continue
-            rows = []
-            for group in range(self.cube.groups):
-                offset = (group * self.cube.tensors + tile) ^ self.me
-                rows.append(ref[self.cube.slot(offset, order), :, first:last])
-            pieces.append(jnp.concatenate(rows, 0))
-        return pieces[0] if len(pieces) == 1 else jnp.concatenate(pieces, 1)
-
-
 class Scattered:
     def __init__(self, cube, me, keep_ref, send_ref, orders):
         self.cube = cube
@@ -268,16 +236,6 @@
                 done += count
 
 
-class Whole:
-    def __init__(self, ref):
-        self.ref = ref
-
-    def store(self, tile, turn, start, value):
-        groups, _, rows, _ = self.ref.shape
-        wide = value.shape[1]
-        self.ref[:, tile, :, start : start + wide] = value.reshape(groups, rows, wide)
-
-
 class Layer:
     def __init__(self, weights, base, hidden):
         self.weights = weights
@@ -322,7 +280,25 @@
     return pl.BlockSpec(memory_space=pltpu.SMEM)
 
 
-def call(kernel, name, ins, in_specs, outs, micros, scratch=()):
+def follow(kernel, first, after):
+    count = len(after)
+    if not count:
+        return kernel
+
+    def late(*refs):
+        return kernel(*refs[:first], *refs[first + count :])
+
+    return late
+
+
+def after_specs(after):
+    return [pl.BlockSpec(memory_space=pl.ANY)] * len(after)
+
+
+def call(kernel, name, ins, in_specs, outs, scratch=(), after=()):
+    kernel = follow(kernel, len(ins), after)
+    ins = (*ins, *after)
+    in_specs = [*in_specs, *after_specs(after)]
     return pl.pallas_call(
         kernel,
         grid=(1,),
@@ -331,7 +307,6 @@
         out_shape=outs,
         scratch_shapes=list(scratch),
         compiler_params=params(),
-        cost_estimate=cost(micros),
         name=name,
     )(*ins)
 
@@ -371,7 +346,7 @@
         jax.ShapeDtypeStruct((2, own, wide), brain),
         jax.ShapeDtypeStruct((own, vocab.shape[1]), single),
     ]
-    return call(embed_kernel, "embed", ins, [whole_spec(x.shape) for x in ins], outs, 6)
+    return call(embed_kernel, "embed", ins, [whole_spec(x.shape) for x in ins], outs)
 
 
 def attend_kernel(heads, chunk, q_ref, own_ref, other_ref, out_ref, logsum_ref):
@@ -411,14 +386,14 @@
             jax.ShapeDtypeStruct((tiles, 8, own), single),
         ],
         compiler_params=params(),
-        cost_estimate=cost(20),
         name="attend",
     )(q, kv_own, kv_other)
 
 
 def attend_back_kernel(
-    heads, chunk, q_ref, kv_own_ref, kv_other_ref, g_ref, logsum_ref, dq_ref, own_ref, other_ref
+    heads, chunk, count, me_ref, q_ref, kv_own_ref, kv_other_ref, g_ref, logsum_ref, *refs
 ):
+    dq_ref, own_ref, other_k_ref, other_v_ref = refs[count:]
     own = q_ref.shape[0]
     q = q_ref[...]
     grad = g_ref[...]
@@ -447,39 +422,50 @@
             if start == 0 and head == 0:
                 own_ref[0] = dk[:own]
                 own_ref[1] = dv[:own]
-                other_ref[0] = dk[own:]
-                other_ref[1] = dv[own:]
+                other_k_ref[...] = dk[own:]
+                other_v_ref[...] = dv[own:]
             else:
                 own_ref[0] += dk[:own]
                 own_ref[1] += dv[:own]
-                other_ref[0] += dk[own:]
-                other_ref[1] += dv[own:]
+                other_k_ref[...] += dk[own:]
+                other_v_ref[...] += dv[own:]
             dq = jnp.where(mine, dot(k_turned, g_scores), dq)
         dq_ref[part, :] = (dq * scale).T
 
 
-def attend_back(q, kv_own, kv_other, grad, logsum, heads):
+def attend_back(q, kv_own, kv_other, grad, logsum, heads, me, turns, tensors, after=()):
     own, wide = q.shape
-    tiles = wide // LANES
-    own_spec = pl.BlockSpec((own, LANES), lambda at: (0, at))
-    pair_spec = pl.BlockSpec((2, own, LANES), lambda at: (0, 0, at))
-    pair_shape = jax.ShapeDtypeStruct((2, own, wide), single)
+    first = turns[0]
+    count = len(turns)
+
+    def tile(at, me):
+        return (at + first) ^ (me[0] & (tensors - 1))
+
+    own_spec = pl.BlockSpec((own, LANES), lambda at, me: (0, tile(at, me)))
+    pair_spec = pl.BlockSpec((2, own, LANES), lambda at, me: (0, 0, tile(at, me)))
+    one_shape = jax.ShapeDtypeStruct((own, count * LANES), single)
+    one_out = pl.BlockSpec((own, LANES), lambda at, me: (0, at))
+    pair_shape = jax.ShapeDtypeStruct((2, own, count * LANES), single)
+    pair_out = pl.BlockSpec((2, own, LANES), lambda at, me: (0, 0, at))
     return pl.pallas_call(
-        functools.partial(attend_back_kernel, heads, own),
-        grid=(tiles,),
-        in_specs=[
-            own_spec,
-            pair_spec,
-            pair_spec,
-            own_spec,
-            pl.BlockSpec((1, 8, own), lambda at: (at, 0, 0)),
-        ],
-        out_specs=[own_spec, pair_spec, pair_spec],
-        out_shape=[jax.ShapeDtypeStruct((own, wide), single), pair_shape, pair_shape],
+        functools.partial(attend_back_kernel, heads, own, len(after)),
+        grid_spec=pltpu.PrefetchScalarGridSpec(
+            num_scalar_prefetch=1,
+            grid=(count,),
+            in_specs=[
+                own_spec,
+                pair_spec,
+                pair_spec,
+                own_spec,
+                pl.BlockSpec((1, 8, own), lambda at, me: (tile(at, me), 0, 0)),
+                *after_specs(after),
+            ],
+            out_specs=[one_out, pair_out, one_out, one_out],
+        ),
+        out_shape=[one_shape, pair_shape, one_shape, one_shape],
         compiler_params=params(),
-        cost_estimate=cost(33),
         name="attend_back",
-    )(q, kv_own, kv_other, grad, logsum)
+    )(me, q, kv_own, kv_other, grad, logsum, *after)
 
 
 def attention_out(mixed, resid, layer, tiles):
@@ -490,13 +476,11 @@
 
 
 def middle_kernel(
-    feats, cube, cuts, orders, hidden, me_ref, mixed_ref, resid_ref, *refs
+    feats, mixed_ref, resid_ref, w_ref, w_next_ref, norms_ref, cos_ref, sin_ref,
+    mid_ref, next_ref, q_ref, kv_ref,
 ):
-    count = len(orders)
-    part_refs = refs[:count]
-    w_next_ref, norms_ref, cos_ref, sin_ref, mid_ref, next_ref, q_ref, kv_ref = refs[count:]
-    layer = Layer(Relative(cube, me_ref[0], part_refs, cuts, orders), 0, hidden)
-    tiles = cube.tensors
+    tiles = w_ref.shape[1]
+    layer = Layer(Gathered(w_ref), 0, (w_ref.shape[3] - LANES) // 2)
     mid = attention_out(mixed_ref[...], resid_ref[...], layer, tiles)
     mid_ref[...] = mid
     normed = feats.norm(mid, norms_ref[2:3], norms_ref[3:4])
@@ -508,39 +492,36 @@
     next_ref[...] = total
     normed = feats.norm(total, norms_ref[4:5], norms_ref[5:6])
     weights = Gathered(w_next_ref)
+    cosine = cos_ref[...]
+    sine = sin_ref[...]
     for at in range(tiles):
         lanes = slice(at * LANES, (at + 1) * LANES)
         rows = dot(normed, weights.block(at, 0, 3 * LANES))
-        cosine = cos_ref[...]
-        sine = sin_ref[...]
         q_ref[:, lanes] = rotate(rows[:, :LANES], cosine, sine).astype(brain)
         kv_ref[0, :, lanes] = rotate(rows[:, LANES : 2 * LANES], cosine, sine).astype(brain)
         kv_ref[1, :, lanes] = rows[:, 2 * LANES :].astype(brain)
 
 
-def middle(feats, cube, cuts, orders, me, mixed, resid, parts, w_next, norms, cosine, sine):
+def middle(feats, mixed, resid, weights, columns, at_heads, norms, cosine, sine):
     own, wide = mixed.shape
-    hidden = (cuts[-1] - LANES) // 2
     plain = jax.ShapeDtypeStruct(resid.shape, single)
+    in_specs = [
+        whole_spec(mixed.shape),
+        whole_spec(resid.shape),
+        columns_spec(weights, columns, 0),
+        columns_spec(weights, 3 * LANES, at_heads),
+        whole_spec(norms.shape),
+        whole_spec(cosine.shape),
+        whole_spec(sine.shape),
+    ]
     outs = [
         plain,
         plain,
         jax.ShapeDtypeStruct((own, wide), brain),
         jax.ShapeDtypeStruct((2, own, wide), brain),
     ]
-    in_specs = [
-        scalar_spec(),
-        whole_spec(mixed.shape),
-        whole_spec(resid.shape),
-        *[whole_spec(part.shape) for part in parts],
-        columns_spec(w_next, 3 * LANES, 0),
-        whole_spec(norms.shape),
-        whole_spec(cosine.shape),
-        whole_spec(sine.shape),
-    ]
-    ins = (me, mixed, resid, *parts, w_next, norms, cosine, sine)
-    kernel = functools.partial(middle_kernel, feats, cube, cuts, orders, hidden)
-    return call(kernel, "middle", ins, in_specs, outs, 12)
+    ins = (mixed, resid, weights, weights, norms, cosine, sine)
+    return call(functools.partial(middle_kernel, feats), "middle", ins, in_specs, outs)
 
 
 def feed_back(
@@ -573,22 +554,25 @@
 
 
 def top_kernel(
-    feats, vocab_count, mixed_ref, resid_ref, w_ref, norms_ref, vocab_ref, slot_ref, target_ref,
-    count_ref, grads_ref, g_mid_ref, g_mixed_ref, g_norms_ref, g_vocab_ref,
-    act_ref, slope_ref,
+    feats, cube, vocab_count, grad_orders, me_ref, mixed_ref, resid_ref, w_ref, norms_ref,
+    vocab_ref, slot_ref, target_ref, count_ref, keep_ref, send_ref, g_mid_ref, g_mixed_ref,
+    g_norms_ref, g_vocab_ref, act_ref, slope_ref,
 ):
-    tiles = w_ref.shape[1]
+    me = me_ref[0]
+    tiles = cube.tensors
+    turns = [(turn, turn ^ (me & (tiles - 1))) for turn in range(tiles)]
+    grads = Scattered(cube, me, keep_ref, send_ref, grad_orders)
     layer = Layer(Gathered(w_ref), 3 * LANES, act_ref.shape[2])
     mid = attention_out(mixed_ref[...], resid_ref[...], layer, tiles)
     normed = feats.norm(mid, norms_ref[6:7], norms_ref[7:8])
     parts = []
-    for at in range(tiles):
-        hidden = dot(normed, layer.up(at))
+    for turn, tile in turns:
+        hidden = dot(normed, layer.up(tile))
         share = normal_share(hidden)
         act = (hidden * share).astype(brain)
-        act_ref[at] = act
-        slope_ref[at] = gelu_slope(hidden, share)
-        parts.append(dot(act, layer.down(at), 1, 1))
+        act_ref[turn] = act
+        slope_ref[turn] = gelu_slope(hidden, share)
+        parts.append(dot(act, layer.down(tile), 1, 1))
     total = mid + add_up(parts)
     unit, inverse = feats.centred(total)
     gain = norms_ref[8:9]
@@ -621,29 +605,36 @@
     g_norms_ref[LOSS_ROW : LOSS_ROW + 1] = jnp.broadcast_to(loss, (1, g_norms_ref.shape[1]))
     g_resid = feats.norm_back(unit, inverse, gain, g_final)
     g_gain, g_shift = feed_back(
-        feats, [(at, at) for at in range(tiles)], g_resid, mid, normed, mixed_ref, layer,
-        norms_ref[6:7], act_ref, slope_ref, Whole(grads_ref), 0, g_mid_ref, g_mixed_ref,
+        feats, turns, g_resid, mid, normed, mixed_ref, layer, norms_ref[6:7], act_ref, slope_ref,
+        grads, 0, g_mid_ref, g_mixed_ref,
     )
     g_norms_ref[6:7] = g_gain
     g_norms_ref[7:8] = g_shift
 
 
-def top(feats, mixed, resid, weights, columns, norms, vocab, vocab_count, slot, target, count):
+def top(
+    feats, cube, grad_orders, me, mixed, resid, weights, columns, at_block, norms, vocab,
+    vocab_count, slot, target, count,
+):
     own, wide = mixed.shape
-    groups, tiles, rows, _ = weights.shape
-    grads = columns - 3 * LANES
-    hidden = (grads - LANES) // 2
+    tiles = cube.tensors
+    rows = weights.shape[2]
+    hidden = (columns - 4 * LANES) // 2
+    pieces = len(grad_orders)
+    grads = (pieces, cube.devices // 2, rows, (columns - 3 * LANES) // pieces)
     outs = [
-        jax.ShapeDtypeStruct((groups, tiles, rows, grads), single),
+        jax.ShapeDtypeStruct(grads, single),
+        jax.ShapeDtypeStruct(grads, single),
         jax.ShapeDtypeStruct(resid.shape, single),
         jax.ShapeDtypeStruct(mixed.shape, brain),
         jax.ShapeDtypeStruct(norms.shape, single),
         jax.ShapeDtypeStruct((TABLE_ROWS, resid.shape[1]), single),
     ]
     in_specs = [
+        scalar_spec(),
         whole_spec(mixed.shape),
         whole_spec(resid.shape),
-        columns_spec(weights, columns, 0),
+        columns_spec(weights, columns, at_block),
         whole_spec(norms.shape),
         whole_spec(vocab.shape),
         whole_spec(slot.shape),
@@ -654,34 +645,32 @@
         pltpu.VMEM((tiles, own, hidden), brain),
         pltpu.VMEM((tiles, own, hidden), single),
     ]
-    ins = (mixed, resid, weights, norms, vocab, slot, target, count)
-    kernel = functools.partial(top_kernel, feats, vocab_count)
-    return call(kernel, "top", ins, in_specs, outs, 21, scratch)
-
-
-def head_grads(tile, dq_ref, own_ref, other_ref, cosine, sine):
-    lanes = tile_lanes(tile)
+    ins = (me, mixed, resid, weights, norms, vocab, slot, target, count)
+    kernel = functools.partial(top_kernel, feats, cube, vocab_count, grad_orders)
+    return call(kernel, "top", ins, in_specs, outs, scratch)
+
+
+def head_grads(turn, heads_refs, cosine, sine):
+    dq_ref, own_ref, other_k_ref, other_v_ref = heads_refs[4 * (turn // 2) : 4 * (turn // 2) + 4]
+    lanes = tile_lanes(turn % 2)
+    other = tile_lanes(1 - turn % 2)
     g_q = unrotate(dq_ref[:, lanes], cosine, sine)
-    g_k = unrotate(own_ref[0, :, lanes] + other_ref[0, :, lanes], cosine, sine)
-    g_v = own_ref[1, :, lanes] + other_ref[1, :, lanes]
+    g_k = unrotate(own_ref[0, :, lanes] + other_k_ref[:, other], cosine, sine)
+    g_v = own_ref[1, :, lanes] + other_v_ref[:, other]
     return jnp.concatenate([g_q, g_k, g_v], 1).astype(brain)
 
 
-def lower_kernel(
-    feats, cube, cuts, orders, grad_orders, me_ref, dq_ref, own_ref, other_ref, g_mid_in_ref,
-    resid_ref, mid_ref, mixed_ref, w_in_ref, *refs
-):
-    count = len(orders)
-    part_refs = refs[:count]
+def lower_kernel(feats, cube, grad_orders, me_ref, *refs):
+    heads_refs = refs[:8]
     (
-        norms_ref, cos_ref, sin_ref, g_norms_in_ref,
-        keep_ref, send_ref, g_mid_ref, g_mixed_ref, g_norms_ref,
+        g_mid_in_ref, resid_ref, mid_ref, mixed_ref, w_in_ref, w_ref, norms_ref, cos_ref, sin_ref,
+        g_norms_in_ref, keep_ref, send_ref, g_mid_ref, g_mixed_ref, g_norms_ref,
         act_ref, slope_ref,
-    ) = refs[count:]
+    ) = refs[8:]
     me = me_ref[0]
     tiles = cube.tensors
     turns = [(turn, turn ^ (me & (tiles - 1))) for turn in range(tiles)]
-    layer = Layer(Relative(cube, me, part_refs, cuts, orders), 0, act_ref.shape[2])
+    layer = Layer(Gathered(w_ref), 0, act_ref.shape[2])
     weights = Gathered(w_in_ref)
     grads = Scattered(cube, me, keep_ref, send_ref, grad_orders)
     unit, inverse = feats.centred(resid_ref[...])
@@ -691,7 +680,7 @@
     sine = sin_ref[...]
     parts = []
     for turn, tile in turns:
-        g_heads = head_grads(tile, dq_ref, own_ref, other_ref, cosine, sine)
+        g_heads = head_grads(turn, heads_refs, cosine, sine)
         grads.store(tile, turn, 0, dot(normed_turned, g_heads))
         parts.append(dot(g_heads, weights.block(tile, 0, 3 * LANES), 1, 1))
     g_normed = add_up(parts)
@@ -715,14 +704,14 @@
 
 
 def lower(
-    feats, cube, cuts, orders, grad_orders, me, dq, own_part, other_part, g_mid, resid, mid,
-    mixed, w_in, parts, norms, cosine, sine, g_norms,
+    feats, cube, grad_orders, me, head_parts, g_mid, resid, mid, mixed, weights, at_heads,
+    feed_columns, norms, cosine, sine, g_norms, after,
 ):
     own, wide = mixed.shape
     tiles = cube.tensors
-    rows = w_in.shape[2]
-    hidden = (cuts[-1] - LANES) // 2
-    columns = cuts[-1] + 3 * LANES
+    rows = weights.shape[2]
+    hidden = (feed_columns - LANES) // 2
+    columns = feed_columns + 3 * LANES
     count = len(grad_orders)
     grads = (count, cube.devices // 2, rows, columns // count)
     outs = [
@@ -732,21 +721,22 @@
         jax.ShapeDtypeStruct(mixed.shape, brain),
         jax.ShapeDtypeStruct(norms.shape, single),
     ]
-    before = (dq, own_part, other_part, g_mid, resid, mid, mixed)
-    after = (norms, cosine, sine, g_norms)
+    before = (*head_parts, g_mid, resid, mid, mixed)
+    rest = (norms, cosine, sine, g_norms)
     in_specs = [
         scalar_spec(),
         *[whole_spec(x.shape) for x in before],
-        columns_spec(w_in, 3 * LANES, 0),
-        *[whole_spec(x.shape) for x in (*parts, *after)],
+        columns_spec(weights, 3 * LANES, at_heads),
+        columns_spec(weights, feed_columns, 0),
+        *[whole_spec(x.shape) for x in rest],
     ]
     scratch = [
         pltpu.VMEM((tiles, own, hidden), brain),
         pltpu.VMEM((tiles, own, hidden), single),
     ]
-    ins = (me, *before, w_in, *parts, *after)
-    kernel = functools.partial(lower_kernel, feats, cube, cuts, orders, grad_orders)
-    return call(kernel, "lower", ins, in_specs, outs, 22, scratch)
+    ins = (me, *before, weights, weights, *rest)
+    kernel = functools.partial(lower_kernel, feats, cube, grad_orders)
+    return call(kernel, "lower", ins, in_specs, outs, scratch, after)
 
 
 def stacked_lanes(ref, row, value):
@@ -762,11 +752,15 @@
 
 
 def bottom_kernel(
-    feats, cube, me_ref, dq_ref, own_ref, other_ref, g_mid_ref, ids_ref, w_ref, norms_ref,
-    vocab_ref, g_vocab_in_ref, g_norms_in_ref, cos_ref, sin_ref, keep_ref, send_ref, norms_out_ref,
+    feats, cube, me_ref, *refs
 ):
+    heads_refs = refs[:8]
+    (
+        g_mid_ref, ids_ref, w_ref, norms_ref, vocab_ref, g_vocab_in_ref, g_norms_in_ref, cos_ref,
+        sin_ref, keep_ref, send_ref, norms_out_ref,
+    ) = refs[8:]
     tiles = cube.tensors
-    own = dq_ref.shape[0]
+    own = g_mid_ref.shape[0]
     mine = me_ref[0] & (tiles - 1)
     hot = lax.broadcasted_iota(jnp.int32, (TABLE_ROWS, own), 0) == ids_ref[...]
     hot = hot.astype(single).astype(brain)
@@ -778,7 +772,7 @@
     parts = []
     for turn in range(tiles):
         tile = turn ^ mine
-        g_table = dot(hot, head_grads(tile, dq_ref, own_ref, other_ref, cosine, sine))
+        g_table = dot(hot, head_grads(turn, heads_refs, cosine, sine))
         rows[turn & 1] = stacked_lanes(refs[turn & 1], rows[turn & 1], g_table)
         weight = weights.block(tile, 0, 3 * LANES)
         high, middle_part, low = split_three(g_table)
@@ -799,30 +793,31 @@
 
 
 def bottom(
-    feats, cube, me, dq, own_part, other_part, g_mid, ids, w_in, at_block, norms, vocab, g_vocab,
-    g_norms, cosine, sine,
+    feats, cube, me, head_parts, g_mid, ids, w_in, at_block, norms, vocab, g_vocab,
+    g_norms, cosine, sine, after,
 ):
     tiles = cube.tensors
     table_rows = 3 * TABLE_ROWS * tiles // 2
     vector_rows = (g_vocab.shape[0] + g_norms.shape[0]) * g_vocab.shape[1] // LANES
     out = jax.ShapeDtypeStruct((table_rows + vector_rows, LANES), single)
-    before = (dq, own_part, other_part, g_mid, ids)
-    after = (norms, vocab, g_vocab, g_norms, cosine, sine)
+    before = (*head_parts, g_mid, ids)
+    rest = (norms, vocab, g_vocab, g_norms, cosine, sine)
     in_specs = [
         scalar_spec(),
         *[whole_spec(x.shape) for x in before],
         columns_spec(w_in, 3 * LANES, at_block),
-        *[whole_spec(x.shape) for x in after],
+        *[whole_spec(x.shape) for x in rest],
     ]
     outs = [out, out, jax.ShapeDtypeStruct(norms.shape, single)]
-    ins = (me, *before, w_in, *after)
+    ins = (me, *before, w_in, *rest)
     kernel = functools.partial(bottom_kernel, feats, cube)
-    return call(kernel, "bottom", ins, in_specs, outs, 7)[:2]
-
-
-def halve_kernel(count, together, keep_ref, *refs):
-    got = refs[:1] if together else refs[:count]
-    outs = refs[len(got) :]
+    return call(kernel, "bottom", ins, in_specs, outs, (), after)[:2]
+
+
+def halve_kernel(count, together, stacked, skip, keep_ref, *refs):
+    got_count = 1 if together else count
+    got = refs[:got_count]
+    outs = refs[got_count + skip :]
     size = keep_ref.shape[1]
     half = size // 2
     for part in range(count):
@@ -831,14 +826,15 @@
             outs[0][part] = keep_ref[part] + arrived[...]
         else:
             outs[0][part] = keep_ref[part, :half] + arrived[:half]
-            outs[1 + part][...] = keep_ref[part, half:] + arrived[half:]
-
-
-def halve(keep, got):
+            send = outs[1].at[part] if stacked else outs[1 + part]
+            send[...] = keep_ref[part, half:] + arrived[half:]
+
+
+def halve(keep, got, through=(), after=(), stacked=False):
     count, size, rows, wide = keep.shape
     together = not isinstance(got, list)
     got = [got] if together else got
-    step = 16
+    step = 16 if size >= 8 else rows
     half = max(size // 2, 1)
 
     def spec(*lead):
@@ -846,28 +842,29 @@
 
     outs = [jax.ShapeDtypeStruct((count, half, rows, wide), single)]
     out_specs = [spec(count, half)]
-    if size > 1:
+    if size > 1 and stacked:
+        outs += outs
+        out_specs += out_specs
+    elif size > 1:
         outs += [jax.ShapeDtypeStruct((half, rows, wide), single)] * count
         out_specs += [spec(half)] * count
+    sends = len(outs) - 1
     got_specs = [spec(count, size)] if together else [spec(size)] * count
-    return pl.pallas_call(
-        functools.partial(halve_kernel, count, together),
+    ins = (keep, *got)
+    aliases = {len(ins) + at: len(outs) + at for at in range(len(through))}
+    outs += [jax.ShapeDtypeStruct(x.shape, x.dtype) for x in through]
+    results = pl.pallas_call(
+        functools.partial(halve_kernel, count, together, stacked, len(through) + len(after)),
         grid=(rows // step,),
-        in_specs=[spec(count, size), *got_specs],
-        out_specs=out_specs,
+        in_specs=[spec(count, size), *got_specs, *after_specs(through), *after_specs(after)],
+        out_specs=[*out_specs, *after_specs(through)],
         out_shape=outs,
+        input_output_aliases=aliases,
         compiler_params=params(),
-        cost_estimate=cost(2),
         name="halve",
-    )(keep, *got)
-
-
-def scatter_sums(cube, keep, send, orders):
-    got = cube.swap(send, 0)
-    for step in range(len(orders[0])):
-        keep, *sends = halve(keep, got)
-        got = [cube.swap(x, order[step]) for x, order in zip(sends, orders)]
-    return halve(keep, got)[0][:, 0]
+    )(*ins, *through, *after)
+    going = results[1] if stacked and sends else results[1 : 1 + sends]
+    return results[0], going, results[1 + sends :]
 
 
 def normalize_features(resid, gain, shift):
@@ -984,17 +981,12 @@
         ids = jnp.take(table[:, ids_row : ids_row + 2, :local_len], sequence, axis=1)
         ids = jnp.take(ids, quarters, axis=0).reshape(1, length).astype(jnp.int32)
 
-        cuts = (0, LANES + hidden_padded, feed_columns)
-        orders = [cube.outer(0) + [0], cube.outer(2) + [0]]
-        feed_low = pad_rows(feed[:, 0])
-        parts = [
-            cube.gather(feed_low[:, low:high], order)
-            for low, high, order in zip(cuts[:-1], cuts[1:], orders)
-        ]
-        rest = pad_rows(jnp.concatenate([heads_in[:, 1], feed[:, 1], heads_in[:, 0]], 1))
-        weights = lax.all_gather(rest, axes, axis=0, tiled=False)
-        weights = weights.reshape((groups, tensors) + rest.shape)
-        low_block = all_columns // (3 * LANES)
+        packed = [feed[:, 0], heads_in[:, 0], heads_in[:, 1], feed[:, 1]]
+        packed = pad_rows(jnp.concatenate(packed, 1))
+        weights = lax.all_gather(packed, axes, axis=0, tiled=False)
+        weights = weights.reshape((groups, tensors) + packed.shape)
+        at_low = feed_columns // (3 * LANES)
+        at_heads = at_low + 1
 
         half = HEAD // 2
         freqs = 10000.0 ** (-jnp.arange(half, dtype=single) * 2.0 / HEAD)
@@ -1020,34 +1012,76 @@
         q_low, kv_low, kv_low_other, resid_low = embed(table, ids, vocab_padded, cosine, sine)
         mixed_low, logsum_low = attend(q_low, kv_low, kv_low_other, heads)
         mid_low, resid, q, kv = middle(
-            feats, cube, cuts, orders, me, mixed_low, resid_low, parts, weights, norms,
-            cos_own, sin_own,
+            feats, mixed_low, resid_low, weights, feed_columns, at_heads, norms, cos_own, sin_own
         )
         kv_other = cube.swap(kv, 0)
         mixed, logsum = attend(q, kv, kv_other, heads)
-        grads_top, g_mid, g_mixed, g_norms, g_vocab = top(
-            feats, mixed, resid, weights, all_columns, norms, vocab_padded, vocab_count, slot,
-            target, count,
+        grad_orders = [cube.outer(turn) for turn in range(3)]
+
+        last_step = cube.size - 2
+
+        class Sums:
+            def __init__(self, keep, send):
+                self.keep = keep
+                self.got = cube.swap(send, 0)
+                self.at = 0
+
+            def step(self, through=(), after=()):
+                stacked = self.at == last_step
+                self.keep, sends, through = halve(self.keep, self.got, through, after, stacked)
+                if stacked:
+                    self.got = cube.swap(sends, grad_orders[0][-1])
+                else:
+                    self.got = [
+                        cube.swap(x, order[self.at]) for x, order in zip(sends, grad_orders)
+                    ]
+                self.at += 1
+                return through
+
+            def finish(self, after=()):
+                return halve(self.keep, self.got, (), after)[0][:, 0]
+
+        def exchange(arrays):
+            return [cube.swap(x, 0) for x in arrays]
+
+        first_turns = list(range(tensors // 2))
+        last_turns = list(range(tensors // 2, tensors))
+        keep, send, g_mid, g_mixed, g_norms, g_vocab = top(
+            feats, cube, grad_orders, me, mixed, resid, weights, all_columns, 1, norms,
+            vocab_padded, vocab_count, slot, target, count,
         )
-        grads_top = grads_top.reshape((cube.devices,) + grads_top.shape[2:])
-        grads_top = lax.psum_scatter(grads_top, axes, scatter_dimension=0, tiled=True)[0]
-        dq, own_part, other_part = attend_back(q, kv, kv_other, g_mixed, logsum, heads)
-        got = cube.swap(other_part, 0)
-        grad_orders = [cube.outer(turn) for turn in range(4)]
+        sums_top = Sums(keep, send)
+        part = (q, kv, kv_other, g_mixed, logsum, heads, me)
+        first = attend_back(*part, first_turns, tensors)
+        got_first = exchange(sums_top.step(first[2:], (first[0],)))
+        last = attend_back(*part, last_turns, tensors, (sums_top.keep, *got_first))
+        got_last = exchange(sums_top.step(last[2:], (last[0],)))
+        head_parts = (*first[:2], *got_first, *last[:2], *got_last)
         keep, send, g_mid, g_mixed, g_norms = lower(
-            feats, cube, cuts, orders, grad_orders, me, dq, own_part, got, g_mid, resid, mid_low,
-            mixed_low, weights, parts, norms, cos_own, sin_own, g_norms,
+            feats, cube, grad_orders, me, head_parts, g_mid, resid, mid_low, mixed_low, weights,
+            at_heads, feed_columns, norms, cos_own, sin_own, g_norms, (sums_top.keep,),
         )
-        grads_low = scatter_sums(cube, keep, send, grad_orders)
-        dq, own_part, other_part = attend_back(
-            q_low, kv_low, kv_low_other, g_mixed, logsum_low, heads
+        (send,) = sums_top.step((send,), (g_mid,))
+        sums_low = Sums(keep, send)
+        part = (q_low, kv_low, kv_low_other, g_mixed, logsum_low, heads, me)
+        first = attend_back(*part, first_turns, tensors, (sums_top.keep,))
+        got_first = exchange(sums_top.step(first[2:], (first[0],)))
+        sums_low.step((), (sums_top.keep,))
+        last = attend_back(*part, last_turns, tensors, (sums_low.keep, *got_first))
+        got_last = exchange(sums_low.step(last[2:], (last[0],)))
+        head_parts = (*first[:2], *got_first, *last[:2], *got_last)
+        keep_table, send_table = bottom(
+            feats, cube, me, head_parts, g_mid, ids[:, :own], weights, at_low, norms,
+            vocab_padded, g_vocab, g_norms, cos_own, sin_own, (sums_low.keep,),
         )
-        got = cube.swap(other_part, 0)
-        keep, send = bottom(
-            feats, cube, me, dq, own_part, got, g_mid, ids[:, :own], weights, low_block, norms,
-            vocab_padded, g_vocab, g_norms, cos_own, sin_own,
-        )
-        total = keep + cube.swap(send, 0)
+        sums_low.step((), (keep_table,))
+        while sums_low.at <= last_step:
+            sums_low.step()
+        while sums_top.at <= last_step:
+            sums_top.step((), (keep_table,))
+        grads_top = jnp.concatenate(list(sums_top.finish((keep_table,))), 1)
+        grads_low = jnp.concatenate(list(sums_low.finish()), 1)
+        total = keep_table + cube.swap(send_table, 0)
         tile_rows = 3 * TABLE_ROWS
         got = cube.swap(total[tile_rows:], 1)
         total = jnp.concatenate(
@@ -1074,7 +1108,6 @@
             grad = grad[:block].reshape(block, 3, LANES)[:, :, :per_heads]
             return grad.reshape(block, 3, heads, HEAD).transpose(0, 2, 1, 3).reshape(block, in_wide)
 
-        grads_low = jnp.concatenate(list(grads_low), 1)
         grad_in = jnp.stack([unpack_in(grads_in_low), unpack_in(grads_low[:, : 3 * LANES])], 1)
         both = jnp.stack([grads_low[:block, 3 * LANES :], grads_top[:block]], 1)
         grad_in = grad_in.transpose(1, 0, 2)

time: 492 us -> 406 us (0.83)
  waiting for transfers between devices: 130 us -> 70.8 us
  starting transfers between devices: 77.3 us -> 40.6 us
  Pallas kernels: 209 us -> 218 us
  local copies, waits for them, and re-layouts: 45.9 us -> 40.2 us
    ppermute x40 -> x41, waiting for transfers between devices: 128 us -> 27 us  [swap(): return lax.ppermute(x, ('dp', 'tensor'), pairs)]
    all_gather x1, waiting for transfers between devices: 1.88 us -> 43.7 us  [shards(): weights = lax.all_gather(packed, axes, axis=0, tiled=False)]
    ppermute x40 -> x41, starting transfers between devices: 77.2 us -> 40.5 us  [swap(): return lax.ppermute(x, ('dp', 'tensor'), pairs)]
    pallas_call x7 -> x14, Pallas kernels: 88.6 us -> 107 us  [the longest x4 69.3 us: attend_back(): pl.pallas_call(functools.partial(attend_back_kernel, heads, own, len(afte...]
    pallas_call x2, Pallas kernels: 48.8 us -> 40.7 us  [attend(): pl.pallas_call(functools.partial(attend_kernel, heads, LANES), grid=(tile...]
    unnamed x128 -> x131, local copies, waits for them, and re-layouts: 27.4 us -> 25.9 us
  transfers between devices with their start and end apart: 42 -> 42, of which waited for: 19 -> 18; matrix products, arithmetic and copies ran while one was open for 6% -> 7% of each run, Pallas kernels for 23% -> 34%
where the time goes in v2:
time: 406 us; the launch traced here: 399 us
  Pallas kernels  218 us (54%)
  waiting for transfers between devices  70.8 us (17%)
  starting transfers between devices  40.6 us (10%)
  local copies, waits for them, and re-layouts  40.2 us (10%)
  between operations  16.7 us (4%)
  other arithmetic  12 us (3%)
    pallas_call x5, Pallas kernels, call(): pl.pallas_call(kernel, grid=(1,), in_specs=in_specs, out_specs=[whole_spe...  70.4 us
    pallas_call x4, Pallas kernels, attend_back(): pl.pallas_call(functools.partial(attend_back_kernel, heads, own, len(afte...  69.3 us
    all_gather x1, waiting for transfers between devices, shards(): weights = lax.all_gather(packed, axes, axis=0, tiled=False)  43.7 us
    pallas_call x2, Pallas kernels, attend(): pl.pallas_call(functools.partial(attend_kernel, heads, LANES), grid=(tile...  40.7 us
    ppermute x41, starting transfers between devices, swap(): return lax.ppermute(x, ('dp', 'tensor'), pairs)  40.5 us
    pallas_call x10, Pallas kernels, halve(): pl.pallas_call(functools.partial(halve_kernel, count, together, stacked,...  37.4 us
    ppermute x41, waiting for transfers between devices, swap(): return lax.ppermute(x, ('dp', 'tensor'), pairs)  27 us
    unnamed x131, local copies, waits for them, and re-layouts  25.9 us
  transfers between devices with their start and end apart: 42, of which 18 were waited for; matrix products, arithmetic and copies ran while one was open for 7% of the time, Pallas kernels for 34%

profile of v2, /device:TPU:0, one launch (start us, length us, event | category | flops | bytes accessed | tf_op | source)
XLA Modules:
  0.0 398.6 jit_solution(4711605054828944026)
XLA Ops:
  15.4 3.0 collective-permute-start
  18.9 1.7 collective-permute-done
  20.6 2.2 collective-permute-start.1
  23.1 1.9 collective-permute-done.1
  25.0 4.1 %collective-permute-start.2 = (f32[40,384]{1,0:T(8,128)S(1)}, f32[40,384]{1,0:T(8,128)S(1)}, u32[]{:S(2)}, u32[]{:S(2)}) collective-permute-start(f32[40,384]{1,0:T(8,128)S(1)} %add.235), channel_id=1, source_target_pairs={{0,24},{1,25},{2,26},{3,27},{4,28},{5,29},{6,30},{7,31},{8,16},{9,... | collective-permute-start | bytes 184328 | tf_op jit(solution)/shard_map/ppermute | solution.py:47
  29.9 2.5 collective-permute-done.2
  32.9 1.8 collective-permute-start.3
  34.8 2.3 collective-permute-done.3
  43.0 6.1 %embed.1 = (bf16[512,512]{1,0:T(8,128)(2,1)}, bf16[2,512,512]{2,1,0:T(8,128)(2,1)}, bf16[2,512,512]{2,1,0:T(8,128)(2,1)}, f32[512,512]{1,0:T(8,128)}) custom-call(f32[4,40,384]{2,1,0:T(8,128)} %bitcast.143, s32[1,1024]{1,0:T(1,128)} %bitcast.157, bf16[64,512]{1,0:T(8,128)(2,1)} %pad.55.vocab_ref.refs_13_, f32[1024,128]{1,0:T(8,128)} %pad.56.cos_ref, ...), custom_call_target="tpu_custom_call" | custom-call | tf_op jit(solution)/shard_map/embed/pallas_call | solution.py:302
  49.1 20.3 %attend.2 = (bf16[512,512]{1,0:T(8,128)(2,1)}, f32[4,8,512]{2,1,0:T(8,128)}) custom-call(bf16[512,512]{1,0:T(8,128)(2,1)} %get-tuple-element.116.q_ref, bf16[2,512,512]{2,1,0:T(8,128)(2,1)} %get-tuple-element.117.own_ref.kv_own_ref, bf16[2,512,512]{2,1,0:T(8,128)(2,1)} %get-tuple-element.118.other_ref.kv_other_ref), custom_call_target="tpu_custom_call" | custom-call | tf_op jit(solution)/shard_map/attend/pallas_call | solution.py:379
  69.4 43.7 %all-gather.3.cloned.1.call-done = bf16[2048,3072]{1,0:T(8,128)(2,1)} async-done(((bf16[64,3072]{1,0:T(8,128)(2,1)}), bf16[2048,3072]{1,0:T(8,128)(2,1)}) %all-gather.3.cloned.1.call-update) | async-done | bytes 12582928 | tf_op jit(solution)/shard_map/all_gather | solution.py:986
  113.1 12.5 %middle.1 = (f32[512,512]{1,0:T(8,128)}, f32[512,512]{1,0:T(8,128)}, bf16[512,512]{1,0:T(8,128)(2,1)}, bf16[2,512,512]{2,1,0:T(8,128)(2,1)}) custom-call(bf16[512,512]{1,0:T(8,128)(2,1)} %get-tuple-element.119.mixed_ref.refs_12_, f32[512,512]{1,0:T(8,128)} %get-tuple-element.120.resid_ref, bf16[8,4,64,3072]{3,2,1,0:T(8,128)(2,1)} %bitcast.132, ...), custom_call_target="tpu_custom_call" | custom-call | tf_op jit(solution)/shard_map/middle/pallas_call | solution.py:302
  129.7 20.4 %attend.3 = (bf16[512,512]{1,0:T(8,128)(2,1)}, f32[4,8,512]{2,1,0:T(8,128)}) custom-call(bf16[512,512]{1,0:T(8,128)(2,1)} %get-tuple-element.121.q_ref, bf16[2,512,512]{2,1,0:T(8,128)(2,1)} %get-tuple-element.122.own_ref.kv_own_ref, bf16[2,512,512]{2,1,0:T(8,128)(2,1)} %copy-done), custom_call_target="tpu_custom_call" | custom-call | tf_op jit(solution)/shard_map/attend/pallas_call | solution.py:379
  151.4 21.9 %top.1 = (f32[3,16,64,384]{3,2,1,0:T(8,128)}, f32[3,16,64,384]{3,2,1,0:T(8,128)}, f32[512,512]{1,0:T(8,128)}, bf16[512,512]{1,0:T(8,128)(2,1)}, f32[16,512]{1,0:T(8,128)}, /*index=5*/f32[40,512]{1,0:T(8,128)}) custom-call(s32[1]{0:T(128)} %bitcast.me_ref.refs_0_, bf16[512,512]{1,0:T(8,128)(2,1)} %get-tuple-element.123.mixed_ref, ...), custom_call_target="tpu_custom_call" | custom-call | tf_op jit(solution)/shard_map/top/pallas_call | solution.py:302
  173.6 17.3 %attend_back.4 = (f32[512,256]{1,0:T(8,128)}, f32[2,512,256]{2,1,0:T(8,128)}, f32[512,256]{1,0:T(8,128)}, f32[512,256]{1,0:T(8,128)}) custom-call(s32[1]{0:T(128)} %bitcast.me_ref.refs_0_, bf16[512,512]{1,0:T(8,128)(2,1)} %get-tuple-element.121.q_ref, bf16[2,512,512]{2,1,0:T(8,128)(2,1)} %get-tuple-element.122.own_ref.kv_own_ref, ...), custom_call_target="tpu_custom_call" | custom-call | tf_op jit(solution)/shard_map/attend_back/pallas_call | solution.py:450
  190.9 6.3 %halve.10 = (f32[3,8,64,384]{3,2,1,0:T(8,128)}, f32[8,64,384]{2,1,0:T(8,128)}, f32[8,64,384]{2,1,0:T(8,128)}, f32[8,64,384]{2,1,0:T(8,128)}, f32[512,256]{1,0:T(8,128)}, /*index=5*/f32[512,256]{1,0:T(8,128)}) custom-call(f32[3,16,64,384]{3,2,1,0:T(8,128)} %get-tuple-element.129.keep_ref, ...), custom_call_target="tpu_custom_call", output_to_operand_aliasing={{4}: (2, {}), {5}: (3, {})} | custom-call | tf_op jit(solution)/shard_map/halve/pallas_call | solution.py:856
  197.2 1.5 collective-permute-start.10
  200.6 1.6 collective-permute-done.7.refs_1_.refs_3_
  203.7 17.3 %attend_back.5 = (f32[512,256]{1,0:T(8,128)}, f32[2,512,256]{2,1,0:T(8,128)}, f32[512,256]{1,0:T(8,128)}, f32[512,256]{1,0:T(8,128)}) custom-call(s32[1]{0:T(128)} %bitcast.me_ref.refs_0_, bf16[512,512]{1,0:T(8,128)(2,1)} %get-tuple-element.121.q_ref, bf16[2,512,512]{2,1,0:T(8,128)(2,1)} %get-tuple-element.122.own_ref.kv_own_ref, ...), custom_call_target="tpu_custom_call" | custom-call | tf_op jit(solution)/shard_map/attend_back/pallas_call | solution.py:450
  222.4 4.7 %halve.11 = (f32[3,4,64,384]{3,2,1,0:T(8,128)}, f32[4,64,384]{2,1,0:T(8,128)}, f32[4,64,384]{2,1,0:T(8,128)}, f32[4,64,384]{2,1,0:T(8,128)}, f32[512,256]{1,0:T(8,128)}, /*index=5*/f32[512,256]{1,0:T(8,128)}) custom-call(f32[3,8,64,384]{3,2,1,0:T(8,128)} %get-tuple-element.135.refs_0_.keep_ref, ...), custom_call_target="tpu_custom_call", output_to_operand_aliasing={{4}: (4, {}), {5}: (5, {})} | custom-call | tf_op jit(solution)/shard_map/halve/pallas_call | solution.py:856
  227.7 1.4 collective-permute-start.14
  231.9 22.7 %lower.1 = (f32[3,16,64,512]{3,2,1,0:T(8,128)}, f32[3,16,64,512]{3,2,1,0:T(8,128)}, f32[512,512]{1,0:T(8,128)}, bf16[512,512]{1,0:T(8,128)(2,1)}, f32[16,512]{1,0:T(8,128)}) custom-call(s32[1]{0:T(128)} %bitcast.me_ref.refs_0_, f32[512,256]{1,0:T(8,128)} %get-tuple-element.127.refs_3_.refs_1_, f32[2,512,256]{2,1,0:T(8,128)} %get-tuple-element.128.refs_2_, ...), custom_call_target="tpu_custom_call" | custom-call | tf_op jit(solution)/shard_map/lower/pallas_call | solution.py:302
  255.6 2.6 halve.12
  259.1 1.4 collective-permute-start.18
  261.2 17.3 %attend_back.6 = (f32[512,256]{1,0:T(8,128)}, f32[2,512,256]{2,1,0:T(8,128)}, f32[512,256]{1,0:T(8,128)}, f32[512,256]{1,0:T(8,128)}) custom-call(s32[1]{0:T(128)} %bitcast.me_ref.refs_0_, bf16[512,512]{1,0:T(8,128)(2,1)} %get-tuple-element.116.q_ref, bf16[2,512,512]{2,1,0:T(8,128)(2,1)} %get-tuple-element.117.own_ref.kv_own_ref, ...), custom_call_target="tpu_custom_call" | custom-call | tf_op jit(solution)/shard_map/attend_back/pallas_call | solution.py:450
  279.2 2.2 halve.13
  281.4 7.5 %halve.14 = (f32[3,8,64,512]{3,2,1,0:T(8,128)}, f32[8,64,512]{2,1,0:T(8,128)}, f32[8,64,512]{2,1,0:T(8,128)}, f32[8,64,512]{2,1,0:T(8,128)}) custom-call(f32[3,16,64,512]{3,2,1,0:T(8,128)} %get-tuple-element.166.keep_ref, f32[3,16,64,512]{3,2,1,0:T(8,128)} %collective-permute-done.22.refs_0_, f32[3,1,64,384]{3,2,1,0:T(8,128)} %get-tuple-element.168.refs_1_.keep_ref), custom_call_target="tpu_custom_call" | custom-call | tf_op jit(solution)/shard_map/halve/pallas_call | solution.py:856
  288.9 1.5 collective-permute-start.23
  292.6 1.4 collective-permute-done.20.refs_1_.refs_3_
  295.6 17.5 %attend_back.7 = (f32[512,256]{1,0:T(8,128)}, f32[2,512,256]{2,1,0:T(8,128)}, f32[512,256]{1,0:T(8,128)}, f32[512,256]{1,0:T(8,128)}) custom-call(s32[1]{0:T(128)} %bitcast.me_ref.refs_0_, bf16[512,512]{1,0:T(8,128)(2,1)} %get-tuple-element.116.q_ref, bf16[2,512,512]{2,1,0:T(8,128)(2,1)} %get-tuple-element.117.own_ref.kv_own_ref, ...), custom_call_target="tpu_custom_call" | custom-call | tf_op jit(solution)/shard_map/attend_back/pallas_call | solution.py:450
  313.9 1.3 collective-permute-done.24.refs_1_
  315.4 5.1 %halve.15 = (f32[3,4,64,512]{3,2,1,0:T(8,128)}, f32[4,64,512]{2,1,0:T(8,128)}, f32[4,64,512]{2,1,0:T(8,128)}, f32[4,64,512]{2,1,0:T(8,128)}, f32[512,256]{1,0:T(8,128)}, /*index=5*/f32[512,256]{1,0:T(8,128)}) custom-call(f32[3,8,64,512]{3,2,1,0:T(8,128)} %get-tuple-element.169.refs_0_.keep_ref, ...), custom_call_target="tpu_custom_call", output_to_operand_aliasing={{4}: (4, {}), {5}: (5, {})} | custom-call | tf_op jit(solution)/shard_map/halve/pallas_call | solution.py:856
  321.2 1.5 collective-permute-start.33
  324.3 1.6 collective-permute-start.40
  327.3 7.1 %bottom.1 = (f32[464,128]{1,0:T(8,128)}, f32[464,128]{1,0:T(8,128)}, f32[16,512]{1,0:T(8,128)}) custom-call(s32[1]{0:T(128)} %bitcast.me_ref.refs_0_, f32[512,256]{1,0:T(8,128)} %get-tuple-element.157.refs_5_.refs_1_, f32[2,512,256]{2,1,0:T(8,128)} %get-tuple-element.158.refs_2_, f32[512,256]{1,0:T(8,128)} %copy-done.4, f32[512,256]{1,0:T(8,128)} %copy-done.5, ...), custom_call_target="tpu_custom_call" | custom-call | tf_op jit(solution)/shard_map/bottom/pallas_call | solution.py:302
  335.3 1.7 collective-permute-done.34.refs_1_
  338.1 3.0 halve.16
  341.1 1.7 collective-permute-start.36
  343.4 1.4 collective-permute-start.38
  347.0 1.8 halve.19
  352.5 2.3 halve.17
  354.8 1.6 collective-permute-start.39
  358.2 1.5 collective-permute-start.30
  359.7 4.0 collective-permute-done.30
  363.8 2.7 collective-permute-done.39.refs_0_
  367.3 1.9 halve.18
  377.8 2.1 collective-permute-start.32
  382.9 2.2 collective-permute-done.32
  (293 shorter events, 68.7 us)
Async XLA Ops:
  7.2 105.9 %all-gather.3.cloned.1.call-start = ((), (), s32[]{:S(2)}) async-start(), calls=%async_computation | async-start | bytes 12976128 | tf_op jit(solution)/shard_map/all_gather | solution.py:986
  15.4 5.2 %collective-permute-start = (f32[40,384]{1,0:T(8,128)S(1)}, f32[40,384]{1,0:T(8,128)S(1)}, u32[]{:S(2)}, u32[]{:S(2)}) collective-permute-start(f32[40,384]{1,0:T(8,128)S(1)} %select_maximum_fusion), channel_id=1, source_target_pairs={{0,4},{1,5},{2,6},{3,7},{4,0},{5,1},{6,2},{7,3},{8,12},{9,13},{10,... | collective-permute-start | bytes 184328 | tf_op jit(solution)/shard_map/ppermute | solution.py:47
  20.6 4.4 %collective-permute-start.1 = (f32[40,384]{1,0:T(8,128)S(1)}, f32[40,384]{1,0:T(8,128)S(1)}, u32[]{:S(2)}, u32[]{:S(2)}) collective-permute-start(f32[40,384]{1,0:T(8,128)S(1)} %fusion.49), channel_id=1, source_target_pairs={{0,8},{1,9},{2,10},{3,11},{4,12},{5,13},{6,14},{7,15},{8,0},{9,1},... | collective-permute-start | bytes 184328 | tf_op jit(solution)/shard_map/ppermute | solution.py:47
  25.0 7.3 %collective-permute-start.2 = (f32[40,384]{1,0:T(8,128)S(1)}, f32[40,384]{1,0:T(8,128)S(1)}, u32[]{:S(2)}, u32[]{:S(2)}) collective-permute-start(f32[40,384]{1,0:T(8,128)S(1)} %add.235), channel_id=1, source_target_pairs={{0,24},{1,25},{2,26},{3,27},{4,28},{5,29},{6,30},{7,31},{8,16},{9,... | collective-permute-start | bytes 184328 | tf_op jit(solution)/shard_map/ppermute | solution.py:47
  32.9 4.2 %collective-permute-start.3 = (f32[40,384]{1,0:T(8,128)S(1)}, f32[40,384]{1,0:T(8,128)S(1)}, u32[]{:S(2)}, u32[]{:S(2)}) collective-permute-start(f32[40,384]{1,0:T(8,128)S(1)} %pad_dynamic-update-slice_fusion), channel_id=1, source_target_pairs={{0,2},{1,3},{2,0},{3,1},{4,6},{5,7},{6,4},{7,5},{8,10},{9,11},{10,... | collective-permute-start | bytes 184328 | tf_op jit(solution)/shard_map/ppermute | solution.py:47
  37.1 4.5 %collective-permute-start.4 = (f32[2,40,384]{2,1,0:T(8,128)S(1)}, f32[2,40,384]{2,1,0:T(8,128)S(1)}, u32[]{:S(2)}, u32[]{:S(2)}) collective-permute-start(f32[2,40,384]{2,1,0:T(8,128)S(1)} %pad_maximum_fusion.7), channel_id=1, source_target_pairs={{0,1},{1,0},{2,3},{3,2},{4,5},{5,4},{6,7},{7,6},{8,9},{9,8},{10,11... | collective-permute-start | bytes 368648 | tf_op jit(solution)/shard_map/ppermute | solution.py:47
  125.6 3.1 collective-permute-start.5
  173.3 17.5 %collective-permute-start.6 = (f32[3,16,64,384]{3,2,1,0:T(8,128)}, f32[3,16,64,384]{3,2,1,0:T(8,128)}, u32[]{:S(2)}, u32[]{:S(2)}) collective-permute-start(f32[3,16,64,384]{3,2,1,0:T(8,128)} %get-tuple-element.130), channel_id=1, source_target_pairs={{0,1},{1,0},{2,3},{3,2},{4,5},{5,4},{6,7},{7,6},{8,9},{9,8},{10,11... | collective-permute-start | bytes 14155784 | tf_op jit(solution)/shard_map/ppermute | solution.py:47
  197.2 23.9 %collective-permute-start.10 = (f32[8,64,384]{2,1,0:T(8,128)}, f32[8,64,384]{2,1,0:T(8,128)S(1)}, u32[]{:S(2)}, u32[]{:S(2)}) collective-permute-start(f32[8,64,384]{2,1,0:T(8,128)} %get-tuple-element.139), channel_id=1, source_target_pairs={{0,2},{1,3},{2,0},{3,1},{4,6},{5,7},{6,4},{7,5},{8,10},{9,11},{10,... | collective-permute-start | bytes 2359304 | tf_op jit(solution)/shard_map/ppermute | solution.py:47
  198.7 22.4 %collective-permute-start.11 = (f32[8,64,384]{2,1,0:T(8,128)}, f32[8,64,384]{2,1,0:T(8,128)S(1)}, u32[]{:S(2)}, u32[]{:S(2)}) collective-permute-start(f32[8,64,384]{2,1,0:T(8,128)} %get-tuple-element.140), channel_id=1, source_target_pairs={{0,8},{1,9},{2,10},{3,11},{4,12},{5,13},{6,14},{7,15},{8,0},{9,1},... | collective-permute-start | bytes 2359304 | tf_op jit(solution)/shard_map/ppermute | solution.py:47
  199.5 21.5 %collective-permute-start.9 = (f32[8,64,384]{2,1,0:T(8,128)}, f32[8,64,384]{2,1,0:T(8,128)S(1)}, u32[]{:S(2)}, u32[]{:S(2)}) collective-permute-start(f32[8,64,384]{2,1,0:T(8,128)} %get-tuple-element.138), channel_id=1, source_target_pairs={{0,4},{1,5},{2,6},{3,7},{4,0},{5,1},{6,2},{7,3},{8,12},{9,13},{10,... | collective-permute-start | bytes 2359304 | tf_op jit(solution)/shard_map/ppermute | solution.py:47
  200.1 2.1 collective-permute-start.7
  200.1 2.9 collective-permute-start.8
  227.2 3.7 collective-permute-start.12
  227.4 3.5 collective-permute-start.13
  227.7 26.8 %collective-permute-start.14 = (f32[4,64,384]{2,1,0:T(8,128)}, f32[4,64,384]{2,1,0:T(8,128)S(1)}, u32[]{:S(2)}, u32[]{:S(2)}) collective-permute-start(f32[4,64,384]{2,1,0:T(8,128)} %get-tuple-element.151), channel_id=1, source_target_pairs={{0,2},{1,3},{2,0},{3,1},{4,6},{5,7},{6,4},{7,5},{8,10},{9,11},{10,... | collective-permute-start | bytes 1179656 | tf_op jit(solution)/shard_map/ppermute | solution.py:47
  229.1 25.4 %collective-permute-start.15 = (f32[4,64,384]{2,1,0:T(8,128)}, f32[4,64,384]{2,1,0:T(8,128)S(1)}, u32[]{:S(2)}, u32[]{:S(2)}) collective-permute-start(f32[4,64,384]{2,1,0:T(8,128)} %get-tuple-element.152), channel_id=1, source_target_pairs={{0,8},{1,9},{2,10},{3,11},{4,12},{5,13},{6,14},{7,15},{8,0},{9,1},... | collective-permute-start | bytes 1179656 | tf_op jit(solution)/shard_map/ppermute | solution.py:47
  230.3 24.3 %collective-permute-start.16 = (f32[4,64,384]{2,1,0:T(8,128)}, f32[4,64,384]{2,1,0:T(8,128)S(1)}, u32[]{:S(2)}, u32[]{:S(2)}) collective-permute-start(f32[4,64,384]{2,1,0:T(8,128)} %get-tuple-element.153), channel_id=1, source_target_pairs={{0,4},{1,5},{2,6},{3,7},{4,0},{5,1},{6,2},{7,3},{8,12},{9,13},{10,... | collective-permute-start | bytes 1179656 | tf_op jit(solution)/shard_map/ppermute | solution.py:47
  258.2 23.2 %collective-permute-start.22 = (f32[3,16,64,512]{3,2,1,0:T(8,128)}, f32[3,16,64,512]{3,2,1,0:T(8,128)}, u32[]{:S(2)}, u32[]{:S(2)}) collective-permute-start(f32[3,16,64,512]{3,2,1,0:T(8,128)} %get-tuple-element.167), channel_id=1, source_target_pairs={{0,1},{1,0},{2,3},{3,2},{4,5},{5,4},{6,7},{7,6},{8,9},{9,8},{10,11... | collective-permute-start | bytes 18874376 | tf_op jit(solution)/shard_map/ppermute | solution.py:47
  258.2 20.2 %collective-permute-start.17 = (f32[2,64,384]{2,1,0:T(8,128)}, f32[2,64,384]{2,1,0:T(8,128)S(1)}, u32[]{:S(2)}, u32[]{:S(2)}) collective-permute-start(f32[2,64,384]{2,1,0:T(8,128)} %get-tuple-element.159), channel_id=1, source_target_pairs={{0,8},{1,9},{2,10},{3,11},{4,12},{5,13},{6,14},{7,15},{8,0},{9,1},... | collective-permute-start | bytes 589832 | tf_op jit(solution)/shard_map/ppermute | solution.py:47
  259.1 19.3 %collective-permute-start.18 = (f32[2,64,384]{2,1,0:T(8,128)}, f32[2,64,384]{2,1,0:T(8,128)S(1)}, u32[]{:S(2)}, u32[]{:S(2)}) collective-permute-start(f32[2,64,384]{2,1,0:T(8,128)} %get-tuple-element.160), channel_id=1, source_target_pairs={{0,4},{1,5},{2,6},{3,7},{4,0},{5,1},{6,2},{7,3},{8,12},{9,13},{10,... | collective-permute-start | bytes 589832 | tf_op jit(solution)/shard_map/ppermute | solution.py:47
  260.5 17.9 %collective-permute-start.19 = (f32[2,64,384]{2,1,0:T(8,128)}, f32[2,64,384]{2,1,0:T(8,128)S(1)}, u32[]{:S(2)}, u32[]{:S(2)}) collective-permute-start(f32[2,64,384]{2,1,0:T(8,128)} %get-tuple-element.161), channel_id=1, source_target_pairs={{0,2},{1,3},{2,0},{3,1},{4,6},{5,7},{6,4},{7,5},{8,10},{9,11},{10,... | collective-permute-start | bytes 589832 | tf_op jit(solution)/shard_map/ppermute | solution.py:47
  288.9 24.9 %collective-permute-start.23 = (f32[8,64,512]{2,1,0:T(8,128)}, f32[8,64,512]{2,1,0:T(8,128)S(1)}, u32[]{:S(2)}, u32[]{:S(2)}) collective-permute-start(f32[8,64,512]{2,1,0:T(8,128)} %get-tuple-element.172), channel_id=1, source_target_pairs={{0,4},{1,5},{2,6},{3,7},{4,0},{5,1},{6,2},{7,3},{8,12},{9,13},{10,... | collective-permute-start | bytes 3145736 | tf_op jit(solution)/shard_map/ppermute | solution.py:47
  290.4 24.7 %collective-permute-start.24 = (f32[8,64,512]{2,1,0:T(8,128)}, f32[8,64,512]{2,1,0:T(8,128)}, u32[]{:S(2)}, u32[]{:S(2)}) collective-permute-start(f32[8,64,512]{2,1,0:T(8,128)} %get-tuple-element.173), channel_id=1, source_target_pairs={{0,2},{1,3},{2,0},{3,1},{4,6},{5,7},{6,4},{7,5},{8,10},{9,11},{10,... | collective-permute-start | bytes 3145736 | tf_op jit(solution)/shard_map/ppermute | solution.py:47
  291.0 24.5 %collective-permute-start.25 = (f32[8,64,512]{2,1,0:T(8,128)}, f32[8,64,512]{2,1,0:T(8,128)}, u32[]{:S(2)}, u32[]{:S(2)}) collective-permute-start(f32[8,64,512]{2,1,0:T(8,128)} %get-tuple-element.174), channel_id=1, source_target_pairs={{0,8},{1,9},{2,10},{3,11},{4,12},{5,13},{6,14},{7,15},{8,0},{9,1},... | collective-permute-start | bytes 3145736 | tf_op jit(solution)/shard_map/ppermute | solution.py:47
  292.1 1.9 collective-permute-start.20
  292.1 2.7 collective-permute-start.21
  320.6 3.8 collective-permute-start.26
  320.7 5.8 %collective-permute-start.27 = (f32[512,256]{1,0:T(8,128)}, f32[512,256]{1,0:T(8,128)S(1)}, u32[]{:S(2)}, u32[]{:S(2)}) collective-permute-start(f32[512,256]{1,0:T(8,128)} %get-tuple-element.178), channel_id=1, source_target_pairs={{0,1},{1,0},{2,3},{3,2},{4,5},{5,4},{6,7},{7,6},{8,9},{9,8},{10,11... | collective-permute-start | bytes 1572872 | tf_op jit(solution)/shard_map/ppermute | solution.py:47
  321.2 14.1 %collective-permute-start.33 = (f32[4,64,512]{2,1,0:T(8,128)}, f32[4,64,512]{2,1,0:T(8,128)S(1)}, u32[]{:S(2)}, u32[]{:S(2)}) collective-permute-start(f32[4,64,512]{2,1,0:T(8,128)} %get-tuple-element.184), channel_id=1, source_target_pairs={{0,2},{1,3},{2,0},{3,1},{4,6},{5,7},{6,4},{7,5},{8,10},{9,11},{10,... | collective-permute-start | bytes 1572872 | tf_op jit(solution)/shard_map/ppermute | solution.py:47
  322.6 14.3 %collective-permute-start.34 = (f32[4,64,512]{2,1,0:T(8,128)}, f32[4,64,512]{2,1,0:T(8,128)S(1)}, u32[]{:S(2)}, u32[]{:S(2)}) collective-permute-start(f32[4,64,512]{2,1,0:T(8,128)} %get-tuple-element.185), channel_id=1, source_target_pairs={{0,8},{1,9},{2,10},{3,11},{4,12},{5,13},{6,14},{7,15},{8,0},{9,1},... | collective-permute-start | bytes 1572872 | tf_op jit(solution)/shard_map/ppermute | solution.py:47
  323.8 13.6 %collective-permute-start.35 = (f32[4,64,512]{2,1,0:T(8,128)}, f32[4,64,512]{2,1,0:T(8,128)S(1)}, u32[]{:S(2)}, u32[]{:S(2)}) collective-permute-start(f32[4,64,512]{2,1,0:T(8,128)} %get-tuple-element.186), channel_id=1, source_target_pairs={{0,4},{1,5},{2,6},{3,7},{4,0},{5,1},{6,2},{7,3},{8,12},{9,13},{10,... | collective-permute-start | bytes 1572872 | tf_op jit(solution)/shard_map/ppermute | solution.py:47
  324.3 22.0 %collective-permute-start.40 = (f32[3,1,64,384]{3,2,1,0:T(8,128)}, f32[3,1,64,384]{3,2,1,0:T(8,128)S(1)}, u32[]{:S(2)}, u32[]{:S(2)}) collective-permute-start(f32[3,1,64,384]{3,2,1,0:T(8,128)} %get-tuple-element.193), channel_id=1, source_target_pairs={{0,24},{1,25},{2,26},{3,27},{4,28},{5,29},{6,30},{7,31},{8,16},{9,... | collective-permute-start | bytes 884744 | tf_op jit(solution)/shard_map/ppermute | solution.py:47
  334.4 14.4 %collective-permute-start.28 = (f32[464,128]{1,0:T(8,128)}, f32[464,128]{1,0:T(8,128)}, u32[]{:S(2)}, u32[]{:S(2)}) collective-permute-start(f32[464,128]{1,0:T(8,128)} %get-tuple-element.183), channel_id=1, source_target_pairs={{0,1},{1,0},{2,3},{3,2},{4,5},{5,4},{6,7},{7,6},{8,9},{9,8},{10,11... | collective-permute-start | bytes 712712 | tf_op jit(solution)/shard_map/ppermute | solution.py:47
  341.1 10.4 %collective-permute-start.36 = (f32[2,64,512]{2,1,0:T(8,128)}, f32[2,64,512]{2,1,0:T(8,128)S(1)}, u32[]{:S(2)}, u32[]{:S(2)}) collective-permute-start(f32[2,64,512]{2,1,0:T(8,128)} %get-tuple-element.188), channel_id=1, source_target_pairs={{0,8},{1,9},{2,10},{3,11},{4,12},{5,13},{6,14},{7,15},{8,0},{9,1},... | collective-permute-start | bytes 786440 | tf_op jit(solution)/shard_map/ppermute | solution.py:47
  342.8 8.8 %collective-permute-start.37 = (f32[2,64,512]{2,1,0:T(8,128)}, f32[2,64,512]{2,1,0:T(8,128)S(1)}, u32[]{:S(2)}, u32[]{:S(2)}) collective-permute-start(f32[2,64,512]{2,1,0:T(8,128)} %get-tuple-element.189), channel_id=1, source_target_pairs={{0,4},{1,5},{2,6},{3,7},{4,0},{5,1},{6,2},{7,3},{8,12},{9,13},{10,... | collective-permute-start | bytes 786440 | tf_op jit(solution)/shard_map/ppermute | solution.py:47
  343.4 8.2 %collective-permute-start.38 = (f32[2,64,512]{2,1,0:T(8,128)}, f32[2,64,512]{2,1,0:T(8,128)S(1)}, u32[]{:S(2)}, u32[]{:S(2)}) collective-permute-start(f32[2,64,512]{2,1,0:T(8,128)} %get-tuple-element.190), channel_id=1, source_target_pairs={{0,2},{1,3},{2,0},{3,1},{4,6},{5,7},{6,4},{7,5},{8,10},{9,11},{10,... | collective-permute-start | bytes 786440 | tf_op jit(solution)/shard_map/ppermute | solution.py:47
  346.3 24.1 %copy-start.9 = (f32[2,480,60]{1,0,2:T(2,128)S(1)}, f32[2,480,60]{1,0,2:T(2,128)}, u32[]{:S(2)}) copy-start(f32[2,480,60]{1,0,2:T(2,128)} %param.33) | copy-start | bytes 691204
  346.3 24.1 %copy-start.32 = (f32[2,480,60]{1,0,2:T(2,128)S(1)}, f32[2,480,60]{1,0,2:T(2,128)}, u32[]{:S(2)}) copy-start(f32[2,480,60]{1,0,2:T(2,128)} %param.39) | copy-start | bytes 691204
  346.3 24.1 %copy-start.33 = (f32[2,480,60]{1,0,2:T(2,128)S(1)}, f32[2,480,60]{1,0,2:T(2,128)}, u32[]{:S(2)}) copy-start(f32[2,480,60]{1,0,2:T(2,128)} %param.45) | copy-start | bytes 691204
  349.9 6.5 %collective-permute-start.29 = (f32[344,128]{1,0:T(8,128)S(1)}, f32[344,128]{1,0:T(8,128)}, u32[]{:S(2)}, u32[]{:S(2)}) collective-permute-start(f32[344,128]{1,0:T(8,128)S(1)} %slice.236), channel_id=1, source_target_pairs={{0,2},{1,3},{2,0},{3,1},{4,6},{5,7},{6,4},{7,5},{8,10},{9,11},{10,... | collective-permute-start | bytes 528392 | tf_op jit(solution)/shard_map/ppermute | solution.py:47
  354.8 19.3 %copy-start.10 = (f32[2,60,480]{2,0,1:T(2,128)S(1)}, f32[2,60,480]{2,0,1:T(2,128)}, u32[]{:S(2)}) copy-start(f32[2,60,480]{2,0,1:T(2,128)} %param.32) | copy-start | bytes 691204
  354.8 19.3 %copy-start.34 = (f32[2,60,480]{2,0,1:T(2,128)S(1)}, f32[2,60,480]{2,0,1:T(2,128)}, u32[]{:S(2)}) copy-start(f32[2,60,480]{2,0,1:T(2,128)} %param.38) | copy-start | bytes 691204
  354.8 19.3 %copy-start.35 = (f32[2,60,480]{2,0,1:T(2,128)S(1)}, f32[2,60,480]{2,0,1:T(2,128)}, u32[]{:S(2)}) copy-start(f32[2,60,480]{2,0,1:T(2,128)} %param.44) | copy-start | bytes 691204
  354.8 11.8 %collective-permute-start.39 = (f32[3,1,64,512]{3,2,1,0:T(8,128)}, f32[3,1,64,512]{3,2,1,0:T(8,128)S(1)}, u32[]{:S(2)}, u32[]{:S(2)}) collective-permute-start(f32[3,1,64,512]{3,2,1,0:T(8,128)} %get-tuple-element.192), channel_id=1, source_target_pairs={{0,24},{1,25},{2,26},{3,27},{4,28},{5,29},{6,30},{7,31},{8,16},{9,... | collective-permute-start | bytes 1179656 | tf_op jit(solution)/shard_map/ppermute | solution.py:47
  358.2 5.5 %collective-permute-start.30 = (f32[344,128]{1,0:T(8,128)S(1)}, f32[344,128]{1,0:T(8,128)S(1)}, u32[]{:S(2)}, u32[]{:S(2)}) collective-permute-start(f32[344,128]{1,0:T(8,128)S(1)} %pad_maximum_fusion.6), channel_id=1, source_target_pairs={{0,4},{1,5},{2,6},{3,7},{4,0},{5,1},{6,2},{7,3},{8,12},{9,13},{10,... | collective-permute-start | bytes 528392 | tf_op jit(solution)/shard_map/ppermute | solution.py:47
  363.7 14.0 %collective-permute-start.31 = (f32[344,128]{1,0:T(8,128)S(1)}, f32[344,128]{1,0:T(8,128)S(1)}, u32[]{:S(2)}, u32[]{:S(2)}) collective-permute-start(f32[344,128]{1,0:T(8,128)S(1)} %fusion.31), channel_id=1, source_target_pairs={{0,8},{1,9},{2,10},{3,11},{4,12},{5,13},{6,14},{7,15},{8,0},{9,1},... | collective-permute-start | bytes 528392 | tf_op jit(solution)/shard_map/ppermute | solution.py:47
  377.8 7.3 %collective-permute-start.32 = (f32[344,128]{1,0:T(8,128)S(1)}, f32[344,128]{1,0:T(8,128)S(1)}, u32[]{:S(2)}, u32[]{:S(2)}) collective-permute-start(f32[344,128]{1,0:T(8,128)S(1)} %add.249), channel_id=1, source_target_pairs={{0,24},{1,25},{2,26},{3,27},{4,28},{5,29},{6,30},{7,31},{8,16},{9,... | collective-permute-start | bytes 528392 | tf_op jit(solution)/shard_map/ppermute | solution.py:47
  (47 other events, 246.4 us)
Sparse Core Ops, SparseCore 0:
  13.4 99.6 all-gather.2

commit v3 on v2

--- a/solution.py
+++ b/solution.py
@@ -5,6 +5,7 @@
 import jax.numpy as jnp
 from jax import lax
 from jax.experimental import pallas as pl
+from jax.experimental.layout import Layout, with_layout_constraint
 from jax.experimental.pallas import tpu as pltpu
 from jax.sharding import PartitionSpec as P
 
@@ -207,9 +208,33 @@
     def __init__(self, ref):
         self.ref = ref
 
-    def block(self, tile, start, stop):
+    def block(self, place, start, stop):
         groups, _, rows, _ = self.ref.shape
-        return self.ref[:, tile, :, start:stop].reshape(groups * rows, stop - start)
+        return self.ref[:, place[1], :, start:stop].reshape(groups * rows, stop - start)
+
+
+class Relative:
+    def __init__(self, cube, me, refs, orders):
+        self.cube = cube
+        self.me = me
+        self.refs = refs
+        self.orders = orders
+
+    def block(self, place, start, stop):
+        turn, tile = place
+        ref = self.refs[turn & 1]
+        wide = ref.shape[-1]
+        pieces = []
+        while start < stop:
+            part, first = divmod(start, wide)
+            last = min(wide, first + stop - start)
+            rows = []
+            for group in range(self.cube.groups):
+                offset = (group * self.cube.tensors + tile) ^ self.me
+                rows.append(ref[part, self.cube.slot(offset, self.orders[part]), :, first:last])
+            pieces.append(jnp.concatenate(rows, 0))
+            start += last - first
+        return pieces[0] if len(pieces) == 1 else jnp.concatenate(pieces, 1)
 
 
 class Scattered:
@@ -242,16 +267,16 @@
         self.base = base
         self.hidden = hidden
 
-    def out(self, tile):
-        return self.weights.block(tile, self.base, self.base + LANES)
-
-    def up(self, tile):
+    def out(self, place):
+        return self.weights.block(place, self.base, self.base + LANES)
+
+    def up(self, place):
         start = self.base + LANES
-        return self.weights.block(tile, start, start + self.hidden)
-
-    def down(self, tile):
+        return self.weights.block(place, start, start + self.hidden)
+
+    def down(self, place):
         start = self.base + LANES + self.hidden
-        return self.weights.block(tile, start, start + self.hidden)
+        return self.weights.block(place, start, start + self.hidden)
 
 
 def tile_lanes(tile):
@@ -293,6 +318,10 @@
 
 def after_specs(after):
     return [pl.BlockSpec(memory_space=pl.ANY)] * len(after)
+
+
+def place_of(at):
+    return (at, at)
 
 
 def call(kernel, name, ins, in_specs, outs, scratch=(), after=()):
@@ -335,7 +364,7 @@
         other_ref[1, :, lanes] = values[own:]
 
 
-def embed(table, ids, vocab, cosine, sine):
+def embed(table, ids, vocab, cosine, sine, after):
     tiles = table.shape[0]
     own = ids.shape[1] // 2
     wide = tiles * LANES
@@ -346,40 +375,45 @@
         jax.ShapeDtypeStruct((2, own, wide), brain),
         jax.ShapeDtypeStruct((own, vocab.shape[1]), single),
     ]
-    return call(embed_kernel, "embed", ins, [whole_spec(x.shape) for x in ins], outs)
-
-
-def attend_kernel(heads, chunk, q_ref, own_ref, other_ref, out_ref, logsum_ref):
+    specs = [whole_spec(x.shape) for x in ins]
+    return call(embed_kernel, "embed", ins, specs, outs, (), after)
+
+
+def attend_kernel(heads, q_ref, own_ref, other_ref, out_ref, logsum_ref):
     own = q_ref.shape[0]
     q_turned = q_ref[...].T
     keys = jnp.concatenate([own_ref[0], other_ref[0]], 0)
     v_turned = jnp.concatenate([own_ref[1], other_ref[1]], 0).T
-    rows = lax.broadcasted_iota(jnp.int32, (LANES, chunk), 0)
-    for start in range(0, own, chunk):
-        part = slice(start, start + chunk)
-        q_part = q_turned[:, part]
-        mixed = jnp.zeros((LANES, chunk), single)
-        for head in range(heads):
-            mine = (rows >= head * HEAD) & (rows < (head + 1) * HEAD)
-            scores = dot(keys, jnp.where(mine, q_part, jnp.zeros_like(q_part)))
-            peak = column_max(scores) * scale_two
-            weights = jnp.exp2(scores * scale_two - peak)
-            total = column_sum(weights)
-            probs = (weights * (1.0 / total)).astype(brain)
-            mixed = jnp.where(mine, dot(v_turned, probs), mixed)
-            logsum_ref[0, head : head + 1, part] = peak + jnp.log2(total)
-        out_ref[part, :] = mixed.T.astype(brain)
-
-
-def attend(q, kv_own, kv_other, heads):
+    rows = lax.broadcasted_iota(jnp.int32, (LANES, own), 0)
+
+    def scores_of(head):
+        mine = (rows >= head * HEAD) & (rows < (head + 1) * HEAD)
+        return mine, dot(keys, jnp.where(mine, q_turned, jnp.zeros_like(q_turned)))
+
+    mixed = jnp.zeros((LANES, own), single)
+    ahead = scores_of(0)
+    for head in range(heads):
+        mine, scores = ahead
+        if head + 1 < heads:
+            ahead = scores_of(head + 1)
+        peak = column_max(scores) * scale_two
+        weights = jnp.exp2(scores * scale_two - peak)
+        total = column_sum(weights)
+        probs = (weights * (1.0 / total)).astype(brain)
+        mixed = jnp.where(mine, dot(v_turned, probs), mixed)
+        logsum_ref[0, head : head + 1, :] = peak + jnp.log2(total)
+    out_ref[...] = mixed.T.astype(brain)
+
+
+def attend(q, kv_own, kv_other, heads, after=()):
     own, wide = q.shape
     tiles = wide // LANES
     own_spec = pl.BlockSpec((own, LANES), lambda at: (0, at))
     pair_spec = pl.BlockSpec((2, own, LANES), lambda at: (0, 0, at))
     return pl.pallas_call(
-        functools.partial(attend_kernel, heads, LANES),
+        follow(functools.partial(attend_kernel, heads), 3, after),
         grid=(tiles,),
-        in_specs=[own_spec, pair_spec, pair_spec],
+        in_specs=[own_spec, pair_spec, pair_spec, *after_specs(after)],
         out_specs=[own_spec, pl.BlockSpec((1, 8, own), lambda at: (at, 0, 0))],
         out_shape=[
             jax.ShapeDtypeStruct((own, wide), brain),
@@ -387,13 +421,13 @@
         ],
         compiler_params=params(),
         name="attend",
-    )(q, kv_own, kv_other)
+    )(q, kv_own, kv_other, *after)
 
 
 def attend_back_kernel(
     heads, chunk, count, me_ref, q_ref, kv_own_ref, kv_other_ref, g_ref, logsum_ref, *refs
 ):
-    dq_ref, own_ref, other_k_ref, other_v_ref = refs[count:]
+    dq_ref, own_ref, other_ref = refs[count:]
     own = q_ref.shape[0]
     q = q_ref[...]
     grad = g_ref[...]
@@ -422,13 +456,13 @@
             if start == 0 and head == 0:
                 own_ref[0] = dk[:own]
                 own_ref[1] = dv[:own]
-                other_k_ref[...] = dk[own:]
-                other_v_ref[...] = dv[own:]
+                other_ref[0] = dk[own:]
+                other_ref[1] = dv[own:]
             else:
                 own_ref[0] += dk[:own]
                 own_ref[1] += dv[:own]
-                other_k_ref[...] += dk[own:]
-                other_v_ref[...] += dv[own:]
+                other_ref[0] += dk[own:]
+                other_ref[1] += dv[own:]
             dq = jnp.where(mine, dot(k_turned, g_scores), dq)
         dq_ref[part, :] = (dq * scale).T
 
@@ -460,17 +494,17 @@
                 pl.BlockSpec((1, 8, own), lambda at, me: (tile(at, me), 0, 0)),
                 *after_specs(after),
             ],
-            out_specs=[one_out, pair_out, one_out, one_out],
+            out_specs=[one_out, pair_out, pair_out],
         ),
-        out_shape=[one_shape, pair_shape, one_shape, one_shape],
+        out_shape=[one_shape, pair_shape, pair_shape],
         compiler_params=params(),
         name="attend_back",
     )(me, q, kv_own, kv_other, grad, logsum, *after)
 
 
-def attention_out(mixed, resid, layer, tiles):
+def attention_out(mixed, resid, layer, places):
     parts = [
-        dot(mixed[:, at * LANES : (at + 1) * LANES], layer.out(at), 1, 1) for at in range(tiles)
+        dot(mixed[:, tile_lanes(place[1])], layer.out(place), 1, 1) for place in places
     ]
     return resid + add_up(parts)
 
@@ -481,13 +515,13 @@
 ):
     tiles = w_ref.shape[1]
     layer = Layer(Gathered(w_ref), 0, (w_ref.shape[3] - LANES) // 2)
-    mid = attention_out(mixed_ref[...], resid_ref[...], layer, tiles)
+    mid = attention_out(mixed_ref, resid_ref[...], layer, [place_of(at) for at in range(tiles)])
     mid_ref[...] = mid
     normed = feats.norm(mid, norms_ref[2:3], norms_ref[3:4])
     parts = []
     for at in range(tiles):
-        act = gelu(dot(normed, layer.up(at))).astype(brain)
-        parts.append(dot(act, layer.down(at), 1, 1))
+        act = gelu(dot(normed, layer.up(place_of(at)))).astype(brain)
+        parts.append(dot(act, layer.down(place_of(at)), 1, 1))
     total = mid + add_up(parts)
     next_ref[...] = total
     normed = feats.norm(total, norms_ref[4:5], norms_ref[5:6])
@@ -496,13 +530,13 @@
     sine = sin_ref[...]
     for at in range(tiles):
         lanes = slice(at * LANES, (at + 1) * LANES)
-        rows = dot(normed, weights.block(at, 0, 3 * LANES))
+        rows = dot(normed, weights.block(place_of(at), 0, 3 * LANES))
         q_ref[:, lanes] = rotate(rows[:, :LANES], cosine, sine).astype(brain)
         kv_ref[0, :, lanes] = rotate(rows[:, LANES : 2 * LANES], cosine, sine).astype(brain)
         kv_ref[1, :, lanes] = rows[:, 2 * LANES :].astype(brain)
 
 
-def middle(feats, mixed, resid, weights, columns, at_heads, norms, cosine, sine):
+def middle(feats, mixed, resid, weights, columns, at_heads, norms, cosine, sine, after):
     own, wide = mixed.shape
     plain = jax.ShapeDtypeStruct(resid.shape, single)
     in_specs = [
@@ -521,7 +555,8 @@
         jax.ShapeDtypeStruct((2, own, wide), brain),
     ]
     ins = (mixed, resid, weights, weights, norms, cosine, sine)
-    return call(functools.partial(middle_kernel, feats), "middle", ins, in_specs, outs)
+    kernel = functools.partial(middle_kernel, feats)
+    return call(kernel, "middle", ins, in_specs, outs, (), after)
 
 
 def feed_back(
@@ -534,10 +569,10 @@
     normed_turned = normed.T
     parts = []
     for turn, tile in turns:
-        g_hidden = (dot(g_low, layer.down(tile)) * slope_ref[turn]).astype(brain)
+        g_hidden = (dot(g_low, layer.down((turn, tile))) * slope_ref[turn]).astype(brain)
         grads.store(tile, turn, base + LANES + hidden, dot(g_turned, act_ref[turn]))
         grads.store(tile, turn, base + LANES, dot(normed_turned, g_hidden))
-        parts.append(dot(g_hidden, layer.up(tile), 1, 1))
+        parts.append(dot(g_hidden, layer.up((turn, tile)), 1, 1))
     g_normed = add_up(parts)
     unit, inverse = feats.centred(mid)
     g_gain = jnp.sum(g_normed * unit, 0, keepdims=True)
@@ -548,53 +583,56 @@
     g_turned = g_low.T
     for turn, tile in turns:
         lanes = tile_lanes(tile)
-        g_mixed_ref[:, lanes] = dot(g_low, layer.out(tile)).astype(brain)
+        g_mixed_ref[:, lanes] = dot(g_low, layer.out((turn, tile))).astype(brain)
         grads.store(tile, turn, base, dot(g_turned, mixed_ref[:, lanes]))
     return g_gain, g_shift
 
 
 def top_kernel(
-    feats, cube, vocab_count, grad_orders, me_ref, mixed_ref, resid_ref, w_ref, norms_ref,
-    vocab_ref, slot_ref, target_ref, count_ref, keep_ref, send_ref, g_mid_ref, g_mixed_ref,
+    feats, cube, vocab_count, orders, grad_orders, me_ref, mixed_ref, resid_ref, w_own_ref,
+    w_other_ref, norms_ref, vocab_ref, marks_ref, table_ref, keep_ref, send_ref, g_mid_ref, g_mixed_ref,
     g_norms_ref, g_vocab_ref, act_ref, slope_ref,
 ):
     me = me_ref[0]
     tiles = cube.tensors
     turns = [(turn, turn ^ (me & (tiles - 1))) for turn in range(tiles)]
     grads = Scattered(cube, me, keep_ref, send_ref, grad_orders)
-    layer = Layer(Gathered(w_ref), 3 * LANES, act_ref.shape[2])
-    mid = attention_out(mixed_ref[...], resid_ref[...], layer, tiles)
+    layer = Layer(Relative(cube, me, (w_own_ref, w_other_ref), orders), 0, act_ref.shape[2])
+    mid = attention_out(mixed_ref, resid_ref[...], layer, turns)
     normed = feats.norm(mid, norms_ref[6:7], norms_ref[7:8])
     parts = []
     for turn, tile in turns:
-        hidden = dot(normed, layer.up(tile))
+        hidden = dot(normed, layer.up((turn, tile)))
         share = normal_share(hidden)
         act = (hidden * share).astype(brain)
         act_ref[turn] = act
         slope_ref[turn] = gelu_slope(hidden, share)
-        parts.append(dot(act, layer.down(tile), 1, 1))
+        parts.append(dot(act, layer.down((turn, tile)), 1, 1))
     total = mid + add_up(parts)
     unit, inverse = feats.centred(total)
     gain = norms_ref[8:9]
     final = (unit * gain + norms_ref[9:10]).astype(brain)
     own = total.shape[0]
-    slots = slot_ref.shape[0]
+    marks = marks_ref[...].T.astype(jnp.int32)
+    slots = marks.shape[0]
+    slot = marks[:, 0:1]
+    target = marks[:, 1:2]
     vocab = vocab_ref[...]
-    where_hot = (lax.broadcasted_iota(jnp.int32, (slots, own), 1) == slot_ref[...]).astype(single)
+    where_hot = (lax.broadcasted_iota(jnp.int32, (slots, own), 1) == slot).astype(single)
     where_hot = where_hot.astype(brain)
-    present = (slot_ref[...] >= 0).astype(single)
+    present = (slot >= 0).astype(single)
     picked = dot(where_hot, final).astype(brain)
     logits = dot(picked, vocab, 1, 1)
     lane = lax.broadcasted_iota(jnp.int32, logits.shape, 1)
     logits = jnp.where(lane < vocab_count, logits, -1e30)
     peak = jnp.max(logits, 1, keepdims=True)
     logsum = peak + jnp.log(jnp.sum(jnp.exp(logits - peak), 1, keepdims=True))
-    target_hot = (lane == target_ref[...]).astype(single)
+    target_hot = (lane == target).astype(single)
     target_logit = jnp.sum(
         jnp.where(lane < vocab_count, logits * target_hot, 0.0), 1, keepdims=True
     )
     loss = jnp.sum((logsum - target_logit) * present, 0, keepdims=True)
-    share = present / count_ref[0:1, 0:1]
+    share = present / table_ref[0, vocab_count : vocab_count + 1, 0:1]
     g_logits = ((jnp.exp(logits - logsum) - target_hot) * share).astype(brain)
     g_vocab_ref[...] = dot(g_logits, picked, 0, 0)[:TABLE_ROWS]
     g_picked = dot(g_logits, vocab)
@@ -613,15 +651,16 @@
 
 
 def top(
-    feats, cube, grad_orders, me, mixed, resid, weights, columns, at_block, norms, vocab,
-    vocab_count, slot, target, count,
+    feats, cube, orders, grad_orders, me, mixed, resid, w_own, w_other, norms, vocab,
+    vocab_count, marks, table,
 ):
     own, wide = mixed.shape
     tiles = cube.tensors
-    rows = weights.shape[2]
-    hidden = (columns - 4 * LANES) // 2
+    rows = w_own.shape[2]
+    columns = w_own.shape[0] * w_own.shape[3] - 3 * LANES
+    hidden = (columns - LANES) // 2
     pieces = len(grad_orders)
-    grads = (pieces, cube.devices // 2, rows, (columns - 3 * LANES) // pieces)
+    grads = (pieces, cube.devices // 2, rows, columns // pieces)
     outs = [
         jax.ShapeDtypeStruct(grads, single),
         jax.ShapeDtypeStruct(grads, single),
@@ -634,39 +673,39 @@
         scalar_spec(),
         whole_spec(mixed.shape),
         whole_spec(resid.shape),
-        columns_spec(weights, columns, at_block),
+        whole_spec(w_own.shape),
+        whole_spec(w_other.shape),
         whole_spec(norms.shape),
         whole_spec(vocab.shape),
-        whole_spec(slot.shape),
-        whole_spec(target.shape),
-        whole_spec(count.shape),
+        whole_spec(marks.shape),
+        whole_spec(table.shape),
     ]
     scratch = [
         pltpu.VMEM((tiles, own, hidden), brain),
         pltpu.VMEM((tiles, own, hidden), single),
     ]
-    ins = (me, mixed, resid, weights, norms, vocab, slot, target, count)
-    kernel = functools.partial(top_kernel, feats, cube, vocab_count, grad_orders)
+    ins = (me, mixed, resid, w_own, w_other, norms, vocab, marks, table)
+    kernel = functools.partial(top_kernel, feats, cube, vocab_count, orders, grad_orders)
     return call(kernel, "top", ins, in_specs, outs, scratch)
 
 
 def head_grads(turn, heads_refs, cosine, sine):
-    dq_ref, own_ref, other_k_ref, other_v_ref = heads_refs[4 * (turn // 2) : 4 * (turn // 2) + 4]
+    dq_ref, own_ref, other_ref = heads_refs[3 * (turn // 2) : 3 * (turn // 2) + 3]
     lanes = tile_lanes(turn % 2)
     other = tile_lanes(1 - turn % 2)
     g_q = unrotate(dq_ref[:, lanes], cosine, sine)
-    g_k = unrotate(own_ref[0, :, lanes] + other_k_ref[:, other], cosine, sine)
-    g_v = own_ref[1, :, lanes] + other_v_ref[:, other]
+    g_k = unrotate(own_ref[0, :, lanes] + other_ref[0, :, other], cosine, sine)
+    g_v = own_ref[1, :, lanes] + other_ref[1, :, other]
     return jnp.concatenate([g_q, g_k, g_v], 1).astype(brain)
 
 
 def lower_kernel(feats, cube, grad_orders, me_ref, *refs):
-    heads_refs = refs[:8]
+    heads_refs = refs[:6]
     (
         g_mid_in_ref, resid_ref, mid_ref, mixed_ref, w_in_ref, w_ref, norms_ref, cos_ref, sin_ref,
         g_norms_in_ref, keep_ref, send_ref, g_mid_ref, g_mixed_ref, g_norms_ref,
         act_ref, slope_ref,
-    ) = refs[8:]
+    ) = refs[6:]
     me = me_ref[0]
     tiles = cube.tensors
     turns = [(turn, turn ^ (me & (tiles - 1))) for turn in range(tiles)]
@@ -682,7 +721,7 @@
     for turn, tile in turns:
         g_heads = head_grads(turn, heads_refs, cosine, sine)
         grads.store(tile, turn, 0, dot(normed_turned, g_heads))
-        parts.append(dot(g_heads, weights.block(tile, 0, 3 * LANES), 1, 1))
+        parts.append(dot(g_heads, weights.block((turn, tile), 0, 3 * LANES), 1, 1))
     g_normed = add_up(parts)
     g_norms_ref[...] = g_norms_in_ref[...]
     g_norms_ref[4:5] = jnp.sum(g_normed * unit, 0, keepdims=True)
@@ -691,7 +730,7 @@
     mid = mid_ref[...]
     normed = feats.norm(mid, norms_ref[2:3], norms_ref[3:4])
     for turn, tile in turns:
-        hidden = dot(normed, layer.up(tile))
+        hidden = dot(normed, layer.up((turn, tile)))
         share = normal_share(hidden)
         act_ref[turn] = (hidden * share).astype(brain)
         slope_ref[turn] = gelu_slope(hidden, share)
@@ -752,13 +791,13 @@
 
 
 def bottom_kernel(
-    feats, cube, me_ref, *refs
+    feats, cube, orders, me_ref, *refs
 ):
-    heads_refs = refs[:8]
+    heads_refs = refs[:6]
     (
-        g_mid_ref, ids_ref, w_ref, norms_ref, vocab_ref, g_vocab_in_ref, g_norms_in_ref, cos_ref,
+        g_mid_ref, ids_ref, w_own_ref, w_other_ref, norms_ref, vocab_ref, g_vocab_in_ref, g_norms_in_ref, cos_ref,
         sin_ref, keep_ref, send_ref, norms_out_ref,
-    ) = refs[8:]
+    ) = refs[6:]
     tiles = cube.tensors
     own = g_mid_ref.shape[0]
     mine = me_ref[0] & (tiles - 1)
@@ -766,7 +805,8 @@
     hot = hot.astype(single).astype(brain)
     cosine = cos_ref[...]
     sine = sin_ref[...]
-    weights = Gathered(w_ref)
+    weights = Relative(cube, me_ref[0], (w_own_ref, w_other_ref), orders)
+    first = w_own_ref.shape[-1] - 3 * LANES
     refs = (keep_ref, send_ref)
     rows = [0, 0]
     parts = []
@@ -774,7 +814,7 @@
         tile = turn ^ mine
         g_table = dot(hot, head_grads(turn, heads_refs, cosine, sine))
         rows[turn & 1] = stacked_lanes(refs[turn & 1], rows[turn & 1], g_table)
-        weight = weights.block(tile, 0, 3 * LANES)
+        weight = weights.block((turn, tile), first, first + 3 * LANES)
         high, middle_part, low = split_three(g_table)
         parts.append(dot(high, weight, 1, 1))
         parts.append(dot(middle_part, weight, 1, 1))
@@ -792,8 +832,13 @@
         stacked_lanes(ref, row, g_norms)
 
 
+def last_part(weights):
+    parts = weights.shape[0]
+    return pl.BlockSpec((1,) + weights.shape[1:], lambda at: (parts - 1, 0, 0, 0))
+
+
 def bottom(
-    feats, cube, me, head_parts, g_mid, ids, w_in, at_block, norms, vocab, g_vocab,
+    feats, cube, orders, me, head_parts, g_mid, ids, w_own, w_other, norms, vocab, g_vocab,
     g_norms, cosine, sine, after,
 ):
     tiles = cube.tensors
@@ -805,12 +850,13 @@
     in_specs = [
         scalar_spec(),
         *[whole_spec(x.shape) for x in before],
-        columns_spec(w_in, 3 * LANES, at_block),
+        last_part(w_own),
+        last_part(w_other),
         *[whole_spec(x.shape) for x in rest],
     ]
     outs = [out, out, jax.ShapeDtypeStruct(norms.shape, single)]
-    ins = (me, *before, w_in, *rest)
-    kernel = functools.partial(bottom_kernel, feats, cube)
+    ins = (me, *before, w_own, w_other, *rest)
+    kernel = functools.partial(bottom_kernel, feats, cube, orders[-1:])
     return call(kernel, "bottom", ins, in_specs, outs, (), after)[:2]
 
 
@@ -834,7 +880,7 @@
     count, size, rows, wide = keep.shape
     together = not isinstance(got, list)
     got = [got] if together else got
-    step = 16 if size >= 8 else rows
+    step = rows // 2 if size >= 8 else rows
     half = max(size // 2, 1)
 
     def spec(*lead):
@@ -865,6 +911,70 @@
     )(*ins, *through, *after)
     going = results[1] if stacked and sends else results[1 : 1 + sends]
     return results[0], going, results[1 + sends :]
+
+
+def join_kernel(count, together, stacked, skip, *refs):
+    ins = 1 if together else count
+    helds, gots = refs[:ins], refs[ins : 2 * ins]
+    outs = refs[2 * ins + skip :]
+    for part in range(count):
+        held = helds[0].at[part] if together else helds[part]
+        got = gots[0].at[part] if together else gots[part]
+        out = outs[0].at[part] if stacked else outs[part]
+        size = held.shape[0]
+        out[:size] = held[...]
+        out[size:] = got[...]
+
+
+def join(held, got, count, stacked, through=(), after=()):
+    together = not isinstance(held, list)
+    ins = (held, got) if together else (*held, *got)
+    size, rows, wide = ins[0].shape[-3:]
+    shape = (2 * size, rows, wide)
+    if stacked:
+        outs = [jax.ShapeDtypeStruct((count,) + shape, ins[0].dtype)]
+    else:
+        outs = [jax.ShapeDtypeStruct(shape, ins[0].dtype)] * count
+    aliases = {len(ins) + at: len(outs) + at for at in range(len(through))}
+    skip = len(through) + len(after)
+    results = pl.pallas_call(
+        functools.partial(join_kernel, count, together, stacked, skip),
+        grid=(1,),
+        in_specs=[
+            *[whole_spec(x.shape) for x in ins], *after_specs(through), *after_specs(after)
+        ],
+        out_specs=[*[whole_spec(out.shape) for out in outs], *after_specs(through)],
+        out_shape=[*outs, *[jax.ShapeDtypeStruct(x.shape, x.dtype) for x in through]],
+        input_output_aliases=aliases,
+        compiler_params=params(),
+        name="join",
+    )(*ins, *through, *after)
+    joined = results[0] if stacked else list(results[:count])
+    return joined, results[len(outs) :]
+
+
+class Gather:
+    def __init__(self, cube, parts):
+        count = len(parts)
+        self.cube = cube
+        self.count = count
+        turning = [cube.outer(turn)[:-1] for turn in range(count)]
+        self.orders = [[cube.size - 1] + turns for turns in turning]
+        self.held = jnp.stack(parts)[:, None]
+        self.got = cube.swap(self.held, cube.size - 1)
+        self.at = 1
+
+    def step(self, through=(), after=()):
+        last = self.at == len(self.orders[0])
+        self.held, through = join(self.held, self.got, self.count, last, through, after)
+        if last:
+            self.got = self.cube.swap(self.held, 0)
+        else:
+            self.got = [
+                self.cube.swap(x, order[self.at]) for x, order in zip(self.held, self.orders)
+            ]
+        self.at += 1
+        return through
 
 
 def normalize_features(resid, gain, shift):
@@ -945,7 +1055,6 @@
             2,
         )
         feed_columns = feed.shape[2]
-        all_columns = 3 * LANES + feed_columns
 
         def pad_rows(x):
             return jnp.pad(x, ((0, feats.padded - block), (0, 0)))
@@ -953,6 +1062,16 @@
         vocab_low = vocab_table.astype(brain)
         vocab_padded = jnp.pad(feats.pad(vocab_low), ((0, 64 - vocab_count), (0, 0)))
         norms = jnp.pad(feats.pad(norm_params), ((0, 16 - norm_params.shape[0]), (0, 0)))
+
+        def gather_all(x):
+            x = lax.all_gather(x, axes, axis=0, tiled=False)
+            return x.reshape((groups, tensors) + x.shape[1:])
+
+        weights = gather_all(pad_rows(jnp.concatenate([feed[:, 0], heads_in[:, 1]], 1)))
+        at_heads = feed_columns // (3 * LANES)
+        later = pad_rows(jnp.concatenate([feed[:, 1], heads_in[:, 0]], 1))
+        third = later.shape[1] // 3
+        gather = Gather(cube, [later[:, at : at + third] for at in range(0, 3 * third, third)])
 
         table_low = normalize_features(
             lax.reduce_precision(vocab_table, 8, 7), norm_params[0], norm_params[1]
@@ -981,13 +1100,6 @@
         ids = jnp.take(table[:, ids_row : ids_row + 2, :local_len], sequence, axis=1)
         ids = jnp.take(ids, quarters, axis=0).reshape(1, length).astype(jnp.int32)
 
-        packed = [feed[:, 0], heads_in[:, 0], heads_in[:, 1], feed[:, 1]]
-        packed = pad_rows(jnp.concatenate(packed, 1))
-        weights = lax.all_gather(packed, axes, axis=0, tiled=False)
-        weights = weights.reshape((groups, tensors) + packed.shape)
-        at_low = feed_columns // (3 * LANES)
-        at_heads = at_low + 1
-
         half = HEAD // 2
         freqs = 10000.0 ** (-jnp.arange(half, dtype=single) * 2.0 / HEAD)
         positions = (quarters[:, None] * local_len + jnp.arange(local_len)[None, :]).reshape(length)
@@ -1005,15 +1117,22 @@
         slot = jnp.where(
             quarter == here, inside, jnp.where(quarter == (here ^ 2), inside + local_len, -1)
         )
-        slot = jnp.where(jnp.arange(slots) < my_count, slot, -1).reshape(slots, 1)
-        target = jnp.take(mask_target, sequence, axis=0).reshape(slots, 1)
-        count = jnp.broadcast_to(count_total, (8, LANES))
-
-        q_low, kv_low, kv_low_other, resid_low = embed(table, ids, vocab_padded, cosine, sine)
+        slot = jnp.where(jnp.arange(slots) < my_count, slot, -1)
+        target = jnp.take(mask_target, sequence, axis=0)
+        marks = jnp.zeros((8, slots), jnp.int32).at[0].set(slot).at[1].set(target)
+        marks = marks.astype(single)
+
+        gather.step((), (table,))
+        q_low, kv_low, kv_low_other, resid_low = embed(table, ids, vocab_padded, cosine, sine, ())
+        while gather.at + 2 < cube.size:
+            gather.step((), (q_low,))
         mixed_low, logsum_low = attend(q_low, kv_low, kv_low_other, heads)
+        gather.step((), (logsum_low,))
         mid_low, resid, q, kv = middle(
-            feats, mixed_low, resid_low, weights, feed_columns, at_heads, norms, cos_own, sin_own
+            feats, mixed_low, resid_low, weights, feed_columns, at_heads, norms, cos_own, sin_own,
+            (),
         )
+        (kv,) = gather.step((kv,), (resid,))
         kv_other = cube.swap(kv, 0)
         mixed, logsum = attend(q, kv, kv_other, heads)
         grad_orders = [cube.outer(turn) for turn in range(3)]
@@ -1038,8 +1157,9 @@
                 self.at += 1
                 return through
 
-            def finish(self, after=()):
-                return halve(self.keep, self.got, (), after)[0][:, 0]
+            def finish(self, through=(), after=()):
+                keep, _, through = halve(self.keep, self.got, through, after)
+                return keep[:, 0], through
 
         def exchange(arrays):
             return [cube.swap(x, 0) for x in arrays]
@@ -1047,14 +1167,14 @@
         first_turns = list(range(tensors // 2))
         last_turns = list(range(tensors // 2, tensors))
         keep, send, g_mid, g_mixed, g_norms, g_vocab = top(
-            feats, cube, grad_orders, me, mixed, resid, weights, all_columns, 1, norms,
-            vocab_padded, vocab_count, slot, target, count,
+            feats, cube, gather.orders, grad_orders, me, mixed, resid, gather.held, gather.got,
+            norms, vocab_padded, vocab_count, marks, table,
         )
         sums_top = Sums(keep, send)
         part = (q, kv, kv_other, g_mixed, logsum, heads, me)
         first = attend_back(*part, first_turns, tensors)
         got_first = exchange(sums_top.step(first[2:], (first[0],)))
-        last = attend_back(*part, last_turns, tensors, (sums_top.keep, *got_first))
+        last = attend_back(*part, last_turns, tensors, (sums_top.keep,))
         got_last = exchange(sums_top.step(last[2:], (last[0],)))
         head_parts = (*first[:2], *got_first, *last[:2], *got_last)
         keep, send, g_mid, g_mixed, g_norms = lower(
@@ -1067,28 +1187,32 @@
         first = attend_back(*part, first_turns, tensors, (sums_top.keep,))
         got_first = exchange(sums_top.step(first[2:], (first[0],)))
         sums_low.step((), (sums_top.keep,))
-        last = attend_back(*part, last_turns, tensors, (sums_low.keep, *got_first))
+        last = attend_back(*part, last_turns, tensors, (sums_low.keep,))
         got_last = exchange(sums_low.step(last[2:], (last[0],)))
         head_parts = (*first[:2], *got_first, *last[:2], *got_last)
         keep_table, send_table = bottom(
-            feats, cube, me, head_parts, g_mid, ids[:, :own], weights, at_low, norms,
-            vocab_padded, g_vocab, g_norms, cos_own, sin_own, (sums_low.keep,),
+            feats, cube, gather.orders, me, head_parts, g_mid, ids[:, :own], gather.held,
+            gather.got, norms, vocab_padded, g_vocab, g_norms, cos_own, sin_own, (sums_low.keep,),
         )
-        sums_low.step((), (keep_table,))
-        while sums_low.at <= last_step:
-            sums_low.step()
-        while sums_top.at <= last_step:
-            sums_top.step((), (keep_table,))
-        grads_top = jnp.concatenate(list(sums_top.finish((keep_table,))), 1)
-        grads_low = jnp.concatenate(list(sums_low.finish()), 1)
-        total = keep_table + cube.swap(send_table, 0)
+        got = cube.swap(send_table, 0)
+        (keep_table,) = sums_low.step((keep_table,))
+        total = keep_table + got
         tile_rows = 3 * TABLE_ROWS
         got = cube.swap(total[tile_rows:], 1)
+        (total,) = sums_low.step((total,))
         total = jnp.concatenate(
             [total[:tile_rows] + got[:tile_rows], total[2 * tile_rows :] + got[tile_rows:]], 0
         )
         for at in range(2, cube.size):
             total = total + cube.swap(total, at)
+        while sums_low.at <= last_step:
+            sums_low.step()
+        while sums_top.at <= last_step:
+            sums_top.step((), (keep_table,))
+        grads_low, _ = sums_low.finish()
+        grads_top, _ = sums_top.finish((), (sums_low.keep,))
+        grads_top = jnp.concatenate(list(grads_top), 1)
+        grads_low = jnp.concatenate(list(grads_low), 1)
         g_table = side_by_side(total[:tile_rows], TABLE_ROWS)[:vocab_count]
         vocab_rows = TABLE_ROWS * feats.total // LANES
         g_vocab = side_by_side(total[tile_rows : tile_rows + vocab_rows], TABLE_ROWS)
@@ -1108,25 +1232,37 @@
             grad = grad[:block].reshape(block, 3, LANES)[:, :, :per_heads]
             return grad.reshape(block, 3, heads, HEAD).transpose(0, 2, 1, 3).reshape(block, in_wide)
 
-        grad_in = jnp.stack([unpack_in(grads_in_low), unpack_in(grads_low[:, : 3 * LANES])], 1)
-        both = jnp.stack([grads_low[:block, 3 * LANES :], grads_top[:block]], 1)
-        grad_in = grad_in.transpose(1, 0, 2)
-        grad_out = both[:, :, :per_heads].transpose(1, 2, 0)
-        grad_up = both[:, :, LANES : LANES + hidden].transpose(1, 0, 2)
+        low_start = 3 * LANES
         start = LANES + hidden_padded
-        grad_down = both[:, :, start : start + hidden].transpose(1, 2, 0)
+        grad_in = jnp.stack([unpack_in(grads_in_low), unpack_in(grads_low[:, :low_start])], 1)
+        both = jnp.stack([grads_low[:block, low_start:], grads_top[:block]], 1)
+        grads = (
+            grad_in,
+            both[:, :, :per_heads],
+            both[:, :, LANES : LANES + hidden],
+            both[:, :, start : start + hidden],
+            g_norms,
+            g_vocab,
+        )
+        by_rows = Layout(major_to_minor=(0, 1, 2))
+        grads = [with_layout_constraint(x, by_rows) for x in grads[:4]] + list(grads[4:])
+        turned = [(1, 0, 2), (2, 0, 1), (1, 0, 2), (2, 0, 1), None, None]
+        turned_back = [(1, 0, 2), (1, 2, 0), (1, 0, 2), (1, 2, 0), None, None]
+
+        def turn_all(arrays, orders):
+            return [x if order is None else x.transpose(order) for x, order in zip(arrays, orders)]
 
         masters = (weight_in, weight_out, weight_up, weight_down, norm_params, vocab_table)
         firsts = (first_in, first_out, first_up, first_down, first_norm, first_vocab)
         seconds = (second_in, second_out, second_up, second_down, second_norm, second_vocab)
-        grads = (grad_in, grad_out, grad_up, grad_down, g_norms, g_vocab)
+        masters, firsts, seconds = [turn_all(x, turned) for x in (masters, firsts, seconds)]
         results = [
             adamw(masters[which], firsts[which], seconds[which], grads[which], step_rates[which])
             for which in range(6)
         ]
-        news = [entry[0] for entry in results]
-        means = [entry[1] for entry in results]
-        squares = [entry[2] for entry in results]
+        news, means, squares = [
+            turn_all([entry[which] for entry in results], turned_back) for which in range(3)
+        ]
         copies = [news[which].astype(brain) for which in (0, 1, 2, 3, 5)]
         return (loss_total, count_total, *news, *means, *squares, *copies)
 

time: 406 us -> 386 us (0.951)
  waiting for transfers between devices: 70.8 us -> 39.9 us
  starting transfers between devices: 40.6 us -> 54.4 us
  local copies, waits for them, and re-layouts: 40.2 us -> 26.5 us
  other arithmetic: 12 us -> 20 us
    all_gather x1, waiting for transfers between devices: 43.7 us -> 1.96 us  [gather_all(): x = lax.all_gather(x, axes, axis=0, tiled=False)]
    ppermute x41 -> x48, starting transfers between devices: 40.5 us -> 54.3 us  [swap(): return lax.ppermute(x, ('dp', 'tensor'), pairs)]
    unnamed x131 -> x123, local copies, waits for them, and re-layouts: 25.9 us -> 14.5 us
    ppermute x41 -> x48, waiting for transfers between devices: 27 us -> 37.9 us  [swap(): return lax.ppermute(x, ('dp', 'tensor'), pairs)]
    pallas_call x2 -> x6, Pallas kernels: 40.7 us -> 46 us  [the longest x2 35.7 us: attend(): pl.pallas_call(follow(functools.partial(attend_kernel, heads), 3, after),...]
  transfers between devices with their start and end apart: 42 -> 49, of which waited for: 18 -> 17; matrix products, arithmetic and copies ran while one was open for 7% -> 6% of each run, Pallas kernels for 34% -> 47%
where the time goes in v3:
time: 386 us; the launch traced here: 379 us
  Pallas kernels  221 us (57%)
  starting transfers between devices  54.4 us (14%)
  waiting for transfers between devices  39.9 us (10%)
  local copies, waits for them, and re-layouts  26.5 us (7%)
  other arithmetic  20 us (5%)
  between operations  16.8 us (4%)
    pallas_call x5, Pallas kernels, call(): pl.pallas_call(kernel, grid=(1,), in_specs=in_specs, out_specs=[whole_spe...  70.6 us
    pallas_call x4, Pallas kernels, attend_back(): pl.pallas_call(functools.partial(attend_back_kernel, heads, own, len(afte...  69.2 us
    ppermute x48, starting transfers between devices, swap(): return lax.ppermute(x, ('dp', 'tensor'), pairs)  54.3 us
    ppermute x48, waiting for transfers between devices, swap(): return lax.ppermute(x, ('dp', 'tensor'), pairs)  37.9 us
    pallas_call x2, Pallas kernels, attend(): pl.pallas_call(follow(functools.partial(attend_kernel, heads), 3, after),...  35.7 us
    pallas_call x10, Pallas kernels, halve(): pl.pallas_call(functools.partial(halve_kernel, count, together, stacked,...  35.7 us
    unnamed x123, local copies, waits for them, and re-layouts  14.5 us
    pallas_call x4, Pallas kernels, join(): pl.pallas_call(functools.partial(join_kernel, count, together, stacked, s...  10.3 us
  transfers between devices with their start and end apart: 49, of which 17 were waited for; matrix products, arithmetic and copies ran while one was open for 6% of the time, Pallas kernels for 47%

profile of v3, /device:TPU:0, one launch (start us, length us, event | category | flops | bytes accessed | tf_op | source)
XLA Modules:
  0.0 379.4 jit_solution(1968478241802251516)
XLA Ops:
  14.6 3.0 collective-permute-start
  17.8 3.7 collective-permute-start.5
  22.3 6.4 %collective-permute-done.1 = f32[40,384]{1,0:T(8,128)S(1)} collective-permute-done((f32[40,384]{1,0:T(8,128)S(1)}, f32[40,384]{1,0:T(8,128)S(1)}, u32[]{:S(2)}, u32[]{:S(2)}) %collective-permute-start.1) | collective-permute-done | bytes 61472 | tf_op jit(solution)/shard_map/ppermute | solution.py:48
  28.7 3.7 collective-permute-start.2
  32.4 3.1 collective-permute-done.2
  37.6 2.7 collective-permute-done.3
  45.1 1.8 join.4
  52.0 6.2 %embed.1 = (bf16[512,512]{1,0:T(8,128)(2,1)}, bf16[2,512,512]{2,1,0:T(8,128)(2,1)}, bf16[2,512,512]{2,1,0:T(8,128)(2,1)}, f32[512,512]{1,0:T(8,128)}) custom-call(f32[4,40,384]{2,1,0:T(8,128)} %bitcast.247, s32[1,1024]{1,0:T(1,128)} %bitcast.269, bf16[64,512]{1,0:T(8,128)(2,1)} %pad.63.vocab_ref.refs_12_, f32[1024,128]{1,0:T(8,128)} %pad.64.cos_ref, ...), custom_call_target="tpu_custom_call" | custom-call | tf_op jit(solution)/shard_map/embed/pallas_call | solution.py:331
  58.9 2.1 join.5
  63.2 17.8 %attend.2 = (bf16[512,512]{1,0:T(8,128)(2,1)}, f32[4,8,512]{2,1,0:T(8,128)}) custom-call(bf16[512,512]{1,0:T(8,128)(2,1)} %get-tuple-element.145.q_ref.refs_6_, bf16[2,512,512]{2,1,0:T(8,128)(2,1)} %get-tuple-element.146.own_ref.kv_own_ref, bf16[2,512,512]{2,1,0:T(8,128)(2,1)} %get-tuple-element.147.other_ref.kv_other_ref), custom_call_target="tpu_custom_call" | custom-call | tf_op jit(solution)/shard_map/attend/pallas_call | solution.py:413
  81.9 2.7 join.6
  90.8 2.0 all-gather.3.cloned.1.call-done
  92.8 12.5 %middle.1 = (f32[512,512]{1,0:T(8,128)}, f32[512,512]{1,0:T(8,128)}, bf16[512,512]{1,0:T(8,128)(2,1)}, bf16[2,512,512]{2,1,0:T(8,128)(2,1)}) custom-call(bf16[512,512]{1,0:T(8,128)(2,1)} %get-tuple-element.148.mixed_ref.refs_10_, f32[512,512]{1,0:T(8,128)} %get-tuple-element.149.resid_ref, bf16[8,4,64,1536]{3,2,1,0:T(8,128)(2,1)} %bitcast.241, ...), custom_call_target="tpu_custom_call" | custom-call | tf_op jit(solution)/shard_map/middle/pallas_call | solution.py:331
  106.5 3.7 join.7
  112.7 4.6 %collective-permute-done.15.other_ref.kv_other_ref = bf16[2,512,512]{2,1,0:T(8,128)(2,1)} collective-permute-done((bf16[2,512,512]{2,1,0:T(8,128)(2,1)}, bf16[2,512,512]{2,1,0:T(8,128)(2,1)}, u32[]{:S(2)}, u32[]{:S(2)}) %collective-permute-start.15) | collective-permute-done | bytes 1048608 | tf_op jit(solution)/shard_map/ppermute | solution.py:48
  117.3 18.0 %attend.3 = (bf16[512,512]{1,0:T(8,128)(2,1)}, f32[4,8,512]{2,1,0:T(8,128)}) custom-call(bf16[512,512]{1,0:T(8,128)(2,1)} %get-tuple-element.150.q_ref, bf16[2,512,512]{2,1,0:T(8,128)(2,1)} %get-tuple-element.163.own_ref.kv_own_ref, bf16[2,512,512]{2,1,0:T(8,128)(2,1)} %collective-permute-done.15.other_ref.kv_other_ref), custom_call_target="tpu_custom_call" | custom-call | tf_op jit(solution)/shard_map/attend/pallas_call | solution.py:413
  135.3 1.6 copy-done
  136.9 22.0 %top.1 = (f32[3,16,64,384]{3,2,1,0:T(8,128)}, f32[3,16,64,384]{3,2,1,0:T(8,128)}, f32[512,512]{1,0:T(8,128)}, bf16[512,512]{1,0:T(8,128)(2,1)}, f32[16,512]{1,0:T(8,128)}, /*index=5*/f32[40,512]{1,0:T(8,128)}) custom-call(s32[1]{0:T(128)} %bitcast.me_ref.refs_0_, bf16[512,512]{1,0:T(8,128)(2,1)} %get-tuple-element.164.mixed_ref, ...), custom_call_target="tpu_custom_call" | custom-call | tf_op jit(solution)/shard_map/top/pallas_call | solution.py:331
  159.2 17.2 %attend_back.4 = (f32[512,256]{1,0:T(8,128)}, f32[2,512,256]{2,1,0:T(8,128)}, f32[2,512,256]{2,1,0:T(8,128)}) custom-call(s32[1]{0:T(128)} %bitcast.me_ref.refs_0_, bf16[512,512]{1,0:T(8,128)(2,1)} %get-tuple-element.150.q_ref, bf16[2,512,512]{2,1,0:T(8,128)(2,1)} %get-tuple-element.163.own_ref.kv_own_ref, ...), custom_call_target="tpu_custom_call" | custom-call | tf_op jit(solution)/shard_map/attend_back/pallas_call | solution.py:484
  176.5 5.9 %halve.10 = (f32[3,8,64,384]{3,2,1,0:T(8,128)}, f32[8,64,384]{2,1,0:T(8,128)}, f32[8,64,384]{2,1,0:T(8,128)}, f32[8,64,384]{2,1,0:T(8,128)}, f32[2,512,256]{2,1,0:T(8,128)}) custom-call(f32[3,16,64,384]{3,2,1,0:T(8,128)} %get-tuple-element.170.keep_ref, f32[3,16,64,384]{3,2,1,0:T(8,128)} %collective-permute-done.17.refs_0_, ...), custom_call_target="tpu_custom_call", output_to_operand_aliasing={{4}: (2, {})} | custom-call | tf_op jit(solution)/shard_map/halve/pallas_call | solution.py:902
  184.6 3.7 collective-permute-start.21
  188.2 17.3 %attend_back.5 = (f32[512,256]{1,0:T(8,128)}, f32[2,512,256]{2,1,0:T(8,128)}, f32[2,512,256]{2,1,0:T(8,128)}) custom-call(s32[1]{0:T(128)} %bitcast.me_ref.refs_0_, bf16[512,512]{1,0:T(8,128)(2,1)} %get-tuple-element.150.q_ref, bf16[2,512,512]{2,1,0:T(8,128)(2,1)} %get-tuple-element.163.own_ref.kv_own_ref, ...), custom_call_target="tpu_custom_call" | custom-call | tf_op jit(solution)/shard_map/attend_back/pallas_call | solution.py:484
  206.9 3.8 %halve.11 = (f32[3,4,64,384]{3,2,1,0:T(8,128)}, f32[4,64,384]{2,1,0:T(8,128)}, f32[4,64,384]{2,1,0:T(8,128)}, f32[4,64,384]{2,1,0:T(8,128)}, f32[2,512,256]{2,1,0:T(8,128)}) custom-call(f32[3,8,64,384]{3,2,1,0:T(8,128)} %get-tuple-element.174.refs_0_.keep_ref, f32[8,64,384]{2,1,0:T(8,128)} %copy-done.16, ...), custom_call_target="tpu_custom_call", output_to_operand_aliasing={{4}: (4, {})} | custom-call | tf_op jit(solution)/shard_map/halve/pallas_call | solution.py:902
  211.3 1.7 collective-permute-start.24
  214.9 22.7 %lower.1 = (f32[3,16,64,512]{3,2,1,0:T(8,128)}, f32[3,16,64,512]{3,2,1,0:T(8,128)}, f32[512,512]{1,0:T(8,128)}, bf16[512,512]{1,0:T(8,128)(2,1)}, f32[16,512]{1,0:T(8,128)}) custom-call(s32[1]{0:T(128)} %bitcast.me_ref.refs_0_, f32[512,256]{1,0:T(8,128)} %get-tuple-element.168.refs_2_.refs_1_, f32[2,512,256]{2,1,0:T(8,128)} %get-tuple-element.169.refs_2_, ...), custom_call_target="tpu_custom_call" | custom-call | tf_op jit(solution)/shard_map/lower/pallas_call | solution.py:331
  238.6 2.6 halve.12
  243.1 1.9 collective-permute-start.29
  245.0 17.2 %attend_back.6 = (f32[512,256]{1,0:T(8,128)}, f32[2,512,256]{2,1,0:T(8,128)}, f32[2,512,256]{2,1,0:T(8,128)}) custom-call(s32[1]{0:T(128)} %bitcast.me_ref.refs_0_, bf16[512,512]{1,0:T(8,128)(2,1)} %get-tuple-element.145.q_ref.refs_6_, bf16[2,512,512]{2,1,0:T(8,128)(2,1)} %get-tuple-element.146.own_ref.kv_own_ref, ...), custom_call_target="tpu_custom_call" | custom-call | tf_op jit(solution)/shard_map/attend_back/pallas_call | solution.py:484
  263.1 2.1 halve.13
  265.2 7.9 %halve.14 = (f32[3,8,64,512]{3,2,1,0:T(8,128)}, f32[8,64,512]{2,1,0:T(8,128)}, f32[8,64,512]{2,1,0:T(8,128)}, f32[8,64,512]{2,1,0:T(8,128)}) custom-call(f32[3,16,64,512]{3,2,1,0:T(8,128)} %get-tuple-element.186.keep_ref, f32[3,16,64,512]{3,2,1,0:T(8,128)} %collective-permute-done.26.refs_0_, f32[3,1,64,384]{3,2,1,0:T(8,128)} %get-tuple-element.200.refs_1_.keep_ref), custom_call_target="tpu_custom_call" | custom-call | tf_op jit(solution)/shard_map/halve/pallas_call | solution.py:902
  275.6 17.5 %attend_back.7 = (f32[512,256]{1,0:T(8,128)}, f32[2,512,256]{2,1,0:T(8,128)}, f32[2,512,256]{2,1,0:T(8,128)}) custom-call(s32[1]{0:T(128)} %bitcast.me_ref.refs_0_, bf16[512,512]{1,0:T(8,128)(2,1)} %get-tuple-element.145.q_ref.refs_6_, bf16[2,512,512]{2,1,0:T(8,128)(2,1)} %get-tuple-element.146.own_ref.kv_own_ref, ...), custom_call_target="tpu_custom_call" | custom-call | tf_op jit(solution)/shard_map/attend_back/pallas_call | solution.py:484
  293.1 4.9 %collective-permute-done.30.refs_0_ = f32[8,64,512]{2,1,0:T(8,128)S(1)} collective-permute-done((f32[8,64,512]{2,1,0:T(8,128)}, f32[8,64,512]{2,1,0:T(8,128)S(1)}, u32[]{:S(2)}, u32[]{:S(2)}) %collective-permute-start.30) | collective-permute-done | bytes 1048608 | tf_op jit(solution)/shard_map/ppermute | solution.py:48
  299.4 4.3 %halve.15 = (f32[3,4,64,512]{3,2,1,0:T(8,128)}, f32[4,64,512]{2,1,0:T(8,128)}, f32[4,64,512]{2,1,0:T(8,128)}, f32[4,64,512]{2,1,0:T(8,128)}, f32[2,512,256]{2,1,0:T(8,128)}) custom-call(f32[3,8,64,512]{3,2,1,0:T(8,128)} %get-tuple-element.201.refs_0_.keep_ref, f32[8,64,512]{2,1,0:T(8,128)} %copy-done.8, ...), custom_call_target="tpu_custom_call", output_to_operand_aliasing={{4}: (4, {})} | custom-call | tf_op jit(solution)/shard_map/halve/pallas_call | solution.py:902
  305.6 1.7 collective-permute-start.35
  307.3 2.4 collective-permute-start.47
  311.3 7.2 %bottom.1 = (f32[464,128]{1,0:T(8,128)}, f32[464,128]{1,0:T(8,128)}, f32[16,512]{1,0:T(8,128)}) custom-call(s32[1]{0:T(128)} %bitcast.me_ref.refs_0_, f32[512,256]{1,0:T(8,128)} %get-tuple-element.199.refs_4_.refs_1_, f32[2,512,256]{2,1,0:T(8,128)} %get-tuple-element.211.refs_2_, f32[2,512,256]{2,1,0:T(8,128)} %copy-done.4, ...), custom_call_target="tpu_custom_call" | custom-call | tf_op jit(solution)/shard_map/bottom/pallas_call | solution.py:331
  320.3 3.0 halve.16
  324.6 1.7 collective-permute-start.39
  327.4 1.7 collective-permute-done.41
  333.6 2.3 halve.17
  335.9 2.5 collective-permute-start.46
  339.1 1.8 halve.19
  344.6 4.6 %collective-permute-done.43 = f32[344,128]{1,0:T(8,128)S(1)} collective-permute-done((f32[344,128]{1,0:T(8,128)S(1)}, f32[344,128]{1,0:T(8,128)S(1)}, u32[]{:S(2)}, u32[]{:S(2)}) %collective-permute-start.43) | collective-permute-done | bytes 176160 | tf_op jit(solution)/shard_map/ppermute | solution.py:48
  350.4 1.9 halve.18
  354.1 2.5 fusion.53
  359.7 1.5 collective-permute-start.45
  361.9 5.2 %collective-permute-done.45 = f32[344,128]{1,0:T(8,128)S(1)} collective-permute-done((f32[344,128]{1,0:T(8,128)S(1)}, f32[344,128]{1,0:T(8,128)S(1)}, u32[]{:S(2)}, u32[]{:S(2)}) %collective-permute-start.45) | collective-permute-done | bytes 176160 | tf_op jit(solution)/shard_map/ppermute | solution.py:48
  370.8 1.5 fusion.59
  (314 shorter events, 72.9 us)
Async XLA Ops:
  7.2 85.5 %all-gather.3.cloned.1.call-start = ((), (), s32[]{:S(2)}) async-start(), calls=%async_computation | async-start | bytes 6488064 | tf_op jit(solution)/shard_map/all_gather | solution.py:1067
  14.6 7.1 %collective-permute-start = (f32[40,384]{1,0:T(8,128)S(1)}, f32[40,384]{1,0:T(8,128)S(1)}, u32[]{:S(2)}, u32[]{:S(2)}) collective-permute-start(f32[40,384]{1,0:T(8,128)S(1)} %select_maximum_fusion), channel_id=1, source_target_pairs={{0,4},{1,5},{2,6},{3,7},{4,0},{5,1},{6,2},{7,3},{8,12},{9,13},{10,... | collective-permute-start | bytes 184328 | tf_op jit(solution)/shard_map/ppermute | solution.py:48
  17.8 25.9 %collective-permute-start.5 = (bf16[3,1,64,512]{3,2,1,0:T(8,128)(2,1)S(1)}, bf16[3,1,64,512]{3,2,1,0:T(8,128)(2,1)S(1)}, u32[]{:S(2)}, u32[]{:S(2)}) collective-permute-start(bf16[3,1,64,512]{3,2,1,0:T(8,128)(2,1)S(1)} %maximum_bitcast_fusion.refs_0_), channel_id=1, source_target_pairs={{0,24},{1,25},{2,26},{3,27},{4,28},{5,29},{6,30},{7,31},{8,16},{9,... | collective-permute-start | bytes 589832 | tf_op jit(solution)/shard_map/ppermute | solution.py:48
  21.7 7.0 %collective-permute-start.1 = (f32[40,384]{1,0:T(8,128)S(1)}, f32[40,384]{1,0:T(8,128)S(1)}, u32[]{:S(2)}, u32[]{:S(2)}) collective-permute-start(f32[40,384]{1,0:T(8,128)S(1)} %fusion.67), channel_id=1, source_target_pairs={{0,8},{1,9},{2,10},{3,11},{4,12},{5,13},{6,14},{7,15},{8,0},{9,1},... | collective-permute-start | bytes 184328 | tf_op jit(solution)/shard_map/ppermute | solution.py:48
  28.7 6.8 %collective-permute-start.2 = (f32[40,384]{1,0:T(8,128)S(1)}, f32[40,384]{1,0:T(8,128)S(1)}, u32[]{:S(2)}, u32[]{:S(2)}) collective-permute-start(f32[40,384]{1,0:T(8,128)S(1)} %add.237), channel_id=1, source_target_pairs={{0,24},{1,25},{2,26},{3,27},{4,28},{5,29},{6,30},{7,31},{8,16},{9,... | collective-permute-start | bytes 184328 | tf_op jit(solution)/shard_map/ppermute | solution.py:48
  36.1 4.2 %collective-permute-start.3 = (f32[40,384]{1,0:T(8,128)S(1)}, f32[40,384]{1,0:T(8,128)S(1)}, u32[]{:S(2)}, u32[]{:S(2)}) collective-permute-start(f32[40,384]{1,0:T(8,128)S(1)} %pad_dynamic-update-slice_fusion), channel_id=1, source_target_pairs={{0,2},{1,3},{2,0},{3,1},{4,6},{5,7},{6,4},{7,5},{8,10},{9,11},{10,... | collective-permute-start | bytes 184328 | tf_op jit(solution)/shard_map/ppermute | solution.py:48
  40.3 3.3 collective-permute-start.4
  46.9 11.3 %collective-permute-start.6 = (bf16[2,64,512]{2,1,0:T(8,128)(2,1)}, bf16[2,64,512]{2,1,0:T(8,128)(2,1)S(1)}, u32[]{:S(2)}, u32[]{:S(2)}) collective-permute-start(bf16[2,64,512]{2,1,0:T(8,128)(2,1)} %get-tuple-element.151.refs_0_), channel_id=1, source_target_pairs={{0,4},{1,5},{2,6},{3,7},{4,0},{5,1},{6,2},{7,3},{8,12},{9,13},{10,... | collective-permute-start | bytes 393224 | tf_op jit(solution)/shard_map/ppermute | solution.py:48
  48.0 10.2 %collective-permute-start.7 = (bf16[2,64,512]{2,1,0:T(8,128)(2,1)}, bf16[2,64,512]{2,1,0:T(8,128)(2,1)S(1)}, u32[]{:S(2)}, u32[]{:S(2)}) collective-permute-start(bf16[2,64,512]{2,1,0:T(8,128)(2,1)} %get-tuple-element.152.refs_1_), channel_id=1, source_target_pairs={{0,2},{1,3},{2,0},{3,1},{4,6},{5,7},{6,4},{7,5},{8,10},{9,11},{10,... | collective-permute-start | bytes 393224 | tf_op jit(solution)/shard_map/ppermute | solution.py:48
  49.3 8.9 %collective-permute-start.8 = (bf16[2,64,512]{2,1,0:T(8,128)(2,1)}, bf16[2,64,512]{2,1,0:T(8,128)(2,1)S(1)}, u32[]{:S(2)}, u32[]{:S(2)}) collective-permute-start(bf16[2,64,512]{2,1,0:T(8,128)(2,1)} %get-tuple-element.153.refs_2_), channel_id=1, source_target_pairs={{0,8},{1,9},{2,10},{3,11},{4,12},{5,13},{6,14},{7,15},{8,0},{9,1},... | collective-permute-start | bytes 393224 | tf_op jit(solution)/shard_map/ppermute | solution.py:48
  61.0 20.0 %collective-permute-start.9 = (bf16[4,64,512]{2,1,0:T(8,128)(2,1)}, bf16[4,64,512]{2,1,0:T(8,128)(2,1)S(1)}, u32[]{:S(2)}, u32[]{:S(2)}) collective-permute-start(bf16[4,64,512]{2,1,0:T(8,128)(2,1)} %get-tuple-element.154.refs_0_), channel_id=1, source_target_pairs={{0,2},{1,3},{2,0},{3,1},{4,6},{5,7},{6,4},{7,5},{8,10},{9,11},{10,... | collective-permute-start | bytes 786440 | tf_op jit(solution)/shard_map/ppermute | solution.py:48
  61.7 19.3 %collective-permute-start.10 = (bf16[4,64,512]{2,1,0:T(8,128)(2,1)}, bf16[4,64,512]{2,1,0:T(8,128)(2,1)S(1)}, u32[]{:S(2)}, u32[]{:S(2)}) collective-permute-start(bf16[4,64,512]{2,1,0:T(8,128)(2,1)} %get-tuple-element.155.refs_1_), channel_id=1, source_target_pairs={{0,8},{1,9},{2,10},{3,11},{4,12},{5,13},{6,14},{7,15},{8,0},{9,1},... | collective-permute-start | bytes 786440 | tf_op jit(solution)/shard_map/ppermute | solution.py:48
  62.5 18.5 %collective-permute-start.11 = (bf16[4,64,512]{2,1,0:T(8,128)(2,1)}, bf16[4,64,512]{2,1,0:T(8,128)(2,1)S(1)}, u32[]{:S(2)}, u32[]{:S(2)}) collective-permute-start(bf16[4,64,512]{2,1,0:T(8,128)(2,1)} %get-tuple-element.156.refs_2_), channel_id=1, source_target_pairs={{0,4},{1,5},{2,6},{3,7},{4,0},{5,1},{6,2},{7,3},{8,12},{9,13},{10,... | collective-permute-start | bytes 786440 | tf_op jit(solution)/shard_map/ppermute | solution.py:48
  84.6 20.7 %collective-permute-start.12 = (bf16[8,64,512]{2,1,0:T(8,128)(2,1)}, bf16[8,64,512]{2,1,0:T(8,128)(2,1)S(1)}, u32[]{:S(2)}, u32[]{:S(2)}) collective-permute-start(bf16[8,64,512]{2,1,0:T(8,128)(2,1)} %get-tuple-element.158.refs_0_), channel_id=1, source_target_pairs={{0,8},{1,9},{2,10},{3,11},{4,12},{5,13},{6,14},{7,15},{8,0},{9,1},... | collective-permute-start | bytes 1572872 | tf_op jit(solution)/shard_map/ppermute | solution.py:48
  86.0 19.3 %collective-permute-start.13 = (bf16[8,64,512]{2,1,0:T(8,128)(2,1)}, bf16[8,64,512]{2,1,0:T(8,128)(2,1)S(1)}, u32[]{:S(2)}, u32[]{:S(2)}) collective-permute-start(bf16[8,64,512]{2,1,0:T(8,128)(2,1)} %get-tuple-element.159.refs_1_), channel_id=1, source_target_pairs={{0,4},{1,5},{2,6},{3,7},{4,0},{5,1},{6,2},{7,3},{8,12},{9,13},{10,... | collective-permute-start | bytes 1572872 | tf_op jit(solution)/shard_map/ppermute | solution.py:48
  87.3 18.1 %collective-permute-start.14 = (bf16[8,64,512]{2,1,0:T(8,128)(2,1)}, bf16[8,64,512]{2,1,0:T(8,128)(2,1)S(1)}, u32[]{:S(2)}, u32[]{:S(2)}) collective-permute-start(bf16[8,64,512]{2,1,0:T(8,128)(2,1)} %get-tuple-element.160.refs_2_), channel_id=1, source_target_pairs={{0,2},{1,3},{2,0},{3,1},{4,6},{5,7},{6,4},{7,5},{8,10},{9,11},{10,... | collective-permute-start | bytes 1572872 | tf_op jit(solution)/shard_map/ppermute | solution.py:48
  110.2 25.1 %collective-permute-start.16 = (bf16[3,16,64,512]{3,2,1,0:T(8,128)(2,1)}, bf16[3,16,64,512]{3,2,1,0:T(8,128)(2,1)S(1)}, u32[]{:S(2)}, u32[]{:S(2)}) collective-permute-start(bf16[3,16,64,512]{3,2,1,0:T(8,128)(2,1)} %get-tuple-element.165.w_own_ref.refs_9_), channel_id=1, source_target_pairs={{0,1},{1,0},{2,3},{3,2},{4,5},{5,4},{6,7},{7,6},{8,9},{9,8},{10,11... | collective-permute-start | bytes 9437192 | tf_op jit(solution)/shard_map/ppermute | solution.py:48
  110.4 6.8 %collective-permute-start.15 = (bf16[2,512,512]{2,1,0:T(8,128)(2,1)}, bf16[2,512,512]{2,1,0:T(8,128)(2,1)}, u32[]{:S(2)}, u32[]{:S(2)}) collective-permute-start(bf16[2,512,512]{2,1,0:T(8,128)(2,1)} %get-tuple-element.163.own_ref.kv_own_ref), channel_id=1, source_target_pairs={{0,1},{1,0},{2,3},{3,2},{4,5},{5,4},{6,7},{7,6},{8,9},{9,8},{10,11... | collective-permute-start | bytes 3145736 | tf_op jit(solution)/shard_map/ppermute | solution.py:48
  158.9 17.6 %collective-permute-start.17 = (f32[3,16,64,384]{3,2,1,0:T(8,128)}, f32[3,16,64,384]{3,2,1,0:T(8,128)}, u32[]{:S(2)}, u32[]{:S(2)}) collective-permute-start(f32[3,16,64,384]{3,2,1,0:T(8,128)} %get-tuple-element.171), channel_id=1, source_target_pairs={{0,1},{1,0},{2,3},{3,2},{4,5},{5,4},{6,7},{7,6},{8,9},{9,8},{10,11... | collective-permute-start | bytes 14155784 | tf_op jit(solution)/shard_map/ppermute | solution.py:48
  182.4 23.2 %collective-permute-start.19 = (f32[8,64,384]{2,1,0:T(8,128)}, f32[8,64,384]{2,1,0:T(8,128)S(1)}, u32[]{:S(2)}, u32[]{:S(2)}) collective-permute-start(f32[8,64,384]{2,1,0:T(8,128)} %get-tuple-element.177), channel_id=1, source_target_pairs={{0,4},{1,5},{2,6},{3,7},{4,0},{5,1},{6,2},{7,3},{8,12},{9,13},{10,... | collective-permute-start | bytes 2359304 | tf_op jit(solution)/shard_map/ppermute | solution.py:48
  183.3 22.2 %collective-permute-start.20 = (f32[8,64,384]{2,1,0:T(8,128)}, f32[8,64,384]{2,1,0:T(8,128)S(1)}, u32[]{:S(2)}, u32[]{:S(2)}) collective-permute-start(f32[8,64,384]{2,1,0:T(8,128)} %get-tuple-element.178), channel_id=1, source_target_pairs={{0,2},{1,3},{2,0},{3,1},{4,6},{5,7},{6,4},{7,5},{8,10},{9,11},{10,... | collective-permute-start | bytes 2359304 | tf_op jit(solution)/shard_map/ppermute | solution.py:48
  184.6 21.4 %collective-permute-start.21 = (f32[8,64,384]{2,1,0:T(8,128)}, f32[8,64,384]{2,1,0:T(8,128)S(1)}, u32[]{:S(2)}, u32[]{:S(2)}) collective-permute-start(f32[8,64,384]{2,1,0:T(8,128)} %get-tuple-element.179), channel_id=1, source_target_pairs={{0,8},{1,9},{2,10},{3,11},{4,12},{5,13},{6,14},{7,15},{8,0},{9,1},... | collective-permute-start | bytes 2359304 | tf_op jit(solution)/shard_map/ppermute | solution.py:48
  188.2 25.4 %collective-permute-start.18 = (f32[2,512,256]{2,1,0:T(8,128)}, f32[2,512,256]{2,1,0:T(8,128)S(1)}, u32[]{:S(2)}, u32[]{:S(2)}) collective-permute-start(f32[2,512,256]{2,1,0:T(8,128)} %get-tuple-element.173), channel_id=1, source_target_pairs={{0,1},{1,0},{2,3},{3,2},{4,5},{5,4},{6,7},{7,6},{8,9},{9,8},{10,11... | collective-permute-start | bytes 3145736 | tf_op jit(solution)/shard_map/ppermute | solution.py:48
  210.8 3.1 collective-permute-start.22
  211.3 26.3 %collective-permute-start.23 = (f32[4,64,384]{2,1,0:T(8,128)}, f32[4,64,384]{2,1,0:T(8,128)S(1)}, u32[]{:S(2)}, u32[]{:S(2)}) collective-permute-start(f32[4,64,384]{2,1,0:T(8,128)} %get-tuple-element.187), channel_id=1, source_target_pairs={{0,2},{1,3},{2,0},{3,1},{4,6},{5,7},{6,4},{7,5},{8,10},{9,11},{10,... | collective-permute-start | bytes 1179656 | tf_op jit(solution)/shard_map/ppermute | solution.py:48
  211.3 26.3 %collective-permute-start.24 = (f32[4,64,384]{2,1,0:T(8,128)}, f32[4,64,384]{2,1,0:T(8,128)S(1)}, u32[]{:S(2)}, u32[]{:S(2)}) collective-permute-start(f32[4,64,384]{2,1,0:T(8,128)} %get-tuple-element.188), channel_id=1, source_target_pairs={{0,8},{1,9},{2,10},{3,11},{4,12},{5,13},{6,14},{7,15},{8,0},{9,1},... | collective-permute-start | bytes 1179656 | tf_op jit(solution)/shard_map/ppermute | solution.py:48
  213.1 24.6 %collective-permute-start.25 = (f32[4,64,384]{2,1,0:T(8,128)}, f32[4,64,384]{2,1,0:T(8,128)S(1)}, u32[]{:S(2)}, u32[]{:S(2)}) collective-permute-start(f32[4,64,384]{2,1,0:T(8,128)} %get-tuple-element.189), channel_id=1, source_target_pairs={{0,4},{1,5},{2,6},{3,7},{4,0},{5,1},{6,2},{7,3},{8,12},{9,13},{10,... | collective-permute-start | bytes 1179656 | tf_op jit(solution)/shard_map/ppermute | solution.py:48
  241.2 24.0 %collective-permute-start.26 = (f32[3,16,64,512]{3,2,1,0:T(8,128)}, f32[3,16,64,512]{3,2,1,0:T(8,128)}, u32[]{:S(2)}, u32[]{:S(2)}) collective-permute-start(f32[3,16,64,512]{3,2,1,0:T(8,128)} %get-tuple-element.192), channel_id=1, source_target_pairs={{0,1},{1,0},{2,3},{3,2},{4,5},{5,4},{6,7},{7,6},{8,9},{9,8},{10,11... | collective-permute-start | bytes 18874376 | tf_op jit(solution)/shard_map/ppermute | solution.py:48
  241.5 20.8 %collective-permute-start.27 = (f32[2,64,384]{2,1,0:T(8,128)}, f32[2,64,384]{2,1,0:T(8,128)S(1)}, u32[]{:S(2)}, u32[]{:S(2)}) collective-permute-start(f32[2,64,384]{2,1,0:T(8,128)} %get-tuple-element.194), channel_id=1, source_target_pairs={{0,8},{1,9},{2,10},{3,11},{4,12},{5,13},{6,14},{7,15},{8,0},{9,1},... | collective-permute-start | bytes 589832 | tf_op jit(solution)/shard_map/ppermute | solution.py:48
  242.8 19.5 %collective-permute-start.28 = (f32[2,64,384]{2,1,0:T(8,128)}, f32[2,64,384]{2,1,0:T(8,128)S(1)}, u32[]{:S(2)}, u32[]{:S(2)}) collective-permute-start(f32[2,64,384]{2,1,0:T(8,128)} %get-tuple-element.195), channel_id=1, source_target_pairs={{0,4},{1,5},{2,6},{3,7},{4,0},{5,1},{6,2},{7,3},{8,12},{9,13},{10,... | collective-permute-start | bytes 589832 | tf_op jit(solution)/shard_map/ppermute | solution.py:48
  243.1 19.2 %collective-permute-start.29 = (f32[2,64,384]{2,1,0:T(8,128)}, f32[2,64,384]{2,1,0:T(8,128)S(1)}, u32[]{:S(2)}, u32[]{:S(2)}) collective-permute-start(f32[2,64,384]{2,1,0:T(8,128)} %get-tuple-element.196), channel_id=1, source_target_pairs={{0,2},{1,3},{2,0},{3,1},{4,6},{5,7},{6,4},{7,5},{8,10},{9,11},{10,... | collective-permute-start | bytes 589832 | tf_op jit(solution)/shard_map/ppermute | solution.py:48
  273.1 24.9 %collective-permute-start.30 = (f32[8,64,512]{2,1,0:T(8,128)}, f32[8,64,512]{2,1,0:T(8,128)S(1)}, u32[]{:S(2)}, u32[]{:S(2)}) collective-permute-start(f32[8,64,512]{2,1,0:T(8,128)} %get-tuple-element.202), channel_id=1, source_target_pairs={{0,4},{1,5},{2,6},{3,7},{4,0},{5,1},{6,2},{7,3},{8,12},{9,13},{10,... | collective-permute-start | bytes 3145736 | tf_op jit(solution)/shard_map/ppermute | solution.py:48
  273.4 24.7 %collective-permute-start.31 = (f32[8,64,512]{2,1,0:T(8,128)}, f32[8,64,512]{2,1,0:T(8,128)S(1)}, u32[]{:S(2)}, u32[]{:S(2)}) collective-permute-start(f32[8,64,512]{2,1,0:T(8,128)} %get-tuple-element.203), channel_id=1, source_target_pairs={{0,2},{1,3},{2,0},{3,1},{4,6},{5,7},{6,4},{7,5},{8,10},{9,11},{10,... | collective-permute-start | bytes 3145736 | tf_op jit(solution)/shard_map/ppermute | solution.py:48
  274.8 24.3 %collective-permute-start.32 = (f32[8,64,512]{2,1,0:T(8,128)}, f32[8,64,512]{2,1,0:T(8,128)}, u32[]{:S(2)}, u32[]{:S(2)}) collective-permute-start(f32[8,64,512]{2,1,0:T(8,128)} %get-tuple-element.204), channel_id=1, source_target_pairs={{0,8},{1,9},{2,10},{3,11},{4,12},{5,13},{6,14},{7,15},{8,0},{9,1},... | collective-permute-start | bytes 3145736 | tf_op jit(solution)/shard_map/ppermute | solution.py:48
  275.6 31.7 %collective-permute-start.36 = (f32[2,512,256]{2,1,0:T(8,128)}, f32[2,512,256]{2,1,0:T(8,128)S(1)}, u32[]{:S(2)}, u32[]{:S(2)}) collective-permute-start(f32[2,512,256]{2,1,0:T(8,128)} %get-tuple-element.212), channel_id=1, source_target_pairs={{0,1},{1,0},{2,3},{3,2},{4,5},{5,4},{6,7},{7,6},{8,9},{9,8},{10,11... | collective-permute-start | bytes 3145736 | tf_op jit(solution)/shard_map/ppermute | solution.py:48
  303.7 6.6 %collective-permute-start.37 = (f32[2,512,256]{2,1,0:T(8,128)}, f32[2,512,256]{2,1,0:T(8,128)S(1)}, u32[]{:S(2)}, u32[]{:S(2)}) collective-permute-start(f32[2,512,256]{2,1,0:T(8,128)} %get-tuple-element.214), channel_id=1, source_target_pairs={{0,1},{1,0},{2,3},{3,2},{4,5},{5,4},{6,7},{7,6},{8,9},{9,8},{10,11... | collective-permute-start | bytes 3145736 | tf_op jit(solution)/shard_map/ppermute | solution.py:48
  303.8 14.7 %collective-permute-start.33 = (f32[4,64,512]{2,1,0:T(8,128)}, f32[4,64,512]{2,1,0:T(8,128)S(1)}, u32[]{:S(2)}, u32[]{:S(2)}) collective-permute-start(f32[4,64,512]{2,1,0:T(8,128)} %get-tuple-element.208), channel_id=1, source_target_pairs={{0,2},{1,3},{2,0},{3,1},{4,6},{5,7},{6,4},{7,5},{8,10},{9,11},{10,... | collective-permute-start | bytes 1572872 | tf_op jit(solution)/shard_map/ppermute | solution.py:48
  304.8 14.2 %collective-permute-start.34 = (f32[4,64,512]{2,1,0:T(8,128)}, f32[4,64,512]{2,1,0:T(8,128)S(1)}, u32[]{:S(2)}, u32[]{:S(2)}) collective-permute-start(f32[4,64,512]{2,1,0:T(8,128)} %get-tuple-element.209), channel_id=1, source_target_pairs={{0,8},{1,9},{2,10},{3,11},{4,12},{5,13},{6,14},{7,15},{8,0},{9,1},... | collective-permute-start | bytes 1572872 | tf_op jit(solution)/shard_map/ppermute | solution.py:48
  305.6 13.9 %collective-permute-start.35 = (f32[4,64,512]{2,1,0:T(8,128)}, f32[4,64,512]{2,1,0:T(8,128)S(1)}, u32[]{:S(2)}, u32[]{:S(2)}) collective-permute-start(f32[4,64,512]{2,1,0:T(8,128)} %get-tuple-element.210), channel_id=1, source_target_pairs={{0,4},{1,5},{2,6},{3,7},{4,0},{5,1},{6,2},{7,3},{8,12},{9,13},{10,... | collective-permute-start | bytes 1572872 | tf_op jit(solution)/shard_map/ppermute | solution.py:48
  307.3 31.1 %collective-permute-start.47 = (f32[3,1,64,384]{3,2,1,0:T(8,128)}, f32[3,1,64,384]{3,2,1,0:T(8,128)S(1)}, u32[]{:S(2)}, u32[]{:S(2)}) collective-permute-start(f32[3,1,64,384]{3,2,1,0:T(8,128)} %get-tuple-element.227), channel_id=1, source_target_pairs={{0,24},{1,25},{2,26},{3,27},{4,28},{5,29},{6,30},{7,31},{8,16},{9,... | collective-permute-start | bytes 884744 | tf_op jit(solution)/shard_map/ppermute | solution.py:48
  323.4 8.8 %collective-permute-start.38 = (f32[2,64,512]{2,1,0:T(8,128)}, f32[2,64,512]{2,1,0:T(8,128)S(1)}, u32[]{:S(2)}, u32[]{:S(2)}) collective-permute-start(f32[2,64,512]{2,1,0:T(8,128)} %get-tuple-element.219), channel_id=1, source_target_pairs={{0,8},{1,9},{2,10},{3,11},{4,12},{5,13},{6,14},{7,15},{8,0},{9,1},... | collective-permute-start | bytes 786440 | tf_op jit(solution)/shard_map/ppermute | solution.py:48
  324.6 7.5 %collective-permute-start.39 = (f32[2,64,512]{2,1,0:T(8,128)}, f32[2,64,512]{2,1,0:T(8,128)S(1)}, u32[]{:S(2)}, u32[]{:S(2)}) collective-permute-start(f32[2,64,512]{2,1,0:T(8,128)} %get-tuple-element.220), channel_id=1, source_target_pairs={{0,4},{1,5},{2,6},{3,7},{4,0},{5,1},{6,2},{7,3},{8,12},{9,13},{10,... | collective-permute-start | bytes 786440 | tf_op jit(solution)/shard_map/ppermute | solution.py:48
  326.3 6.6 %collective-permute-start.40 = (f32[2,64,512]{2,1,0:T(8,128)}, f32[2,64,512]{2,1,0:T(8,128)S(1)}, u32[]{:S(2)}, u32[]{:S(2)}) collective-permute-start(f32[2,64,512]{2,1,0:T(8,128)} %get-tuple-element.221), channel_id=1, source_target_pairs={{0,2},{1,3},{2,0},{3,1},{4,6},{5,7},{6,4},{7,5},{8,10},{9,11},{10,... | collective-permute-start | bytes 786440 | tf_op jit(solution)/shard_map/ppermute | solution.py:48
  330.1 11.8 %collective-permute-start.42 = (f32[344,128]{1,0:T(8,128)S(1)}, f32[344,128]{1,0:T(8,128)S(1)}, u32[]{:S(2)}, u32[]{:S(2)}) collective-permute-start(f32[344,128]{1,0:T(8,128)S(1)} %slice.278), channel_id=1, source_target_pairs={{0,2},{1,3},{2,0},{3,1},{4,6},{5,7},{6,4},{7,5},{8,10},{9,11},{10,... | collective-permute-start | bytes 528392 | tf_op jit(solution)/shard_map/ppermute | solution.py:48
  335.9 13.7 %collective-permute-start.46 = (f32[3,1,64,512]{3,2,1,0:T(8,128)}, f32[3,1,64,512]{3,2,1,0:T(8,128)S(1)}, u32[]{:S(2)}, u32[]{:S(2)}) collective-permute-start(f32[3,1,64,512]{3,2,1,0:T(8,128)} %get-tuple-element.226), channel_id=1, source_target_pairs={{0,24},{1,25},{2,26},{3,27},{4,28},{5,29},{6,30},{7,31},{8,16},{9,... | collective-permute-start | bytes 1179656 | tf_op jit(solution)/shard_map/ppermute | solution.py:48
  343.7 5.5 %collective-permute-start.43 = (f32[344,128]{1,0:T(8,128)S(1)}, f32[344,128]{1,0:T(8,128)S(1)}, u32[]{:S(2)}, u32[]{:S(2)}) collective-permute-start(f32[344,128]{1,0:T(8,128)S(1)} %pad_maximum_fusion.8), channel_id=1, source_target_pairs={{0,4},{1,5},{2,6},{3,7},{4,0},{5,1},{6,2},{7,3},{8,12},{9,13},{10,... | collective-permute-start | bytes 528392 | tf_op jit(solution)/shard_map/ppermute | solution.py:48
  349.2 10.4 %collective-permute-start.44 = (f32[344,128]{1,0:T(8,128)S(1)}, f32[344,128]{1,0:T(8,128)S(1)}, u32[]{:S(2)}, u32[]{:S(2)}) collective-permute-start(f32[344,128]{1,0:T(8,128)S(1)} %fusion.44), channel_id=1, source_target_pairs={{0,8},{1,9},{2,10},{3,11},{4,12},{5,13},{6,14},{7,15},{8,0},{9,1},... | collective-permute-start | bytes 528392 | tf_op jit(solution)/shard_map/ppermute | solution.py:48
  359.7 7.4 %collective-permute-start.45 = (f32[344,128]{1,0:T(8,128)S(1)}, f32[344,128]{1,0:T(8,128)S(1)}, u32[]{:S(2)}, u32[]{:S(2)}) collective-permute-start(f32[344,128]{1,0:T(8,128)S(1)} %add.251), channel_id=1, source_target_pairs={{0,24},{1,25},{2,26},{3,27},{4,28},{5,29},{6,30},{7,31},{8,16},{9,... | collective-permute-start | bytes 528392 | tf_op jit(solution)/shard_map/ppermute | solution.py:48
  (60 other events, 354.4 us)
Sparse Core Ops, SparseCore 0:
  12.6 80.0 all-gather.2

commit v4 on v3

--- a/solution.py
+++ b/solution.py
@@ -42,8 +42,10 @@
         if self.folded:
             self.masks[-1] |= self.masks[-2]
 
-    def swap(self, x, at):
-        mask = self.masks[at]
+    def swap(self, x, *dimensions):
+        mask = 0
+        for at in dimensions:
+            mask ^= self.masks[at]
         pairs = [(device, device ^ mask) for device in range(self.devices)]
         return lax.ppermute(x, ("dp", "tensor"), pairs)
 
@@ -103,46 +105,29 @@
     return jnp.sum(fold_rows(x, jnp.add), 0, keepdims=True)
 
 
-erf_top = (
-    -2.72614225801306e-10,
-    2.77068142495902e-08,
-    -2.10102402082508e-06,
-    -5.69250639462346e-05,
-    -7.34990630326855e-04,
-    -2.95459980854025e-03,
-    -1.60960333262415e-02,
+tail_slope = 0.3275911 * math.sqrt(0.5)
+tail_terms = tuple(
+    0.5 * term for term in (1.061405429, -1.453152027, 1.421413741, -0.284496736, 0.254829592)
 )
-erf_bottom = (
-    -1.45660718464996e-05,
-    -2.13374055278905e-04,
-    -1.68282697438203e-03,
-    -7.37332916720468e-03,
-    -1.42647390514189e-02,
-)
-
-
-def erf(x):
-    x = jnp.clip(x, -4.0, 4.0)
-    square = x * x
-    top = jnp.full_like(x, erf_top[0])
-    for term in erf_top[1:]:
-        top = top * square + term
-    bottom = jnp.full_like(x, erf_bottom[0])
-    for term in erf_bottom[1:]:
-        bottom = bottom * square + term
-    return x * top / bottom
 
 
 def normal_share(x):
-    return 0.5 + 0.5 * erf(x * math.sqrt(0.5))
+    bell = jnp.exp2(x * x * (-0.5 * math.log2(math.e)))
+    below = 1.0 + jnp.abs(x) * tail_slope
+    t = 1.0 / below
+    tail = tail_terms[0] * t + tail_terms[1]
+    for term in tail_terms[2:]:
+        tail = tail * t + term
+    tail = tail * (t * bell)
+    return jnp.where(x < 0.0, tail, 1.0 - tail), bell
 
 
 def gelu(x):
-    return x * normal_share(x)
-
-
-def gelu_slope(x, share):
-    return share + x * jnp.exp(-0.5 * x * x) * (1.0 / math.sqrt(2.0 * math.pi))
+    return x * normal_share(x)[0]
+
+
+def gelu_slope(x, share, bell):
+    return share + (x * (1.0 / math.sqrt(2.0 * math.pi))) * bell
 
 
 def rotary_partner(x):
@@ -238,11 +223,29 @@
 
 
 class Scattered:
-    def __init__(self, cube, me, keep_ref, send_ref, orders):
+    def __init__(self, cube, me, refs, outs, semaphores, orders):
         self.cube = cube
         self.me = me
-        self.refs = (keep_ref, send_ref)
+        self.refs = refs
+        self.outs = outs
+        self.semaphores = semaphores
         self.orders = orders
+
+    def copies(self, part):
+        return [
+            pltpu.make_async_copy(ref.at[part], out.at[part], self.semaphores.at[part, at])
+            for at, (ref, out) in enumerate(zip(self.refs, self.outs))
+        ]
+
+    def flush(self, parts):
+        for part in parts:
+            for copy in self.copies(part):
+                copy.start()
+
+    def wait(self):
+        for part in range(len(self.orders)):
+            for copy in self.copies(part):
+                copy.wait()
 
     def store(self, tile, turn, start, value):
         rows, wide = self.refs[0].shape[2:]
@@ -324,7 +327,7 @@
     return (at, at)
 
 
-def call(kernel, name, ins, in_specs, outs, scratch=(), after=()):
+def call(kernel, name, ins, in_specs, outs, scratch=(), after=(), unblocked=0):
     kernel = follow(kernel, len(ins), after)
     ins = (*ins, *after)
     in_specs = [*in_specs, *after_specs(after)]
@@ -332,7 +335,9 @@
         kernel,
         grid=(1,),
         in_specs=in_specs,
-        out_specs=[whole_spec(out.shape) for out in outs],
+        out_specs=[
+            *after_specs(outs[:unblocked]), *[whole_spec(out.shape) for out in outs[unblocked:]]
+        ],
         out_shape=outs,
         scratch_shapes=list(scratch),
         compiler_params=params(),
@@ -511,13 +516,24 @@
 
 def middle_kernel(
     feats, mixed_ref, resid_ref, w_ref, w_next_ref, norms_ref, cos_ref, sin_ref,
-    mid_ref, next_ref, q_ref, kv_ref,
+    mid_ref, next_ref, q_ref, kv_ref, w_held, w_semaphores,
 ):
     tiles = w_ref.shape[1]
-    layer = Layer(Gathered(w_ref), 0, (w_ref.shape[3] - LANES) // 2)
+    columns = w_held.shape[3]
+    copies = [
+        pltpu.make_async_copy(
+            w_ref.at[:, :, :, first:last], w_held.at[:, :, :, first:last], w_semaphores.at[at]
+        )
+        for at, (first, last) in enumerate(((0, LANES), (LANES, columns)))
+    ]
+    for copy in copies:
+        copy.start()
+    copies[0].wait()
+    layer = Layer(Gathered(w_held), 0, (columns - LANES) // 2)
     mid = attention_out(mixed_ref, resid_ref[...], layer, [place_of(at) for at in range(tiles)])
     mid_ref[...] = mid
     normed = feats.norm(mid, norms_ref[2:3], norms_ref[3:4])
+    copies[1].wait()
     parts = []
     for at in range(tiles):
         act = gelu(dot(normed, layer.up(place_of(at)))).astype(brain)
@@ -542,7 +558,7 @@
     in_specs = [
         whole_spec(mixed.shape),
         whole_spec(resid.shape),
-        columns_spec(weights, columns, 0),
+        *after_specs((weights,)),
         columns_spec(weights, 3 * LANES, at_heads),
         whole_spec(norms.shape),
         whole_spec(cosine.shape),
@@ -555,8 +571,11 @@
         jax.ShapeDtypeStruct((2, own, wide), brain),
     ]
     ins = (mixed, resid, weights, weights, norms, cosine, sine)
+    scratch = [
+        pltpu.VMEM(weights.shape[:3] + (columns,), brain), pltpu.SemaphoreType.DMA((2,))
+    ]
     kernel = functools.partial(middle_kernel, feats)
-    return call(kernel, "middle", ins, in_specs, outs, (), after)
+    return call(kernel, "middle", ins, in_specs, outs, scratch, after)
 
 
 def feed_back(
@@ -573,6 +592,7 @@
         grads.store(tile, turn, base + LANES + hidden, dot(g_turned, act_ref[turn]))
         grads.store(tile, turn, base + LANES, dot(normed_turned, g_hidden))
         parts.append(dot(g_hidden, layer.up((turn, tile)), 1, 1))
+    grads.flush(range(1, len(grads.orders)))
     g_normed = add_up(parts)
     unit, inverse = feats.centred(mid)
     g_gain = jnp.sum(g_normed * unit, 0, keepdims=True)
@@ -585,28 +605,47 @@
         lanes = tile_lanes(tile)
         g_mixed_ref[:, lanes] = dot(g_low, layer.out((turn, tile))).astype(brain)
         grads.store(tile, turn, base, dot(g_turned, mixed_ref[:, lanes]))
+    grads.flush([0])
     return g_gain, g_shift
 
 
 def top_kernel(
     feats, cube, vocab_count, orders, grad_orders, me_ref, mixed_ref, resid_ref, w_own_ref,
     w_other_ref, norms_ref, vocab_ref, marks_ref, table_ref, keep_ref, send_ref, g_mid_ref, g_mixed_ref,
-    g_norms_ref, g_vocab_ref, act_ref, slope_ref,
+    g_norms_ref, g_vocab_ref, act_ref, slope_ref, keep_held, send_held, grad_semaphores,
+    w_own_held, w_other_held, w_semaphores,
 ):
     me = me_ref[0]
     tiles = cube.tensors
     turns = [(turn, turn ^ (me & (tiles - 1))) for turn in range(tiles)]
-    grads = Scattered(cube, me, keep_ref, send_ref, grad_orders)
-    layer = Layer(Relative(cube, me, (w_own_ref, w_other_ref), orders), 0, act_ref.shape[2])
+    grads = Scattered(
+        cube, me, (keep_held, send_held), (keep_ref, send_ref), grad_semaphores, grad_orders
+    )
+    copies = [
+        [
+            pltpu.make_async_copy(ref.at[part], held.at[part], w_semaphores.at[part, at])
+            for at, (ref, held) in enumerate(((w_own_ref, w_own_held), (w_other_ref, w_other_held)))
+        ]
+        for part in range(len(orders))
+    ]
+    for part in copies:
+        for copy in part:
+            copy.start()
+    for copy in copies[0]:
+        copy.wait()
+    layer = Layer(Relative(cube, me, (w_own_held, w_other_held), orders), 0, act_ref.shape[2])
     mid = attention_out(mixed_ref, resid_ref[...], layer, turns)
     normed = feats.norm(mid, norms_ref[6:7], norms_ref[7:8])
+    for part in copies[1:]:
+        for copy in part:
+            copy.wait()
     parts = []
     for turn, tile in turns:
         hidden = dot(normed, layer.up((turn, tile)))
-        share = normal_share(hidden)
+        share, bell = normal_share(hidden)
         act = (hidden * share).astype(brain)
         act_ref[turn] = act
-        slope_ref[turn] = gelu_slope(hidden, share)
+        slope_ref[turn] = gelu_slope(hidden, share, bell)
         parts.append(dot(act, layer.down((turn, tile)), 1, 1))
     total = mid + add_up(parts)
     unit, inverse = feats.centred(total)
@@ -648,6 +687,7 @@
     )
     g_norms_ref[6:7] = g_gain
     g_norms_ref[7:8] = g_shift
+    grads.wait()
 
 
 def top(
@@ -673,8 +713,7 @@
         scalar_spec(),
         whole_spec(mixed.shape),
         whole_spec(resid.shape),
-        whole_spec(w_own.shape),
-        whole_spec(w_other.shape),
+        *after_specs((w_own, w_other)),
         whole_spec(norms.shape),
         whole_spec(vocab.shape),
         whole_spec(marks.shape),
@@ -683,10 +722,16 @@
     scratch = [
         pltpu.VMEM((tiles, own, hidden), brain),
         pltpu.VMEM((tiles, own, hidden), single),
+        pltpu.VMEM(grads, single),
+        pltpu.VMEM(grads, single),
+        pltpu.SemaphoreType.DMA((pieces, 2)),
+        pltpu.VMEM(w_own.shape, brain),
+        pltpu.VMEM(w_other.shape, brain),
+        pltpu.SemaphoreType.DMA((w_own.shape[0], 2)),
     ]
     ins = (me, mixed, resid, w_own, w_other, norms, vocab, marks, table)
     kernel = functools.partial(top_kernel, feats, cube, vocab_count, orders, grad_orders)
-    return call(kernel, "top", ins, in_specs, outs, scratch)
+    return call(kernel, "top", ins, in_specs, outs, scratch, (), 2)
 
 
 def head_grads(turn, heads_refs, cosine, sine):
@@ -704,14 +749,18 @@
     (
         g_mid_in_ref, resid_ref, mid_ref, mixed_ref, w_in_ref, w_ref, norms_ref, cos_ref, sin_ref,
         g_norms_in_ref, keep_ref, send_ref, g_mid_ref, g_mixed_ref, g_norms_ref,
-        act_ref, slope_ref,
+        act_ref, slope_ref, keep_held, send_held, grad_semaphores, w_held, w_semaphore,
     ) = refs[6:]
+    copy = pltpu.make_async_copy(w_ref.at[:, :, :, : w_held.shape[3]], w_held, w_semaphore)
+    copy.start()
     me = me_ref[0]
     tiles = cube.tensors
     turns = [(turn, turn ^ (me & (tiles - 1))) for turn in range(tiles)]
-    layer = Layer(Gathered(w_ref), 0, act_ref.shape[2])
+    layer = Layer(Gathered(w_held), 0, act_ref.shape[2])
     weights = Gathered(w_in_ref)
-    grads = Scattered(cube, me, keep_ref, send_ref, grad_orders)
+    grads = Scattered(
+        cube, me, (keep_held, send_held), (keep_ref, send_ref), grad_semaphores, grad_orders
+    )
     unit, inverse = feats.centred(resid_ref[...])
     gain = norms_ref[4:5]
     normed_turned = (unit * gain + norms_ref[5:6]).astype(brain).T
@@ -729,17 +778,19 @@
     g_resid = g_mid_in_ref[...] + feats.norm_back(unit, inverse, gain, g_normed)
     mid = mid_ref[...]
     normed = feats.norm(mid, norms_ref[2:3], norms_ref[3:4])
+    copy.wait()
     for turn, tile in turns:
         hidden = dot(normed, layer.up((turn, tile)))
-        share = normal_share(hidden)
+        share, bell = normal_share(hidden)
         act_ref[turn] = (hidden * share).astype(brain)
-        slope_ref[turn] = gelu_slope(hidden, share)
+        slope_ref[turn] = gelu_slope(hidden, share, bell)
     g_gain, g_shift = feed_back(
         feats, turns, g_resid, mid, normed, mixed_ref, layer, norms_ref[2:3], act_ref, slope_ref,
         grads, 3 * LANES, g_mid_ref, g_mixed_ref,
     )
     g_norms_ref[2:3] = g_gain
     g_norms_ref[3:4] = g_shift
+    grads.wait()
 
 
 def lower(
@@ -766,16 +817,21 @@
         scalar_spec(),
         *[whole_spec(x.shape) for x in before],
         columns_spec(weights, 3 * LANES, at_heads),
-        columns_spec(weights, feed_columns, 0),
+        *after_specs((weights,)),
         *[whole_spec(x.shape) for x in rest],
     ]
     scratch = [
         pltpu.VMEM((tiles, own, hidden), brain),
         pltpu.VMEM((tiles, own, hidden), single),
+        pltpu.VMEM(grads, single),
+        pltpu.VMEM(grads, single),
+        pltpu.SemaphoreType.DMA((count, 2)),
+        pltpu.VMEM(weights.shape[:3] + (feed_columns,), brain),
+        pltpu.SemaphoreType.DMA,
     ]
     ins = (me, *before, weights, weights, *rest)
     kernel = functools.partial(lower_kernel, feats, cube, grad_orders)
-    return call(kernel, "lower", ins, in_specs, outs, scratch, after)
+    return call(kernel, "lower", ins, in_specs, outs, scratch, after, 2)
 
 
 def stacked_lanes(ref, row, value):
@@ -860,26 +916,63 @@
     return call(kernel, "bottom", ins, in_specs, outs, (), after)[:2]
 
 
-def halve_kernel(count, together, stacked, skip, keep_ref, *refs):
+def send_kernel(count, skip, keep_ref, got_ref, *refs):
+    outs = refs[skip:]
+    for part in range(count):
+        outs[part][...] = keep_ref[part] + got_ref[part]
+
+
+def send_upper(keep, got, through, after):
+    count, size, rows, wide = keep.shape
+    half = size // 2
+    step = rows // 2
+    upper = pl.BlockSpec((count, half, step, wide), lambda at: (0, 1, at, 0))
+    out = jax.ShapeDtypeStruct((half, rows, wide), single)
+    results = pl.pallas_call(
+        functools.partial(send_kernel, count, len(through) + len(after)),
+        grid=(rows // step,),
+        in_specs=[upper, upper, *after_specs(through), *after_specs(after)],
+        out_specs=[
+            *[pl.BlockSpec((half, step, wide), lambda at: (0, at, 0))] * count,
+            *after_specs(through),
+        ],
+        out_shape=[
+            *[out] * count,
+            *[jax.ShapeDtypeStruct(x.shape, x.dtype) for x in through],
+        ],
+        input_output_aliases={2 + at: count + at for at in range(len(through))},
+        compiler_params=params(),
+        name="send_upper",
+    )(keep, got, *through, *after)
+    return results[:count], results[count:]
+
+
+def halve_kernel(count, together, stacked, keeps, skip, *refs):
+    held = refs[:keeps]
     got_count = 1 if together else count
-    got = refs[:got_count]
-    outs = refs[got_count + skip :]
-    size = keep_ref.shape[1]
+    got = refs[keeps : keeps + got_count]
+    outs = refs[keeps + got_count + skip :]
+    size = held[0].shape[1]
     half = size // 2
     for part in range(count):
         arrived = got[0].at[part] if together else got[part]
+
+        def total(rows):
+            return add_up([x[part, rows] for x in held]) + arrived[rows]
+
         if size == 1:
-            outs[0][part] = keep_ref[part] + arrived[...]
+            outs[0][part] = total(slice(0, 1))
         else:
-            outs[0][part] = keep_ref[part, :half] + arrived[:half]
+            outs[0][part] = total(slice(0, half))
             send = outs[1].at[part] if stacked else outs[1 + part]
-            send[...] = keep_ref[part, half:] + arrived[half:]
-
-
-def halve(keep, got, through=(), after=(), stacked=False):
-    count, size, rows, wide = keep.shape
+            send[...] = total(slice(half, size))
+
+
+def halve(keeps, got, through=(), after=(), stacked=False):
     together = not isinstance(got, list)
     got = [got] if together else got
+    count, _, rows, wide = keeps[0].shape
+    size = got[0].shape[-3]
     step = rows // 2 if size >= 8 else rows
     half = max(size // 2, 1)
 
@@ -896,13 +989,19 @@
         out_specs += [spec(half)] * count
     sends = len(outs) - 1
     got_specs = [spec(count, size)] if together else [spec(size)] * count
-    ins = (keep, *got)
+    ins = (*keeps, *got)
     aliases = {len(ins) + at: len(outs) + at for at in range(len(through))}
     outs += [jax.ShapeDtypeStruct(x.shape, x.dtype) for x in through]
+    skip = len(through) + len(after)
     results = pl.pallas_call(
-        functools.partial(halve_kernel, count, together, stacked, len(through) + len(after)),
+        functools.partial(halve_kernel, count, together, stacked, len(keeps), skip),
         grid=(rows // step,),
-        in_specs=[spec(count, size), *got_specs, *after_specs(through), *after_specs(after)],
+        in_specs=[
+            *[spec(count, size)] * len(keeps),
+            *got_specs,
+            *after_specs(through),
+            *after_specs(after),
+        ],
         out_specs=[*out_specs, *after_specs(through)],
         out_shape=outs,
         input_output_aliases=aliases,
@@ -953,6 +1052,22 @@
     return joined, results[len(outs) :]
 
 
+def wait_kernel(*refs):
+    pass
+
+
+def wait_for(x, after):
+    return pl.pallas_call(
+        wait_kernel,
+        in_specs=after_specs((x, *after)),
+        out_specs=after_specs((x,))[0],
+        out_shape=jax.ShapeDtypeStruct(x.shape, x.dtype),
+        input_output_aliases={0: 0},
+        compiler_params=params(),
+        name="wait_for",
+    )(x, *after)
+
+
 class Gather:
     def __init__(self, cube, parts):
         count = len(parts)
@@ -967,14 +1082,16 @@
     def step(self, through=(), after=()):
         last = self.at == len(self.orders[0])
         self.held, through = join(self.held, self.got, self.count, last, through, after)
-        if last:
-            self.got = self.cube.swap(self.held, 0)
-        else:
+        if not last:
             self.got = [
                 self.cube.swap(x, order[self.at]) for x, order in zip(self.held, self.orders)
             ]
         self.at += 1
         return through
+
+    def finish(self, after):
+        self.held = wait_for(self.held, after)
+        self.got = self.cube.swap(self.held, 0)
 
 
 def normalize_features(resid, gain, shift):
@@ -1134,6 +1251,7 @@
         )
         (kv,) = gather.step((kv,), (resid,))
         kv_other = cube.swap(kv, 0)
+        gather.finish((kv_other,))
         mixed, logsum = attend(q, kv, kv_other, heads)
         grad_orders = [cube.outer(turn) for turn in range(3)]
 
@@ -1141,13 +1259,20 @@
 
         class Sums:
             def __init__(self, keep, send):
-                self.keep = keep
+                self.keeps = (keep,)
                 self.got = cube.swap(send, 0)
                 self.at = 0
 
             def step(self, through=(), after=()):
                 stacked = self.at == last_step
-                self.keep, sends, through = halve(self.keep, self.got, through, after, stacked)
+                if self.at == 0:
+                    sends, through = send_upper(*self.keeps, self.got, through, after)
+                    self.keeps = (*self.keeps, self.got)
+                    self.done = sends[0]
+                else:
+                    keep, sends, through = halve(self.keeps, self.got, through, after, stacked)
+                    self.keeps = (keep,)
+                    self.done = keep
                 if stacked:
                     self.got = cube.swap(sends, grad_orders[0][-1])
                 else:
@@ -1158,7 +1283,7 @@
                 return through
 
             def finish(self, through=(), after=()):
-                keep, _, through = halve(self.keep, self.got, through, after)
+                keep, _, through = halve(self.keeps, self.got, through, after)
                 return keep[:, 0], through
 
         def exchange(arrays):
@@ -1174,25 +1299,25 @@
         part = (q, kv, kv_other, g_mixed, logsum, heads, me)
         first = attend_back(*part, first_turns, tensors)
         got_first = exchange(sums_top.step(first[2:], (first[0],)))
-        last = attend_back(*part, last_turns, tensors, (sums_top.keep,))
+        last = attend_back(*part, last_turns, tensors, (sums_top.done,))
         got_last = exchange(sums_top.step(last[2:], (last[0],)))
         head_parts = (*first[:2], *got_first, *last[:2], *got_last)
         keep, send, g_mid, g_mixed, g_norms = lower(
             feats, cube, grad_orders, me, head_parts, g_mid, resid, mid_low, mixed_low, weights,
-            at_heads, feed_columns, norms, cos_own, sin_own, g_norms, (sums_top.keep,),
+            at_heads, feed_columns, norms, cos_own, sin_own, g_norms, (sums_top.done,),
         )
         (send,) = sums_top.step((send,), (g_mid,))
         sums_low = Sums(keep, send)
         part = (q_low, kv_low, kv_low_other, g_mixed, logsum_low, heads, me)
-        first = attend_back(*part, first_turns, tensors, (sums_top.keep,))
+        first = attend_back(*part, first_turns, tensors, (sums_top.done,))
         got_first = exchange(sums_top.step(first[2:], (first[0],)))
-        sums_low.step((), (sums_top.keep,))
-        last = attend_back(*part, last_turns, tensors, (sums_low.keep,))
+        sums_low.step((), (sums_top.done,))
+        last = attend_back(*part, last_turns, tensors, (sums_low.done,))
         got_last = exchange(sums_low.step(last[2:], (last[0],)))
         head_parts = (*first[:2], *got_first, *last[:2], *got_last)
         keep_table, send_table = bottom(
             feats, cube, gather.orders, me, head_parts, g_mid, ids[:, :own], gather.held,
-            gather.got, norms, vocab_padded, g_vocab, g_norms, cos_own, sin_own, (sums_low.keep,),
+            gather.got, norms, vocab_padded, g_vocab, g_norms, cos_own, sin_own, (sums_low.done,),
         )
         got = cube.swap(send_table, 0)
         (keep_table,) = sums_low.step((keep_table,))
@@ -1203,14 +1328,19 @@
         total = jnp.concatenate(
             [total[:tile_rows] + got[:tile_rows], total[2 * tile_rows :] + got[tile_rows:]], 0
         )
-        for at in range(2, cube.size):
+        done = 2
+        if cube.size > 4:
+            near, far, both = cube.swap(total, 2), cube.swap(total, 3), cube.swap(total, 2, 3)
+            total = (total + near) + (far + both)
+            done = 4
+        for at in range(done, cube.size):
             total = total + cube.swap(total, at)
         while sums_low.at <= last_step:
             sums_low.step()
         while sums_top.at <= last_step:
             sums_top.step((), (keep_table,))
         grads_low, _ = sums_low.finish()
-        grads_top, _ = sums_top.finish((), (sums_low.keep,))
+        grads_top, _ = sums_top.finish((), (sums_low.done,))
         grads_top = jnp.concatenate(list(grads_top), 1)
         grads_low = jnp.concatenate(list(grads_low), 1)
         g_table = side_by_side(total[:tile_rows], TABLE_ROWS)[:vocab_count]

time: 386 us -> 379 us (0.982)
  Pallas kernels: 221 us -> 214 us
    pallas_call x10 -> x8, Pallas kernels: 35.7 us -> 24.1 us  [halve(): pl.pallas_call(functools.partial(halve_kernel, count, together, stacked,...]
    ppermute x48 -> x49, starting transfers between devices: 54.3 us -> 57.8 us  [swap(): return lax.ppermute(x, ('dp', 'tensor'), pairs)]
    pallas_call x5 -> x8, Pallas kernels: 70.6 us -> 73.5 us  [the longest x5 65.7 us: call(): pl.pallas_call(kernel, grid=(1,), in_specs=in_specs, out_specs=[*after_sp...]
    ppermute x48 -> x49, waiting for transfers between devices: 37.9 us -> 36 us  [swap(): return lax.ppermute(x, ('dp', 'tensor'), pairs)]
    unnamed x123 -> x127, local copies, waits for them, and re-layouts: 14.5 us -> 16.4 us
  transfers between devices with their start and end apart: 49 -> 50, of which waited for: 17 -> 17; matrix products, arithmetic and copies ran while one was open for 6% -> 6% of each run, Pallas kernels for 47% -> 48%
where the time goes in v4:
time: 379 us; the launch traced here: 374 us
  Pallas kernels  214 us (56%)
  starting transfers between devices  57.9 us (15%)
  waiting for transfers between devices  37.9 us (10%)
  local copies, waits for them, and re-layouts  28.3 us (7%)
  other arithmetic  19.2 us (5%)
  between operations  16.7 us (4%)
    pallas_call x4, Pallas kernels, attend_back(): pl.pallas_call(functools.partial(attend_back_kernel, heads, own, len(afte...  70.3 us
    pallas_call x5, Pallas kernels, call(): pl.pallas_call(kernel, grid=(1,), in_specs=in_specs, out_specs=[*after_sp...  65.7 us
    ppermute x49, starting transfers between devices, swap(): return lax.ppermute(x, ('dp', 'tensor'), pairs)  57.8 us
    ppermute x49, waiting for transfers between devices, swap(): return lax.ppermute(x, ('dp', 'tensor'), pairs)  36 us
    pallas_call x2, Pallas kernels, attend(): pl.pallas_call(follow(functools.partial(attend_kernel, heads), 3, after),...  35.8 us
    pallas_call x8, Pallas kernels, halve(): pl.pallas_call(functools.partial(halve_kernel, count, together, stacked,...  24.1 us
    unnamed x127, local copies, waits for them, and re-layouts  16.4 us
    pallas_call x4, Pallas kernels, join(): pl.pallas_call(functools.partial(join_kernel, count, together, stacked, s...  10.1 us
  transfers between devices with their start and end apart: 50, of which 17 were waited for; matrix products, arithmetic and copies ran while one was open for 6% of the time, Pallas kernels for 48%

profile of v4, /device:TPU:0, one launch (start us, length us, event | category | flops | bytes accessed | tf_op | source)
XLA Modules:
  0.0 374.3 jit_solution(9934586453886572880)
XLA Ops:
  14.6 3.0 collective-permute-start
  17.8 3.7 collective-permute-start.5
  22.3 6.4 %collective-permute-done.1 = f32[40,384]{1,0:T(8,128)S(1)} collective-permute-done((f32[40,384]{1,0:T(8,128)S(1)}, f32[40,384]{1,0:T(8,128)S(1)}, u32[]{:S(2)}, u32[]{:S(2)}) %collective-permute-start.1) | collective-permute-done | bytes 61472 | tf_op jit(solution)/shard_map/ppermute | solution.py:50
  28.7 3.7 collective-permute-start.2
  32.4 3.1 collective-permute-done.2
  37.6 2.8 collective-permute-done.3
  45.1 1.8 join.4
  52.0 6.2 %embed.1 = (bf16[512,512]{1,0:T(8,128)(2,1)}, bf16[2,512,512]{2,1,0:T(8,128)(2,1)}, bf16[2,512,512]{2,1,0:T(8,128)(2,1)}, f32[512,512]{1,0:T(8,128)}) custom-call(f32[4,40,384]{2,1,0:T(8,128)} %bitcast.247, s32[1,1024]{1,0:T(1,128)} %bitcast.269, bf16[64,512]{1,0:T(8,128)(2,1)} %pad.63.vocab_ref.refs_12_, f32[1024,128]{1,0:T(8,128)} %pad.64.cos_ref, ...), custom_call_target="tpu_custom_call" | custom-call | tf_op jit(solution)/shard_map/embed/pallas_call | solution.py:334
  58.9 2.1 join.5
  63.3 18.0 %attend.2 = (bf16[512,512]{1,0:T(8,128)(2,1)}, f32[4,8,512]{2,1,0:T(8,128)}) custom-call(bf16[512,512]{1,0:T(8,128)(2,1)} %get-tuple-element.143.q_ref.refs_6_, bf16[2,512,512]{2,1,0:T(8,128)(2,1)} %get-tuple-element.144.own_ref.kv_own_ref, bf16[2,512,512]{2,1,0:T(8,128)(2,1)} %get-tuple-element.145.other_ref.kv_other_ref), custom_call_target="tpu_custom_call" | custom-call | tf_op jit(solution)/shard_map/attend/pallas_call | solution.py:418
  82.2 2.5 join.6
  91.0 1.9 all-gather.3.cloned.1.call-done
  92.9 11.3 %middle.1 = (f32[512,512]{1,0:T(8,128)}, f32[512,512]{1,0:T(8,128)}, bf16[512,512]{1,0:T(8,128)(2,1)}, bf16[2,512,512]{2,1,0:T(8,128)(2,1)}) custom-call(bf16[512,512]{1,0:T(8,128)(2,1)} %get-tuple-element.146.mixed_ref.refs_10_, f32[512,512]{1,0:T(8,128)} %get-tuple-element.147.resid_ref, bf16[8,4,64,1536]{3,2,1,0:T(8,128)(2,1)} %bitcast.241, ...), custom_call_target="tpu_custom_call" | custom-call | tf_op jit(solution)/shard_map/middle/pallas_call | solution.py:334
  105.3 3.6 join.7
  109.2 2.6 collective-permute-done.15.other_ref.refs_1_.kv_other_ref
  115.0 17.7 %attend.3 = (bf16[512,512]{1,0:T(8,128)(2,1)}, f32[4,8,512]{2,1,0:T(8,128)}) custom-call(bf16[512,512]{1,0:T(8,128)(2,1)} %get-tuple-element.148.q_ref, bf16[2,512,512]{2,1,0:T(8,128)(2,1)} %get-tuple-element.161.own_ref.kv_own_ref, bf16[2,512,512]{2,1,0:T(8,128)(2,1)} %copy-done), custom_call_target="tpu_custom_call" | custom-call | tf_op jit(solution)/shard_map/attend/pallas_call | solution.py:418
  132.7 1.7 copy-done.1
  134.4 19.8 %top.1 = (f32[3,16,64,384]{3,2,1,0:T(8,128)}, f32[3,16,64,384]{3,2,1,0:T(8,128)}, f32[512,512]{1,0:T(8,128)}, bf16[512,512]{1,0:T(8,128)(2,1)}, f32[16,512]{1,0:T(8,128)}, /*index=5*/f32[40,512]{1,0:T(8,128)}) custom-call(s32[1]{0:T(128)} %bitcast.me_ref.refs_0_, bf16[512,512]{1,0:T(8,128)(2,1)} %get-tuple-element.162.mixed_ref, ...), custom_call_target="tpu_custom_call" | custom-call | tf_op jit(solution)/shard_map/top/pallas_call | solution.py:334
  154.5 17.5 %attend_back.4 = (f32[512,256]{1,0:T(8,128)}, f32[2,512,256]{2,1,0:T(8,128)}, f32[2,512,256]{2,1,0:T(8,128)}) custom-call(s32[1]{0:T(128)} %bitcast.me_ref.refs_0_, bf16[512,512]{1,0:T(8,128)(2,1)} %get-tuple-element.148.q_ref, bf16[2,512,512]{2,1,0:T(8,128)(2,1)} %get-tuple-element.161.own_ref.kv_own_ref, bf16[2,512,512]{2,1,0:T(8,128)(2,1)} %copy-done, ...), custom_call_target="tpu_custom_call" | custom-call | tf_op jit(solution)/shard_map/attend_back/pallas_call | solution.py:489
  172.0 3.5 send_upper.2
  176.8 2.4 collective-permute-start.21
  179.2 1.7 collective-permute-start.19
  180.9 17.7 %attend_back.5 = (f32[512,256]{1,0:T(8,128)}, f32[2,512,256]{2,1,0:T(8,128)}, f32[2,512,256]{2,1,0:T(8,128)}) custom-call(s32[1]{0:T(128)} %bitcast.me_ref.refs_0_, bf16[512,512]{1,0:T(8,128)(2,1)} %get-tuple-element.148.q_ref, bf16[2,512,512]{2,1,0:T(8,128)(2,1)} %get-tuple-element.161.own_ref.kv_own_ref, bf16[2,512,512]{2,1,0:T(8,128)(2,1)} %copy-done, ...), custom_call_target="tpu_custom_call" | custom-call | tf_op jit(solution)/shard_map/attend_back/pallas_call | solution.py:489
  200.1 4.4 %halve.8 = (f32[3,4,64,384]{3,2,1,0:T(8,128)}, f32[4,64,384]{2,1,0:T(8,128)}, f32[4,64,384]{2,1,0:T(8,128)}, f32[4,64,384]{2,1,0:T(8,128)}, f32[2,512,256]{2,1,0:T(8,128)}) custom-call(f32[3,16,64,384]{3,2,1,0:T(8,128)} %get-tuple-element.168.keep_ref.refs_0_, ...), custom_call_target="tpu_custom_call", output_to_operand_aliasing={{4}: (5, {})} | custom-call | tf_op jit(solution)/shard_map/halve/pallas_call | solution.py:996
  205.1 1.7 collective-permute-start.25
  208.5 21.4 %lower.1 = (f32[3,16,64,512]{3,2,1,0:T(8,128)}, f32[3,16,64,512]{3,2,1,0:T(8,128)}, f32[512,512]{1,0:T(8,128)}, bf16[512,512]{1,0:T(8,128)(2,1)}, f32[16,512]{1,0:T(8,128)}) custom-call(s32[1]{0:T(128)} %bitcast.me_ref.refs_0_, f32[512,256]{1,0:T(8,128)} %get-tuple-element.166.refs_1_, f32[2,512,256]{2,1,0:T(8,128)} %get-tuple-element.167.refs_2_, ...), custom_call_target="tpu_custom_call" | custom-call | tf_op jit(solution)/shard_map/lower/pallas_call | solution.py:334
  230.9 2.6 halve.9
  235.4 2.0 collective-permute-start.29
  237.4 17.5 %attend_back.6 = (f32[512,256]{1,0:T(8,128)}, f32[2,512,256]{2,1,0:T(8,128)}, f32[2,512,256]{2,1,0:T(8,128)}) custom-call(s32[1]{0:T(128)} %bitcast.me_ref.refs_0_, bf16[512,512]{1,0:T(8,128)(2,1)} %get-tuple-element.143.q_ref.refs_6_, bf16[2,512,512]{2,1,0:T(8,128)(2,1)} %get-tuple-element.144.own_ref.kv_own_ref, ...), custom_call_target="tpu_custom_call" | custom-call | tf_op jit(solution)/shard_map/attend_back/pallas_call | solution.py:489
  255.7 2.2 halve.10
  257.9 4.3 %send_upper.3 = (f32[8,64,512]{2,1,0:T(8,128)}, f32[8,64,512]{2,1,0:T(8,128)}, f32[8,64,512]{2,1,0:T(8,128)}) custom-call(f32[3,16,64,512]{3,2,1,0:T(8,128)} %get-tuple-element.183.keep_ref.refs_0_, f32[3,16,64,512]{3,2,1,0:T(8,128)} %collective-permute-done.26.got_ref.refs_1_, f32[3,1,64,384]{3,2,1,0:T(8,128)} %get-tuple-element.197.refs_0_), custom_call_target="tpu_custom_call" | custom-call | tf_op jit(solution)/shard_map/send_upper/pallas_call | solution.py:931
  264.6 17.7 %attend_back.7 = (f32[512,256]{1,0:T(8,128)}, f32[2,512,256]{2,1,0:T(8,128)}, f32[2,512,256]{2,1,0:T(8,128)}) custom-call(s32[1]{0:T(128)} %bitcast.me_ref.refs_0_, bf16[512,512]{1,0:T(8,128)(2,1)} %get-tuple-element.143.q_ref.refs_6_, bf16[2,512,512]{2,1,0:T(8,128)(2,1)} %get-tuple-element.144.own_ref.kv_own_ref, ...), custom_call_target="tpu_custom_call" | custom-call | tf_op jit(solution)/shard_map/attend_back/pallas_call | solution.py:489
  282.3 4.8 %collective-permute-done.31.refs_3_ = f32[8,64,512]{2,1,0:T(8,128)S(1)} collective-permute-done((f32[8,64,512]{2,1,0:T(8,128)}, f32[8,64,512]{2,1,0:T(8,128)S(1)}, u32[]{:S(2)}, u32[]{:S(2)}) %collective-permute-start.31) | collective-permute-done | bytes 1048608 | tf_op jit(solution)/shard_map/ppermute | solution.py:50
  288.4 6.0 %halve.11 = (f32[3,4,64,512]{3,2,1,0:T(8,128)}, f32[4,64,512]{2,1,0:T(8,128)}, f32[4,64,512]{2,1,0:T(8,128)}, f32[4,64,512]{2,1,0:T(8,128)}, f32[2,512,256]{2,1,0:T(8,128)}) custom-call(f32[3,16,64,512]{3,2,1,0:T(8,128)} %get-tuple-element.183.keep_ref.refs_0_, ...), custom_call_target="tpu_custom_call", output_to_operand_aliasing={{4}: (5, {})} | custom-call | tf_op jit(solution)/shard_map/halve/pallas_call | solution.py:996
  297.5 2.5 collective-permute-start.48
  301.6 7.2 %bottom.1 = (f32[464,128]{1,0:T(8,128)}, f32[464,128]{1,0:T(8,128)}, f32[16,512]{1,0:T(8,128)}) custom-call(s32[1]{0:T(128)} %bitcast.me_ref.refs_0_, f32[512,256]{1,0:T(8,128)} %get-tuple-element.196.refs_5_.refs_1_, f32[2,512,256]{2,1,0:T(8,128)} %get-tuple-element.207.refs_2_, f32[2,512,256]{2,1,0:T(8,128)} %copy-done.5, ...), custom_call_target="tpu_custom_call" | custom-call | tf_op jit(solution)/shard_map/bottom/pallas_call | solution.py:334
  311.5 3.0 halve.12
  317.1 1.7 collective-permute-done.41
  321.3 2.1 collective-permute-done.38.refs_1_
  324.6 2.3 halve.13
  327.0 4.7 %collective-permute-start.47 = (f32[3,1,64,512]{3,2,1,0:T(8,128)}, f32[3,1,64,512]{3,2,1,0:T(8,128)S(1)}, u32[]{:S(2)}, u32[]{:S(2)}) collective-permute-start(f32[3,1,64,512]{3,2,1,0:T(8,128)} %get-tuple-element.222), channel_id=1, source_target_pairs={{0,24},{1,25},{2,26},{3,27},{4,28},{5,29},{6,30},{7,31},{8,16},{9,... | collective-permute-start | bytes 1179656 | tf_op jit(solution)/shard_map/ppermute | solution.py:50
  332.4 1.8 halve.15
  338.1 2.4 collective-permute-start.45
  340.8 3.9 %collective-permute-done.44 = f32[344,128]{1,0:T(8,128)S(1)} collective-permute-done((f32[344,128]{1,0:T(8,128)S(1)}, f32[344,128]{1,0:T(8,128)S(1)}, u32[]{:S(2)}, u32[]{:S(2)}) %collective-permute-start.44) | collective-permute-done | bytes 176160 | tf_op jit(solution)/shard_map/ppermute | solution.py:50
  344.6 3.9 %collective-permute-done.45 = f32[344,128]{1,0:T(8,128)S(1)} collective-permute-done((f32[344,128]{1,0:T(8,128)S(1)}, f32[344,128]{1,0:T(8,128)S(1)}, u32[]{:S(2)}, u32[]{:S(2)}) %collective-permute-start.45) | collective-permute-done | bytes 176160 | tf_op jit(solution)/shard_map/ppermute | solution.py:50
  349.4 2.7 collective-permute-start.46
  352.8 1.9 halve.14
  356.5 2.5 fusion.52
  (320 shorter events, 76.0 us)
Async XLA Ops:
  7.2 85.6 %all-gather.3.cloned.1.call-start = ((), (), s32[]{:S(2)}) async-start(), calls=%async_computation | async-start | bytes 6488064 | tf_op jit(solution)/shard_map/all_gather | solution.py:1184
  14.6 7.1 %collective-permute-start = (f32[40,384]{1,0:T(8,128)S(1)}, f32[40,384]{1,0:T(8,128)S(1)}, u32[]{:S(2)}, u32[]{:S(2)}) collective-permute-start(f32[40,384]{1,0:T(8,128)S(1)} %select_maximum_fusion), channel_id=1, source_target_pairs={{0,4},{1,5},{2,6},{3,7},{4,0},{5,1},{6,2},{7,3},{8,12},{9,13},{10,... | collective-permute-start | bytes 184328 | tf_op jit(solution)/shard_map/ppermute | solution.py:50
  17.8 25.9 %collective-permute-start.5 = (bf16[3,1,64,512]{3,2,1,0:T(8,128)(2,1)S(1)}, bf16[3,1,64,512]{3,2,1,0:T(8,128)(2,1)S(1)}, u32[]{:S(2)}, u32[]{:S(2)}) collective-permute-start(bf16[3,1,64,512]{3,2,1,0:T(8,128)(2,1)S(1)} %maximum_bitcast_fusion.refs_0_), channel_id=1, source_target_pairs={{0,24},{1,25},{2,26},{3,27},{4,28},{5,29},{6,30},{7,31},{8,16},{9,... | collective-permute-start | bytes 589832 | tf_op jit(solution)/shard_map/ppermute | solution.py:50
  21.7 7.0 %collective-permute-start.1 = (f32[40,384]{1,0:T(8,128)S(1)}, f32[40,384]{1,0:T(8,128)S(1)}, u32[]{:S(2)}, u32[]{:S(2)}) collective-permute-start(f32[40,384]{1,0:T(8,128)S(1)} %fusion.66), channel_id=1, source_target_pairs={{0,8},{1,9},{2,10},{3,11},{4,12},{5,13},{6,14},{7,15},{8,0},{9,1},... | collective-permute-start | bytes 184328 | tf_op jit(solution)/shard_map/ppermute | solution.py:50
  28.7 6.8 %collective-permute-start.2 = (f32[40,384]{1,0:T(8,128)S(1)}, f32[40,384]{1,0:T(8,128)S(1)}, u32[]{:S(2)}, u32[]{:S(2)}) collective-permute-start(f32[40,384]{1,0:T(8,128)S(1)} %add.240), channel_id=1, source_target_pairs={{0,24},{1,25},{2,26},{3,27},{4,28},{5,29},{6,30},{7,31},{8,16},{9,... | collective-permute-start | bytes 184328 | tf_op jit(solution)/shard_map/ppermute | solution.py:50
  36.1 4.2 %collective-permute-start.3 = (f32[40,384]{1,0:T(8,128)S(1)}, f32[40,384]{1,0:T(8,128)S(1)}, u32[]{:S(2)}, u32[]{:S(2)}) collective-permute-start(f32[40,384]{1,0:T(8,128)S(1)} %pad_dynamic-update-slice_fusion), channel_id=1, source_target_pairs={{0,2},{1,3},{2,0},{3,1},{4,6},{5,7},{6,4},{7,5},{8,10},{9,11},{10,... | collective-permute-start | bytes 184328 | tf_op jit(solution)/shard_map/ppermute | solution.py:50
  40.3 3.3 collective-permute-start.4
  46.8 11.3 %collective-permute-start.6 = (bf16[2,64,512]{2,1,0:T(8,128)(2,1)}, bf16[2,64,512]{2,1,0:T(8,128)(2,1)S(1)}, u32[]{:S(2)}, u32[]{:S(2)}) collective-permute-start(bf16[2,64,512]{2,1,0:T(8,128)(2,1)} %get-tuple-element.149.refs_0_), channel_id=1, source_target_pairs={{0,4},{1,5},{2,6},{3,7},{4,0},{5,1},{6,2},{7,3},{8,12},{9,13},{10,... | collective-permute-start | bytes 393224 | tf_op jit(solution)/shard_map/ppermute | solution.py:50
  48.0 10.2 %collective-permute-start.7 = (bf16[2,64,512]{2,1,0:T(8,128)(2,1)}, bf16[2,64,512]{2,1,0:T(8,128)(2,1)S(1)}, u32[]{:S(2)}, u32[]{:S(2)}) collective-permute-start(bf16[2,64,512]{2,1,0:T(8,128)(2,1)} %get-tuple-element.150.refs_1_), channel_id=1, source_target_pairs={{0,2},{1,3},{2,0},{3,1},{4,6},{5,7},{6,4},{7,5},{8,10},{9,11},{10,... | collective-permute-start | bytes 393224 | tf_op jit(solution)/shard_map/ppermute | solution.py:50
  49.3 8.9 %collective-permute-start.8 = (bf16[2,64,512]{2,1,0:T(8,128)(2,1)}, bf16[2,64,512]{2,1,0:T(8,128)(2,1)S(1)}, u32[]{:S(2)}, u32[]{:S(2)}) collective-permute-start(bf16[2,64,512]{2,1,0:T(8,128)(2,1)} %get-tuple-element.151.refs_2_), channel_id=1, source_target_pairs={{0,8},{1,9},{2,10},{3,11},{4,12},{5,13},{6,14},{7,15},{8,0},{9,1},... | collective-permute-start | bytes 393224 | tf_op jit(solution)/shard_map/ppermute | solution.py:50
  61.0 20.3 %collective-permute-start.9 = (bf16[4,64,512]{2,1,0:T(8,128)(2,1)}, bf16[4,64,512]{2,1,0:T(8,128)(2,1)S(1)}, u32[]{:S(2)}, u32[]{:S(2)}) collective-permute-start(bf16[4,64,512]{2,1,0:T(8,128)(2,1)} %get-tuple-element.152.refs_0_), channel_id=1, source_target_pairs={{0,2},{1,3},{2,0},{3,1},{4,6},{5,7},{6,4},{7,5},{8,10},{9,11},{10,... | collective-permute-start | bytes 786440 | tf_op jit(solution)/shard_map/ppermute | solution.py:50
  61.8 19.6 %collective-permute-start.10 = (bf16[4,64,512]{2,1,0:T(8,128)(2,1)}, bf16[4,64,512]{2,1,0:T(8,128)(2,1)S(1)}, u32[]{:S(2)}, u32[]{:S(2)}) collective-permute-start(bf16[4,64,512]{2,1,0:T(8,128)(2,1)} %get-tuple-element.153.refs_1_), channel_id=1, source_target_pairs={{0,8},{1,9},{2,10},{3,11},{4,12},{5,13},{6,14},{7,15},{8,0},{9,1},... | collective-permute-start | bytes 786440 | tf_op jit(solution)/shard_map/ppermute | solution.py:50
  62.5 18.8 %collective-permute-start.11 = (bf16[4,64,512]{2,1,0:T(8,128)(2,1)}, bf16[4,64,512]{2,1,0:T(8,128)(2,1)S(1)}, u32[]{:S(2)}, u32[]{:S(2)}) collective-permute-start(bf16[4,64,512]{2,1,0:T(8,128)(2,1)} %get-tuple-element.154.refs_2_), channel_id=1, source_target_pairs={{0,4},{1,5},{2,6},{3,7},{4,0},{5,1},{6,2},{7,3},{8,12},{9,13},{10,... | collective-permute-start | bytes 786440 | tf_op jit(solution)/shard_map/ppermute | solution.py:50
  84.8 19.4 %collective-permute-start.12 = (bf16[8,64,512]{2,1,0:T(8,128)(2,1)}, bf16[8,64,512]{2,1,0:T(8,128)(2,1)S(1)}, u32[]{:S(2)}, u32[]{:S(2)}) collective-permute-start(bf16[8,64,512]{2,1,0:T(8,128)(2,1)} %get-tuple-element.156.refs_0_), channel_id=1, source_target_pairs={{0,8},{1,9},{2,10},{3,11},{4,12},{5,13},{6,14},{7,15},{8,0},{9,1},... | collective-permute-start | bytes 1572872 | tf_op jit(solution)/shard_map/ppermute | solution.py:50
  86.2 18.0 %collective-permute-start.13 = (bf16[8,64,512]{2,1,0:T(8,128)(2,1)}, bf16[8,64,512]{2,1,0:T(8,128)(2,1)S(1)}, u32[]{:S(2)}, u32[]{:S(2)}) collective-permute-start(bf16[8,64,512]{2,1,0:T(8,128)(2,1)} %get-tuple-element.157.refs_1_), channel_id=1, source_target_pairs={{0,4},{1,5},{2,6},{3,7},{4,0},{5,1},{6,2},{7,3},{8,12},{9,13},{10,... | collective-permute-start | bytes 1572872 | tf_op jit(solution)/shard_map/ppermute | solution.py:50
  87.3 16.9 %collective-permute-start.14 = (bf16[8,64,512]{2,1,0:T(8,128)(2,1)}, bf16[8,64,512]{2,1,0:T(8,128)(2,1)S(1)}, u32[]{:S(2)}, u32[]{:S(2)}) collective-permute-start(bf16[8,64,512]{2,1,0:T(8,128)(2,1)} %get-tuple-element.158.refs_2_), channel_id=1, source_target_pairs={{0,2},{1,3},{2,0},{3,1},{4,6},{5,7},{6,4},{7,5},{8,10},{9,11},{10,... | collective-permute-start | bytes 1572872 | tf_op jit(solution)/shard_map/ppermute | solution.py:50
  112.8 19.9 %collective-permute-start.16 = (bf16[3,16,64,512]{3,2,1,0:T(8,128)(2,1)}, bf16[3,16,64,512]{3,2,1,0:T(8,128)(2,1)S(1)}, u32[]{:S(2)}, u32[]{:S(2)}) collective-permute-start(bf16[3,16,64,512]{3,2,1,0:T(8,128)(2,1)} %wait_for.1.w_own_ref.refs_9_), channel_id=1, source_target_pairs={{0,1},{1,0},{2,3},{3,2},{4,5},{5,4},{6,7},{7,6},{8,9},{9,8},{10,11... | collective-permute-start | bytes 9437192 | tf_op jit(solution)/shard_map/ppermute | solution.py:50
  154.2 17.8 %collective-permute-start.17 = (f32[3,16,64,384]{3,2,1,0:T(8,128)}, f32[3,16,64,384]{3,2,1,0:T(8,128)}, u32[]{:S(2)}, u32[]{:S(2)}) collective-permute-start(f32[3,16,64,384]{3,2,1,0:T(8,128)} %get-tuple-element.169), channel_id=1, source_target_pairs={{0,1},{1,0},{2,3},{3,2},{4,5},{5,4},{6,7},{7,6},{8,9},{9,8},{10,11... | collective-permute-start | bytes 14155784 | tf_op jit(solution)/shard_map/ppermute | solution.py:50
  175.5 23.2 %collective-permute-start.20 = (f32[8,64,384]{2,1,0:T(8,128)}, f32[8,64,384]{2,1,0:T(8,128)S(1)}, u32[]{:S(2)}, u32[]{:S(2)}) collective-permute-start(f32[8,64,384]{2,1,0:T(8,128)} %get-tuple-element.175), channel_id=1, source_target_pairs={{0,2},{1,3},{2,0},{3,1},{4,6},{5,7},{6,4},{7,5},{8,10},{9,11},{10,... | collective-permute-start | bytes 2359304 | tf_op jit(solution)/shard_map/ppermute | solution.py:50
  176.8 21.9 %collective-permute-start.21 = (f32[8,64,384]{2,1,0:T(8,128)}, f32[8,64,384]{2,1,0:T(8,128)S(1)}, u32[]{:S(2)}, u32[]{:S(2)}) collective-permute-start(f32[8,64,384]{2,1,0:T(8,128)} %get-tuple-element.176), channel_id=1, source_target_pairs={{0,8},{1,9},{2,10},{3,11},{4,12},{5,13},{6,14},{7,15},{8,0},{9,1},... | collective-permute-start | bytes 2359304 | tf_op jit(solution)/shard_map/ppermute | solution.py:50
  179.2 19.5 %collective-permute-start.19 = (f32[8,64,384]{2,1,0:T(8,128)}, f32[8,64,384]{2,1,0:T(8,128)S(1)}, u32[]{:S(2)}, u32[]{:S(2)}) collective-permute-start(f32[8,64,384]{2,1,0:T(8,128)} %get-tuple-element.172.refs_0_), channel_id=1, source_target_pairs={{0,4},{1,5},{2,6},{3,7},{4,0},{5,1},{6,2},{7,3},{8,12},{9,13},{10,... | collective-permute-start | bytes 2359304 | tf_op jit(solution)/shard_map/ppermute | solution.py:50
  180.9 25.8 %collective-permute-start.18 = (f32[2,512,256]{2,1,0:T(8,128)}, f32[2,512,256]{2,1,0:T(8,128)S(1)}, u32[]{:S(2)}, u32[]{:S(2)}) collective-permute-start(f32[2,512,256]{2,1,0:T(8,128)} %get-tuple-element.171), channel_id=1, source_target_pairs={{0,1},{1,0},{2,3},{3,2},{4,5},{5,4},{6,7},{7,6},{8,9},{9,8},{10,11... | collective-permute-start | bytes 3145736 | tf_op jit(solution)/shard_map/ppermute | solution.py:50
  204.4 3.0 collective-permute-start.22
  205.0 24.8 %collective-permute-start.23 = (f32[4,64,384]{2,1,0:T(8,128)}, f32[4,64,384]{2,1,0:T(8,128)S(1)}, u32[]{:S(2)}, u32[]{:S(2)}) collective-permute-start(f32[4,64,384]{2,1,0:T(8,128)} %get-tuple-element.184), channel_id=1, source_target_pairs={{0,2},{1,3},{2,0},{3,1},{4,6},{5,7},{6,4},{7,5},{8,10},{9,11},{10,... | collective-permute-start | bytes 1179656 | tf_op jit(solution)/shard_map/ppermute | solution.py:50
  205.0 24.8 %collective-permute-start.24 = (f32[4,64,384]{2,1,0:T(8,128)}, f32[4,64,384]{2,1,0:T(8,128)S(1)}, u32[]{:S(2)}, u32[]{:S(2)}) collective-permute-start(f32[4,64,384]{2,1,0:T(8,128)} %get-tuple-element.185), channel_id=1, source_target_pairs={{0,8},{1,9},{2,10},{3,11},{4,12},{5,13},{6,14},{7,15},{8,0},{9,1},... | collective-permute-start | bytes 1179656 | tf_op jit(solution)/shard_map/ppermute | solution.py:50
  205.1 24.8 %collective-permute-start.25 = (f32[4,64,384]{2,1,0:T(8,128)}, f32[4,64,384]{2,1,0:T(8,128)S(1)}, u32[]{:S(2)}, u32[]{:S(2)}) collective-permute-start(f32[4,64,384]{2,1,0:T(8,128)} %get-tuple-element.186), channel_id=1, source_target_pairs={{0,4},{1,5},{2,6},{3,7},{4,0},{5,1},{6,2},{7,3},{8,12},{9,13},{10,... | collective-permute-start | bytes 1179656 | tf_op jit(solution)/shard_map/ppermute | solution.py:50
  233.5 24.4 %collective-permute-start.26 = (f32[3,16,64,512]{3,2,1,0:T(8,128)}, f32[3,16,64,512]{3,2,1,0:T(8,128)}, u32[]{:S(2)}, u32[]{:S(2)}) collective-permute-start(f32[3,16,64,512]{3,2,1,0:T(8,128)} %get-tuple-element.189), channel_id=1, source_target_pairs={{0,1},{1,0},{2,3},{3,2},{4,5},{5,4},{6,7},{7,6},{8,9},{9,8},{10,11... | collective-permute-start | bytes 18874376 | tf_op jit(solution)/shard_map/ppermute | solution.py:50
  233.8 21.0 %collective-permute-start.27 = (f32[2,64,384]{2,1,0:T(8,128)}, f32[2,64,384]{2,1,0:T(8,128)S(1)}, u32[]{:S(2)}, u32[]{:S(2)}) collective-permute-start(f32[2,64,384]{2,1,0:T(8,128)} %get-tuple-element.191), channel_id=1, source_target_pairs={{0,8},{1,9},{2,10},{3,11},{4,12},{5,13},{6,14},{7,15},{8,0},{9,1},... | collective-permute-start | bytes 589832 | tf_op jit(solution)/shard_map/ppermute | solution.py:50
  234.4 20.5 %collective-permute-start.28 = (f32[2,64,384]{2,1,0:T(8,128)}, f32[2,64,384]{2,1,0:T(8,128)S(1)}, u32[]{:S(2)}, u32[]{:S(2)}) collective-permute-start(f32[2,64,384]{2,1,0:T(8,128)} %get-tuple-element.192), channel_id=1, source_target_pairs={{0,4},{1,5},{2,6},{3,7},{4,0},{5,1},{6,2},{7,3},{8,12},{9,13},{10,... | collective-permute-start | bytes 589832 | tf_op jit(solution)/shard_map/ppermute | solution.py:50
  235.4 19.5 %collective-permute-start.29 = (f32[2,64,384]{2,1,0:T(8,128)}, f32[2,64,384]{2,1,0:T(8,128)S(1)}, u32[]{:S(2)}, u32[]{:S(2)}) collective-permute-start(f32[2,64,384]{2,1,0:T(8,128)} %get-tuple-element.193), channel_id=1, source_target_pairs={{0,2},{1,3},{2,0},{3,1},{4,6},{5,7},{6,4},{7,5},{8,10},{9,11},{10,... | collective-permute-start | bytes 589832 | tf_op jit(solution)/shard_map/ppermute | solution.py:50
  262.1 24.9 %collective-permute-start.31 = (f32[8,64,512]{2,1,0:T(8,128)}, f32[8,64,512]{2,1,0:T(8,128)S(1)}, u32[]{:S(2)}, u32[]{:S(2)}) collective-permute-start(f32[8,64,512]{2,1,0:T(8,128)} %get-tuple-element.199), channel_id=1, source_target_pairs={{0,2},{1,3},{2,0},{3,1},{4,6},{5,7},{6,4},{7,5},{8,10},{9,11},{10,... | collective-permute-start | bytes 3145736 | tf_op jit(solution)/shard_map/ppermute | solution.py:50
  262.2 24.9 %collective-permute-start.32 = (f32[8,64,512]{2,1,0:T(8,128)}, f32[8,64,512]{2,1,0:T(8,128)S(1)}, u32[]{:S(2)}, u32[]{:S(2)}) collective-permute-start(f32[8,64,512]{2,1,0:T(8,128)} %get-tuple-element.200), channel_id=1, source_target_pairs={{0,8},{1,9},{2,10},{3,11},{4,12},{5,13},{6,14},{7,15},{8,0},{9,1},... | collective-permute-start | bytes 3145736 | tf_op jit(solution)/shard_map/ppermute | solution.py:50
  263.4 24.3 %collective-permute-start.30 = (f32[8,64,512]{2,1,0:T(8,128)}, f32[8,64,512]{2,1,0:T(8,128)}, u32[]{:S(2)}, u32[]{:S(2)}) collective-permute-start(f32[8,64,512]{2,1,0:T(8,128)} %get-tuple-element.198.refs_0_), channel_id=1, source_target_pairs={{0,4},{1,5},{2,6},{3,7},{4,0},{5,1},{6,2},{7,3},{8,12},{9,13},{10,... | collective-permute-start | bytes 3145736 | tf_op jit(solution)/shard_map/ppermute | solution.py:50
  264.6 32.8 %collective-permute-start.36 = (f32[2,512,256]{2,1,0:T(8,128)}, f32[2,512,256]{2,1,0:T(8,128)S(1)}, u32[]{:S(2)}, u32[]{:S(2)}) collective-permute-start(f32[2,512,256]{2,1,0:T(8,128)} %get-tuple-element.208), channel_id=1, source_target_pairs={{0,1},{1,0},{2,3},{3,2},{4,5},{5,4},{6,7},{7,6},{8,9},{9,8},{10,11... | collective-permute-start | bytes 3145736 | tf_op jit(solution)/shard_map/ppermute | solution.py:50
  294.4 6.1 %collective-permute-start.37 = (f32[2,512,256]{2,1,0:T(8,128)}, f32[2,512,256]{2,1,0:T(8,128)S(1)}, u32[]{:S(2)}, u32[]{:S(2)}) collective-permute-start(f32[2,512,256]{2,1,0:T(8,128)} %get-tuple-element.210), channel_id=1, source_target_pairs={{0,1},{1,0},{2,3},{3,2},{4,5},{5,4},{6,7},{7,6},{8,9},{9,8},{10,11... | collective-permute-start | bytes 3145736 | tf_op jit(solution)/shard_map/ppermute | solution.py:50
  294.5 14.6 %collective-permute-start.33 = (f32[4,64,512]{2,1,0:T(8,128)}, f32[4,64,512]{2,1,0:T(8,128)S(1)}, u32[]{:S(2)}, u32[]{:S(2)}) collective-permute-start(f32[4,64,512]{2,1,0:T(8,128)} %get-tuple-element.204), channel_id=1, source_target_pairs={{0,2},{1,3},{2,0},{3,1},{4,6},{5,7},{6,4},{7,5},{8,10},{9,11},{10,... | collective-permute-start | bytes 1572872 | tf_op jit(solution)/shard_map/ppermute | solution.py:50
  295.9 14.2 %collective-permute-start.34 = (f32[4,64,512]{2,1,0:T(8,128)}, f32[4,64,512]{2,1,0:T(8,128)S(1)}, u32[]{:S(2)}, u32[]{:S(2)}) collective-permute-start(f32[4,64,512]{2,1,0:T(8,128)} %get-tuple-element.205), channel_id=1, source_target_pairs={{0,8},{1,9},{2,10},{3,11},{4,12},{5,13},{6,14},{7,15},{8,0},{9,1},... | collective-permute-start | bytes 1572872 | tf_op jit(solution)/shard_map/ppermute | solution.py:50
  296.8 13.9 %collective-permute-start.35 = (f32[4,64,512]{2,1,0:T(8,128)}, f32[4,64,512]{2,1,0:T(8,128)S(1)}, u32[]{:S(2)}, u32[]{:S(2)}) collective-permute-start(f32[4,64,512]{2,1,0:T(8,128)} %get-tuple-element.206), channel_id=1, source_target_pairs={{0,4},{1,5},{2,6},{3,7},{4,0},{5,1},{6,2},{7,3},{8,12},{9,13},{10,... | collective-permute-start | bytes 1572872 | tf_op jit(solution)/shard_map/ppermute | solution.py:50
  297.5 34.2 %collective-permute-start.48 = (f32[3,1,64,384]{3,2,1,0:T(8,128)}, f32[3,1,64,384]{3,2,1,0:T(8,128)S(1)}, u32[]{:S(2)}, u32[]{:S(2)}) collective-permute-start(f32[3,1,64,384]{3,2,1,0:T(8,128)} %get-tuple-element.223), channel_id=1, source_target_pairs={{0,24},{1,25},{2,26},{3,27},{4,28},{5,29},{6,30},{7,31},{8,16},{9,... | collective-permute-start | bytes 884744 | tf_op jit(solution)/shard_map/ppermute | solution.py:50
  314.5 8.9 %collective-permute-start.38 = (f32[2,64,512]{2,1,0:T(8,128)}, f32[2,64,512]{2,1,0:T(8,128)S(1)}, u32[]{:S(2)}, u32[]{:S(2)}) collective-permute-start(f32[2,64,512]{2,1,0:T(8,128)} %get-tuple-element.215), channel_id=1, source_target_pairs={{0,8},{1,9},{2,10},{3,11},{4,12},{5,13},{6,14},{7,15},{8,0},{9,1},... | collective-permute-start | bytes 786440 | tf_op jit(solution)/shard_map/ppermute | solution.py:50
  315.7 7.6 %collective-permute-start.39 = (f32[2,64,512]{2,1,0:T(8,128)}, f32[2,64,512]{2,1,0:T(8,128)S(1)}, u32[]{:S(2)}, u32[]{:S(2)}) collective-permute-start(f32[2,64,512]{2,1,0:T(8,128)} %get-tuple-element.216), channel_id=1, source_target_pairs={{0,4},{1,5},{2,6},{3,7},{4,0},{5,1},{6,2},{7,3},{8,12},{9,13},{10,... | collective-permute-start | bytes 786440 | tf_op jit(solution)/shard_map/ppermute | solution.py:50
  316.4 7.5 %collective-permute-start.40 = (f32[2,64,512]{2,1,0:T(8,128)}, f32[2,64,512]{2,1,0:T(8,128)S(1)}, u32[]{:S(2)}, u32[]{:S(2)}) collective-permute-start(f32[2,64,512]{2,1,0:T(8,128)} %get-tuple-element.217), channel_id=1, source_target_pairs={{0,2},{1,3},{2,0},{3,1},{4,6},{5,7},{6,4},{7,5},{8,10},{9,11},{10,... | collective-permute-start | bytes 786440 | tf_op jit(solution)/shard_map/ppermute | solution.py:50
  319.8 15.4 %collective-permute-start.42 = (f32[344,128]{1,0:T(8,128)S(1)}, f32[344,128]{1,0:T(8,128)S(1)}, u32[]{:S(2)}, u32[]{:S(2)}) collective-permute-start(f32[344,128]{1,0:T(8,128)S(1)} %slice.278), channel_id=1, source_target_pairs={{0,2},{1,3},{2,0},{3,1},{4,6},{5,7},{6,4},{7,5},{8,10},{9,11},{10,... | collective-permute-start | bytes 528392 | tf_op jit(solution)/shard_map/ppermute | solution.py:50
  327.0 25.1 %collective-permute-start.47 = (f32[3,1,64,512]{3,2,1,0:T(8,128)}, f32[3,1,64,512]{3,2,1,0:T(8,128)S(1)}, u32[]{:S(2)}, u32[]{:S(2)}) collective-permute-start(f32[3,1,64,512]{3,2,1,0:T(8,128)} %get-tuple-element.222), channel_id=1, source_target_pairs={{0,24},{1,25},{2,26},{3,27},{4,28},{5,29},{6,30},{7,31},{8,16},{9,... | collective-permute-start | bytes 1179656 | tf_op jit(solution)/shard_map/ppermute | solution.py:50
  337.0 7.6 %collective-permute-start.44 = (f32[344,128]{1,0:T(8,128)S(1)}, f32[344,128]{1,0:T(8,128)S(1)}, u32[]{:S(2)}, u32[]{:S(2)}) collective-permute-start(f32[344,128]{1,0:T(8,128)S(1)} %pad_maximum_fusion.8), channel_id=1, source_target_pairs={{0,8},{1,9},{2,10},{3,11},{4,12},{5,13},{6,14},{7,15},{8,0},{9,1},... | collective-permute-start | bytes 528392 | tf_op jit(solution)/shard_map/ppermute | solution.py:50
  338.1 10.4 %collective-permute-start.45 = (f32[344,128]{1,0:T(8,128)S(1)}, f32[344,128]{1,0:T(8,128)S(1)}, u32[]{:S(2)}, u32[]{:S(2)}) collective-permute-start(f32[344,128]{1,0:T(8,128)S(1)} %pad_maximum_fusion.8), channel_id=1, source_target_pairs={{0,12},{1,13},{2,14},{3,15},{4,8},{5,9},{6,10},{7,11},{8,4},{9,5},... | collective-permute-start | bytes 528392 | tf_op jit(solution)/shard_map/ppermute | solution.py:50
  340.5 8.8 %collective-permute-start.43 = (f32[344,128]{1,0:T(8,128)S(1)}, f32[344,128]{1,0:T(8,128)S(1)}, u32[]{:S(2)}, u32[]{:S(2)}) collective-permute-start(f32[344,128]{1,0:T(8,128)S(1)} %pad_maximum_fusion.8), channel_id=1, source_target_pairs={{0,4},{1,5},{2,6},{3,7},{4,0},{5,1},{6,2},{7,3},{8,12},{9,13},{10,... | collective-permute-start | bytes 528392 | tf_op jit(solution)/shard_map/ppermute | solution.py:50
  349.4 13.4 %collective-permute-start.46 = (f32[344,128]{1,0:T(8,128)S(1)}, f32[344,128]{1,0:T(8,128)S(1)}, u32[]{:S(2)}, u32[]{:S(2)}) collective-permute-start(f32[344,128]{1,0:T(8,128)S(1)} %add_add_fusion), channel_id=1, source_target_pairs={{0,24},{1,25},{2,26},{3,27},{4,28},{5,29},{6,30},{7,31},{8,16},{9,... | collective-permute-start | bytes 528392 | tf_op jit(solution)/shard_map/ppermute | solution.py:50
  (63 other events, 382.1 us)
Sparse Core Ops, SparseCore 0:
  12.6 80.1 all-gather.2

commit v5 on v4

--- a/solution.py
+++ b/solution.py
@@ -454,10 +454,11 @@
             scores = dot(keys, jnp.where(mine, q_turned[:, part], none))
             probs = jnp.exp2(scores * scale_two - logsum_ref[0, head : head + 1, part])
             g_probs = dot(values, jnp.where(mine, g_turned[:, part], none))
-            inner = column_sum(probs * g_probs)
-            g_scores = (probs * (g_probs - inner)).astype(brain)
+            product = probs * g_probs
+            inner = column_sum(product)
+            g_scores = (product - probs * inner).astype(brain)
             dv = dot(probs.astype(brain), jnp.where(mine_low, grad[part, :], none_low))
-            dk = dot(g_scores, jnp.where(mine_low, q[part, :], none_low)) * scale
+            dk = dot(g_scores, jnp.where(mine_low, q[part, :], none_low))
             if start == 0 and head == 0:
                 own_ref[0] = dk[:own]
                 own_ref[1] = dv[:own]
@@ -470,6 +471,8 @@
                 other_ref[1] += dv[own:]
             dq = jnp.where(mine, dot(k_turned, g_scores), dq)
         dq_ref[part, :] = (dq * scale).T
+    own_ref[0] = own_ref[0] * scale
+    other_ref[0] = other_ref[0] * scale
 
 
 def attend_back(q, kv_own, kv_other, grad, logsum, heads, me, turns, tensors, after=()):

time: 379 us -> 378 us (level)
  transfers between devices with their start and end apart: 50 -> 50, of which waited for: 17 -> 16; matrix products, arithmetic and copies ran while one was open for 6% -> 6% of each run, Pallas kernels for 48% -> 48%
where the time goes in v5:
time: 378 us; the launch traced here: 370 us
  Pallas kernels  213 us (56%)
  starting transfers between devices  55.1 us (15%)
  waiting for transfers between devices  37.8 us (10%)
  local copies, waits for them, and re-layouts  28 us (7%)
  other arithmetic  19.2 us (5%)
  between operations  16.7 us (4%)
    pallas_call x4, Pallas kernels, attend_back(): pl.pallas_call(functools.partial(attend_back_kernel, heads, own, len(afte...  69.3 us
    pallas_call x5, Pallas kernels, call(): pl.pallas_call(kernel, grid=(1,), in_specs=in_specs, out_specs=[*after_sp...  65.7 us
    ppermute x49, starting transfers between devices, swap(): return lax.ppermute(x, ('dp', 'tensor'), pairs)  55.1 us
    ppermute x49, waiting for transfers between devices, swap(): return lax.ppermute(x, ('dp', 'tensor'), pairs)  35.9 us
    pallas_call x2, Pallas kernels, attend(): pl.pallas_call(follow(functools.partial(attend_kernel, heads), 3, after),...  35.8 us
    pallas_call x8, Pallas kernels, halve(): pl.pallas_call(functools.partial(halve_kernel, count, together, stacked,...  24.1 us
    unnamed x127, local copies, waits for them, and re-layouts  16 us
    pallas_call x4, Pallas kernels, join(): pl.pallas_call(functools.partial(join_kernel, count, together, stacked, s...  10.1 us
  transfers between devices with their start and end apart: 50, of which 16 were waited for; matrix products, arithmetic and copies ran while one was open for 6% of the time, Pallas kernels for 48%

profile of v5, /device:TPU:0, one launch (start us, length us, event | category | flops | bytes accessed | tf_op | source)
XLA Modules:
  0.0 370.2 jit_solution(4140440785603443476)
XLA Ops:
  14.6 3.0 collective-permute-start
  17.8 3.7 collective-permute-start.5
  22.3 6.4 %collective-permute-done.1 = f32[40,384]{1,0:T(8,128)S(1)} collective-permute-done((f32[40,384]{1,0:T(8,128)S(1)}, f32[40,384]{1,0:T(8,128)S(1)}, u32[]{:S(2)}, u32[]{:S(2)}) %collective-permute-start.1) | collective-permute-done | bytes 61472 | tf_op jit(solution)/shard_map/ppermute | solution.py:50
  28.7 3.7 collective-permute-start.2
  32.4 3.1 collective-permute-done.2
  37.6 2.8 collective-permute-done.3
  45.1 1.8 join.4
  52.0 6.2 %embed.1 = (bf16[512,512]{1,0:T(8,128)(2,1)}, bf16[2,512,512]{2,1,0:T(8,128)(2,1)}, bf16[2,512,512]{2,1,0:T(8,128)(2,1)}, f32[512,512]{1,0:T(8,128)}) custom-call(f32[4,40,384]{2,1,0:T(8,128)} %bitcast.247, s32[1,1024]{1,0:T(1,128)} %bitcast.269, bf16[64,512]{1,0:T(8,128)(2,1)} %pad.63.vocab_ref.refs_12_, f32[1024,128]{1,0:T(8,128)} %pad.64.cos_ref, ...), custom_call_target="tpu_custom_call" | custom-call | tf_op jit(solution)/shard_map/embed/pallas_call | solution.py:334
  58.9 2.1 join.5
  63.3 18.0 %attend.2 = (bf16[512,512]{1,0:T(8,128)(2,1)}, f32[4,8,512]{2,1,0:T(8,128)}) custom-call(bf16[512,512]{1,0:T(8,128)(2,1)} %get-tuple-element.143.q_ref.refs_6_, bf16[2,512,512]{2,1,0:T(8,128)(2,1)} %get-tuple-element.144.own_ref.kv_own_ref, bf16[2,512,512]{2,1,0:T(8,128)(2,1)} %get-tuple-element.145.other_ref.kv_other_ref), custom_call_target="tpu_custom_call" | custom-call | tf_op jit(solution)/shard_map/attend/pallas_call | solution.py:418
  82.2 2.5 join.6
  91.0 1.9 all-gather.3.cloned.1.call-done
  92.9 11.3 %middle.1 = (f32[512,512]{1,0:T(8,128)}, f32[512,512]{1,0:T(8,128)}, bf16[512,512]{1,0:T(8,128)(2,1)}, bf16[2,512,512]{2,1,0:T(8,128)(2,1)}) custom-call(bf16[512,512]{1,0:T(8,128)(2,1)} %get-tuple-element.146.mixed_ref.refs_10_, f32[512,512]{1,0:T(8,128)} %get-tuple-element.147.resid_ref, bf16[8,4,64,1536]{3,2,1,0:T(8,128)(2,1)} %bitcast.241, ...), custom_call_target="tpu_custom_call" | custom-call | tf_op jit(solution)/shard_map/middle/pallas_call | solution.py:334
  105.3 3.6 join.7
  109.2 2.6 collective-permute-done.15.other_ref.refs_1_.kv_other_ref
  115.0 17.7 %attend.3 = (bf16[512,512]{1,0:T(8,128)(2,1)}, f32[4,8,512]{2,1,0:T(8,128)}) custom-call(bf16[512,512]{1,0:T(8,128)(2,1)} %get-tuple-element.148.q_ref, bf16[2,512,512]{2,1,0:T(8,128)(2,1)} %get-tuple-element.161.own_ref.kv_own_ref, bf16[2,512,512]{2,1,0:T(8,128)(2,1)} %copy-done), custom_call_target="tpu_custom_call" | custom-call | tf_op jit(solution)/shard_map/attend/pallas_call | solution.py:418
  132.7 1.7 copy-done.1
  134.4 19.8 %top.1 = (f32[3,16,64,384]{3,2,1,0:T(8,128)}, f32[3,16,64,384]{3,2,1,0:T(8,128)}, f32[512,512]{1,0:T(8,128)}, bf16[512,512]{1,0:T(8,128)(2,1)}, f32[16,512]{1,0:T(8,128)}, /*index=5*/f32[40,512]{1,0:T(8,128)}) custom-call(s32[1]{0:T(128)} %bitcast.me_ref.refs_0_, bf16[512,512]{1,0:T(8,128)(2,1)} %get-tuple-element.162.mixed_ref, ...), custom_call_target="tpu_custom_call" | custom-call | tf_op jit(solution)/shard_map/top/pallas_call | solution.py:334
  154.5 17.2 %attend_back.4 = (f32[512,256]{1,0:T(8,128)}, f32[2,512,256]{2,1,0:T(8,128)}, f32[2,512,256]{2,1,0:T(8,128)}) custom-call(s32[1]{0:T(128)} %bitcast.me_ref.refs_0_, bf16[512,512]{1,0:T(8,128)(2,1)} %get-tuple-element.148.q_ref, bf16[2,512,512]{2,1,0:T(8,128)(2,1)} %get-tuple-element.161.own_ref.kv_own_ref, bf16[2,512,512]{2,1,0:T(8,128)(2,1)} %copy-done, ...), custom_call_target="tpu_custom_call" | custom-call | tf_op jit(solution)/shard_map/attend_back/pallas_call | solution.py:492
  171.7 3.5 send_upper.2
  176.6 2.4 collective-permute-start.21
  179.0 1.7 collective-permute-start.19
  180.7 17.5 %attend_back.5 = (f32[512,256]{1,0:T(8,128)}, f32[2,512,256]{2,1,0:T(8,128)}, f32[2,512,256]{2,1,0:T(8,128)}) custom-call(s32[1]{0:T(128)} %bitcast.me_ref.refs_0_, bf16[512,512]{1,0:T(8,128)(2,1)} %get-tuple-element.148.q_ref, bf16[2,512,512]{2,1,0:T(8,128)(2,1)} %get-tuple-element.161.own_ref.kv_own_ref, bf16[2,512,512]{2,1,0:T(8,128)(2,1)} %copy-done, ...), custom_call_target="tpu_custom_call" | custom-call | tf_op jit(solution)/shard_map/attend_back/pallas_call | solution.py:492
  199.6 4.4 %halve.8 = (f32[3,4,64,384]{3,2,1,0:T(8,128)}, f32[4,64,384]{2,1,0:T(8,128)}, f32[4,64,384]{2,1,0:T(8,128)}, f32[4,64,384]{2,1,0:T(8,128)}, f32[2,512,256]{2,1,0:T(8,128)}) custom-call(f32[3,16,64,384]{3,2,1,0:T(8,128)} %get-tuple-element.168.keep_ref.refs_0_, ...), custom_call_target="tpu_custom_call", output_to_operand_aliasing={{4}: (5, {})} | custom-call | tf_op jit(solution)/shard_map/halve/pallas_call | solution.py:999
  204.8 1.7 collective-permute-start.25
  208.0 21.4 %lower.1 = (f32[3,16,64,512]{3,2,1,0:T(8,128)}, f32[3,16,64,512]{3,2,1,0:T(8,128)}, f32[512,512]{1,0:T(8,128)}, bf16[512,512]{1,0:T(8,128)(2,1)}, f32[16,512]{1,0:T(8,128)}) custom-call(s32[1]{0:T(128)} %bitcast.me_ref.refs_0_, f32[512,256]{1,0:T(8,128)} %get-tuple-element.166.refs_1_, f32[2,512,256]{2,1,0:T(8,128)} %get-tuple-element.167.refs_2_, ...), custom_call_target="tpu_custom_call" | custom-call | tf_op jit(solution)/shard_map/lower/pallas_call | solution.py:334
  230.4 2.6 halve.9
  234.9 2.0 collective-permute-start.29
  236.9 17.2 %attend_back.6 = (f32[512,256]{1,0:T(8,128)}, f32[2,512,256]{2,1,0:T(8,128)}, f32[2,512,256]{2,1,0:T(8,128)}) custom-call(s32[1]{0:T(128)} %bitcast.me_ref.refs_0_, bf16[512,512]{1,0:T(8,128)(2,1)} %get-tuple-element.143.q_ref.refs_6_, bf16[2,512,512]{2,1,0:T(8,128)(2,1)} %get-tuple-element.144.own_ref.kv_own_ref, ...), custom_call_target="tpu_custom_call" | custom-call | tf_op jit(solution)/shard_map/attend_back/pallas_call | solution.py:492
  255.0 2.2 halve.10
  257.2 4.3 %send_upper.3 = (f32[8,64,512]{2,1,0:T(8,128)}, f32[8,64,512]{2,1,0:T(8,128)}, f32[8,64,512]{2,1,0:T(8,128)}) custom-call(f32[3,16,64,512]{3,2,1,0:T(8,128)} %get-tuple-element.183.keep_ref.refs_0_, f32[3,16,64,512]{3,2,1,0:T(8,128)} %collective-permute-done.26.got_ref.refs_1_, f32[3,1,64,384]{3,2,1,0:T(8,128)} %get-tuple-element.197.refs_0_), custom_call_target="tpu_custom_call" | custom-call | tf_op jit(solution)/shard_map/send_upper/pallas_call | solution.py:934
  263.9 17.4 %attend_back.7 = (f32[512,256]{1,0:T(8,128)}, f32[2,512,256]{2,1,0:T(8,128)}, f32[2,512,256]{2,1,0:T(8,128)}) custom-call(s32[1]{0:T(128)} %bitcast.me_ref.refs_0_, bf16[512,512]{1,0:T(8,128)(2,1)} %get-tuple-element.143.q_ref.refs_6_, bf16[2,512,512]{2,1,0:T(8,128)(2,1)} %get-tuple-element.144.own_ref.kv_own_ref, ...), custom_call_target="tpu_custom_call" | custom-call | tf_op jit(solution)/shard_map/attend_back/pallas_call | solution.py:492
  281.3 5.0 %collective-permute-done.31.refs_3_ = f32[8,64,512]{2,1,0:T(8,128)S(1)} collective-permute-done((f32[8,64,512]{2,1,0:T(8,128)}, f32[8,64,512]{2,1,0:T(8,128)S(1)}, u32[]{:S(2)}, u32[]{:S(2)}) %collective-permute-start.31) | collective-permute-done | bytes 1048608 | tf_op jit(solution)/shard_map/ppermute | solution.py:50
  287.7 6.0 %halve.11 = (f32[3,4,64,512]{3,2,1,0:T(8,128)}, f32[4,64,512]{2,1,0:T(8,128)}, f32[4,64,512]{2,1,0:T(8,128)}, f32[4,64,512]{2,1,0:T(8,128)}, f32[2,512,256]{2,1,0:T(8,128)}) custom-call(f32[3,16,64,512]{3,2,1,0:T(8,128)} %get-tuple-element.183.keep_ref.refs_0_, ...), custom_call_target="tpu_custom_call", output_to_operand_aliasing={{4}: (5, {})} | custom-call | tf_op jit(solution)/shard_map/halve/pallas_call | solution.py:999
  297.0 2.5 collective-permute-start.48
  301.1 7.2 %bottom.1 = (f32[464,128]{1,0:T(8,128)}, f32[464,128]{1,0:T(8,128)}, f32[16,512]{1,0:T(8,128)}) custom-call(s32[1]{0:T(128)} %bitcast.me_ref.refs_0_, f32[512,256]{1,0:T(8,128)} %get-tuple-element.196.refs_5_.refs_1_, f32[2,512,256]{2,1,0:T(8,128)} %get-tuple-element.207.refs_2_, f32[2,512,256]{2,1,0:T(8,128)} %copy-done.5, ...), custom_call_target="tpu_custom_call" | custom-call | tf_op jit(solution)/shard_map/bottom/pallas_call | solution.py:334
  310.8 3.0 halve.12
  316.6 1.7 collective-permute-done.41
  320.8 1.9 collective-permute-done.38.refs_1_
  324.2 2.3 halve.13
  326.6 2.5 collective-permute-start.47
  329.8 1.8 halve.15
  334.5 2.5 collective-permute-start.45
  338.2 5.0 %collective-permute-done.44 = f32[344,128]{1,0:T(8,128)S(1)} collective-permute-done((f32[344,128]{1,0:T(8,128)S(1)}, f32[344,128]{1,0:T(8,128)S(1)}, u32[]{:S(2)}, u32[]{:S(2)}) %collective-permute-start.44) | collective-permute-done | bytes 176160 | tf_op jit(solution)/shard_map/ppermute | solution.py:50
  343.2 3.3 collective-permute-done.45
  348.7 1.9 halve.14
  352.4 2.5 fusion.52
  361.6 1.5 fusion.58
  (320 shorter events, 75.5 us)
Async XLA Ops:
  7.2 85.6 %all-gather.3.cloned.1.call-start = ((), (), s32[]{:S(2)}) async-start(), calls=%async_computation | async-start | bytes 6488064 | tf_op jit(solution)/shard_map/all_gather | solution.py:1187
  14.6 7.1 %collective-permute-start = (f32[40,384]{1,0:T(8,128)S(1)}, f32[40,384]{1,0:T(8,128)S(1)}, u32[]{:S(2)}, u32[]{:S(2)}) collective-permute-start(f32[40,384]{1,0:T(8,128)S(1)} %select_maximum_fusion), channel_id=1, source_target_pairs={{0,4},{1,5},{2,6},{3,7},{4,0},{5,1},{6,2},{7,3},{8,12},{9,13},{10,... | collective-permute-start | bytes 184328 | tf_op jit(solution)/shard_map/ppermute | solution.py:50
  17.8 25.9 %collective-permute-start.5 = (bf16[3,1,64,512]{3,2,1,0:T(8,128)(2,1)S(1)}, bf16[3,1,64,512]{3,2,1,0:T(8,128)(2,1)S(1)}, u32[]{:S(2)}, u32[]{:S(2)}) collective-permute-start(bf16[3,1,64,512]{3,2,1,0:T(8,128)(2,1)S(1)} %maximum_bitcast_fusion.refs_0_), channel_id=1, source_target_pairs={{0,24},{1,25},{2,26},{3,27},{4,28},{5,29},{6,30},{7,31},{8,16},{9,... | collective-permute-start | bytes 589832 | tf_op jit(solution)/shard_map/ppermute | solution.py:50
  21.7 7.0 %collective-permute-start.1 = (f32[40,384]{1,0:T(8,128)S(1)}, f32[40,384]{1,0:T(8,128)S(1)}, u32[]{:S(2)}, u32[]{:S(2)}) collective-permute-start(f32[40,384]{1,0:T(8,128)S(1)} %fusion.66), channel_id=1, source_target_pairs={{0,8},{1,9},{2,10},{3,11},{4,12},{5,13},{6,14},{7,15},{8,0},{9,1},... | collective-permute-start | bytes 184328 | tf_op jit(solution)/shard_map/ppermute | solution.py:50
  28.7 6.8 %collective-permute-start.2 = (f32[40,384]{1,0:T(8,128)S(1)}, f32[40,384]{1,0:T(8,128)S(1)}, u32[]{:S(2)}, u32[]{:S(2)}) collective-permute-start(f32[40,384]{1,0:T(8,128)S(1)} %add.240), channel_id=1, source_target_pairs={{0,24},{1,25},{2,26},{3,27},{4,28},{5,29},{6,30},{7,31},{8,16},{9,... | collective-permute-start | bytes 184328 | tf_op jit(solution)/shard_map/ppermute | solution.py:50
  36.1 4.2 %collective-permute-start.3 = (f32[40,384]{1,0:T(8,128)S(1)}, f32[40,384]{1,0:T(8,128)S(1)}, u32[]{:S(2)}, u32[]{:S(2)}) collective-permute-start(f32[40,384]{1,0:T(8,128)S(1)} %pad_dynamic-update-slice_fusion), channel_id=1, source_target_pairs={{0,2},{1,3},{2,0},{3,1},{4,6},{5,7},{6,4},{7,5},{8,10},{9,11},{10,... | collective-permute-start | bytes 184328 | tf_op jit(solution)/shard_map/ppermute | solution.py:50
  40.3 3.3 collective-permute-start.4
  46.8 11.3 %collective-permute-start.6 = (bf16[2,64,512]{2,1,0:T(8,128)(2,1)}, bf16[2,64,512]{2,1,0:T(8,128)(2,1)S(1)}, u32[]{:S(2)}, u32[]{:S(2)}) collective-permute-start(bf16[2,64,512]{2,1,0:T(8,128)(2,1)} %get-tuple-element.149.refs_0_), channel_id=1, source_target_pairs={{0,4},{1,5},{2,6},{3,7},{4,0},{5,1},{6,2},{7,3},{8,12},{9,13},{10,... | collective-permute-start | bytes 393224 | tf_op jit(solution)/shard_map/ppermute | solution.py:50
  48.0 10.2 %collective-permute-start.7 = (bf16[2,64,512]{2,1,0:T(8,128)(2,1)}, bf16[2,64,512]{2,1,0:T(8,128)(2,1)S(1)}, u32[]{:S(2)}, u32[]{:S(2)}) collective-permute-start(bf16[2,64,512]{2,1,0:T(8,128)(2,1)} %get-tuple-element.150.refs_1_), channel_id=1, source_target_pairs={{0,2},{1,3},{2,0},{3,1},{4,6},{5,7},{6,4},{7,5},{8,10},{9,11},{10,... | collective-permute-start | bytes 393224 | tf_op jit(solution)/shard_map/ppermute | solution.py:50
  49.3 8.9 %collective-permute-start.8 = (bf16[2,64,512]{2,1,0:T(8,128)(2,1)}, bf16[2,64,512]{2,1,0:T(8,128)(2,1)S(1)}, u32[]{:S(2)}, u32[]{:S(2)}) collective-permute-start(bf16[2,64,512]{2,1,0:T(8,128)(2,1)} %get-tuple-element.151.refs_2_), channel_id=1, source_target_pairs={{0,8},{1,9},{2,10},{3,11},{4,12},{5,13},{6,14},{7,15},{8,0},{9,1},... | collective-permute-start | bytes 393224 | tf_op jit(solution)/shard_map/ppermute | solution.py:50
  61.0 20.3 %collective-permute-start.9 = (bf16[4,64,512]{2,1,0:T(8,128)(2,1)}, bf16[4,64,512]{2,1,0:T(8,128)(2,1)S(1)}, u32[]{:S(2)}, u32[]{:S(2)}) collective-permute-start(bf16[4,64,512]{2,1,0:T(8,128)(2,1)} %get-tuple-element.152.refs_0_), channel_id=1, source_target_pairs={{0,2},{1,3},{2,0},{3,1},{4,6},{5,7},{6,4},{7,5},{8,10},{9,11},{10,... | collective-permute-start | bytes 786440 | tf_op jit(solution)/shard_map/ppermute | solution.py:50
  61.8 19.6 %collective-permute-start.10 = (bf16[4,64,512]{2,1,0:T(8,128)(2,1)}, bf16[4,64,512]{2,1,0:T(8,128)(2,1)S(1)}, u32[]{:S(2)}, u32[]{:S(2)}) collective-permute-start(bf16[4,64,512]{2,1,0:T(8,128)(2,1)} %get-tuple-element.153.refs_1_), channel_id=1, source_target_pairs={{0,8},{1,9},{2,10},{3,11},{4,12},{5,13},{6,14},{7,15},{8,0},{9,1},... | collective-permute-start | bytes 786440 | tf_op jit(solution)/shard_map/ppermute | solution.py:50
  62.5 18.8 %collective-permute-start.11 = (bf16[4,64,512]{2,1,0:T(8,128)(2,1)}, bf16[4,64,512]{2,1,0:T(8,128)(2,1)S(1)}, u32[]{:S(2)}, u32[]{:S(2)}) collective-permute-start(bf16[4,64,512]{2,1,0:T(8,128)(2,1)} %get-tuple-element.154.refs_2_), channel_id=1, source_target_pairs={{0,4},{1,5},{2,6},{3,7},{4,0},{5,1},{6,2},{7,3},{8,12},{9,13},{10,... | collective-permute-start | bytes 786440 | tf_op jit(solution)/shard_map/ppermute | solution.py:50
  84.8 19.4 %collective-permute-start.12 = (bf16[8,64,512]{2,1,0:T(8,128)(2,1)}, bf16[8,64,512]{2,1,0:T(8,128)(2,1)S(1)}, u32[]{:S(2)}, u32[]{:S(2)}) collective-permute-start(bf16[8,64,512]{2,1,0:T(8,128)(2,1)} %get-tuple-element.156.refs_0_), channel_id=1, source_target_pairs={{0,8},{1,9},{2,10},{3,11},{4,12},{5,13},{6,14},{7,15},{8,0},{9,1},... | collective-permute-start | bytes 1572872 | tf_op jit(solution)/shard_map/ppermute | solution.py:50
  86.2 18.0 %collective-permute-start.13 = (bf16[8,64,512]{2,1,0:T(8,128)(2,1)}, bf16[8,64,512]{2,1,0:T(8,128)(2,1)S(1)}, u32[]{:S(2)}, u32[]{:S(2)}) collective-permute-start(bf16[8,64,512]{2,1,0:T(8,128)(2,1)} %get-tuple-element.157.refs_1_), channel_id=1, source_target_pairs={{0,4},{1,5},{2,6},{3,7},{4,0},{5,1},{6,2},{7,3},{8,12},{9,13},{10,... | collective-permute-start | bytes 1572872 | tf_op jit(solution)/shard_map/ppermute | solution.py:50
  87.3 16.9 %collective-permute-start.14 = (bf16[8,64,512]{2,1,0:T(8,128)(2,1)}, bf16[8,64,512]{2,1,0:T(8,128)(2,1)S(1)}, u32[]{:S(2)}, u32[]{:S(2)}) collective-permute-start(bf16[8,64,512]{2,1,0:T(8,128)(2,1)} %get-tuple-element.158.refs_2_), channel_id=1, source_target_pairs={{0,2},{1,3},{2,0},{3,1},{4,6},{5,7},{6,4},{7,5},{8,10},{9,11},{10,... | collective-permute-start | bytes 1572872 | tf_op jit(solution)/shard_map/ppermute | solution.py:50
  112.8 19.9 %collective-permute-start.16 = (bf16[3,16,64,512]{3,2,1,0:T(8,128)(2,1)}, bf16[3,16,64,512]{3,2,1,0:T(8,128)(2,1)S(1)}, u32[]{:S(2)}, u32[]{:S(2)}) collective-permute-start(bf16[3,16,64,512]{3,2,1,0:T(8,128)(2,1)} %wait_for.1.w_own_ref.refs_9_), channel_id=1, source_target_pairs={{0,1},{1,0},{2,3},{3,2},{4,5},{5,4},{6,7},{7,6},{8,9},{9,8},{10,11... | collective-permute-start | bytes 9437192 | tf_op jit(solution)/shard_map/ppermute | solution.py:50
  154.2 17.6 %collective-permute-start.17 = (f32[3,16,64,384]{3,2,1,0:T(8,128)}, f32[3,16,64,384]{3,2,1,0:T(8,128)}, u32[]{:S(2)}, u32[]{:S(2)}) collective-permute-start(f32[3,16,64,384]{3,2,1,0:T(8,128)} %get-tuple-element.169), channel_id=1, source_target_pairs={{0,1},{1,0},{2,3},{3,2},{4,5},{5,4},{6,7},{7,6},{8,9},{9,8},{10,11... | collective-permute-start | bytes 14155784 | tf_op jit(solution)/shard_map/ppermute | solution.py:50
  175.3 22.9 %collective-permute-start.20 = (f32[8,64,384]{2,1,0:T(8,128)}, f32[8,64,384]{2,1,0:T(8,128)S(1)}, u32[]{:S(2)}, u32[]{:S(2)}) collective-permute-start(f32[8,64,384]{2,1,0:T(8,128)} %get-tuple-element.175), channel_id=1, source_target_pairs={{0,2},{1,3},{2,0},{3,1},{4,6},{5,7},{6,4},{7,5},{8,10},{9,11},{10,... | collective-permute-start | bytes 2359304 | tf_op jit(solution)/shard_map/ppermute | solution.py:50
  176.6 21.6 %collective-permute-start.21 = (f32[8,64,384]{2,1,0:T(8,128)}, f32[8,64,384]{2,1,0:T(8,128)S(1)}, u32[]{:S(2)}, u32[]{:S(2)}) collective-permute-start(f32[8,64,384]{2,1,0:T(8,128)} %get-tuple-element.176), channel_id=1, source_target_pairs={{0,8},{1,9},{2,10},{3,11},{4,12},{5,13},{6,14},{7,15},{8,0},{9,1},... | collective-permute-start | bytes 2359304 | tf_op jit(solution)/shard_map/ppermute | solution.py:50
  179.0 19.4 %collective-permute-start.19 = (f32[8,64,384]{2,1,0:T(8,128)}, f32[8,64,384]{2,1,0:T(8,128)S(1)}, u32[]{:S(2)}, u32[]{:S(2)}) collective-permute-start(f32[8,64,384]{2,1,0:T(8,128)} %get-tuple-element.172.refs_0_), channel_id=1, source_target_pairs={{0,4},{1,5},{2,6},{3,7},{4,0},{5,1},{6,2},{7,3},{8,12},{9,13},{10,... | collective-permute-start | bytes 2359304 | tf_op jit(solution)/shard_map/ppermute | solution.py:50
  180.7 25.8 %collective-permute-start.18 = (f32[2,512,256]{2,1,0:T(8,128)}, f32[2,512,256]{2,1,0:T(8,128)S(1)}, u32[]{:S(2)}, u32[]{:S(2)}) collective-permute-start(f32[2,512,256]{2,1,0:T(8,128)} %get-tuple-element.171), channel_id=1, source_target_pairs={{0,1},{1,0},{2,3},{3,2},{4,5},{5,4},{6,7},{7,6},{8,9},{9,8},{10,11... | collective-permute-start | bytes 3145736 | tf_op jit(solution)/shard_map/ppermute | solution.py:50
  204.0 3.0 collective-permute-start.22
  204.5 24.8 %collective-permute-start.23 = (f32[4,64,384]{2,1,0:T(8,128)}, f32[4,64,384]{2,1,0:T(8,128)S(1)}, u32[]{:S(2)}, u32[]{:S(2)}) collective-permute-start(f32[4,64,384]{2,1,0:T(8,128)} %get-tuple-element.184), channel_id=1, source_target_pairs={{0,2},{1,3},{2,0},{3,1},{4,6},{5,7},{6,4},{7,5},{8,10},{9,11},{10,... | collective-permute-start | bytes 1179656 | tf_op jit(solution)/shard_map/ppermute | solution.py:50
  204.5 24.8 %collective-permute-start.24 = (f32[4,64,384]{2,1,0:T(8,128)}, f32[4,64,384]{2,1,0:T(8,128)S(1)}, u32[]{:S(2)}, u32[]{:S(2)}) collective-permute-start(f32[4,64,384]{2,1,0:T(8,128)} %get-tuple-element.185), channel_id=1, source_target_pairs={{0,8},{1,9},{2,10},{3,11},{4,12},{5,13},{6,14},{7,15},{8,0},{9,1},... | collective-permute-start | bytes 1179656 | tf_op jit(solution)/shard_map/ppermute | solution.py:50
  204.8 24.6 %collective-permute-start.25 = (f32[4,64,384]{2,1,0:T(8,128)}, f32[4,64,384]{2,1,0:T(8,128)S(1)}, u32[]{:S(2)}, u32[]{:S(2)}) collective-permute-start(f32[4,64,384]{2,1,0:T(8,128)} %get-tuple-element.186), channel_id=1, source_target_pairs={{0,4},{1,5},{2,6},{3,7},{4,0},{5,1},{6,2},{7,3},{8,12},{9,13},{10,... | collective-permute-start | bytes 1179656 | tf_op jit(solution)/shard_map/ppermute | solution.py:50
  233.0 24.2 %collective-permute-start.26 = (f32[3,16,64,512]{3,2,1,0:T(8,128)}, f32[3,16,64,512]{3,2,1,0:T(8,128)}, u32[]{:S(2)}, u32[]{:S(2)}) collective-permute-start(f32[3,16,64,512]{3,2,1,0:T(8,128)} %get-tuple-element.189), channel_id=1, source_target_pairs={{0,1},{1,0},{2,3},{3,2},{4,5},{5,4},{6,7},{7,6},{8,9},{9,8},{10,11... | collective-permute-start | bytes 18874376 | tf_op jit(solution)/shard_map/ppermute | solution.py:50
  233.4 20.8 %collective-permute-start.27 = (f32[2,64,384]{2,1,0:T(8,128)}, f32[2,64,384]{2,1,0:T(8,128)S(1)}, u32[]{:S(2)}, u32[]{:S(2)}) collective-permute-start(f32[2,64,384]{2,1,0:T(8,128)} %get-tuple-element.191), channel_id=1, source_target_pairs={{0,8},{1,9},{2,10},{3,11},{4,12},{5,13},{6,14},{7,15},{8,0},{9,1},... | collective-permute-start | bytes 589832 | tf_op jit(solution)/shard_map/ppermute | solution.py:50
  234.1 20.1 %collective-permute-start.28 = (f32[2,64,384]{2,1,0:T(8,128)}, f32[2,64,384]{2,1,0:T(8,128)S(1)}, u32[]{:S(2)}, u32[]{:S(2)}) collective-permute-start(f32[2,64,384]{2,1,0:T(8,128)} %get-tuple-element.192), channel_id=1, source_target_pairs={{0,4},{1,5},{2,6},{3,7},{4,0},{5,1},{6,2},{7,3},{8,12},{9,13},{10,... | collective-permute-start | bytes 589832 | tf_op jit(solution)/shard_map/ppermute | solution.py:50
  234.9 19.3 %collective-permute-start.29 = (f32[2,64,384]{2,1,0:T(8,128)}, f32[2,64,384]{2,1,0:T(8,128)S(1)}, u32[]{:S(2)}, u32[]{:S(2)}) collective-permute-start(f32[2,64,384]{2,1,0:T(8,128)} %get-tuple-element.193), channel_id=1, source_target_pairs={{0,2},{1,3},{2,0},{3,1},{4,6},{5,7},{6,4},{7,5},{8,10},{9,11},{10,... | collective-permute-start | bytes 589832 | tf_op jit(solution)/shard_map/ppermute | solution.py:50
  261.4 24.9 %collective-permute-start.31 = (f32[8,64,512]{2,1,0:T(8,128)}, f32[8,64,512]{2,1,0:T(8,128)S(1)}, u32[]{:S(2)}, u32[]{:S(2)}) collective-permute-start(f32[8,64,512]{2,1,0:T(8,128)} %get-tuple-element.199), channel_id=1, source_target_pairs={{0,2},{1,3},{2,0},{3,1},{4,6},{5,7},{6,4},{7,5},{8,10},{9,11},{10,... | collective-permute-start | bytes 3145736 | tf_op jit(solution)/shard_map/ppermute | solution.py:50
  261.5 24.9 %collective-permute-start.32 = (f32[8,64,512]{2,1,0:T(8,128)}, f32[8,64,512]{2,1,0:T(8,128)S(1)}, u32[]{:S(2)}, u32[]{:S(2)}) collective-permute-start(f32[8,64,512]{2,1,0:T(8,128)} %get-tuple-element.200), channel_id=1, source_target_pairs={{0,8},{1,9},{2,10},{3,11},{4,12},{5,13},{6,14},{7,15},{8,0},{9,1},... | collective-permute-start | bytes 3145736 | tf_op jit(solution)/shard_map/ppermute | solution.py:50
  262.9 24.3 %collective-permute-start.30 = (f32[8,64,512]{2,1,0:T(8,128)}, f32[8,64,512]{2,1,0:T(8,128)}, u32[]{:S(2)}, u32[]{:S(2)}) collective-permute-start(f32[8,64,512]{2,1,0:T(8,128)} %get-tuple-element.198.refs_0_), channel_id=1, source_target_pairs={{0,4},{1,5},{2,6},{3,7},{4,0},{5,1},{6,2},{7,3},{8,12},{9,13},{10,... | collective-permute-start | bytes 3145736 | tf_op jit(solution)/shard_map/ppermute | solution.py:50
  263.9 33.1 %collective-permute-start.36 = (f32[2,512,256]{2,1,0:T(8,128)}, f32[2,512,256]{2,1,0:T(8,128)S(1)}, u32[]{:S(2)}, u32[]{:S(2)}) collective-permute-start(f32[2,512,256]{2,1,0:T(8,128)} %get-tuple-element.208), channel_id=1, source_target_pairs={{0,1},{1,0},{2,3},{3,2},{4,5},{5,4},{6,7},{7,6},{8,9},{9,8},{10,11... | collective-permute-start | bytes 3145736 | tf_op jit(solution)/shard_map/ppermute | solution.py:50
  293.7 6.4 %collective-permute-start.37 = (f32[2,512,256]{2,1,0:T(8,128)}, f32[2,512,256]{2,1,0:T(8,128)S(1)}, u32[]{:S(2)}, u32[]{:S(2)}) collective-permute-start(f32[2,512,256]{2,1,0:T(8,128)} %get-tuple-element.210), channel_id=1, source_target_pairs={{0,1},{1,0},{2,3},{3,2},{4,5},{5,4},{6,7},{7,6},{8,9},{9,8},{10,11... | collective-permute-start | bytes 3145736 | tf_op jit(solution)/shard_map/ppermute | solution.py:50
  293.8 14.6 %collective-permute-start.33 = (f32[4,64,512]{2,1,0:T(8,128)}, f32[4,64,512]{2,1,0:T(8,128)S(1)}, u32[]{:S(2)}, u32[]{:S(2)}) collective-permute-start(f32[4,64,512]{2,1,0:T(8,128)} %get-tuple-element.204), channel_id=1, source_target_pairs={{0,2},{1,3},{2,0},{3,1},{4,6},{5,7},{6,4},{7,5},{8,10},{9,11},{10,... | collective-permute-start | bytes 1572872 | tf_op jit(solution)/shard_map/ppermute | solution.py:50
  295.2 14.2 %collective-permute-start.34 = (f32[4,64,512]{2,1,0:T(8,128)}, f32[4,64,512]{2,1,0:T(8,128)S(1)}, u32[]{:S(2)}, u32[]{:S(2)}) collective-permute-start(f32[4,64,512]{2,1,0:T(8,128)} %get-tuple-element.205), channel_id=1, source_target_pairs={{0,8},{1,9},{2,10},{3,11},{4,12},{5,13},{6,14},{7,15},{8,0},{9,1},... | collective-permute-start | bytes 1572872 | tf_op jit(solution)/shard_map/ppermute | solution.py:50
  296.0 13.9 %collective-permute-start.35 = (f32[4,64,512]{2,1,0:T(8,128)}, f32[4,64,512]{2,1,0:T(8,128)S(1)}, u32[]{:S(2)}, u32[]{:S(2)}) collective-permute-start(f32[4,64,512]{2,1,0:T(8,128)} %get-tuple-element.206), channel_id=1, source_target_pairs={{0,4},{1,5},{2,6},{3,7},{4,0},{5,1},{6,2},{7,3},{8,12},{9,13},{10,... | collective-permute-start | bytes 1572872 | tf_op jit(solution)/shard_map/ppermute | solution.py:50
  297.0 32.1 %collective-permute-start.48 = (f32[3,1,64,384]{3,2,1,0:T(8,128)}, f32[3,1,64,384]{3,2,1,0:T(8,128)S(1)}, u32[]{:S(2)}, u32[]{:S(2)}) collective-permute-start(f32[3,1,64,384]{3,2,1,0:T(8,128)} %get-tuple-element.223), channel_id=1, source_target_pairs={{0,24},{1,25},{2,26},{3,27},{4,28},{5,29},{6,30},{7,31},{8,16},{9,... | collective-permute-start | bytes 884744 | tf_op jit(solution)/shard_map/ppermute | solution.py:50
  313.8 8.9 %collective-permute-start.38 = (f32[2,64,512]{2,1,0:T(8,128)}, f32[2,64,512]{2,1,0:T(8,128)S(1)}, u32[]{:S(2)}, u32[]{:S(2)}) collective-permute-start(f32[2,64,512]{2,1,0:T(8,128)} %get-tuple-element.215), channel_id=1, source_target_pairs={{0,8},{1,9},{2,10},{3,11},{4,12},{5,13},{6,14},{7,15},{8,0},{9,1},... | collective-permute-start | bytes 786440 | tf_op jit(solution)/shard_map/ppermute | solution.py:50
  315.0 7.6 %collective-permute-start.39 = (f32[2,64,512]{2,1,0:T(8,128)}, f32[2,64,512]{2,1,0:T(8,128)S(1)}, u32[]{:S(2)}, u32[]{:S(2)}) collective-permute-start(f32[2,64,512]{2,1,0:T(8,128)} %get-tuple-element.216), channel_id=1, source_target_pairs={{0,4},{1,5},{2,6},{3,7},{4,0},{5,1},{6,2},{7,3},{8,12},{9,13},{10,... | collective-permute-start | bytes 786440 | tf_op jit(solution)/shard_map/ppermute | solution.py:50
  316.0 7.5 %collective-permute-start.40 = (f32[2,64,512]{2,1,0:T(8,128)}, f32[2,64,512]{2,1,0:T(8,128)S(1)}, u32[]{:S(2)}, u32[]{:S(2)}) collective-permute-start(f32[2,64,512]{2,1,0:T(8,128)} %get-tuple-element.217), channel_id=1, source_target_pairs={{0,2},{1,3},{2,0},{3,1},{4,6},{5,7},{6,4},{7,5},{8,10},{9,11},{10,... | collective-permute-start | bytes 786440 | tf_op jit(solution)/shard_map/ppermute | solution.py:50
  319.3 13.3 %collective-permute-start.42 = (f32[344,128]{1,0:T(8,128)S(1)}, f32[344,128]{1,0:T(8,128)S(1)}, u32[]{:S(2)}, u32[]{:S(2)}) collective-permute-start(f32[344,128]{1,0:T(8,128)S(1)} %slice.278), channel_id=1, source_target_pairs={{0,2},{1,3},{2,0},{3,1},{4,6},{5,7},{6,4},{7,5},{8,10},{9,11},{10,... | collective-permute-start | bytes 528392 | tf_op jit(solution)/shard_map/ppermute | solution.py:50
  326.6 21.4 %collective-permute-start.47 = (f32[3,1,64,512]{3,2,1,0:T(8,128)}, f32[3,1,64,512]{3,2,1,0:T(8,128)S(1)}, u32[]{:S(2)}, u32[]{:S(2)}) collective-permute-start(f32[3,1,64,512]{3,2,1,0:T(8,128)} %get-tuple-element.222), channel_id=1, source_target_pairs={{0,24},{1,25},{2,26},{3,27},{4,28},{5,29},{6,30},{7,31},{8,16},{9,... | collective-permute-start | bytes 1179656 | tf_op jit(solution)/shard_map/ppermute | solution.py:50
  334.4 8.8 %collective-permute-start.44 = (f32[344,128]{1,0:T(8,128)S(1)}, f32[344,128]{1,0:T(8,128)S(1)}, u32[]{:S(2)}, u32[]{:S(2)}) collective-permute-start(f32[344,128]{1,0:T(8,128)S(1)} %pad_maximum_fusion.8), channel_id=1, source_target_pairs={{0,8},{1,9},{2,10},{3,11},{4,12},{5,13},{6,14},{7,15},{8,0},{9,1},... | collective-permute-start | bytes 528392 | tf_op jit(solution)/shard_map/ppermute | solution.py:50
  334.5 12.0 %collective-permute-start.45 = (f32[344,128]{1,0:T(8,128)S(1)}, f32[344,128]{1,0:T(8,128)S(1)}, u32[]{:S(2)}, u32[]{:S(2)}) collective-permute-start(f32[344,128]{1,0:T(8,128)S(1)} %pad_maximum_fusion.8), channel_id=1, source_target_pairs={{0,12},{1,13},{2,14},{3,15},{4,8},{5,9},{6,10},{7,11},{8,4},{9,5},... | collective-permute-start | bytes 528392 | tf_op jit(solution)/shard_map/ppermute | solution.py:50
  337.0 9.5 %collective-permute-start.43 = (f32[344,128]{1,0:T(8,128)S(1)}, f32[344,128]{1,0:T(8,128)S(1)}, u32[]{:S(2)}, u32[]{:S(2)}) collective-permute-start(f32[344,128]{1,0:T(8,128)S(1)} %pad_maximum_fusion.8), channel_id=1, source_target_pairs={{0,4},{1,5},{2,6},{3,7},{4,0},{5,1},{6,2},{7,3},{8,12},{9,13},{10,... | collective-permute-start | bytes 528392 | tf_op jit(solution)/shard_map/ppermute | solution.py:50
  346.6 12.1 %collective-permute-start.46 = (f32[344,128]{1,0:T(8,128)S(1)}, f32[344,128]{1,0:T(8,128)S(1)}, u32[]{:S(2)}, u32[]{:S(2)}) collective-permute-start(f32[344,128]{1,0:T(8,128)S(1)} %add_add_fusion), channel_id=1, source_target_pairs={{0,24},{1,25},{2,26},{3,27},{4,28},{5,29},{6,30},{7,31},{8,16},{9,... | collective-permute-start | bytes 528392 | tf_op jit(solution)/shard_map/ppermute | solution.py:50
  (63 other events, 360.5 us)
Sparse Core Ops, SparseCore 0:
  12.6 80.1 all-gather.2
